TPU v7x, 256 devices: a whole 4x4x8 slice. The times are simulated.
256 devices in a mesh: ctx: 64 (over x, y, z_hi), head: 4 (over z_lo, core).
Axes of the slice: x: 4, y: 4, z: 8 (z_hi: 4, z_lo: 2; z = z_hi * 2 + z_lo), core: 2. Of those that a mesh axis runs over, the one named last changes fastest.
Arguments:
- queries: bfloat16 [16384, 2048], P('ctx', 'head'), may hold values from -160 to 160
- key_rows: bfloat16 [16384, 2048], P('ctx', 'head'), may hold values from -30 to 30
- value_rows: bfloat16 [16384, 2048], P('ctx', 'head'), may hold values from -6 to 6
- out_weight: bfloat16 [2048, 4096], P('head'), may hold values from -0.125 to 0.125
- upstream: bfloat16 [16384, 4096], P('ctx', 'head'), may hold values from -6 to 6
- summary_index: int32 [64, 128], P('ctx'), may hold values from 0 to 255, as said below
- stride_offset: int32 [64, 4], replicated, may hold values from 0 to 15
Outputs:
- layer_out: bfloat16 [16384, 4096], P('ctx', 'head')
- query_grad: bfloat16 [16384, 2048], P('ctx', 'head')
- key_grad: bfloat16 [16384, 2048], P('ctx', 'head')
- value_grad: bfloat16 [16384, 2048], P('ctx', 'head')
Inputs may be any that keep to these rules, and one draw needn't show every extreme that they name: `summary_index`: each row t lists 128 distinct positions within shard t.
All inputs are finite; a program needn't handle non-finite values.
Results may differ from a plain program's by a relative error of at most 0.015.
Values may be sent and summed in bfloat16 or wider, within the bound.
No kernel may reach another device: no remote copies, remote signals or barrier semaphores. Data moves between devices by JAX's collectives and lax.ppermute only.
A program may use at most 128 MiB of HBM per device.

v0:
```python
import jax
import jax.numpy as jnp
from jax import lax
from jax.sharding import PartitionSpec as P

HEAD_DIM = 128
STRIDE = 16


masked_fill = -1e30


def shifted(array, axis, by):
    count = lax.axis_size(axis)
    pairs = [(i, i + by) for i in range(count) if 0 <= i + by < count]
    return lax.ppermute(array, axis, pairs)


def attend_head(query_block, key_block, value_block, grad_block, allowed):
    scale_factor = query_block.shape[1] ** (-0.5)
    scores = (
        jnp.einsum("td,kd->tk", query_block, key_block, preferred_element_type=jnp.float32)
        * scale_factor
    )
    scores = jnp.where(allowed, scores, masked_fill)
    row_max = jnp.max(scores, axis=1, keepdims=True)
    exp_scores = jnp.exp(scores - row_max)
    row_sum = jnp.sum(exp_scores, axis=1, keepdims=True)
    normed = exp_scores / row_sum
    weights = normed.astype(jnp.bfloat16)
    attended = jnp.dot(weights, value_block, preferred_element_type=jnp.float32).astype(
        jnp.bfloat16
    )
    dprob = jnp.einsum("td,kd->tk", grad_block, value_block, preferred_element_type=jnp.float32)
    row_delta = jnp.sum(
        grad_block.astype(jnp.float32) * attended.astype(jnp.float32), axis=1, keepdims=True
    )
    dscore = (normed * (dprob - row_delta) * scale_factor).astype(jnp.bfloat16)
    query_part = jnp.dot(dscore, key_block, preferred_element_type=jnp.float32)
    return (attended, query_part, weights, dscore)


def shards(queries, key_rows, value_rows, out_weight, upstream, summary_index, stride_offset):
    per_shard = queries.shape[0]
    head_dim = HEAD_DIM
    width_local = queries.shape[1]
    groups = width_local // (4 * head_dim)
    triple = groups * 3
    summ = summary_index.shape[1]
    reach = per_shard // STRIDE
    shard_count = lax.axis_size("ctx")
    shard_at = lax.axis_index("ctx")
    attn_grad = jnp.einsum(
        "tc,rc->tr",
        lax.all_gather(upstream, "head", axis=1, tiled=True),
        out_weight,
        preferred_element_type=jnp.float32,
    ).astype(jnp.bfloat16)

    def split_heads(block):
        shaped = block.reshape(per_shard, groups, 4, head_dim)
        return (shaped[:, :, 0, :], shaped[:, :, 1:, :].reshape(per_shard, triple, head_dim))

    fixed_q, strided_q = split_heads(queries)
    fixed_k, strided_k = split_heads(key_rows)
    fixed_v, strided_v = split_heads(value_rows)
    fixed_g, strided_g = split_heads(attn_grad)
    positions = jnp.arange(per_shard, dtype=jnp.int32)
    causal = positions[:, None] >= positions[None, :]
    picked = summary_index[0]
    own_stack = jnp.stack(
        [
            fixed_k[picked].reshape(summ, groups * head_dim),
            fixed_v[picked].reshape(summ, groups * head_dim),
        ]
    )
    all_stack = lax.all_gather(own_stack, "ctx", axis=1, tiled=True)
    all_stack = all_stack.reshape(2, shard_count * summ, groups, head_dim)
    owners = jnp.arange(shard_count * summ, dtype=jnp.int32) // summ
    allowed_fixed = jnp.concatenate(
        [causal, jnp.broadcast_to((owners < shard_at)[None], (per_shard, shard_count * summ))], 1
    )
    fixed_out, fixed_qgrad, fixed_kgrad, fixed_vgrad, summary_weights, summary_dscore = (
        [],
        [],
        [],
        [],
        [],
        [],
    )
    group_num = 0
    key_set = jnp.concatenate([fixed_k[:, group_num], all_stack[0, :, group_num]], 0)
    value_set = jnp.concatenate([fixed_v[:, group_num], all_stack[1, :, group_num]], 0)
    attended, query_part, weights, dscore = attend_head(
        fixed_q[:, group_num], key_set, value_set, fixed_g[:, group_num], allowed_fixed
    )
    fixed_out.append(attended)
    fixed_qgrad.append(query_part)
    fixed_kgrad.append(
        jnp.einsum(
            "tk,td->kd",
            dscore[:, :per_shard],
            fixed_q[:, group_num],
            preferred_element_type=jnp.float32,
        )
    )
    fixed_vgrad.append(
        jnp.einsum(
            "tk,td->kd",
            weights[:, :per_shard],
            fixed_g[:, group_num],
            preferred_element_type=jnp.float32,
        )
    )
    summary_weights.append(weights[:, per_shard:])
    summary_dscore.append(dscore[:, per_shard:])
    count = shard_count * summ
    group_num = 0
    dscore_cols = summary_dscore[group_num]
    weight_cols = summary_weights[group_num]
    key_terms = [
        jnp.einsum(
            "tk,td->kd", dscore_cols, fixed_q[:, group_num], preferred_element_type=jnp.float32
        )
    ]
    value_terms = [
        jnp.einsum(
            "tk,td->kd", weight_cols, fixed_g[:, group_num], preferred_element_type=jnp.float32
        )
    ]
    returned_summary = lax.psum_scatter(
        jnp.concatenate(
            [
                jnp.stack(key_terms, 1).reshape(count, groups * head_dim),
                jnp.stack(value_terms, 1).reshape(count, groups * head_dim),
            ],
            1,
        ),
        "ctx",
        scatter_dimension=0,
        tiled=True,
    )
    summary_key_back = returned_summary[:, : groups * head_dim].reshape(summ, groups, head_dim)
    summary_value_back = returned_summary[:, groups * head_dim :].reshape(summ, groups, head_dim)
    fixed_kgrad = jnp.stack(fixed_kgrad, 1).at[picked].add(summary_key_back)
    fixed_vgrad = jnp.stack(fixed_vgrad, 1).at[picked].add(summary_value_back)
    fixed_out = jnp.stack(fixed_out, 1)
    fixed_qgrad = jnp.stack(fixed_qgrad, 1)
    flat_stack = jnp.stack(
        [
            strided_k.reshape(per_shard, triple * head_dim),
            strided_v.reshape(per_shard, triple * head_dim),
        ]
    )
    phases = jnp.arange(reach, dtype=jnp.int32) * STRIDE
    own_rows, target_rows, far_pieces, far_masks = ([], [], [], [])
    for slot_num in range(4):
        rows_here = stride_offset[shard_at, slot_num] + phases
        target = jnp.minimum(shard_at + slot_num + 1, shard_count - 1)
        rows_there = stride_offset[target, slot_num] + phases
        own_rows.append(rows_here)
        target_rows.append(rows_there)
        arrived = shifted(flat_stack, "ctx", slot_num + 1)
        far_pieces.append(jnp.take(arrived, rows_here, axis=1))
        far_masks.append(jnp.broadcast_to(shard_at - 1 - slot_num >= 0, (per_shard, reach)))
    far_stack = jnp.concatenate(far_pieces, 1).reshape(2, 4 * reach, triple, head_dim)
    allowed_strided = jnp.concatenate([causal] + far_masks, 1)
    strided_out, strided_qgrad, strided_kgrad, strided_vgrad, far_kgrad, far_vgrad = (
        [],
        [],
        [],
        [],
        [],
        [],
    )
    for head_num in range(triple):
        key_set = jnp.concatenate([strided_k[:, head_num], far_stack[0, :, head_num]], 0)
        value_set = jnp.concatenate([strided_v[:, head_num], far_stack[1, :, head_num]], 0)
        attended, query_part, weights, dscore = attend_head(
            strided_q[:, head_num], key_set, value_set, strided_g[:, head_num], allowed_strided
        )
        key_part = jnp.einsum(
            "tk,td->kd", dscore, strided_q[:, head_num], preferred_element_type=jnp.float32
        )
        value_part = jnp.einsum(
            "tk,td->kd", weights, strided_g[:, head_num], preferred_element_type=jnp.float32
        )
        strided_out.append(attended)
        strided_qgrad.append(query_part)
        strided_kgrad.append(key_part[:per_shard])
        strided_vgrad.append(value_part[:per_shard])
        far_kgrad.append(key_part[per_shard:])
        far_vgrad.append(value_part[per_shard:])
    far_terms = jnp.stack(
        [
            jnp.stack(far_kgrad, 1).reshape(4 * reach, triple * head_dim),
            jnp.stack(far_vgrad, 1).reshape(4 * reach, triple * head_dim),
        ]
    )
    strided_total = jnp.stack(
        [
            jnp.stack(strided_kgrad, 1).reshape(per_shard, triple * head_dim),
            jnp.stack(strided_vgrad, 1).reshape(per_shard, triple * head_dim),
        ]
    )
    for slot_num in range(4):
        piece = far_terms[:, slot_num * reach : (slot_num + 1) * reach]
        spread = (
            jnp.zeros((2, per_shard, triple * head_dim), jnp.float32)
            .at[:, own_rows[slot_num]]
            .set(piece)
        )
        strided_total = strided_total + shifted(
            spread.astype(jnp.bfloat16), "ctx", -(slot_num + 1)
        ).astype(spread.dtype)

    def join_heads(fixed, strided):
        joined = jnp.concatenate(
            [fixed[:, :, None, :], strided.reshape(per_shard, groups, 3, head_dim)], 2
        )
        return joined.reshape(per_shard, width_local)

    attended_all = join_heads(fixed_out, jnp.stack(strided_out, 1))
    partial_out = jnp.dot(attended_all, out_weight, preferred_element_type=jnp.float32)
    layer_out = lax.psum_scatter(
        partial_out.astype(jnp.bfloat16), "head", scatter_dimension=1, tiled=True
    )
    query_grad = join_heads(fixed_qgrad, jnp.stack(strided_qgrad, 1)).astype(jnp.bfloat16)
    key_grad = join_heads(
        fixed_kgrad, strided_total[0].reshape(per_shard, triple, head_dim)
    ).astype(jnp.bfloat16)
    value_grad = join_heads(
        fixed_vgrad, strided_total[1].reshape(per_shard, triple, head_dim)
    ).astype(jnp.bfloat16)
    return (layer_out, query_grad, key_grad, value_grad)


def solution(mesh):
    return jax.shard_map(
        shards,
        mesh=mesh,
        in_specs=(
            P("ctx", "head"),
            P("ctx", "head"),
            P("ctx", "head"),
            P("head", None),
            P("ctx", "head"),
            P("ctx", None),
            P(),
        ),
        out_specs=(P("ctx", "head"), P("ctx", "head"), P("ctx", "head"), P("ctx", "head")),
        check_vma=False,
    )
```

profile of v0, /device:TPU:24, one launch (start us, length us, event | category | flops | bytes accessed | tf_op | source)
XLA Modules:
  0.0 640.7 jit_solution(463656224135915347)
XLA Ops:
  14.9 29.2 %all-gather.5.cloned.1.call-done = bf16[256,4096]{1,0:T(8,128)(2,1)} async-done(((bf16[256,1024]{1,0:T(8,128)(2,1)}), bf16[256,4096]{1,0:T(8,128)(2,1)}) %all-gather.5.cloned.1.call-update) | async-done | bytes 2097168 | tf_op jit(solution)/shard_map/all_gather | solution.py:55
  44.1 4.1 convolution_convert_fusion.1
  48.4 89.1 %all-gather.3.cloned.1.call-done = bf16[2,8192,128]{2,1,0:T(8,128)(2,1)} async-done(((bf16[2,128,128]{2,1,0:T(8,128)(2,1)}), bf16[2,8192,128]{2,1,0:T(8,128)(2,1)}) %all-gather.3.cloned.1.call-update) | async-done | bytes 4194320 | tf_op jit(solution)/shard_map/all_gather | solution.py:77
  137.5 2.5 slice_bitcast_fusion
  140.0 1.8 fusion.96
  146.5 1.7 multiply_reduce_fusion.3
  148.2 2.7 fusion.4
  152.9 3.8 pad_maximum_fusion
  161.1 1.6 pad_maximum_fusion.13
  162.7 3.3 collective-permute-start.3
  166.0 3.8 collective-permute-start.2
  169.8 6.4 collective-permute-start.1
  176.1 1.9 collective-permute-start
  188.8 1.6 slice_bitcast_fusion.22
  191.7 1.7 gather_fusion.5
  193.4 20.9 %collective-permute-done.2 = bf16[2,256,384]{2,0,1:T(2,128)(2,1)} collective-permute-done((bf16[2,256,384]{2,0,1:T(2,128)(2,1)}, bf16[2,256,384]{2,0,1:T(2,128)(2,1)}, u32[]{:S(2)}, u32[]{:S(2)}) %collective-permute-start.2) | collective-permute-done | bytes 393248 | tf_op jit(solution)/shard_map/ppermute | solution.py:16
  228.4 1.9 multiply_reduce_fusion.2
  238.3 4.8 convolution_convert_fusion
  246.8 5.3 collective-permute-start.5
  252.4 1.9 scatter_fusion.2
  255.3 1.9 collective-permute-start.6
  257.5 1.9 scatter_fusion.3
  260.4 1.9 collective-permute-start.7
  264.6 4.4 collective-permute-start.4
  270.1 1.8 fusion.32
  279.2 22.1 %collective-permute-done.6 = bf16[2,256,384]{2,0,1:T(2,128)(2,1)} collective-permute-done((bf16[2,256,384]{2,0,1:T(2,128)(2,1)}, bf16[2,256,384]{2,0,1:T(2,128)(2,1)}, u32[]{:S(2)}, u32[]{:S(2)}) %collective-permute-start.6) | collective-permute-done | bytes 393248 | tf_op jit(solution)/shard_map/ppermute | solution.py:16
  301.3 10.8 %collective-permute-done.4 = bf16[2,256,384]{2,0,1:T(2,128)(2,1)} collective-permute-done((bf16[2,256,384]{2,0,1:T(2,128)(2,1)}, bf16[2,256,384]{2,0,1:T(2,128)(2,1)}, u32[]{:S(2)}, u32[]{:S(2)}) %collective-permute-start.4) | collective-permute-done | bytes 393248 | tf_op jit(solution)/shard_map/ppermute | solution.py:16
  312.1 2.9 fusion.38
  316.4 3.3 fusion.34
  322.8 234.4 %reduce-scatter.5.cloned.1.call-done = f32[128,256]{1,0:T(8,128)} async-done(((f32[8192,256]{1,0:T(8,128)}), f32[128,256]{1,0:T(8,128)}) %reduce-scatter.5.cloned.1.call-update) | async-done | bytes 131088 | tf_op jit(solution)/shard_map/reduce_scatter | solution.py:131
  557.2 1.6 scatter_custom_fusion.5
  562.5 71.7 %reduce-scatter.3.cloned.1.call-done = bf16[256,1024]{1,0:T(8,128)(2,1)} async-done(((bf16[256,4096]{1,0:T(8,128)(2,1)}), bf16[256,1024]{1,0:T(8,128)(2,1)}) %reduce-scatter.3.cloned.1.call-update) | async-done | bytes 524304 | tf_op jit(solution)/shard_map/reduce_scatter | solution.py:225
  (224 shorter events, 76.9 us)
Async XLA Ops:
  7.2 36.9 %all-gather.5.cloned.1.call-start = ((), (), s32[]{:S(2)}) async-start(), calls=%async_computation.4 | async-start | bytes 2621440 | tf_op jit(solution)/shard_map/all_gather | solution.py:55
  7.9 129.6 %all-gather.3.cloned.1.call-start = ((), (), s32[]{:S(2)}) async-start(), calls=%async_computation.2 | async-start | bytes 4259840 | tf_op jit(solution)/shard_map/all_gather | solution.py:77
  13.7 543.5 %reduce-scatter.5.cloned.1.call-start = ((), (), s32[]{:S(2)}) async-start(), calls=%async_computation.5 | async-start | bytes 8519680 | tf_op jit(solution)/shard_map/reduce_scatter | solution.py:131
  14.8 176.8 %copy-start.2 = (bf16[256,512]{0,1:T(8,128)(2,1)}, bf16[256,512]{0,1:T(8,128)(2,1)S(1)}, u32[]{:S(2)}) copy-start(bf16[256,512]{0,1:T(8,128)(2,1)S(1)} %copy.56) | copy-start | bytes 786436
  48.4 177.9 %copy-start.3 = (bf16[256,512]{0,1:T(8,128)(2,1)}, bf16[256,512]{0,1:T(8,128)(2,1)S(1)}, u32[]{:S(2)}) copy-start(bf16[256,512]{0,1:T(8,128)(2,1)S(1)} %copy.70) | copy-start | bytes 786436
  156.7 21.4 %copy-start.33 = (s32[64,4]{0,1:T(4,128)S(1)}, s32[64,4]{0,1:T(4,128)}, u32[]{:S(2)}) copy-start(s32[64,4]{0,1:T(4,128)} %param.15) | copy-start | bytes 3076
  156.7 477.5 %reduce-scatter.3.cloned.1.call-start = ((), (), s32[]{:S(2)}) async-start(), calls=%async_computation.3 | async-start | bytes 2621440 | tf_op jit(solution)/shard_map/reduce_scatter | solution.py:225
  162.7 28.9 %collective-permute-start.3 = (bf16[2,256,384]{2,0,1:T(2,128)(2,1)}, bf16[2,256,384]{2,0,1:T(2,128)(2,1)}, u32[]{:S(2)}, u32[]{:S(2)}) collective-permute-start(bf16[2,256,384]{2,0,1:T(2,128)(2,1)} %pad_maximum_fusion.13), channel_id=1, source_target_pairs={{0,16},{4,20},{8,24},{12,28},{16,32},{20,36},{24,40},{28,44},{32,4... | collective-permute-start | bytes 1179656 | tf_op jit(solution)/shard_map/ppermute | solution.py:16
  166.0 48.2 %collective-permute-start.2 = (bf16[2,256,384]{2,0,1:T(2,128)(2,1)}, bf16[2,256,384]{2,0,1:T(2,128)(2,1)}, u32[]{:S(2)}, u32[]{:S(2)}) collective-permute-start(bf16[2,256,384]{2,0,1:T(2,128)(2,1)} %pad_maximum_fusion.13), channel_id=1, source_target_pairs={{0,12},{4,16},{8,20},{12,24},{16,28},{20,32},{24,36},{28,40},{32,4... | collective-permute-start | bytes 1179656 | tf_op jit(solution)/shard_map/ppermute | solution.py:16
  169.8 46.1 %collective-permute-start.1 = (bf16[2,256,384]{2,0,1:T(2,128)(2,1)}, bf16[2,256,384]{2,0,1:T(2,128)(2,1)}, u32[]{:S(2)}, u32[]{:S(2)}) collective-permute-start(bf16[2,256,384]{2,0,1:T(2,128)(2,1)} %pad_maximum_fusion.13), channel_id=1, source_target_pairs={{0,8},{4,12},{8,16},{12,20},{16,24},{20,28},{24,32},{28,36},{32,40... | collective-permute-start | bytes 1179656 | tf_op jit(solution)/shard_map/ppermute | solution.py:16
  176.1 41.3 %collective-permute-start = (bf16[2,256,384]{2,0,1:T(2,128)(2,1)}, bf16[2,256,384]{2,0,1:T(2,128)(2,1)}, u32[]{:S(2)}, u32[]{:S(2)}) collective-permute-start(bf16[2,256,384]{2,0,1:T(2,128)(2,1)} %pad_maximum_fusion.13), channel_id=1, source_target_pairs={{0,4},{4,8},{8,12},{12,16},{16,20},{20,24},{24,28},{28,32},{32,36}... | collective-permute-start | bytes 1179656 | tf_op jit(solution)/shard_map/ppermute | solution.py:16
  188.8 37.9 %copy-start.17 = (bf16[256,128]{0,1:T(8,128)(2,1)}, bf16[256,128]{0,1:T(8,128)(2,1)S(1)}, u32[]{:S(2)}) copy-start(bf16[256,128]{0,1:T(8,128)(2,1)S(1)} %get-tuple-element.41) | copy-start | bytes 196612
  188.8 37.9 %copy-start.18 = (bf16[256,128]{0,1:T(8,128)(2,1)}, bf16[256,128]{0,1:T(8,128)(2,1)S(1)}, u32[]{:S(2)}) copy-start(bf16[256,128]{0,1:T(8,128)(2,1)S(1)} %get-tuple-element.42) | copy-start | bytes 196612
  188.8 37.9 %copy-start.19 = (bf16[256,128]{0,1:T(8,128)(2,1)}, bf16[256,128]{0,1:T(8,128)(2,1)S(1)}, u32[]{:S(2)}) copy-start(bf16[256,128]{0,1:T(8,128)(2,1)S(1)} %get-tuple-element.43) | copy-start | bytes 196612
  191.6 28.9 %copy-start.30 = (pred[256,320]{0,1:T(8,128)(4,1)}, pred[256,320]{0,1:T(8,128)(4,1)S(1)}, u32[]{:S(2)}) copy-start(pred[256,320]{0,1:T(8,128)(4,1)S(1)} %constant_dynamic-update-slice_fusion) | copy-start | bytes 245764
  191.6 30.2 %copy-start.5 = (bf16[256,3,128]{0,2,1:T(8,128)(2,1)}, bf16[256,3,128]{0,2,1:T(8,128)(2,1)S(1)}, u32[]{:S(2)}) copy-start(bf16[256,3,128]{0,2,1:T(8,128)(2,1)S(1)} %slice_bitcast_fusion.3) | copy-start | bytes 589828
  191.7 32.8 %copy-start.20 = (bf16[256,128]{0,1:T(8,128)(2,1)S(1)}, bf16[256,128]{0,1:T(8,128)(2,1)}, u32[]{:S(2)}) copy-start(bf16[256,128]{0,1:T(8,128)(2,1)} %get-tuple-element.33) | copy-start | bytes 196612
  219.9 5.5 copy-start.21
  220.5 5.7 copy-start.29
  223.0 8.7 %copy-start.6 = (bf16[256,3,128]{0,2,1:T(8,128)(2,1)S(1)}, bf16[256,3,128]{0,2,1:T(8,128)(2,1)}, u32[]{:S(2)}) copy-start(bf16[256,3,128]{0,2,1:T(8,128)(2,1)} %copy-done.5) | copy-start | bytes 589828
  226.3 7.0 %copy-start.28 = (bf16[64,128]{0,1:T(8,128)(2,1)S(1)}, bf16[64,128]{0,1:T(8,128)(2,1)}, u32[]{:S(2)}) copy-start(bf16[64,128]{0,1:T(8,128)(2,1)} %copy-done.27) | copy-start | bytes 49156
  233.3 9.8 %copy-start.15 = (f32[320,128]{1,0:T(8,128)}, f32[320,128]{1,0:T(8,128)S(1)}, u32[]{:S(2)}) copy-start(f32[320,128]{1,0:T(8,128)S(1)} %fusion.58) | copy-start | bytes 491524
  234.5 8.6 %copy-start.8 = (bf16[256,320]{0,1:T(8,128)(2,1)}, bf16[256,320]{0,1:T(8,128)(2,1)S(1)}, u32[]{:S(2)}) copy-start(bf16[256,320]{0,1:T(8,128)(2,1)S(1)} %fusion.26) | copy-start | bytes 491524
  238.3 6.5 %copy-start.35 = (s32[16]{0:T(128)S(1)}, s32[16]{0:T(128)}, u32[]{:S(2)}) copy-start(s32[16]{0:T(128)} %fusion.73) | copy-start | bytes 196
  243.2 19.4 %copy-start.34 = (s32[16]{0:T(128)S(1)}, s32[16]{0:T(128)}, u32[]{:S(2)}) copy-start(s32[16]{0:T(128)} %fusion.72) | copy-start | bytes 196
  245.8 24.3 %copy-start.26 = (bf16[64,128]{0,1:T(8,128)(2,1)S(1)}, bf16[64,128]{0,1:T(8,128)(2,1)}, u32[]{:S(2)}) copy-start(bf16[64,128]{0,1:T(8,128)(2,1)} %copy-done.25) | copy-start | bytes 49156
  246.8 25.0 %copy-start.10 = (f32[320,128]{1,0:T(8,128)S(1)}, f32[320,128]{1,0:T(8,128)}, u32[]{:S(2)}) copy-start(f32[320,128]{1,0:T(8,128)} %copy-done.9) | copy-start | bytes 491524
  246.8 32.4 %collective-permute-start.5 = (bf16[2,256,384]{2,0,1:T(2,128)(2,1)}, bf16[2,256,384]{2,0,1:T(2,128)(2,1)}, u32[]{:S(2)}, u32[]{:S(2)}) collective-permute-start(bf16[2,256,384]{2,0,1:T(2,128)(2,1)} %convert_element_type.127), channel_id=1, source_target_pairs={{8,0},{12,4},{16,8},{20,12},{24,16},{28,20},{32,24},{36,28},{40,32... | collective-permute-start | bytes 1179656 | tf_op jit(solution)/shard_map/ppermute | solution.py:16
  255.3 46.0 %collective-permute-start.6 = (bf16[2,256,384]{2,0,1:T(2,128)(2,1)}, bf16[2,256,384]{2,0,1:T(2,128)(2,1)}, u32[]{:S(2)}, u32[]{:S(2)}) collective-permute-start(bf16[2,256,384]{2,0,1:T(2,128)(2,1)} %convert_element_type.129), channel_id=1, source_target_pairs={{12,0},{16,4},{20,8},{24,12},{28,16},{32,20},{36,24},{40,28},{44,3... | collective-permute-start | bytes 1179656 | tf_op jit(solution)/shard_map/ppermute | solution.py:16
  260.4 40.9 %collective-permute-start.7 = (bf16[2,256,384]{2,0,1:T(2,128)(2,1)}, bf16[2,256,384]{2,0,1:T(2,128)(2,1)}, u32[]{:S(2)}, u32[]{:S(2)}) collective-permute-start(bf16[2,256,384]{2,0,1:T(2,128)(2,1)} %convert_element_type.131), channel_id=1, source_target_pairs={{16,0},{20,4},{24,8},{28,12},{32,16},{36,20},{40,24},{44,28},{48,3... | collective-permute-start | bytes 1179656 | tf_op jit(solution)/shard_map/ppermute | solution.py:16
  263.6 12.2 %copy-start.23 = (bf16[64,128]{0,1:T(8,128)(2,1)S(1)}, bf16[64,128]{0,1:T(8,128)(2,1)}, u32[]{:S(2)}) copy-start(bf16[64,128]{0,1:T(8,128)(2,1)} %copy-done.22) | copy-start | bytes 49156
  264.6 47.5 %collective-permute-start.4 = (bf16[2,256,384]{2,0,1:T(2,128)(2,1)}, bf16[2,256,384]{2,0,1:T(2,128)(2,1)}, u32[]{:S(2)}, u32[]{:S(2)}) collective-permute-start(bf16[2,256,384]{2,0,1:T(2,128)(2,1)} %convert_element_type.125), channel_id=1, source_target_pairs={{4,0},{8,4},{12,8},{16,12},{20,16},{24,20},{28,24},{32,28},{36,32}... | collective-permute-start | bytes 1179656 | tf_op jit(solution)/shard_map/ppermute | solution.py:16
  (17 other events, 31.8 us)
Sparse Core Ops, SparseCore 0:
  9.8 34.2 all-gather.4
  48.0 89.4 all-gather.2
  156.8 400.3 reduce-scatter.4
  560.2 73.9 reduce-scatter.2
where the time goes:
time: 644 us; the launch traced here: 641 us
  waiting for transfers between devices  480 us (75%)
  local copies, waits for them, and re-layouts  43.5 us (7%)
  matrix products  38.9 us (6%)
  other arithmetic  33.6 us (5%)
  starting transfers between devices  29.2 us (5%)
  between operations  15 us (2%)
    reduce_scatter x1, waiting for transfers between devices, shards(): lax.psum_scatter(jnp.concatenate([jnp.stack(key_terms, 1).reshape(count,...  234 us
    all_gather x1, waiting for transfers between devices, shards(): all_stack = lax.all_gather(own_stack, 'ctx', axis=1, tiled=True)  89.1 us
    reduce_scatter x1, waiting for transfers between devices, shards(): lax.psum_scatter(partial_out.astype(jnp.bfloat16), 'head', scatter_dimens...  71.7 us
    ppermute x8, waiting for transfers between devices, shifted(): return lax.ppermute(array, axis, pairs)  55.3 us
    all_gather x1, waiting for transfers between devices, shards(): lax.all_gather(upstream, 'head', axis=1, tiled=True)  29.2 us
    ppermute x8, starting transfers between devices, shifted(): return lax.ppermute(array, axis, pairs)  28.9 us
  transfers between devices with their start and end apart: 12, of which 8 were waited for; matrix products, arithmetic and copies ran while one was open for 15% of the time, Pallas kernels for 0%

commit v1 on v0

v1 whole, which is shorter than its diff:
```python
import functools

import jax
import jax.numpy as jnp
from jax import lax
from jax.experimental import pallas as pl
from jax.experimental.pallas import tpu as pltpu
from jax.sharding import Mesh
from jax.sharding import PartitionSpec as P

HEAD = 128
TOK = 256
SUMM = 128
STRIDE = 16
REACH = TOK // STRIDE
ROWS = 16
GROUP = 4
STAT = 64
FAR = 6 * REACH
SCALE = HEAD ** (-0.5)
NEG = -1e30
F32 = jnp.float32
BF = jnp.bfloat16

VM = pl.BlockSpec(memory_space=pltpu.VMEM)
SM = pl.BlockSpec(memory_space=pltpu.SMEM)


def nn(a, b):
    return lax.dot_general(a, b, (((1,), (0,)), ((), ())), preferred_element_type=F32)


def nt(a, b):
    return lax.dot_general(a, b, (((1,), (1,)), ((), ())), preferred_element_type=F32)


def tn(a, b):
    return lax.dot_general(a, b, (((0,), (0,)), ((), ())), preferred_element_type=F32)


def iota(shape, dim):
    return lax.broadcasted_iota(jnp.int32, shape, dim)


def summary_select(sidx):
    return (iota((TOK, SUMM), 0) == sidx).astype(F32).astype(BF)


def stride_select(soff, shard):
    row, col = iota((4 * REACH, TOK), 0), iota((4 * REACH, TOK), 1)
    slot = row // REACH
    want = (row % REACH) * STRIDE
    for u in range(4):
        there = jnp.minimum(shard + 1 + u, ROWS * GROUP - 1)
        want = want + jnp.where(slot == u, soff[there, u], 0)
    return (want == col).astype(F32).astype(BF)


def call(kernel, outs, ins, flops, scratch=(), name=None, vmem=50):
    moved = sum(
        s.size * jnp.dtype(s.dtype).itemsize for s in list(outs) + list(ins)
    )
    return pl.pallas_call(
        kernel,
        out_shape=tuple(outs),
        in_specs=[SM if s.dtype == jnp.int32 and s.shape != (1, SUMM) else VM for s in ins],
        out_specs=tuple(VM for _ in outs),
        scratch_shapes=list(scratch),
        compiler_params=pltpu.CompilerParams(vmem_limit_bytes=vmem * 2**20),
        cost_estimate=pl.CostEstimate(
            flops=flops, bytes_accessed=moved, transcendentals=0
        ),
        name=name,
    )(*ins)


def sds(shape, dtype=BF):
    return jax.ShapeDtypeStruct(shape, dtype)


def prep_kernel(meta, soff, sidx, q, k, v, kvb, qb, picks):
    pick = summary_select(sidx[...])
    kv = jnp.concatenate([k[:, :HEAD], v[:, :HEAD]], 1)
    kv = tn(pick, kv).astype(BF)
    for i in range(ROWS):
        kvb[i] = kv
    for i in range(GROUP):
        qb[i] = q[:, :HEAD]
    shard = GROUP * meta[0] + meta[1]
    sel = stride_select(soff, shard)
    got = nn(sel, jnp.concatenate([k[:, HEAD:], v[:, HEAD:]], 1)).astype(BF)
    for u in range(4):
        for h in range(6):
            picks[u, h * REACH : (h + 1) * REACH, :] = got[
                u * REACH : (u + 1) * REACH, h * HEAD : (h + 1) * HEAD
            ]


def grad_kernel(meta, up, up_c, up_z, up_zc, w, picks, before, g, gb):
    zl, c = meta[2], meta[3]
    wide = up.shape[1]
    acc = None
    for ref, z, core in (
        (up, zl, c),
        (up_c, zl, 1 - c),
        (up_z, 1 - zl, c),
        (up_zc, 1 - zl, 1 - c),
    ):
        at = pl.multiple_of((2 * z + core) * wide, wide)
        part = nt(ref[...], w[:, pl.ds(at, wide)])
        acc = part if acc is None else acc + part
    full = acc.astype(BF)
    g[...] = full
    zh = meta[1]
    for t in range(GROUP):
        gb[t, :TOK, :] = full[:, :HEAD]
        u = lax.rem(t - zh - 1 + 2 * GROUP, GROUP)

        @pl.when(t > zh)
        def _(t=t, u=u):
            gb[t, TOK:, :] = picks[u]

        @pl.when(t <= zh)
        def _(t=t, u=u):
            gb[t, TOK:, :] = before[u]


def causal_mask():
    return iota((TOK, TOK), 0) >= iota((TOK, TOK), 1)


def lanes(a):
    return jnp.broadcast_to(a, (a.shape[0], HEAD))


def fold(a, how):
    out = a[:, :HEAD]
    for j in range(1, a.shape[1] // HEAD):
        out = how(out, a[:, j * HEAD : (j + 1) * HEAD])
    return out


def split3(a):
    hi = a.astype(BF).astype(F32)
    mid = (a - hi).astype(BF).astype(F32)
    return hi, mid, (a - hi - mid).astype(BF).astype(F32)


def stat_rows(log_sums, dots):
    eye = (iota((TOK, TOK), 0) == iota((TOK, TOK), 1)).astype(F32).astype(BF)
    lane = iota((TOK, HEAD), 1)
    total = None
    for z in range(GROUP):
        parts = split3(log_sums[z]) + split3(dots[z])
        cols = jnp.zeros((TOK, HEAD), F32)
        for j, part in enumerate(parts):
            cols = jnp.where(lane == 8 * z + j, part, cols)
        rows = tn(cols.astype(BF), eye)[: 8 * GROUP]
        total = rows if total is None else total + rows
    return jnp.concatenate([total[:, :HEAD], total[:, HEAD:]], 0).astype(BF)


def read_stats(stats, z):
    row = iota((8 * GROUP, 2 * HEAD), 0)
    col = iota((8 * GROUP, 2 * HEAD), 1)
    first = jnp.where(col < HEAD, 8 * z, 8 * z + 3)
    pick = ((row >= first) & (row < first + 3)).astype(F32).astype(BF)
    both = jnp.concatenate(
        [tn(stats[: STAT // 2], pick), tn(stats[STAT // 2 :], pick)], 0
    )
    return both[:, :HEAD], both[:, HEAD:]


def forward_kernel(meta, qa, kva, ga, k, v, ob, s_ref):
    row, zh = meta[0], meta[1]
    total = GROUP * TOK
    q = qa[...].reshape(total, HEAD)
    g = ga[:, :TOK, :].reshape(total, HEAD)
    limit = HEAD * (row + (iota((total, 1), 0) // TOK > zh).astype(jnp.int32))
    wide = 2 * SUMM
    tiles = ROWS * SUMM // wide
    top = jnp.full((total, HEAD), NEG, F32)
    for j in range(tiles):
        s = nt(q, kva[j * wide : (j + 1) * wide, :HEAD]) * SCALE
        s = jnp.where(iota((total, wide), 1) + j * wide < limit, s, NEG)
        s_ref[:, j * wide : (j + 1) * wide] = s
        top = jnp.maximum(top, fold(s, jnp.maximum))
    top = jnp.max(top, axis=1, keepdims=True)
    shift = jnp.maximum(top, 0.5 * NEG)
    sums = jnp.zeros((total, HEAD), F32)
    dots = jnp.zeros((total, HEAD), F32)
    out = jnp.zeros((total, HEAD), F32)
    for j in range(tiles):
        at = slice(j * wide, (j + 1) * wide)
        e = jnp.exp(s_ref[:, at] - shift)
        value = kva[at, HEAD:]
        sums = sums + fold(e, jnp.add)
        dots = dots + fold(e * nt(g, value), jnp.add)
        out = out + nn(e.astype(BF), value)
    sums = jnp.sum(sums, axis=1, keepdims=True)
    dots = jnp.sum(dots, axis=1, keepdims=True)
    some = sums > 0
    safe = jnp.where(some, sums, 1.0)
    log_sum = lanes(jnp.where(some, top + jnp.log(safe), NEG))
    inv = 1.0 / safe
    dots = lanes(dots * inv)
    out = out * inv

    own_q, own_g = qa[zh], ga[zh, :TOK, :]
    s = jnp.where(causal_mask(), nt(own_q, k[...]) * SCALE, NEG)
    own_top = jnp.max(s, axis=1, keepdims=True)
    e = jnp.exp(s - own_top)
    own_sum = jnp.sum(e, axis=1, keepdims=True)
    own_inv = 1.0 / own_sum
    own_dot = lanes(
        jnp.sum(e * nt(own_g, v[...]), axis=1, keepdims=True) * own_inv
    )
    own_out = nn(e.astype(BF), v[...]) * own_inv
    own_log = lanes(own_top + jnp.log(own_sum))

    all_logs, all_dots = [], []
    for z in range(GROUP):
        at = slice(z * TOK, (z + 1) * TOK)
        la = log_sum[at]
        lb = jnp.where(zh == z, own_log, NEG)
        most = jnp.maximum(la, lb)
        wa, wb = jnp.exp(la - most), jnp.exp(lb - most)
        both = wa + wb
        wa, wb = wa / both, wb / both
        all_logs.append(most + jnp.log(both))
        all_dots.append(wa * dots[at] + wb * own_dot)
        ob[z, :TOK, :] = (wa * out[at] + wb * own_out).astype(BF)
    stats = stat_rows(all_logs, all_dots)
    for z in range(GROUP):
        ob[z, TOK:, :] = stats


def merged(oa, z):
    parts = [read_stats(oa[d, TOK:, :], z) for d in range(GROUP)]
    most = functools.reduce(jnp.maximum, [p[0] for p in parts])
    shares = [jnp.exp(p[0] - most) for p in parts]
    both = functools.reduce(jnp.add, shares)
    shares = [s / both for s in shares]
    dot = functools.reduce(jnp.add, [s * p[1] for s, p in zip(shares, parts)])
    return most + jnp.log(both), dot, shares


def backward_kernel(meta, oa, qa, kva, ga, k, v, far, dkv, dqb, own, dq_ref, stat_ref):
    row, zh = meta[0], meta[1]
    total = GROUP * TOK
    for z in range(GROUP):
        at = slice(z * TOK, (z + 1) * TOK)
        log_sum, dot, _ = merged(oa, z)
        stat_ref[0, at] = log_sum
        stat_ref[1, at] = dot
        dqb[z, TOK:, :] = far[z]
    dq_ref[...] = jnp.zeros((total, HEAD), F32)
    wide = 2 * SUMM
    for j in range(ROWS * SUMM // wide):
        at = slice(j * wide, (j + 1) * wide)

        @pl.when(2 * j <= row)
        def _(j=j, at=at):
            q = qa[...].reshape(total, HEAD)
            g = ga[:, :TOK, :].reshape(total, HEAD)
            limit = HEAD * (row + (iota((total, 1), 0) // TOK > zh).astype(jnp.int32))
            key, value = kva[at, :HEAD], kva[at, HEAD:]
            log_sum = jnp.concatenate([stat_ref[0]] * 2, 1)
            dot = jnp.concatenate([stat_ref[1]] * 2, 1)
            s = nt(q, key) * SCALE
            s = jnp.where(iota((total, wide), 1) + j * wide < limit, s, NEG)
            p = jnp.exp(s - log_sum)
            dv = tn(p.astype(BF), g)
            ds = (p * (nt(g, value) - dot) * SCALE).astype(BF)
            dk = tn(ds, q)
            dq_ref[...] += nn(ds, key)
            dkv[at, :HEAD] = dk.astype(BF)
            dkv[at, HEAD:] = dv.astype(BF)

        @pl.when(2 * j > row)
        def _(at=at):
            dkv[at, :] = jnp.zeros((wide, 2 * HEAD), BF)

    own_at = pl.ds(pl.multiple_of(zh * TOK, TOK), TOK)
    own_q, own_g = qa[zh], ga[zh, :TOK, :]
    log_sum = jnp.concatenate([stat_ref[0, own_at]] * 2, 1)
    dot = jnp.concatenate([stat_ref[1, own_at]] * 2, 1)
    s = jnp.where(causal_mask(), nt(own_q, k[...]) * SCALE, NEG)
    p = jnp.exp(s - log_sum)
    own[:, HEAD:] = tn(p.astype(BF), own_g)
    ds = (p * (nt(own_g, v[...]) - dot) * SCALE).astype(BF)
    own[:, :HEAD] = tn(ds, own_q)
    dq_ref[own_at] += nn(ds, k[...])
    for z in range(GROUP):
        dqb[z, :TOK, :] = dq_ref[z * TOK : (z + 1) * TOK].astype(BF)


def strided_kernel(meta, q, k, v, g, ga, o, dq, dkv, far):
    row, zh = meta[0], meta[1]
    source = iota((TOK, 4 * REACH), 1) // REACH
    far_ok = (source < zh) | (jnp.full((TOK, 4 * REACH), row, jnp.int32) > 0)
    near_ok = causal_mask()
    for h in range(3):
        at = slice((h + 1) * HEAD, (h + 2) * HEAD)
        to = slice(h * HEAD, (h + 1) * HEAD)
        qh, kh, vh, gh = q[:, at], k[:, at], v[:, at], g[:, at]
        kf = ga[:, TOK + h * REACH : TOK + (h + 1) * REACH, :]
        vf = ga[:, TOK + (h + 3) * REACH : TOK + (h + 4) * REACH, :]
        kf, vf = kf.reshape(4 * REACH, HEAD), vf.reshape(4 * REACH, HEAD)
        s = jnp.where(near_ok, nt(qh, kh) * SCALE, NEG)
        sf = jnp.where(far_ok, nt(qh, kf) * SCALE, NEG)
        top = jnp.maximum(
            jnp.max(s, axis=1, keepdims=True), jnp.max(sf, axis=1, keepdims=True)
        )
        e, ef = jnp.exp(s - top), jnp.exp(sf - top)
        inv = 1.0 / (
            jnp.sum(e, axis=1, keepdims=True) + jnp.sum(ef, axis=1, keepdims=True)
        )
        p, pf = e * inv, ef * inv
        w, wf = p.astype(BF), pf.astype(BF)
        out = (nn(w, vh) + nn(wf, vf)).astype(BF)
        o[:, to] = out
        delta = jnp.sum(gh.astype(F32) * out.astype(F32), axis=1, keepdims=True)
        ds = (p * (nt(gh, vh) - delta) * SCALE).astype(BF)
        dsf = (pf * (nt(gh, vf) - delta) * SCALE).astype(BF)
        dq[:, to] = (nn(ds, kh) + nn(dsf, kf)).astype(BF)
        dkv[:, to] = tn(ds, qh)
        dkv[:, 3 * HEAD + h * HEAD : 3 * HEAD + (h + 1) * HEAD] = tn(w, gh)
        dkf = tn(dsf, qh).astype(BF)
        dvf = tn(wf, gh).astype(BF)
        for z in range(GROUP):
            rows = slice(z * REACH, (z + 1) * REACH)
            far[z, h * REACH : (h + 1) * REACH, :] = dkf[rows]
            far[z, (h + 3) * REACH : (h + 4) * REACH, :] = dvf[rows]


def project_kernel(meta, oa, o, w, keep, keep_z, send, send_z):
    zh, zl, c = meta[1], meta[2], meta[3]
    _, _, shares = merged(oa, zh)
    fixed = functools.reduce(
        jnp.add, [shares[d] * oa[d, :TOK, :].astype(F32) for d in range(GROUP)]
    )
    att = jnp.concatenate([fixed.astype(BF), o[...]], 1)
    wide = keep.shape[1]
    for ref, z, core in (
        (send_z, 1 - zl, 1 - c),
        (send, zl, 1 - c),
        (keep_z, 1 - zl, c),
        (keep, zl, c),
    ):
        at = pl.multiple_of((2 * z + core) * wide, wide)
        ref[...] = nn(att, w[:, pl.ds(at, wide)]).astype(BF)


def final_kernel(
    meta, soff, sidx, dkv, own, dq, after, strided_dq, strided, qg, kg, vg
):
    zh = meta[1]
    shard = GROUP * meta[0] + meta[1]
    pick = summary_select(sidx[...])
    fixed = own[...] + nn(jnp.concatenate([pick] * ROWS, 1), dkv[...])
    kg[:, :HEAD] = fixed[:, :HEAD].astype(BF)
    vg[:, :HEAD] = fixed[:, HEAD:].astype(BF)
    fixed = functools.reduce(
        jnp.add, [dq[z, :TOK, :].astype(F32) for z in range(GROUP)]
    )
    qg[:, :HEAD] = fixed.astype(BF)
    qg[:, HEAD:] = strided_dq[...]
    sel = stride_select(soff, shard)
    slots = []
    for u in range(4):
        t = lax.rem(zh + 1 + u, GROUP)
        here = dq[t, TOK:, :].astype(F32)
        there = after[t].astype(F32)
        block = jnp.where(t > zh, here, there).astype(BF)
        slots.append(
            jnp.concatenate(
                [block[h * REACH : (h + 1) * REACH] for h in range(6)], 1
            )
        )
    total = strided[...] + tn(sel, jnp.concatenate(slots, 0))
    kg[:, HEAD:] = total[:, : 3 * HEAD].astype(BF)
    vg[:, HEAD:] = total[:, 3 * HEAD :].astype(BF)


def swap(a, axis):
    return lax.ppermute(a, axis, [(0, 1), (1, 0)])


def shards(queries, key_rows, value_rows, out_weight, upstream, summary_index, soff):
    row = lax.axis_index(("x", "y"))
    zh, zl, c = lax.axis_index("zh"), lax.axis_index("zl"), lax.axis_index("c")
    meta = jnp.stack([row, zh, zl, c]).astype(jnp.int32)
    width = queries.shape[1]
    quarter = upstream.shape[1]
    plane = ("x", "y")
    matmul = 2 * GROUP * TOK * ROWS * SUMM * HEAD

    up_z = swap(upstream, "zl")
    up_c = swap(upstream, "c")
    kvb, qb, picks = call(
        prep_kernel,
        [sds((ROWS, SUMM, 2 * HEAD)), sds((GROUP, TOK, HEAD)), sds((4, FAR, HEAD))],
        [meta, soff, summary_index, queries, key_rows, value_rows],
        10**8,
        name="pick_rows",
    )
    before = lax.ppermute(picks, plane, [(i, i + 1) for i in range(ROWS - 1)])
    qa = lax.all_to_all(qb, "zh", 0, 0, tiled=True)
    kva = lax.all_to_all(kvb, plane, 0, 0, tiled=True).reshape(ROWS * SUMM, 2 * HEAD)
    up_zc = swap(up_z, "c")
    g, gb = call(
        grad_kernel,
        [sds((TOK, width)), sds((GROUP, TOK + FAR, HEAD))],
        [meta, upstream, up_c, up_z, up_zc, out_weight, picks, before],
        2 * TOK * 4 * quarter * width,
        name="attention_grad",
    )
    ga = lax.all_to_all(gb, "zh", 0, 0, tiled=True)
    key0, value0 = key_rows[:, :HEAD], value_rows[:, :HEAD]
    (ob,) = call(
        forward_kernel,
        [sds((GROUP, TOK + STAT, HEAD))],
        [meta, qa, kva, ga, key0, value0],
        3 * matmul,
        [pltpu.VMEM((GROUP * TOK, ROWS * SUMM), F32)],
        name="fixed_forward",
    )
    oa = lax.all_to_all(ob, "zh", 0, 0, tiled=True)
    o_s, dq_s, dkv_s, far = call(
        strided_kernel,
        [
            sds((TOK, 3 * HEAD)),
            sds((TOK, 3 * HEAD)),
            sds((TOK, 6 * HEAD), F32),
            sds((GROUP, FAR, HEAD)),
        ],
        [meta, queries, key_rows, value_rows, g, ga],
        3 * 6 * 2 * TOK * 320 * HEAD,
        name="strided_heads",
    )
    keep, keep_z, send, send_z = call(
        project_kernel,
        [sds((TOK, quarter))] * 4,
        [meta, oa, o_s, out_weight],
        2 * TOK * 4 * quarter * width,
        name="project",
    )
    dkv, dqb, own = call(
        backward_kernel,
        [
            sds((ROWS * SUMM, 2 * HEAD)),
            sds((GROUP, TOK + FAR, HEAD)),
            sds((TOK, 2 * HEAD), F32),
        ],
        [meta, oa, qa, kva, ga, key0, value0, far],
        5 * matmul,
        [
            pltpu.VMEM((GROUP * TOK, HEAD), F32),
            pltpu.VMEM((2, GROUP * TOK, HEAD), F32),
        ],
        name="fixed_backward",
    )
    got_z = swap(send_z, "c")
    got = swap(send, "c")
    over = swap((keep_z.astype(F32) + got_z.astype(F32)).astype(BF), "zl")
    dkva = lax.all_to_all(
        dkv.reshape(ROWS, SUMM, 2 * HEAD), plane, 0, 0, tiled=True
    ).reshape(ROWS * SUMM, 2 * HEAD)
    dqa = lax.all_to_all(dqb, "zh", 0, 0, tiled=True)
    after = lax.ppermute(
        dqa[:, TOK:, :], plane, [(i + 1, i) for i in range(ROWS - 1)]
    )
    layer_out = (keep.astype(F32) + got.astype(F32) + over.astype(F32)).astype(BF)
    query_grad, key_grad, value_grad = call(
        final_kernel,
        [sds((TOK, width))] * 3,
        [meta, soff, summary_index, dkva, own, dqa, after, dq_s, dkv_s],
        3 * 10**8,
        name="join_grads",
    )
    return layer_out, query_grad, key_grad, value_grad


def solution(mesh):
    grid = Mesh(mesh.devices.reshape(4, 4, 4, 2, 2), ("x", "y", "zh", "zl", "c"))
    ctx, head = ("x", "y", "zh"), ("zl", "c")
    return jax.shard_map(
        shards,
        mesh=grid,
        in_specs=(
            P(ctx, head),
            P(ctx, head),
            P(ctx, head),
            P(head, None),
            P(ctx, head),
            P(ctx, None),
            P(),
        ),
        out_specs=(P(ctx, head),) * 4,
        check_vma=False,
    )
```

time: 644 us -> 148 us (0.23)
  waiting for transfers between devices: 480 us -> 52 us
  matrix products: 38.9 us -> 0 us
  local copies, waits for them, and re-layouts: 43.5 us -> 11.3 us
  Pallas kernels: 0 us -> 29.4 us
  other arithmetic: 33.6 us -> 4.37 us
  starting transfers between devices: 29.2 us -> 47.7 us
  between operations: 15 us -> 0.82 us
    reduce_scatter x2 -> x0, waiting for transfers between devices: 306 us -> none  [the longest x1 234 us: shards(): lax.psum_scatter(jnp.concatenate([jnp.stack(key_terms, 1).reshape(count,...]
    all_gather x2 -> x0, waiting for transfers between devices: 118 us -> none  [the longest x1 89.1 us: shards(): all_stack = lax.all_gather(own_stack, 'ctx', axis=1, tiled=True)]
    ppermute x8, waiting for transfers between devices: 55.3 us -> 15.3 us  [the longest x1 7.75 us: shards(): before = lax.ppermute(picks, plane, [(i, i + 1) for i in range(ROWS - 1)])]
    all_to_all x0 -> x6, starting transfers between devices: none -> 39.1 us  [the longest x1 11.7 us: shards(): lax.all_to_all(dkv.reshape(ROWS, SUMM, 2 * HEAD), plane, 0, 0, tiled=True)]
    dot_general x28 -> x0, matrix products: 38.9 us -> none  [the longest x4 7.2 us: attend_head(): query_part = jnp.dot(dscore, key_block, preferred_element_type=jnp.float32)]
    all_to_all x0 -> x6, waiting for transfers between devices: none -> 36.7 us  [the longest x1 12.5 us: shards(): ga = lax.all_to_all(gb, 'zh', 0, 0, tiled=True)]
    pallas_call x0 -> x7, Pallas kernels: none -> 29.4 us  [call(): pl.pallas_call(kernel, out_shape=tuple(outs), in_specs=[SM if s.dtype ==...]
    ppermute x8, starting transfers between devices: 28.9 us -> 8.65 us  [the longest x1 3.36 us: shards(): before = lax.ppermute(picks, plane, [(i, i + 1) for i in range(ROWS - 1)])]
  transfers between devices with their start and end apart: 12 -> 14, of which waited for: 8 -> 6; matrix products, arithmetic and copies ran while one was open for 15% -> 1% of each run, Pallas kernels for 0% -> 10%
where the time goes in v1:
time: 148 us; the launch traced here: 146 us
  waiting for transfers between devices  52 us (35%)
  starting transfers between devices  47.7 us (32%)
  Pallas kernels  29.4 us (20%)
  local copies, waits for them, and re-layouts  11.3 us (8%)
  other arithmetic  4.37 us (3%)
    pallas_call x7, Pallas kernels, call(): pl.pallas_call(kernel, out_shape=tuple(outs), in_specs=[SM if s.dtype ==...  29.4 us
    all_to_all x1, waiting for transfers between devices, shards(): ga = lax.all_to_all(gb, 'zh', 0, 0, tiled=True)  12.5 us
    all_to_all x1, waiting for transfers between devices, shards(): qa = lax.all_to_all(qb, 'zh', 0, 0, tiled=True)  11.8 us
    all_to_all x1, starting transfers between devices, shards(): lax.all_to_all(dkv.reshape(ROWS, SUMM, 2 * HEAD), plane, 0, 0, tiled=True)  11.7 us
    unnamed x45, local copies, waits for them, and re-layouts  11.3 us
    all_to_all x1, starting transfers between devices, shards(): qa = lax.all_to_all(qb, 'zh', 0, 0, tiled=True)  8.46 us
    ppermute x1, waiting for transfers between devices, shards(): before = lax.ppermute(picks, plane, [(i, i + 1) for i in range(ROWS - 1)])  7.75 us
    ppermute x1, waiting for transfers between devices, shards(): lax.ppermute(dqa[:, TOK:, :], plane, [(i + 1, i) for i in range(ROWS - 1)])  7.49 us
  transfers between devices with their start and end apart: 14, of which 6 were waited for; matrix products, arithmetic and copies ran while one was open for 1% of the time, Pallas kernels for 10%

profile of v1, /device:TPU:24, one launch (start us, length us, event | category | flops | bytes accessed | tf_op | source)
XLA Modules:
  0.0 145.6 jit_solution(14813363683525217596)
XLA Ops:
  1.5 0.9 copy-done
  2.4 0.9 copy-done.2
  3.4 0.9 copy-done.4
  5.0 2.4 %pick_rows.1 = (bf16[16,128,256]{2,1,0:T(8,128)(2,1)}, bf16[4,256,128]{2,1,0:T(8,128)(2,1)}, bf16[4,96,128]{2,1,0:T(8,128)(2,1)S(1)}) custom-call(s32[4]{0:T(128)S(1)} %pad_add_fusion.meta, s32[64,4]{1,0:T(8,128)S(1)} %copy.11.soff, s32[1,128]{1,0:T(1,128)S(1)} %copy-done.19, bf16[256,512]{1,0:T(8,128)(2,1)S(1)} %copy-done.4, bf16[256,512]{1,0:T(8,128)(2,1)S(1)} %copy-done, ...), custom_call_target="tpu_custom_call" | custom-call | flops 100000000 | bytes 2197008 | tf_op jit(solution)/shard_map/pick_rows/pallas_call | solution.py:63
  7.4 8.5 %all-to-all-start = ((bf16[4,256,128]{2,1,0:T(8,128)(2,1)}), bf16[4,256,128]{2,1,0:T(8,128)(2,1)S(1)}, u32[]{:S(2)}, u32[]{:S(2)}) async-start(bf16[4,256,128]{2,1,0:T(8,128)(2,1)} %get-tuple-element.23), calls=%async_computation | async-start | bytes 524288 | tf_op jit(solution)/shard_map/all_to_all | solution.py:409
  15.8 1.0 collective-permute-start.1
  16.8 11.8 %all-to-all-done.qa = bf16[4,256,128]{2,1,0:T(8,128)(2,1)S(1)} async-done(((bf16[4,256,128]{2,1,0:T(8,128)(2,1)}), bf16[4,256,128]{2,1,0:T(8,128)(2,1)S(1)}, u32[]{:S(2)}, u32[]{:S(2)}) %all-to-all-start) | async-done | bytes 262176 | tf_op jit(solution)/shard_map/all_to_all | solution.py:409
  28.6 7.3 %all-to-all-start.1 = ((bf16[16,128,256]{2,1,0:T(8,128)(2,1)}), bf16[16,128,256]{2,1,0:T(8,128)(2,1)S(1)}, u32[]{:S(2)}, u32[]{:S(2)}) async-start(bf16[16,128,256]{2,1,0:T(8,128)(2,1)} %get-tuple-element.24), calls=%async_computation.1 | async-start | bytes 2097152 | tf_op jit(solution)/shard_map/all_to_all | solution.py:410
  36.5 3.4 %collective-permute-start.3 = (bf16[4,96,128]{2,1,0:T(8,128)(2,1)S(1)}, bf16[4,96,128]{2,1,0:T(8,128)(2,1)S(1)}, u32[]{:S(2)}, u32[]{:S(2)}) collective-permute-start(bf16[4,96,128]{2,1,0:T(8,128)(2,1)S(1)} %get-tuple-element.25.picks), channel_id=1, source_target_pairs={{0,16},{16,32},{32,48},{48,64},{64,80},{80,96},{96,112},{112,128},... | collective-permute-start | bytes 294920 | tf_op jit(solution)/shard_map/ppermute | solution.py:408
  39.9 7.8 %collective-permute-done.3.before = bf16[4,96,128]{2,1,0:T(8,128)(2,1)S(1)} collective-permute-done((bf16[4,96,128]{2,1,0:T(8,128)(2,1)S(1)}, bf16[4,96,128]{2,1,0:T(8,128)(2,1)S(1)}, u32[]{:S(2)}, u32[]{:S(2)}) %collective-permute-start.3) | collective-permute-done | bytes 98336 | tf_op jit(solution)/shard_map/ppermute | solution.py:408
  47.7 1.0 copy-done.8
  48.7 4.3 %attention_grad.1 = (bf16[256,512]{1,0:T(8,128)(2,1)S(1)}, bf16[4,352,128]{2,1,0:T(8,128)(2,1)}) custom-call(s32[4]{0:T(128)S(1)} %pad_add_fusion.meta, bf16[256,1024]{1,0:T(8,128)(2,1)S(1)} %copy-done.8, bf16[256,1024]{1,0:T(8,128)(2,1)S(1)} %collective-permute-done.up_c, bf16[256,1024]{1,0:T(8,128)(2,1)S(1)} %collective-permute-done.1.up_z, ...), custom_call_target="tpu_custom_call" | custom-call | flops 1073741824 | bytes 7110672 | tf_op jit(solution)/shard_map/attention_grad/pallas_call | solution.py:63
  53.0 4.1 %all-to-all-start.2 = ((bf16[4,352,128]{2,1,0:T(8,128)(2,1)}), bf16[4,352,128]{2,1,0:T(8,128)(2,1)S(1)}, u32[]{:S(2)}, u32[]{:S(2)}) async-start(bf16[4,352,128]{2,1,0:T(8,128)(2,1)} %get-tuple-element.26), calls=%async_computation.2 | async-start | bytes 720896 | tf_op jit(solution)/shard_map/all_to_all | solution.py:419
  57.1 12.5 %all-to-all-done.2.ga = bf16[4,352,128]{2,1,0:T(8,128)(2,1)S(1)} async-done(((bf16[4,352,128]{2,1,0:T(8,128)(2,1)}), bf16[4,352,128]{2,1,0:T(8,128)(2,1)S(1)}, u32[]{:S(2)}, u32[]{:S(2)}) %all-to-all-start.2) | async-done | bytes 360480 | tf_op jit(solution)/shard_map/all_to_all | solution.py:419
  69.6 7.5 %fixed_forward.1 = bf16[4,320,128]{2,1,0:T(8,128)(2,1)} custom-call(s32[4]{0:T(128)S(1)} %pad_add_fusion.meta, bf16[4,256,128]{2,1,0:T(8,128)(2,1)S(1)} %all-to-all-done.qa, bf16[2048,256]{1,0:T(8,128)(2,1)S(1)} %bitcast.8, bf16[4,352,128]{2,1,0:T(8,128)(2,1)S(1)} %all-to-all-done.2.ga, bf16[256,128]{1,0:T(8,128)(2,1)S(1)} %slice.9.k, ...), custom_call_target="tpu_custom_call" | custom-call | flops 1610612736 | bytes 2129936 | tf_op jit(solution)/shard_map/fixed_forward/pallas_call | solution.py:63
  77.1 3.6 %all-to-all-start.3 = ((bf16[4,320,128]{2,1,0:T(8,128)(2,1)}), bf16[4,320,128]{2,1,0:T(8,128)(2,1)S(1)}, u32[]{:S(2)}, u32[]{:S(2)}) async-start(bf16[4,320,128]{2,1,0:T(8,128)(2,1)} %fixed_forward.1), calls=%async_computation.3 | async-start | bytes 655360 | tf_op jit(solution)/shard_map/all_to_all | solution.py:429
  80.7 3.1 %strided_heads.1 = (bf16[256,384]{1,0:T(8,128)(2,1)S(1)}, bf16[256,384]{1,0:T(8,128)(2,1)S(1)}, f32[256,768]{1,0:T(8,128)S(1)}, bf16[4,96,128]{2,1,0:T(8,128)(2,1)S(1)}) custom-call(s32[4]{0:T(128)S(1)} %pad_add_fusion.meta, bf16[256,512]{1,0:T(8,128)(2,1)S(1)} %copy-done.5, bf16[256,512]{1,0:T(8,128)(2,1)S(1)} %copy-done.1, bf16[256,512]{1,0:T(8,128)(2,1)S(1)} %copy-done.3, ...), custom_call_target="tpu_custom_call" | custom-call | flops 377487360 | bytes 2686992 | tf_op jit(solution)/shard_map/strided_heads/pallas_call | solution.py:63
  83.8 0.9 copy-done.6
  85.4 5.8 %all-to-all-done.3.oa = bf16[4,320,128]{2,1,0:T(8,128)(2,1)S(1)} async-done(((bf16[4,320,128]{2,1,0:T(8,128)(2,1)}), bf16[4,320,128]{2,1,0:T(8,128)(2,1)S(1)}, u32[]{:S(2)}, u32[]{:S(2)}) %all-to-all-start.3) | async-done | bytes 327712 | tf_op jit(solution)/shard_map/all_to_all | solution.py:429
  91.2 0.9 copy-done.12
  93.8 5.5 %fixed_backward.1 = (bf16[2048,256]{1,0:T(8,128)(2,1)}, bf16[4,352,128]{2,1,0:T(8,128)(2,1)}, f32[256,256]{1,0:T(8,128)S(1)}) custom-call(s32[4]{0:T(128)S(1)} %pad_add_fusion.meta, bf16[4,320,128]{2,1,0:T(8,128)(2,1)S(1)} %all-to-all-done.3.oa, bf16[4,256,128]{2,1,0:T(8,128)(2,1)S(1)} %copy-done.12, bf16[2048,256]{1,0:T(8,128)(2,1)S(1)} %bitcast.9, ...), custom_call_target="tpu_custom_call" | custom-call | flops 2684354560 | bytes 3899408 | tf_op jit(solution)/shard_map/fixed_backward/pallas_call | solution.py:63
  99.4 3.8 %all-to-all-start.5 = ((bf16[4,352,128]{2,1,0:T(8,128)(2,1)}), bf16[4,352,128]{2,1,0:T(8,128)(2,1)S(1)}, u32[]{:S(2)}, u32[]{:S(2)}) async-start(bf16[4,352,128]{2,1,0:T(8,128)(2,1)} %get-tuple-element.36), calls=%async_computation.5 | async-start | bytes 720896 | tf_op jit(solution)/shard_map/all_to_all | solution.py:470
  103.2 4.2 %project.1 = (bf16[256,1024]{1,0:T(8,128)(2,1)S(1)}, bf16[256,1024]{1,0:T(8,128)(2,1)S(1)}, bf16[256,1024]{1,0:T(8,128)(2,1)S(1)}, bf16[256,1024]{1,0:T(8,128)(2,1)}) custom-call(s32[4]{0:T(128)S(1)} %pad_add_fusion.meta, bf16[4,320,128]{2,1,0:T(8,128)(2,1)S(1)} %all-to-all-done.3.oa, bf16[256,384]{1,0:T(8,128)(2,1)S(1)} %get-tuple-element.28.o, ...), custom_call_target="tpu_custom_call" | custom-call | flops 1073741824 | bytes 6815760 | tf_op jit(solution)/shard_map/project/pallas_call | solution.py:63
  108.2 6.6 %all-to-all-done.5.dq = bf16[4,352,128]{2,1,0:T(8,128)(2,1)S(1)} async-done(((bf16[4,352,128]{2,1,0:T(8,128)(2,1)}), bf16[4,352,128]{2,1,0:T(8,128)(2,1)S(1)}, u32[]{:S(2)}, u32[]{:S(2)}) %all-to-all-start.5) | async-done | bytes 360480 | tf_op jit(solution)/shard_map/all_to_all | solution.py:470
  114.8 11.7 %all-to-all-start.4 = ((bf16[16,128,256]{2,1,0:T(8,128)(2,1)}), bf16[16,128,256]{2,1,0:T(8,128)(2,1)S(1)}, u32[]{:S(2)}, u32[]{:S(2)}) async-start(bf16[16,128,256]{2,1,0:T(8,128)(2,1)} %bitcast.5), calls=%async_computation.4 | async-start | bytes 2097152 | tf_op jit(solution)/shard_map/all_to_all | solution.py:467
  126.6 2.0 %add_convert_fusion.1 = bf16[256,1024]{1,0:T(8,128)(2,1)} fusion(bf16[256,1024]{1,0:T(8,128)(2,1)} %collective-permute-done.5, bf16[256,1024]{1,0:T(8,128)(2,1)S(1)} %get-tuple-element.31), kind=kLoop, calls=%fused_computation.1 | loop fusion | flops 1048576 | bytes 1572864 | tf_op jit(solution)/shard_map/convert_element_type | solution.py:466
  128.6 0.9 collective-permute-start.6
  129.6 2.8 %collective-permute-start.7 = (bf16[4,96,128]{2,1,0:T(8,128)(2,1)S(1)}, bf16[4,96,128]{2,1,0:T(8,128)(2,1)S(1)}, u32[]{:S(2)}, u32[]{:S(2)}) collective-permute-start(bf16[4,96,128]{2,1,0:T(8,128)(2,1)S(1)} %slice.12), channel_id=1, source_target_pairs={{16,0},{32,16},{48,32},{64,48},{80,64},{96,80},{112,96},{128,112},... | collective-permute-start | bytes 294920 | tf_op jit(solution)/shard_map/ppermute | solution.py:471
  132.3 7.5 %collective-permute-done.7.after = bf16[4,96,128]{2,1,0:T(8,128)(2,1)S(1)} collective-permute-done((bf16[4,96,128]{2,1,0:T(8,128)(2,1)S(1)}, bf16[4,96,128]{2,1,0:T(8,128)(2,1)S(1)}, u32[]{:S(2)}, u32[]{:S(2)}) %collective-permute-start.7) | collective-permute-done | bytes 98336 | tf_op jit(solution)/shard_map/ppermute | solution.py:471
  139.8 0.9 copy-done.14
  140.7 2.5 %join_grads.1 = (bf16[256,512]{1,0:T(8,128)(2,1)}, bf16[256,512]{1,0:T(8,128)(2,1)}, bf16[256,512]{1,0:T(8,128)(2,1)}) custom-call(s32[4]{0:T(128)S(1)} %pad_add_fusion.meta, s32[64,4]{1,0:T(8,128)S(1)} %copy.11.soff, s32[1,128]{1,0:T(1,128)S(1)} %copy-done.20, bf16[2048,256]{1,0:T(8,128)(2,1)S(1)} %bitcast.7, f32[256,256]{1,0:T(8,128)S(1)} %get-tuple-element.35.own, ...), custom_call_target="tpu_custom_call" | custom-call | flops 300000000 | bytes 3540496 | tf_op jit(solution)/shard_map/join_grads/pallas_call | solution.py:63
  143.3 2.3 %add_convert_fusion = bf16[256,1024]{1,0:T(8,128)(2,1)} fusion(bf16[256,1024]{1,0:T(8,128)(2,1)} %collective-permute-done.6, bf16[256,1024]{1,0:T(8,128)(2,1)} %collective-permute-done.4, bf16[256,1024]{1,0:T(8,128)(2,1)S(1)} %copy-done.10), kind=kLoop, calls=%fused_computation | loop fusion | flops 1572864 | bytes 2097152 | tf_op jit(solution)/shard_map/convert_element_type | solution.py:474
  (54 shorter events, 5.4 us)
Async XLA Ops:
  1.5 1.0 copy-start
  2.4 0.9 copy-start.2
  3.4 0.9 copy-start.4
  7.4 21.3 %all-to-all-start = ((bf16[4,256,128]{2,1,0:T(8,128)(2,1)}), bf16[4,256,128]{2,1,0:T(8,128)(2,1)S(1)}, u32[]{:S(2)}, u32[]{:S(2)}) async-start(bf16[4,256,128]{2,1,0:T(8,128)(2,1)} %get-tuple-element.23), calls=%async_computation | async-start | bytes 524288 | tf_op jit(solution)/shard_map/all_to_all | solution.py:409
  15.8 20.2 %collective-permute-start.1 = (bf16[256,1024]{1,0:T(8,128)(2,1)}, bf16[256,1024]{1,0:T(8,128)(2,1)S(1)}, u32[]{:S(2)}, u32[]{:S(2)}) collective-permute-start(bf16[256,1024]{1,0:T(8,128)(2,1)} %up.1), channel_id=1, source_target_pairs={{0,2},{2,0},{1,3},{3,1},{4,6},{6,4},{5,7},{7,5},{8,10},{10,8},{9,1... | collective-permute-start | bytes 1572872 | tf_op jit(solution)/shard_map/ppermute | solution.py:387
  28.6 41.0 %copy-start.11 = (bf16[4,256,128]{2,1,0:T(8,128)(2,1)}, bf16[4,256,128]{2,1,0:T(8,128)(2,1)S(1)}, u32[]{:S(2)}) copy-start(bf16[4,256,128]{2,1,0:T(8,128)(2,1)S(1)} %all-to-all-done.qa) | copy-start | bytes 786436
  28.6 28.4 %copy-start.1 = (bf16[256,512]{1,0:T(8,128)(2,1)S(1)}, bf16[256,512]{1,0:T(8,128)(2,1)}, u32[]{:S(2)}) copy-start(bf16[256,512]{1,0:T(8,128)(2,1)} %k.3) | copy-start | bytes 786436
  28.6 24.3 %all-to-all-start.1 = ((bf16[16,128,256]{2,1,0:T(8,128)(2,1)}), bf16[16,128,256]{2,1,0:T(8,128)(2,1)S(1)}, u32[]{:S(2)}, u32[]{:S(2)}) async-start(bf16[16,128,256]{2,1,0:T(8,128)(2,1)} %get-tuple-element.24), calls=%async_computation.1 | async-start | bytes 2097152 | tf_op jit(solution)/shard_map/all_to_all | solution.py:410
  35.9 21.1 %copy-start.3 = (bf16[256,512]{1,0:T(8,128)(2,1)S(1)}, bf16[256,512]{1,0:T(8,128)(2,1)}, u32[]{:S(2)}) copy-start(bf16[256,512]{1,0:T(8,128)(2,1)} %v.3) | copy-start | bytes 786436
  35.9 11.7 %collective-permute-start = (bf16[256,1024]{1,0:T(8,128)(2,1)}, bf16[256,1024]{1,0:T(8,128)(2,1)S(1)}, u32[]{:S(2)}, u32[]{:S(2)}) collective-permute-start(bf16[256,1024]{1,0:T(8,128)(2,1)} %up.1), channel_id=1, source_target_pairs={{0,1},{1,0},{2,3},{3,2},{4,5},{5,4},{6,7},{7,6},{8,9},{9,8},{10,11... | collective-permute-start | bytes 1572872 | tf_op jit(solution)/shard_map/ppermute | solution.py:387
  36.0 11.6 %collective-permute-start.2 = (bf16[256,1024]{1,0:T(8,128)(2,1)S(1)}, bf16[256,1024]{1,0:T(8,128)(2,1)S(1)}, u32[]{:S(2)}, u32[]{:S(2)}) collective-permute-start(bf16[256,1024]{1,0:T(8,128)(2,1)S(1)} %collective-permute-done.1.up_z), channel_id=1, source_target_pairs={{0,1},{1,0},{2,3},{3,2},{4,5},{5,4},{6,7},{7,6},{8,9},{9,8},{10,11... | collective-permute-start | bytes 1572872 | tf_op jit(solution)/shard_map/ppermute | solution.py:387
  36.5 11.1 %collective-permute-start.3 = (bf16[4,96,128]{2,1,0:T(8,128)(2,1)S(1)}, bf16[4,96,128]{2,1,0:T(8,128)(2,1)S(1)}, u32[]{:S(2)}, u32[]{:S(2)}) collective-permute-start(bf16[4,96,128]{2,1,0:T(8,128)(2,1)S(1)} %get-tuple-element.25.picks), channel_id=1, source_target_pairs={{0,16},{16,32},{32,48},{48,64},{64,80},{80,96},{96,112},{112,128},... | collective-permute-start | bytes 294920 | tf_op jit(solution)/shard_map/ppermute | solution.py:408
  47.7 1.0 copy-start.8
  53.0 27.8 %copy-start.5 = (bf16[256,512]{1,0:T(8,128)(2,1)S(1)}, bf16[256,512]{1,0:T(8,128)(2,1)}, u32[]{:S(2)}) copy-start(bf16[256,512]{1,0:T(8,128)(2,1)} %q.3) | copy-start | bytes 786436
  53.0 16.6 %all-to-all-start.2 = ((bf16[4,352,128]{2,1,0:T(8,128)(2,1)}), bf16[4,352,128]{2,1,0:T(8,128)(2,1)S(1)}, u32[]{:S(2)}, u32[]{:S(2)}) async-start(bf16[4,352,128]{2,1,0:T(8,128)(2,1)} %get-tuple-element.26), calls=%async_computation.2 | async-start | bytes 720896 | tf_op jit(solution)/shard_map/all_to_all | solution.py:419
  57.1 20.0 %copy-start.15 = (bf16[256,128]{1,0:T(8,128)(2,1)}, bf16[256,128]{1,0:T(8,128)(2,1)S(1)}, u32[]{:S(2)}) copy-start(bf16[256,128]{1,0:T(8,128)(2,1)S(1)} %slice.9.k) | copy-start | bytes 196612
  57.1 20.0 %copy-start.17 = (bf16[256,128]{1,0:T(8,128)(2,1)}, bf16[256,128]{1,0:T(8,128)(2,1)S(1)}, u32[]{:S(2)}) copy-start(bf16[256,128]{1,0:T(8,128)(2,1)S(1)} %slice.10.v) | copy-start | bytes 196612
  77.1 14.1 %all-to-all-start.3 = ((bf16[4,320,128]{2,1,0:T(8,128)(2,1)}), bf16[4,320,128]{2,1,0:T(8,128)(2,1)S(1)}, u32[]{:S(2)}, u32[]{:S(2)}) async-start(bf16[4,320,128]{2,1,0:T(8,128)(2,1)} %fixed_forward.1), calls=%async_computation.3 | async-start | bytes 655360 | tf_op jit(solution)/shard_map/all_to_all | solution.py:429
  83.8 0.9 copy-start.6
  91.2 1.0 copy-start.12
  92.2 0.8 copy-start.16
  99.4 15.4 %all-to-all-start.5 = ((bf16[4,352,128]{2,1,0:T(8,128)(2,1)}), bf16[4,352,128]{2,1,0:T(8,128)(2,1)S(1)}, u32[]{:S(2)}, u32[]{:S(2)}) async-start(bf16[4,352,128]{2,1,0:T(8,128)(2,1)} %get-tuple-element.36), calls=%async_computation.5 | async-start | bytes 720896 | tf_op jit(solution)/shard_map/all_to_all | solution.py:470
  103.2 36.6 %copy-start.7 = (f32[256,768]{1,0:T(8,128)S(1)}, f32[256,768]{1,0:T(8,128)}, u32[]{:S(2)}) copy-start(f32[256,768]{1,0:T(8,128)} %copy-done.6) | copy-start | bytes 2359300
  103.2 36.6 %copy-start.20 = (s32[1,128]{1,0:T(1,128)S(1)}, s32[1,128]{1,0:T(1,128)}, u32[]{:S(2)}) copy-start(s32[1,128]{1,0:T(1,128)} %sidx.3) | copy-start | bytes 1540
  108.2 6.6 %copy-start.21 = (bf16[256,1024]{1,0:T(8,128)(2,1)}, bf16[256,1024]{1,0:T(8,128)(2,1)S(1)}, u32[]{:S(2)}) copy-start(bf16[256,1024]{1,0:T(8,128)(2,1)S(1)} %get-tuple-element.30) | copy-start | bytes 1572868
  108.2 35.1 %copy-start.10 = (bf16[256,1024]{1,0:T(8,128)(2,1)S(1)}, bf16[256,1024]{1,0:T(8,128)(2,1)}, u32[]{:S(2)}) copy-start(bf16[256,1024]{1,0:T(8,128)(2,1)} %copy-done.9) | copy-start | bytes 1572868
  108.2 18.4 %collective-permute-start.5 = (bf16[256,1024]{1,0:T(8,128)(2,1)}, bf16[256,1024]{1,0:T(8,128)(2,1)}, u32[]{:S(2)}, u32[]{:S(2)}) collective-permute-start(bf16[256,1024]{1,0:T(8,128)(2,1)} %get-tuple-element.32), channel_id=1, source_target_pairs={{0,1},{1,0},{2,3},{3,2},{4,5},{5,4},{6,7},{7,6},{8,9},{9,8},{10,11... | collective-permute-start | bytes 1572872 | tf_op jit(solution)/shard_map/ppermute | solution.py:387
  114.8 25.0 %all-to-all-start.4 = ((bf16[16,128,256]{2,1,0:T(8,128)(2,1)}), bf16[16,128,256]{2,1,0:T(8,128)(2,1)S(1)}, u32[]{:S(2)}, u32[]{:S(2)}) async-start(bf16[16,128,256]{2,1,0:T(8,128)(2,1)} %bitcast.5), calls=%async_computation.4 | async-start | bytes 2097152 | tf_op jit(solution)/shard_map/all_to_all | solution.py:467
  126.6 16.7 %collective-permute-start.4 = (bf16[256,1024]{1,0:T(8,128)(2,1)}, bf16[256,1024]{1,0:T(8,128)(2,1)}, u32[]{:S(2)}, u32[]{:S(2)}) collective-permute-start(bf16[256,1024]{1,0:T(8,128)(2,1)} %copy-done.21), channel_id=1, source_target_pairs={{0,1},{1,0},{2,3},{3,2},{4,5},{5,4},{6,7},{7,6},{8,9},{9,8},{10,11... | collective-permute-start | bytes 1572872 | tf_op jit(solution)/shard_map/ppermute | solution.py:387
  128.6 14.7 %collective-permute-start.6 = (bf16[256,1024]{1,0:T(8,128)(2,1)}, bf16[256,1024]{1,0:T(8,128)(2,1)}, u32[]{:S(2)}, u32[]{:S(2)}) collective-permute-start(bf16[256,1024]{1,0:T(8,128)(2,1)} %add_convert_fusion.1), channel_id=1, source_target_pairs={{0,2},{2,0},{1,3},{3,1},{4,6},{6,4},{5,7},{7,5},{8,10},{10,8},{9,1... | collective-permute-start | bytes 1572872 | tf_op jit(solution)/shard_map/ppermute | solution.py:387
  129.6 10.3 %collective-permute-start.7 = (bf16[4,96,128]{2,1,0:T(8,128)(2,1)S(1)}, bf16[4,96,128]{2,1,0:T(8,128)(2,1)S(1)}, u32[]{:S(2)}, u32[]{:S(2)}) collective-permute-start(bf16[4,96,128]{2,1,0:T(8,128)(2,1)S(1)} %slice.12), channel_id=1, source_target_pairs={{16,0},{32,16},{48,32},{64,48},{80,64},{96,80},{112,96},{128,112},... | collective-permute-start | bytes 294920 | tf_op jit(solution)/shard_map/ppermute | solution.py:471
  139.8 0.9 copy-start.14
  (4 other events, 3.0 us)

commit v2 on v1

v2 whole, which is shorter than its diff:
```python
import functools

import jax
import jax.numpy as jnp
from jax import lax
from jax.experimental import pallas as pl
from jax.experimental.pallas import tpu as pltpu
from jax.sharding import Mesh
from jax.sharding import PartitionSpec as P

HEAD = 128
TOK = 256
SUMM = 128
STRIDE = 16
REACH = TOK // STRIDE
ROWS = 16
GROUP = 4
ALL = GROUP * TOK
KEYS = ROWS * SUMM
TILE = 256
STAT = 64
FAR = 6 * REACH
SCALE = HEAD ** (-0.5)
LOG2E = 1.4426950408889634
SCALE2 = SCALE * LOG2E
NEG = -1e30
F32 = jnp.float32
BF = jnp.bfloat16

VM = pl.BlockSpec(memory_space=pltpu.VMEM)
SM = pl.BlockSpec(memory_space=pltpu.SMEM)
ANY = pl.BlockSpec(memory_space=pl.ANY)


def nn(a, b):
    return lax.dot_general(a, b, (((1,), (0,)), ((), ())), preferred_element_type=F32)


def nt(a, b):
    return lax.dot_general(a, b, (((1,), (1,)), ((), ())), preferred_element_type=F32)


def tn(a, b):
    return lax.dot_general(a, b, (((0,), (0,)), ((), ())), preferred_element_type=F32)


def iota(shape, dim):
    return lax.broadcasted_iota(jnp.int32, shape, dim)


def ones_where(condition):
    return condition.astype(F32).astype(BF)


def summary_select(sidx):
    return ones_where(iota((TOK, SUMM), 0) == sidx)


def stride_select(soff_t, shard):
    there = jnp.minimum(shard + 1 + iota((4, ROWS * GROUP), 0), ROWS * GROUP - 1)
    offset = jnp.where(iota((4, ROWS * GROUP), 1) == there, soff_t, 0)
    offset = jnp.sum(offset.astype(F32), axis=1, keepdims=True).astype(jnp.int32)
    row, col = iota((4 * REACH, TOK), 0), iota((4 * REACH, TOK), 1)
    slot = row // REACH
    want = (row % REACH) * STRIDE
    for u in range(4):
        want = want + jnp.where(slot == u, offset[u : u + 1], 0)
    return ones_where(want == col)


def call(kernel, outs, ins, flops, scratch=(), name=None, vmem=24, specs=None):
    moved = sum(
        s.size * jnp.dtype(s.dtype).itemsize for s in list(outs) + list(ins)
    )
    return pl.pallas_call(
        kernel,
        out_shape=tuple(outs),
        in_specs=specs or [SM] + [VM] * (len(ins) - 1),
        out_specs=tuple(VM for _ in outs),
        scratch_shapes=list(scratch),
        compiler_params=pltpu.CompilerParams(vmem_limit_bytes=vmem * 2**20),
        cost_estimate=pl.CostEstimate(
            flops=flops, bytes_accessed=moved, transcendentals=0
        ),
        name=name,
    )(*ins)


def sds(shape, dtype=BF):
    return jax.ShapeDtypeStruct(shape, dtype)


def prep_kernel(
    meta, soff_t, sidx, q, k, v, kvb, q0, kv0, picks, kb, vb, ib, sb, sems
):
    copies = [
        pltpu.make_async_copy(k, kb, sems.at[0]),
        pltpu.make_async_copy(v, vb, sems.at[1]),
        pltpu.make_async_copy(sidx, ib, sems.at[2]),
        pltpu.make_async_copy(soff_t, sb, sems.at[3]),
        pltpu.make_async_copy(q.at[:, pl.ds(0, HEAD)], q0, sems.at[4]),
    ]
    for copy in copies:
        copy.start()
    for copy in copies:
        copy.wait()
    pick = summary_select(ib[...])
    kv = jnp.concatenate([kb[:, :HEAD], vb[:, :HEAD]], 1)
    kv0[...] = kv
    kv = tn(pick, kv).astype(BF)
    for i in range(ROWS):
        kvb[i] = kv
    sel = stride_select(sb[...], GROUP * meta[0] + meta[1])
    got = nn(sel, jnp.concatenate([kb[:, HEAD:], vb[:, HEAD:]], 1)).astype(BF)
    for u in range(4):
        for h in range(6):
            picks[u, h * REACH : (h + 1) * REACH, :] = got[
                u * REACH : (u + 1) * REACH, h * HEAD : (h + 1) * HEAD
            ]


def bundle_kernel(meta, q0, picks, before, *outs):
    zh = meta[1]
    for d in (1, 2, 3):
        outs[d - 1][:TOK, :] = q0[...]

        @pl.when(zh + d < GROUP)
        def _(d=d):
            outs[d - 1][TOK:, :] = picks[d - 1]

        @pl.when(zh + d >= GROUP)
        def _(d=d):
            outs[d - 1][TOK:, :] = before[d - 1]


def grad_near_kernel(meta, up, up_c, w, acc):
    zl, c = meta[2], meta[3]
    wide = up.shape[1]
    here = pl.multiple_of((2 * zl + c) * wide, wide)
    beside = pl.multiple_of((2 * zl + 1 - c) * wide, wide)
    acc[...] = nt(up[...], w[:, pl.ds(here, wide)]) + nt(
        up_c[...], w[:, pl.ds(beside, wide)]
    )


def grad_far_kernel(meta, up_z, up_zc, w, acc, g, g0):
    zl, c = 1 - meta[2], meta[3]
    wide = up_z.shape[1]
    here = pl.multiple_of((2 * zl + c) * wide, wide)
    beside = pl.multiple_of((2 * zl + 1 - c) * wide, wide)
    full = acc[...] + nt(up_z[...], w[:, pl.ds(here, wide)])
    full = (full + nt(up_zc[...], w[:, pl.ds(beside, wide)])).astype(BF)
    g[...] = full
    g0[...] = full[:, :HEAD]


def fold8(a, how):
    return how(a.reshape(a.shape[0] // 8, 8, a.shape[1]), axis=0)


def causal_t():
    return iota((TOK, TOK), 0) <= iota((TOK, TOK), 1)


def block_masks(row, zh):
    slot = iota((1, ALL), 1) // TOK
    edge = jnp.where(slot > zh, 0.0, NEG)
    none = jnp.full((1, ALL), NEG, F32)
    return [
        jnp.where(jnp.full((1, ALL), b, jnp.int32) < row, 0.0,
                  jnp.where(jnp.full((1, ALL), b, jnp.int32) == row, edge, none))
        for b in range(ROWS)
    ]


def split3(a):
    hi = a.astype(BF).astype(F32)
    mid = (a - hi).astype(BF).astype(F32)
    return [hi, mid, (a - hi - mid).astype(BF).astype(F32)]


def halves(a):
    return jnp.concatenate([a[:, :HEAD], a[:, HEAD:]], 0)


def whole(a):
    n = a.shape[0] // 2
    return jnp.concatenate([a[:n], a[n:]], 1)


def forward_kernel(
    meta, q0, q1, q2, q3, g0, g1, g2, g3, kva, kv0, far, ob, s_ref
):
    row, zh = meta[0], meta[1]
    q = jnp.concatenate([q0[...], q1[:TOK], q2[:TOK], q3[:TOK]], 0)
    g = jnp.concatenate([g0[...], g1[...], g2[...], g3[...]], 0)
    masks = block_masks(row, zh)
    per = TILE // SUMM
    top = jnp.full((8, ALL), NEG, F32)
    for j in range(KEYS // TILE):
        s = nt(kva[j * TILE : (j + 1) * TILE, :HEAD], q)
        s_ref[j * TILE : (j + 1) * TILE, :] = s
        for i in range(per):
            most = fold8(s[i * SUMM : (i + 1) * SUMM], jnp.max)
            top = jnp.maximum(top, most + masks[per * j + i])
    top = jnp.max(top, axis=0, keepdims=True) * SCALE2
    sums = jnp.zeros((8, ALL), F32)
    dots = jnp.zeros((8, ALL), F32)
    out = jnp.zeros((HEAD, ALL), F32)
    for j in range(KEYS // TILE):
        at = slice(j * TILE, (j + 1) * TILE)
        value = kva[at, HEAD:]
        parts = []
        for i in range(per):
            b = per * j + i
            shift = jnp.where(masks[b] < 0, -NEG, top)
            parts.append(
                jnp.exp2(s_ref[b * SUMM : (b + 1) * SUMM, :] * SCALE2 - shift)
            )
        e = jnp.concatenate(parts, 0)
        sums = sums + fold8(e, jnp.sum)
        dots = dots + fold8(e * nt(value, g), jnp.sum)
        out = out + tn(value, e.astype(BF))
    sums = jnp.sum(sums, axis=0, keepdims=True)
    dots = jnp.sum(dots, axis=0, keepdims=True)
    some = sums > 0
    safe = jnp.where(some, sums, 1.0)
    inv = 1.0 / safe
    log_sum = jnp.where(some, top + jnp.log(safe) * LOG2E, NEG)
    dots = dots * inv
    out = out * inv

    key, value = kv0[:, :HEAD], kv0[:, HEAD:]
    s = jnp.where(causal_t(), nt(key, q0[...]) * SCALE2, NEG)
    own_top = jnp.max(s, axis=0, keepdims=True)
    e = jnp.exp2(s - own_top)
    own_sum = jnp.sum(e, axis=0, keepdims=True)
    own_dot = jnp.sum(e * nt(value, g0[...]), axis=0, keepdims=True)
    own_out = tn(value, e.astype(BF))
    own_log = own_top + jnp.log(own_sum) * LOG2E
    near = log_sum[:, :TOK]
    most = jnp.maximum(near, own_log)
    wa, wb = jnp.exp2(near - most), jnp.exp2(own_log - most)
    inv = 1.0 / (wa + wb)
    wa, wb = wa * inv, wb * inv / own_sum
    log_sum = jnp.concatenate(
        [most - jnp.log(inv) * LOG2E, log_sum[:, TOK:]], 1
    )
    dots = jnp.concatenate(
        [wa * dots[:, :TOK] + wb * own_dot, dots[:, TOK:]], 1
    )

    stats = jnp.concatenate(
        split3(log_sum) + split3(dots) + [jnp.zeros((2, ALL), F32)], 0
    )
    stats = jnp.concatenate(
        [stats[:, i * HEAD : (i + 1) * HEAD] for i in range(ALL // HEAD)], 0
    ).astype(BF)
    for d in range(GROUP):
        part = out[:, d * TOK : (d + 1) * TOK]
        if d == 0:
            part = wa * part + wb * own_out
        to = lax.rem(zh - d + GROUP, GROUP)
        ob[to, :TOK, :] = halves(part).astype(BF)
        ob[to, TOK : TOK + STAT, :] = stats
        ob[to, TOK + STAT :, :] = far[(d + 3) % 4]


def combine_kernel(meta, oa, o, stat):
    zh = meta[1]
    got = []
    for f in range(GROUP):
        rows = oa[lax.rem(zh - f + GROUP, GROUP), TOK : TOK + STAT, :].astype(F32)
        got.append(
            jnp.concatenate([rows[8 * i : 8 * i + 8] for i in range(STAT // 8)], 1)
        )
    for d in range(GROUP):
        logs, dots = [], []
        for f in range(GROUP):
            e = (d - f) % GROUP
            part = got[f][:, e * TOK : (e + 1) * TOK]
            logs.append(part[0:1] + part[1:2] + part[2:3])
            dots.append(part[3:4] + part[4:5] + part[5:6])
        most = functools.reduce(jnp.maximum, logs)
        shares = [jnp.exp2(x - most) for x in logs]
        both = functools.reduce(jnp.add, shares)
        shares = [x / both for x in shares]
        at = slice(d * TOK, (d + 1) * TOK)
        stat[0:1, at] = most + jnp.log(both) * LOG2E
        stat[1:2, at] = functools.reduce(
            jnp.add, [x * y for x, y in zip(shares, dots)]
        )
        if d == 0:
            full = functools.reduce(
                jnp.add,
                [
                    shares[f]
                    * whole(oa[lax.rem(zh - f + GROUP, GROUP), :TOK, :].astype(F32))
                    for f in range(GROUP)
                ],
            )
            eye = ones_where(iota((HEAD, HEAD), 0) == iota((HEAD, HEAD), 1))
            o[...] = tn(full.astype(BF), eye).astype(BF)
    stat[2:8, :] = jnp.zeros((6, ALL), F32)


def backward_kernel(
    meta, q0, q1, q2, q3, g0, g1, g2, g3, kva, kv0, stat, dkv, own, dq0, dq1, dq2, dq3
):
    row, zh = meta[0], meta[1]
    q = jnp.concatenate([q0[...], q1[:TOK], q2[:TOK], q3[:TOK]], 0)
    g = jnp.concatenate([g0[...], g1[...], g2[...], g3[...]], 0)
    masks = block_masks(row, zh)
    log_sum, dot = stat[0:1, :], stat[1:2, :]
    per = TILE // SUMM
    dq = jnp.zeros((HEAD, ALL), F32)
    for j in range(KEYS // TILE):
        at = slice(j * TILE, (j + 1) * TILE)
        key, value = kva[at, :HEAD], kva[at, HEAD:]
        s = nt(key, q)
        parts = []
        for i in range(per):
            shift = jnp.where(masks[per * j + i] < 0, -NEG, log_sum)
            parts.append(
                jnp.exp2(s[i * SUMM : (i + 1) * SUMM] * SCALE2 - shift)
            )
        p = jnp.concatenate(parts, 0)
        dkv[at, HEAD:] = nn(p.astype(BF), g).astype(BF)
        ds = (p * (nt(value, g) - dot)).astype(BF)
        dkv[at, :HEAD] = (nn(ds, q) * SCALE).astype(BF)
        dq = dq + tn(key, ds)
    key, value = kv0[:, :HEAD], kv0[:, HEAD:]
    s = jnp.where(causal_t(), nt(key, q0[...]) * SCALE2, NEG)
    p = jnp.exp2(s - log_sum[:, :TOK])
    own[:, HEAD:] = nn(p.astype(BF), g0[...])
    ds = (p * (nt(value, g0[...]) - dot[:, :TOK])).astype(BF)
    own[:, :HEAD] = nn(ds, q0[...]) * SCALE
    dq0[...] = (dq[:, :TOK] + tn(key, ds)) * SCALE
    for d, ref in ((1, dq1), (2, dq2), (3, dq3)):
        ref[...] = (halves(dq[:, d * TOK : (d + 1) * TOK]) * SCALE).astype(BF)


def strided_kernel(meta, q, k, v, g, f1, f2, f3, before, o, dq, dkv, far):
    row, zh = meta[0], meta[1]
    slot = iota((TOK, 4 * REACH), 1) // REACH
    far_ok = (slot < zh) | (jnp.full((TOK, 4 * REACH), row, jnp.int32) > 0)
    near_ok = iota((TOK, TOK), 0) >= iota((TOK, TOK), 1)

    def far_rows(i):
        at = slice(TOK + i * REACH, TOK + (i + 1) * REACH)
        last = before[3, i * REACH : (i + 1) * REACH, :]
        return jnp.concatenate([f1[at], f2[at], f3[at], last], 0)

    for h in range(3):
        at = slice((h + 1) * HEAD, (h + 2) * HEAD)
        to = slice(h * HEAD, (h + 1) * HEAD)
        qh, kh, vh, gh = q[:, at], k[:, at], v[:, at], g[:, at]
        kf, vf = far_rows(h), far_rows(h + 3)
        s = jnp.where(near_ok, nt(qh, kh) * SCALE, NEG)
        sf = jnp.where(far_ok, nt(qh, kf) * SCALE, NEG)
        top = jnp.maximum(
            jnp.max(s, axis=1, keepdims=True), jnp.max(sf, axis=1, keepdims=True)
        )
        e, ef = jnp.exp(s - top), jnp.exp(sf - top)
        inv = 1.0 / (
            jnp.sum(e, axis=1, keepdims=True) + jnp.sum(ef, axis=1, keepdims=True)
        )
        p, pf = e * inv, ef * inv
        w, wf = p.astype(BF), pf.astype(BF)
        out = (nn(w, vh) + nn(wf, vf)).astype(BF)
        o[:, to] = out
        delta = jnp.sum(gh.astype(F32) * out.astype(F32), axis=1, keepdims=True)
        ds = (p * (nt(gh, vh) - delta) * SCALE).astype(BF)
        dsf = (pf * (nt(gh, vf) - delta) * SCALE).astype(BF)
        dq[:, to] = (nn(ds, kh) + nn(dsf, kf)).astype(BF)
        dkv[:, to] = tn(ds, qh)
        dkv[:, 3 * HEAD + h * HEAD : 3 * HEAD + (h + 1) * HEAD] = tn(w, gh)
        dkf = tn(dsf, qh).astype(BF)
        dvf = tn(wf, gh).astype(BF)
        for u in range(4):
            rows = slice(u * REACH, (u + 1) * REACH)
            far[u, h * REACH : (h + 1) * REACH, :] = dkf[rows]
            far[u, (h + 3) * REACH : (h + 4) * REACH, :] = dvf[rows]


def project_strided_kernel(meta, o, o_c, w, w_c, acc, wa, wb, sems):
    zl, c = meta[2], meta[3]
    wide = wa.shape[2]
    copies = []
    for i, z in enumerate((zl, 1 - zl)):
        at = pl.ds(pl.multiple_of((2 * z + c) * wide, wide), wide)
        rows = pl.ds(HEAD, 3 * HEAD)
        copies.append(
            (
                pltpu.make_async_copy(w.at[rows, at], wa.at[i], sems.at[2 * i]),
                pltpu.make_async_copy(w_c.at[rows, at], wb.at[i], sems.at[2 * i + 1]),
            )
        )
    for pair in copies:
        for copy in pair:
            copy.start()
    for i, pair in enumerate(copies):
        for copy in pair:
            copy.wait()
        acc[i] = nn(o[...], wa[i]) + nn(o_c[...], wb[i])


def project_fixed_kernel(meta, o, o_c, w, w_c, acc, keep, send, wa, wb, sems):
    zl, c = meta[2], meta[3]
    wide = wa.shape[2]
    copies = []
    for i, z in enumerate((zl, 1 - zl)):
        at = pl.ds(pl.multiple_of((2 * z + c) * wide, wide), wide)
        rows = pl.ds(0, HEAD)
        copies.append(
            (
                pltpu.make_async_copy(w.at[rows, at], wa.at[i], sems.at[2 * i]),
                pltpu.make_async_copy(w_c.at[rows, at], wb.at[i], sems.at[2 * i + 1]),
            )
        )
    for pair in copies:
        for copy in pair:
            copy.start()
    for i, ref in ((1, send), (0, keep)):
        for copy in copies[i]:
            copy.wait()
        total = acc[i] + nn(o[...], wa[i]) + nn(o_c[...], wb[i])
        ref[...] = total.astype(ref.dtype)


def final_kernel(
    meta,
    soff_t,
    sidx,
    dkv,
    own,
    dq0,
    dq1,
    dq2,
    dq3,
    oa,
    after,
    strided_dq,
    strided,
    keep,
    over,
    out,
    qg,
    kg,
    vg,
):
    zh = meta[1]
    shard = GROUP * meta[0] + meta[1]
    out[...] = (keep[...] + over[...].astype(F32)).astype(BF)
    pick = summary_select(sidx[...])
    fixed = own[...] + nn(jnp.concatenate([pick] * ROWS, 1), dkv[...])
    kg[:, :HEAD] = fixed[:, :HEAD].astype(BF)
    vg[:, :HEAD] = fixed[:, HEAD:].astype(BF)
    fixed = dq0[...]
    for ref in (dq1, dq2, dq3):
        fixed = fixed + whole(ref[...].astype(F32))
    eye = ones_where(iota((HEAD, HEAD), 0) == iota((HEAD, HEAD), 1))
    qg[:, :HEAD] = tn(fixed.astype(BF), eye).astype(BF)
    qg[:, HEAD:] = strided_dq[...]
    sel = stride_select(soff_t[...], shard)
    slots = []
    for u in range(4):
        t = lax.rem(zh + 1 + u, GROUP)
        here = oa[t, TOK + STAT :, :].astype(F32)
        there = after[t].astype(F32)
        block = jnp.where(zh + 1 + u < GROUP, here, there).astype(BF)
        slots.append(
            jnp.concatenate(
                [block[h * REACH : (h + 1) * REACH] for h in range(6)], 1
            )
        )
    total = strided[...] + tn(sel, jnp.concatenate(slots, 0))
    kg[:, HEAD:] = total[:, : 3 * HEAD].astype(BF)
    vg[:, HEAD:] = total[:, 3 * HEAD :].astype(BF)


def swap(a, axis):
    return lax.ppermute(a, axis, [(0, 1), (1, 0)])


def turn(a, by):
    return lax.ppermute(a, "zh", [(i, (i + by) % GROUP) for i in range(GROUP)])


def dma(n):
    return pltpu.SemaphoreType.DMA((n,))


def shards(queries, key_rows, value_rows, out_weight, upstream, summary_index, soff):
    row = lax.axis_index(("x", "y"))
    zh, zl, c = lax.axis_index("zh"), lax.axis_index("zl"), lax.axis_index("c")
    meta = jnp.stack([row, zh, zl, c]).astype(jnp.int32)
    soff_t = soff.T
    width = queries.shape[1]
    quarter = upstream.shape[1]
    plane = ("x", "y")
    matmul = 2 * ALL * KEYS * HEAD
    half_grad = 2 * TOK * 2 * quarter * width

    up_z = swap(upstream, "zl")
    up_c = swap(upstream, "c")
    kvb, q0, kv0, picks = call(
        prep_kernel,
        [
            sds((ROWS, SUMM, 2 * HEAD)),
            sds((TOK, HEAD)),
            sds((TOK, 2 * HEAD)),
            sds((4, FAR, HEAD)),
        ],
        [meta, soff_t, summary_index, queries, key_rows, value_rows],
        10**8,
        [
            pltpu.VMEM((TOK, width), BF),
            pltpu.VMEM((TOK, width), BF),
            pltpu.VMEM((1, SUMM), jnp.int32),
            pltpu.VMEM((4, ROWS * GROUP), jnp.int32),
            dma(5),
        ],
        name="pick_rows",
        specs=[SM] + [ANY] * 5,
    )
    before = lax.ppermute(picks, plane, [(i, i + 1) for i in range(ROWS - 1)])
    kva = lax.all_to_all(kvb, plane, 0, 0, tiled=True).reshape(KEYS, 2 * HEAD)
    sent = call(
        bundle_kernel,
        [sds((TOK + FAR, HEAD))] * 3,
        [meta, q0, picks, before],
        10**5,
        name="bundle_queries",
    )
    qs = [q0] + [turn(sent[d - 1], d) for d in (1, 2, 3)]
    (acc,) = call(
        grad_near_kernel,
        [sds((TOK, width), F32)],
        [meta, upstream, up_c, out_weight],
        half_grad,
        name="attention_grad_near",
    )
    up_zc = swap(up_z, "c")
    g, g0 = call(
        grad_far_kernel,
        [sds((TOK, width)), sds((TOK, HEAD))],
        [meta, up_z, up_zc, out_weight, acc],
        half_grad,
        name="attention_grad_far",
    )
    gs = [g0] + [turn(g0, d) for d in (1, 2, 3)]
    o_s, dq_s, dkv_s, far = call(
        strided_kernel,
        [
            sds((TOK, 3 * HEAD)),
            sds((TOK, 3 * HEAD)),
            sds((TOK, 6 * HEAD), F32),
            sds((4, FAR, HEAD)),
        ],
        [meta, queries, key_rows, value_rows, g, *qs[1:], before],
        3 * 6 * 2 * TOK * 320 * HEAD,
        name="strided_heads",
    )
    late_weight, _ = lax.optimization_barrier((out_weight, g0))
    weight_c = swap(late_weight, "c")
    o_sc = swap(o_s, "c")
    (ob,) = call(
        forward_kernel,
        [sds((GROUP, TOK + STAT + FAR, HEAD))],
        [meta, *qs, *gs, kva, kv0, far],
        3 * matmul,
        [pltpu.VMEM((KEYS, ALL), F32)],
        name="fixed_forward",
    )
    oa = lax.all_to_all(ob, "zh", 0, 0, tiled=True)
    (acc_out,) = call(
        project_strided_kernel,
        [sds((2, TOK, quarter), F32)],
        [meta, o_s, o_sc, out_weight, weight_c],
        2 * TOK * 6 * HEAD * 2 * quarter,
        [
            pltpu.VMEM((2, 3 * HEAD, quarter), BF),
            pltpu.VMEM((2, 3 * HEAD, quarter), BF),
            dma(4),
        ],
        name="project_strided",
        specs=[SM, VM, VM, ANY, ANY],
    )
    o_f, stat = call(
        combine_kernel,
        [sds((TOK, HEAD)), sds((8, ALL), F32)],
        [meta, oa],
        10**6,
        name="combine",
    )
    o_fc = swap(o_f, "c")
    after = lax.ppermute(
        oa[:, TOK + STAT :, :], plane, [(i + 1, i) for i in range(ROWS - 1)]
    )
    dkv, own, dq0, *dqs = call(
        backward_kernel,
        [
            sds((KEYS, 2 * HEAD)),
            sds((TOK, 2 * HEAD), F32),
            sds((HEAD, TOK), F32),
        ]
        + [sds((TOK, HEAD))] * 3,
        [meta, *qs, *gs, kva, kv0, stat],
        5 * matmul,
        name="fixed_backward",
    )
    dkva = lax.all_to_all(
        dkv.reshape(ROWS, SUMM, 2 * HEAD), plane, 0, 0, tiled=True
    ).reshape(KEYS, 2 * HEAD)
    dqs = [turn(dqs[d - 1], -d) for d in (1, 2, 3)]
    keep, send = call(
        project_fixed_kernel,
        [sds((TOK, quarter), F32), sds((TOK, quarter))],
        [meta, o_f, o_fc, out_weight, weight_c, acc_out],
        2 * TOK * 2 * HEAD * 2 * quarter,
        [
            pltpu.VMEM((2, HEAD, quarter), BF),
            pltpu.VMEM((2, HEAD, quarter), BF),
            dma(4),
        ],
        name="project_fixed",
        specs=[SM, VM, VM, ANY, ANY, VM],
    )
    over = swap(send, "zl")
    return call(
        final_kernel,
        [sds((TOK, quarter))] + [sds((TOK, width))] * 3,
        [meta, soff_t, summary_index, dkva, own, dq0, *dqs, oa, after, dq_s, dkv_s]
        + [keep, over],
        3 * 10**8,
        name="join_results",
    )


def solution(mesh):
    grid = Mesh(mesh.devices.reshape(4, 4, 4, 2, 2), ("x", "y", "zh", "zl", "c"))
    ctx, head = ("x", "y", "zh"), ("zl", "c")
    return jax.shard_map(
        shards,
        mesh=grid,
        in_specs=(
            P(ctx, head),
            P(ctx, head),
            P(ctx, head),
            P(head, None),
            P(ctx, head),
            P(ctx, None),
            P(),
        ),
        out_specs=(P(ctx, head),) * 4,
        check_vma=False,
    )
```

time: 148 us -> 159 us (1.074)
  blocking collectives: 0 us -> 15.6 us
  waiting for transfers between devices: 52 us -> 37.4 us
  local copies, waits for them, and re-layouts: 11.3 us -> 19.4 us
  Pallas kernels: 29.4 us -> 34.2 us
  other arithmetic: 4.37 us -> 0.08 us
  starting transfers between devices: 47.7 us -> 50 us
    all_to_all x5 -> x1, waiting for transfers between devices: 36.7 us -> 0.01 us  [shards(): kva = lax.all_to_all(kvb, plane, 0, 0, tiled=True).reshape(KEYS, 2 * HEAD)]
    ppermute x1 -> x10, starting transfers between devices: 2.76 us -> 25.1 us  [the longest x9 22.3 us: turn(): return lax.ppermute(a, 'zh', [(i, (i + by) % GROUP) for i in range(GROUP)])]
    all_to_all x5 -> x1, starting transfers between devices: 27.3 us -> 7.18 us  [shards(): kva = lax.all_to_all(kvb, plane, 0, 0, tiled=True).reshape(KEYS, 2 * HEAD)]
    all_to_all x0 -> x1, blocking collectives: none -> 15.6 us  [shards(): oa = lax.all_to_all(ob, 'zh', 0, 0, tiled=True)]
    ppermute x6 -> x7, waiting for transfers between devices: 0.02 us -> 13.1 us  [swap(): return lax.ppermute(a, axis, [(0, 1), (1, 0)])]
    unnamed x45 -> x80, local copies, waits for them, and re-layouts: 11.3 us -> 19.3 us
    ppermute x1 -> x10, waiting for transfers between devices: 7.49 us -> 14.1 us  [the longest x9 14.1 us: turn(): return lax.ppermute(a, 'zh', [(i, (i + by) % GROUP) for i in range(GROUP)])]
    pallas_call x7 -> x11, Pallas kernels: 29.4 us -> 34.2 us  [call(): pl.pallas_call(kernel, out_shape=tuple(outs), in_specs=specs or [SM] + [V...]
  transfers between devices with their start and end apart: 14 -> 20, of which waited for: 6 -> 6; matrix products, arithmetic and copies ran while one was open for 1% -> 0% of each run, Pallas kernels for 10% -> 18%
where the time goes in v2:
time: 159 us; the launch traced here: 158 us
  starting transfers between devices  50 us (31%)
  waiting for transfers between devices  37.4 us (24%)
  Pallas kernels  34.2 us (22%)
  local copies, waits for them, and re-layouts  19.4 us (12%)
  blocking collectives  15.6 us (10%)
    pallas_call x11, Pallas kernels, call(): pl.pallas_call(kernel, out_shape=tuple(outs), in_specs=specs or [SM] + [V...  34.2 us
    ppermute x9, starting transfers between devices, turn(): return lax.ppermute(a, 'zh', [(i, (i + by) % GROUP) for i in range(GROUP)])  22.3 us
    unnamed x80, local copies, waits for them, and re-layouts  19.3 us
    all_to_all x1, blocking collectives, shards(): oa = lax.all_to_all(ob, 'zh', 0, 0, tiled=True)  15.6 us
    ppermute x9, waiting for transfers between devices, turn(): return lax.ppermute(a, 'zh', [(i, (i + by) % GROUP) for i in range(GROUP)])  14.1 us
    ppermute x7, waiting for transfers between devices, swap(): return lax.ppermute(a, axis, [(0, 1), (1, 0)])  13.1 us
    all_to_all x1, starting transfers between devices, shards(): lax.all_to_all(dkv.reshape(ROWS, SUMM, 2 * HEAD), plane, 0, 0, tiled=True)  11.3 us
    ppermute x1, waiting for transfers between devices, shards(): before = lax.ppermute(picks, plane, [(i, i + 1) for i in range(ROWS - 1)])  10.2 us
  transfers between devices with their start and end apart: 20, of which 6 were waited for; matrix products, arithmetic and copies ran while one was open for 0% of the time, Pallas kernels for 18%

profile of v2, /device:TPU:24, one launch (start us, length us, event | category | flops | bytes accessed | tf_op | source)
XLA Modules:
  0.0 157.6 jit_solution(12842913075627672252)
XLA Ops:
  0.6 2.0 %collective-permute-start.4 = (bf16[256,1024]{1,0:T(8,128)(2,1)}, bf16[256,1024]{1,0:T(8,128)(2,1)S(1)}, u32[]{:S(2)}, u32[]{:S(2)}) collective-permute-start(bf16[256,1024]{1,0:T(8,128)(2,1)} %up.1), channel_id=1, source_target_pairs={{0,2},{2,0},{1,3},{3,1},{4,6},{6,4},{5,7},{7,5},{8,10},{10,8},{9,1... | collective-permute-start | bytes 1572872 | tf_op jit(solution)/shard_map/ppermute | solution.py:483
  2.6 12.1 %collective-permute-done.4.up_z = bf16[256,1024]{1,0:T(8,128)(2,1)S(1)} collective-permute-done((bf16[256,1024]{1,0:T(8,128)(2,1)}, bf16[256,1024]{1,0:T(8,128)(2,1)S(1)}, u32[]{:S(2)}, u32[]{:S(2)}) %collective-permute-start.4) | collective-permute-done | bytes 524320 | tf_op jit(solution)/shard_map/ppermute | solution.py:483
  14.9 1.0 copy-done.3
  15.9 2.9 %attention_grad_near.1.acc = f32[256,512]{1,0:T(8,128)S(1)} custom-call(s32[4]{0:T(128)S(1)} %pad_add_fusion.meta, bf16[256,1024]{1,0:T(8,128)(2,1)S(1)} %copy-done.3, bf16[256,1024]{1,0:T(8,128)(2,1)S(1)} %collective-permute-done.6.up_c, bf16[512,4096]{1,0:T(8,128)(2,1)} %w.7), custom_call_target="tpu_custom_call" | custom-call | flops 536870912 | bytes 5767184 | tf_op jit(solution)/shard_map/attention_grad_near/pallas_call | solution.py:75
  18.9 3.6 %attention_grad_far.1 = (bf16[256,512]{1,0:T(8,128)(2,1)S(1)}, bf16[256,128]{1,0:T(8,128)(2,1)}) custom-call(s32[4]{0:T(128)S(1)} %pad_add_fusion.meta, bf16[256,1024]{1,0:T(8,128)(2,1)S(1)} %collective-permute-done.4.up_z, bf16[256,1024]{1,0:T(8,128)(2,1)S(1)} %collective-permute-done.5.up_zc, bf16[512,4096]{1,0:T(8,128)(2,1)} %w.7, ...), custom_call_target="tpu_custom_call" | custom-call | flops 536870912 | bytes 6094864 | tf_op jit(solution)/shard_map/attention_grad_far/pallas_call | solution.py:75
  23.1 2.0 %pick_rows.1 = (bf16[16,128,256]{2,1,0:T(8,128)(2,1)}, bf16[256,128]{1,0:T(8,128)(2,1)S(1)}, bf16[256,256]{1,0:T(8,128)(2,1)S(1)}, bf16[4,96,128]{2,1,0:T(8,128)(2,1)S(1)}) custom-call(s32[4]{0:T(128)S(1)} %pad_add_fusion.meta, s32[4,64]{1,0:T(4,128)S(1)} %bitcast.11, s32[1,128]{1,0:T(1,128)S(1)} %copy-done.29, bf16[256,512]{1,0:T(8,128)(2,1)S(1)} %copy-done, ...), custom_call_target="tpu_custom_call" | custom-call | flops 100000000 | bytes 2131472 | tf_op jit(solution)/shard_map/pick_rows/pallas_call | solution.py:75
  25.1 7.2 %all-to-all-start = ((bf16[16,128,256]{2,1,0:T(8,128)(2,1)}), bf16[16,128,256]{2,1,0:T(8,128)(2,1)S(1)}, u32[]{:S(2)}, u32[]{:S(2)}) async-start(bf16[16,128,256]{2,1,0:T(8,128)(2,1)} %get-tuple-element.34), calls=%async_computation | async-start | bytes 2097152 | tf_op jit(solution)/shard_map/all_to_all | solution.py:528
  32.3 3.4 %collective-permute-start = (bf16[4,96,128]{2,1,0:T(8,128)(2,1)S(1)}, bf16[4,96,128]{2,1,0:T(8,128)(2,1)S(1)}, u32[]{:S(2)}, u32[]{:S(2)}) collective-permute-start(bf16[4,96,128]{2,1,0:T(8,128)(2,1)S(1)} %get-tuple-element.29.picks), channel_id=1, source_target_pairs={{0,16},{16,32},{32,48},{48,64},{64,80},{80,96},{96,112},{112,128},... | collective-permute-start | bytes 294920 | tf_op jit(solution)/shard_map/ppermute | solution.py:527
  35.6 10.2 %collective-permute-done.before = bf16[4,96,128]{2,1,0:T(8,128)(2,1)S(1)} collective-permute-done((bf16[4,96,128]{2,1,0:T(8,128)(2,1)S(1)}, bf16[4,96,128]{2,1,0:T(8,128)(2,1)S(1)}, u32[]{:S(2)}, u32[]{:S(2)}) %collective-permute-start) | collective-permute-done | bytes 98336 | tf_op jit(solution)/shard_map/ppermute | solution.py:527
  46.4 3.3 %collective-permute-start.1 = (bf16[352,128]{1,0:T(8,128)(2,1)S(1)}, bf16[352,128]{1,0:T(8,128)(2,1)S(1)}, u32[]{:S(2)}, u32[]{:S(2)}) collective-permute-start(bf16[352,128]{1,0:T(8,128)(2,1)S(1)} %get-tuple-element.30), channel_id=1, source_target_pairs={{0,4},{4,8},{8,12},{12,0},{1,5},{5,9},{9,13},{13,1},{2,6},{6,10},{... | collective-permute-start | bytes 270344 | tf_op jit(solution)/shard_map/ppermute | solution.py:487
  49.7 5.2 %collective-permute-start.2 = (bf16[352,128]{1,0:T(8,128)(2,1)S(1)}, bf16[352,128]{1,0:T(8,128)(2,1)S(1)}, u32[]{:S(2)}, u32[]{:S(2)}) collective-permute-start(bf16[352,128]{1,0:T(8,128)(2,1)S(1)} %get-tuple-element.31), channel_id=1, source_target_pairs={{0,8},{4,12},{8,0},{12,4},{1,9},{5,13},{9,1},{13,5},{2,10},{6,14},... | collective-permute-start | bytes 270344 | tf_op jit(solution)/shard_map/ppermute | solution.py:487
  55.0 2.7 %collective-permute-start.3 = (bf16[352,128]{1,0:T(8,128)(2,1)S(1)}, bf16[352,128]{1,0:T(8,128)(2,1)S(1)}, u32[]{:S(2)}, u32[]{:S(2)}) collective-permute-start(bf16[352,128]{1,0:T(8,128)(2,1)S(1)} %get-tuple-element.32), channel_id=1, source_target_pairs={{0,12},{4,0},{8,4},{12,8},{1,13},{5,1},{9,5},{13,9},{2,14},{6,2},{... | collective-permute-start | bytes 270344 | tf_op jit(solution)/shard_map/ppermute | solution.py:487
  57.7 4.1 %collective-permute-start.8 = (bf16[256,128]{1,0:T(8,128)(2,1)}, bf16[256,128]{1,0:T(8,128)(2,1)}, u32[]{:S(2)}, u32[]{:S(2)}) collective-permute-start(bf16[256,128]{1,0:T(8,128)(2,1)} %get-tuple-element.33.g0), channel_id=1, source_target_pairs={{0,8},{4,12},{8,0},{12,4},{1,9},{5,13},{9,1},{13,5},{2,10},{6,14},... | collective-permute-start | bytes 196616 | tf_op jit(solution)/shard_map/ppermute | solution.py:487
  61.7 1.8 %collective-permute-start.7 = (bf16[256,128]{1,0:T(8,128)(2,1)}, bf16[256,128]{1,0:T(8,128)(2,1)}, u32[]{:S(2)}, u32[]{:S(2)}) collective-permute-start(bf16[256,128]{1,0:T(8,128)(2,1)} %get-tuple-element.33.g0), channel_id=1, source_target_pairs={{0,4},{4,8},{8,12},{12,0},{1,5},{5,9},{9,13},{13,1},{2,6},{6,10},{... | collective-permute-start | bytes 196616 | tf_op jit(solution)/shard_map/ppermute | solution.py:487
  63.5 3.5 %collective-permute-done.3.f3.q3 = bf16[352,128]{1,0:T(8,128)(2,1)S(1)} collective-permute-done((bf16[352,128]{1,0:T(8,128)(2,1)S(1)}, bf16[352,128]{1,0:T(8,128)(2,1)S(1)}, u32[]{:S(2)}, u32[]{:S(2)}) %collective-permute-start.3) | collective-permute-done | bytes 90144 | tf_op jit(solution)/shard_map/ppermute | solution.py:487
  67.0 3.1 %strided_heads.1 = (bf16[256,384]{1,0:T(8,128)(2,1)S(1)}, bf16[256,384]{1,0:T(8,128)(2,1)S(1)}, f32[256,768]{1,0:T(8,128)S(1)}, bf16[4,96,128]{2,1,0:T(8,128)(2,1)S(1)}) custom-call(s32[4]{0:T(128)S(1)} %pad_add_fusion.meta, bf16[256,512]{1,0:T(8,128)(2,1)S(1)} %copy-done, bf16[256,512]{1,0:T(8,128)(2,1)S(1)} %copy-done.1, bf16[256,512]{1,0:T(8,128)(2,1)S(1)} %copy-done.2, ...), custom_call_target="tpu_custom_call" | custom-call | flops 377487360 | bytes 2695184 | tf_op jit(solution)/shard_map/strided_heads/pallas_call | solution.py:75
  74.7 0.9 copy-done.31
  76.5 5.1 %fixed_forward.1 = bf16[4,416,128]{2,1,0:T(8,128)(2,1)S(1)} custom-call(s32[4]{0:T(128)S(1)} %pad_add_fusion.meta, bf16[256,128]{1,0:T(8,128)(2,1)S(1)} %get-tuple-element.28.q0, bf16[352,128]{1,0:T(8,128)(2,1)S(1)} %copy-done.11, bf16[352,128]{1,0:T(8,128)(2,1)S(1)} %copy-done.13, bf16[352,128]{1,0:T(8,128)(2,1)S(1)} %copy-done.16, ...), custom_call_target="tpu_custom_call" | custom-call | flops 1610612736 | bytes 2301968 | tf_op jit(solution)/shard_map/fixed_forward/pallas_call | solution.py:75
  81.7 15.6 %all_to_all.15.oa = bf16[4,416,128]{2,1,0:T(8,128)(2,1)S(1)} all-to-all(bf16[4,416,128]{2,1,0:T(8,128)(2,1)S(1)} %fixed_forward.1), channel_id=1, replica_groups=mesh['x'=4,'y'=4,'zh'=4,'zl'=2,'c'=2] {'zh'}, dimensions={0} | all-to-all | bytes 851968 | tf_op jit(solution)/shard_map/all_to_all | solution.py:576
  99.0 7.1 %fixed_backward.1 = (bf16[2048,256]{1,0:T(8,128)(2,1)}, f32[256,256]{1,0:T(8,128)S(1)}, f32[128,256]{1,0:T(8,128)S(1)}, bf16[256,128]{1,0:T(8,128)(2,1)S(1)}, bf...) custom-call(s32[4]{0:T(128)S(1)} %pad_add_fusion.meta, bf16[256,128]{1,0:T(8,128)(2,1)S(1)} %copy-done.27, ...), custom_call_target="tpu_custom_call" | custom-call | flops 2684354560 | bytes 3448848 | tf_op jit(solution)/shard_map/fixed_backward/pallas_call | solution.py:75
  109.3 11.3 %all-to-all-start.2 = ((bf16[16,128,256]{2,1,0:T(8,128)(2,1)}), bf16[16,128,256]{2,1,0:T(8,128)(2,1)S(1)}, u32[]{:S(2)}, u32[]{:S(2)}) async-start(bf16[16,128,256]{2,1,0:T(8,128)(2,1)} %bitcast.6), calls=%async_computation.2 | async-start | bytes 2097152 | tf_op jit(solution)/shard_map/all_to_all | solution.py:613
  121.1 0.9 collective-permute-done.16.o_c
  122.0 3.4 %project_strided.1.acc = f32[2,256,1024]{2,1,0:T(8,128)S(1)} custom-call(s32[4]{0:T(128)S(1)} %pad_add_fusion.meta, bf16[256,384]{1,0:T(8,128)(2,1)S(1)} %get-tuple-element.49.o, bf16[256,384]{1,0:T(8,128)(2,1)S(1)} %collective-permute-done.16.o_c, bf16[512,4096]{1,0:T(8,128)(2,1)} %w.7, bf16[512,4096]{1,0:T(8,128)(2,1)} %collective-permute-done.15.w_c), custom_call_target="tpu_custom_call" | custom-call | flops 805306368 | bytes 10878992 | tf_op jit(solution)/shard_map/project_strided/pallas_call | solution.py:75
  125.4 3.0 %project_fixed.1 = (f32[256,1024]{1,0:T(8,128)S(1)}, bf16[256,1024]{1,0:T(8,128)(2,1)}) custom-call(s32[4]{0:T(128)S(1)} %pad_add_fusion.meta, bf16[256,128]{1,0:T(8,128)(2,1)S(1)} %copy-done.21, bf16[256,128]{1,0:T(8,128)(2,1)S(1)} %collective-permute-done.14.o_c, bf16[512,4096]{1,0:T(8,128)(2,1)} %w.7, bf16[512,4096]{1,0:T(8,128)(2,1)} %collective-permute-done.15.w_c, ...), custom_call_target="tpu_custom_call" | custom-call | flops 268435456 | bytes 12189712 | tf_op jit(solution)/shard_map/project_fixed/pallas_call | solution.py:75
  128.6 2.8 %collective-permute-start.13 = (bf16[4,96,128]{2,1,0:T(8,128)(2,1)S(1)}, bf16[4,96,128]{2,1,0:T(8,128)(2,1)S(1)}, u32[]{:S(2)}, u32[]{:S(2)}) collective-permute-start(bf16[4,96,128]{2,1,0:T(8,128)(2,1)S(1)} %slice.4), channel_id=1, source_target_pairs={{16,0},{32,16},{48,32},{64,48},{80,64},{96,80},{112,96},{128,112},... | collective-permute-start | bytes 294920 | tf_op jit(solution)/shard_map/ppermute | solution.py:598
  131.4 2.1 %collective-permute-start.10 = (bf16[256,128]{1,0:T(8,128)(2,1)S(1)}, bf16[256,128]{1,0:T(8,128)(2,1)S(1)}, u32[]{:S(2)}, u32[]{:S(2)}) collective-permute-start(bf16[256,128]{1,0:T(8,128)(2,1)S(1)} %copy-done.39), channel_id=1, source_target_pairs={{0,12},{4,0},{8,4},{12,8},{1,13},{5,1},{9,5},{13,9},{2,14},{6,2},{... | collective-permute-start | bytes 196616 | tf_op jit(solution)/shard_map/ppermute | solution.py:487
  133.5 1.9 %collective-permute-start.11 = (bf16[256,128]{1,0:T(8,128)(2,1)S(1)}, bf16[256,128]{1,0:T(8,128)(2,1)S(1)}, u32[]{:S(2)}, u32[]{:S(2)}) collective-permute-start(bf16[256,128]{1,0:T(8,128)(2,1)S(1)} %copy-done.37), channel_id=1, source_target_pairs={{0,8},{4,12},{8,0},{12,4},{1,9},{5,13},{9,1},{13,5},{2,10},{6,14},... | collective-permute-start | bytes 196616 | tf_op jit(solution)/shard_map/ppermute | solution.py:487
  135.4 1.2 collective-permute-start.12
  137.3 10.5 %collective-permute-done.11.dq2 = bf16[256,128]{1,0:T(8,128)(2,1)S(1)} collective-permute-done((bf16[256,128]{1,0:T(8,128)(2,1)S(1)}, bf16[256,128]{1,0:T(8,128)(2,1)S(1)}, u32[]{:S(2)}, u32[]{:S(2)}) %collective-permute-start.11) | collective-permute-done | bytes 65568 | tf_op jit(solution)/shard_map/ppermute | solution.py:487
  149.7 0.9 copy-done.5
  150.7 0.9 copy-done.7
  155.0 2.6 %join_results.1 = (bf16[256,1024]{1,0:T(8,128)(2,1)}, bf16[256,512]{1,0:T(8,128)(2,1)}, bf16[256,512]{1,0:T(8,128)(2,1)}, bf16[256,512]{1,0:T(8,128)(2,1)}) custom-call(s32[4]{0:T(128)S(1)} %pad_add_fusion.meta, s32[4,64]{1,0:T(4,128)S(1)} %bitcast.12, s32[1,128]{1,0:T(1,128)S(1)} %copy-done.29, bf16[2048,256]{1,0:T(8,128)(2,1)S(1)} %bitcast.8, ...), custom_call_target="tpu_custom_call" | custom-call | flops 300000000 | bytes 6030864 | tf_op jit(solution)/shard_map/join_results/pallas_call | solution.py:75
  (102 shorter events, 18.3 us)
Async XLA Ops:
  0.6 14.1 %collective-permute-start.4 = (bf16[256,1024]{1,0:T(8,128)(2,1)}, bf16[256,1024]{1,0:T(8,128)(2,1)S(1)}, u32[]{:S(2)}, u32[]{:S(2)}) collective-permute-start(bf16[256,1024]{1,0:T(8,128)(2,1)} %up.1), channel_id=1, source_target_pairs={{0,2},{2,0},{1,3},{3,1},{4,6},{6,4},{5,7},{7,5},{8,10},{10,8},{9,1... | collective-permute-start | bytes 1572872 | tf_op jit(solution)/shard_map/ppermute | solution.py:483
  2.6 12.2 %collective-permute-start.6 = (bf16[256,1024]{1,0:T(8,128)(2,1)}, bf16[256,1024]{1,0:T(8,128)(2,1)S(1)}, u32[]{:S(2)}, u32[]{:S(2)}) collective-permute-start(bf16[256,1024]{1,0:T(8,128)(2,1)} %up.1), channel_id=1, source_target_pairs={{0,1},{1,0},{2,3},{3,2},{4,5},{5,4},{6,7},{7,6},{8,9},{9,8},{10,11... | collective-permute-start | bytes 1572872 | tf_op jit(solution)/shard_map/ppermute | solution.py:483
  14.8 4.1 %collective-permute-start.5 = (bf16[256,1024]{1,0:T(8,128)(2,1)S(1)}, bf16[256,1024]{1,0:T(8,128)(2,1)S(1)}, u32[]{:S(2)}, u32[]{:S(2)}) collective-permute-start(bf16[256,1024]{1,0:T(8,128)(2,1)S(1)} %collective-permute-done.4.up_z), channel_id=1, source_target_pairs={{0,1},{1,0},{2,3},{3,2},{4,5},{5,4},{6,7},{7,6},{8,9},{9,8},{10,11... | collective-permute-start | bytes 1572872 | tf_op jit(solution)/shard_map/ppermute | solution.py:483
  18.8 4.2 %copy-start = (bf16[256,512]{1,0:T(8,128)(2,1)S(1)}, bf16[256,512]{1,0:T(8,128)(2,1)}, u32[]{:S(2)}) copy-start(bf16[256,512]{1,0:T(8,128)(2,1)} %q.3) | copy-start | bytes 786436
  18.9 4.2 %copy-start.1 = (bf16[256,512]{1,0:T(8,128)(2,1)S(1)}, bf16[256,512]{1,0:T(8,128)(2,1)}, u32[]{:S(2)}) copy-start(bf16[256,512]{1,0:T(8,128)(2,1)} %k.3) | copy-start | bytes 786436
  22.6 99.5 %collective-permute-start.15 = (bf16[512,4096]{1,0:T(8,128)(2,1)}, bf16[512,4096]{1,0:T(8,128)(2,1)}, u32[]{:S(2)}, u32[]{:S(2)}) collective-permute-start(bf16[512,4096]{1,0:T(8,128)(2,1)} %w.7), channel_id=1, source_target_pairs={{0,1},{1,0},{2,3},{3,2},{4,5},{5,4},{6,7},{7,6},{8,9},{9,8},{10,11... | collective-permute-start | bytes 12582920 | tf_op jit(solution)/shard_map/ppermute | solution.py:483
  25.1 42.0 %copy-start.30 = (bf16[256,256]{1,0:T(8,128)(2,1)}, bf16[256,256]{1,0:T(8,128)(2,1)S(1)}, u32[]{:S(2)}) copy-start(bf16[256,256]{1,0:T(8,128)(2,1)S(1)} %get-tuple-element.35.kv0) | copy-start | bytes 393220
  25.1 56.6 %copy-start.26 = (bf16[256,128]{1,0:T(8,128)(2,1)}, bf16[256,128]{1,0:T(8,128)(2,1)S(1)}, u32[]{:S(2)}) copy-start(bf16[256,128]{1,0:T(8,128)(2,1)S(1)} %get-tuple-element.28.q0) | copy-start | bytes 196612
  25.1 46.9 %all-to-all-start = ((bf16[16,128,256]{2,1,0:T(8,128)(2,1)}), bf16[16,128,256]{2,1,0:T(8,128)(2,1)S(1)}, u32[]{:S(2)}, u32[]{:S(2)}) async-start(bf16[16,128,256]{2,1,0:T(8,128)(2,1)} %get-tuple-element.34), calls=%async_computation | async-start | bytes 2097152 | tf_op jit(solution)/shard_map/all_to_all | solution.py:528
  32.3 13.5 %collective-permute-start = (bf16[4,96,128]{2,1,0:T(8,128)(2,1)S(1)}, bf16[4,96,128]{2,1,0:T(8,128)(2,1)S(1)}, u32[]{:S(2)}, u32[]{:S(2)}) collective-permute-start(bf16[4,96,128]{2,1,0:T(8,128)(2,1)S(1)} %get-tuple-element.29.picks), channel_id=1, source_target_pairs={{0,16},{16,32},{32,48},{48,64},{64,80},{80,96},{96,112},{112,128},... | collective-permute-start | bytes 294920 | tf_op jit(solution)/shard_map/ppermute | solution.py:527
  46.4 11.3 %collective-permute-start.1 = (bf16[352,128]{1,0:T(8,128)(2,1)S(1)}, bf16[352,128]{1,0:T(8,128)(2,1)S(1)}, u32[]{:S(2)}, u32[]{:S(2)}) collective-permute-start(bf16[352,128]{1,0:T(8,128)(2,1)S(1)} %get-tuple-element.30), channel_id=1, source_target_pairs={{0,4},{4,8},{8,12},{12,0},{1,5},{5,9},{9,13},{13,1},{2,6},{6,10},{... | collective-permute-start | bytes 270344 | tf_op jit(solution)/shard_map/ppermute | solution.py:487
  49.7 12.0 %collective-permute-start.2 = (bf16[352,128]{1,0:T(8,128)(2,1)S(1)}, bf16[352,128]{1,0:T(8,128)(2,1)S(1)}, u32[]{:S(2)}, u32[]{:S(2)}) collective-permute-start(bf16[352,128]{1,0:T(8,128)(2,1)S(1)} %get-tuple-element.31), channel_id=1, source_target_pairs={{0,8},{4,12},{8,0},{12,4},{1,9},{5,13},{9,1},{13,5},{2,10},{6,14},... | collective-permute-start | bytes 270344 | tf_op jit(solution)/shard_map/ppermute | solution.py:487
  55.0 12.1 %collective-permute-start.3 = (bf16[352,128]{1,0:T(8,128)(2,1)S(1)}, bf16[352,128]{1,0:T(8,128)(2,1)S(1)}, u32[]{:S(2)}, u32[]{:S(2)}) collective-permute-start(bf16[352,128]{1,0:T(8,128)(2,1)S(1)} %get-tuple-element.32), channel_id=1, source_target_pairs={{0,12},{4,0},{8,4},{12,8},{1,13},{5,1},{9,5},{13,9},{2,14},{6,2},{... | collective-permute-start | bytes 270344 | tf_op jit(solution)/shard_map/ppermute | solution.py:487
  57.6 14.4 %collective-permute-start.9 = (bf16[256,128]{1,0:T(8,128)(2,1)}, bf16[256,128]{1,0:T(8,128)(2,1)}, u32[]{:S(2)}, u32[]{:S(2)}) collective-permute-start(bf16[256,128]{1,0:T(8,128)(2,1)} %get-tuple-element.33.g0), channel_id=1, source_target_pairs={{0,12},{4,0},{8,4},{12,8},{1,13},{5,1},{9,5},{13,9},{2,14},{6,2},{... | collective-permute-start | bytes 196616 | tf_op jit(solution)/shard_map/ppermute | solution.py:487
  57.7 14.4 %copy-start.10 = (bf16[352,128]{1,0:T(8,128)(2,1)}, bf16[352,128]{1,0:T(8,128)(2,1)S(1)}, u32[]{:S(2)}) copy-start(bf16[352,128]{1,0:T(8,128)(2,1)S(1)} %collective-permute-done.1.f1.q1) | copy-start | bytes 270340
  57.7 14.4 %collective-permute-start.8 = (bf16[256,128]{1,0:T(8,128)(2,1)}, bf16[256,128]{1,0:T(8,128)(2,1)}, u32[]{:S(2)}, u32[]{:S(2)}) collective-permute-start(bf16[256,128]{1,0:T(8,128)(2,1)} %get-tuple-element.33.g0), channel_id=1, source_target_pairs={{0,8},{4,12},{8,0},{12,4},{1,9},{5,13},{9,1},{13,5},{2,10},{6,14},... | collective-permute-start | bytes 196616 | tf_op jit(solution)/shard_map/ppermute | solution.py:487
  61.7 10.3 %collective-permute-start.7 = (bf16[256,128]{1,0:T(8,128)(2,1)}, bf16[256,128]{1,0:T(8,128)(2,1)}, u32[]{:S(2)}, u32[]{:S(2)}) collective-permute-start(bf16[256,128]{1,0:T(8,128)(2,1)} %get-tuple-element.33.g0), channel_id=1, source_target_pairs={{0,4},{4,8},{8,12},{12,0},{1,5},{5,9},{9,13},{13,1},{2,6},{6,10},{... | collective-permute-start | bytes 196616 | tf_op jit(solution)/shard_map/ppermute | solution.py:487
  76.5 21.6 %copy-start.14 = (bf16[352,128]{1,0:T(8,128)(2,1)S(1)}, bf16[352,128]{1,0:T(8,128)(2,1)}, u32[]{:S(2)}) copy-start(bf16[352,128]{1,0:T(8,128)(2,1)} %copy-done.12) | copy-start | bytes 270340
  76.5 21.6 %copy-start.17 = (bf16[352,128]{1,0:T(8,128)(2,1)S(1)}, bf16[352,128]{1,0:T(8,128)(2,1)}, u32[]{:S(2)}) copy-start(bf16[352,128]{1,0:T(8,128)(2,1)} %copy-done.15) | copy-start | bytes 270340
  98.1 22.5 %copy-start.20 = (bf16[256,128]{1,0:T(8,128)(2,1)}, bf16[256,128]{1,0:T(8,128)(2,1)S(1)}, u32[]{:S(2)}) copy-start(bf16[256,128]{1,0:T(8,128)(2,1)S(1)} %get-tuple-element.47.o) | copy-start | bytes 196612
  109.3 40.4 %all-to-all-start.2 = ((bf16[16,128,256]{2,1,0:T(8,128)(2,1)}), bf16[16,128,256]{2,1,0:T(8,128)(2,1)S(1)}, u32[]{:S(2)}, u32[]{:S(2)}) async-start(bf16[16,128,256]{2,1,0:T(8,128)(2,1)} %bitcast.6), calls=%async_computation.2 | async-start | bytes 2097152 | tf_op jit(solution)/shard_map/all_to_all | solution.py:613
  120.6 1.4 collective-permute-start.16
  120.6 4.8 %collective-permute-start.14 = (bf16[256,128]{1,0:T(8,128)(2,1)S(1)}, bf16[256,128]{1,0:T(8,128)(2,1)S(1)}, u32[]{:S(2)}, u32[]{:S(2)}) collective-permute-start(bf16[256,128]{1,0:T(8,128)(2,1)S(1)} %get-tuple-element.47.o), channel_id=1, source_target_pairs={{0,1},{1,0},{2,3},{3,2},{4,5},{5,4},{6,7},{7,6},{8,9},{9,8},{10,11... | collective-permute-start | bytes 196616 | tf_op jit(solution)/shard_map/ppermute | solution.py:483
  121.1 4.4 %copy-start.21 = (bf16[256,128]{1,0:T(8,128)(2,1)S(1)}, bf16[256,128]{1,0:T(8,128)(2,1)}, u32[]{:S(2)}) copy-start(bf16[256,128]{1,0:T(8,128)(2,1)} %copy-done.20) | copy-start | bytes 196612
  125.4 5.9 %copy-start.39 = (bf16[256,128]{1,0:T(8,128)(2,1)S(1)}, bf16[256,128]{1,0:T(8,128)(2,1)}, u32[]{:S(2)}) copy-start(bf16[256,128]{1,0:T(8,128)(2,1)} %copy-done.38) | copy-start | bytes 196612
  125.4 8.1 %copy-start.37 = (bf16[256,128]{1,0:T(8,128)(2,1)S(1)}, bf16[256,128]{1,0:T(8,128)(2,1)}, u32[]{:S(2)}) copy-start(bf16[256,128]{1,0:T(8,128)(2,1)} %copy-done.36) | copy-start | bytes 196612
  125.4 10.0 %copy-start.35 = (bf16[256,128]{1,0:T(8,128)(2,1)S(1)}, bf16[256,128]{1,0:T(8,128)(2,1)}, u32[]{:S(2)}) copy-start(bf16[256,128]{1,0:T(8,128)(2,1)} %copy-done.34) | copy-start | bytes 196612
  128.4 21.3 %collective-permute-start.17 = (bf16[256,1024]{1,0:T(8,128)(2,1)}, bf16[256,1024]{1,0:T(8,128)(2,1)}, u32[]{:S(2)}, u32[]{:S(2)}) collective-permute-start(bf16[256,1024]{1,0:T(8,128)(2,1)} %get-tuple-element.51), channel_id=1, source_target_pairs={{0,2},{2,0},{1,3},{3,1},{4,6},{6,4},{5,7},{7,5},{8,10},{10,8},{9,1... | collective-permute-start | bytes 1572872 | tf_op jit(solution)/shard_map/ppermute | solution.py:483
  128.6 20.5 %collective-permute-start.13 = (bf16[4,96,128]{2,1,0:T(8,128)(2,1)S(1)}, bf16[4,96,128]{2,1,0:T(8,128)(2,1)S(1)}, u32[]{:S(2)}, u32[]{:S(2)}) collective-permute-start(bf16[4,96,128]{2,1,0:T(8,128)(2,1)S(1)} %slice.4), channel_id=1, source_target_pairs={{16,0},{32,16},{48,32},{64,48},{80,64},{96,80},{112,96},{128,112},... | collective-permute-start | bytes 294920 | tf_op jit(solution)/shard_map/ppermute | solution.py:598
  131.4 5.3 %collective-permute-start.10 = (bf16[256,128]{1,0:T(8,128)(2,1)S(1)}, bf16[256,128]{1,0:T(8,128)(2,1)S(1)}, u32[]{:S(2)}, u32[]{:S(2)}) collective-permute-start(bf16[256,128]{1,0:T(8,128)(2,1)S(1)} %copy-done.39), channel_id=1, source_target_pairs={{0,12},{4,0},{8,4},{12,8},{1,13},{5,1},{9,5},{13,9},{2,14},{6,2},{... | collective-permute-start | bytes 196616 | tf_op jit(solution)/shard_map/ppermute | solution.py:487
  133.5 14.3 %collective-permute-start.11 = (bf16[256,128]{1,0:T(8,128)(2,1)S(1)}, bf16[256,128]{1,0:T(8,128)(2,1)S(1)}, u32[]{:S(2)}, u32[]{:S(2)}) collective-permute-start(bf16[256,128]{1,0:T(8,128)(2,1)S(1)} %copy-done.37), channel_id=1, source_target_pairs={{0,8},{4,12},{8,0},{12,4},{1,9},{5,13},{9,1},{13,5},{2,10},{6,14},... | collective-permute-start | bytes 196616 | tf_op jit(solution)/shard_map/ppermute | solution.py:487
  135.4 13.0 %collective-permute-start.12 = (bf16[256,128]{1,0:T(8,128)(2,1)S(1)}, bf16[256,128]{1,0:T(8,128)(2,1)S(1)}, u32[]{:S(2)}, u32[]{:S(2)}) collective-permute-start(bf16[256,128]{1,0:T(8,128)(2,1)S(1)} %copy-done.35), channel_id=1, source_target_pairs={{0,4},{4,8},{8,12},{12,0},{1,5},{5,9},{9,13},{13,1},{2,6},{6,10},{... | collective-permute-start | bytes 196616 | tf_op jit(solution)/shard_map/ppermute | solution.py:487
  (28 other events, 31.9 us)

commit v3 on v2

v3 whole, which is shorter than its diff:
```python
import functools

import jax
import jax.numpy as jnp
from jax import lax
from jax.experimental import pallas as pl
from jax.experimental.pallas import tpu as pltpu
from jax.sharding import Mesh
from jax.sharding import PartitionSpec as P

HEAD = 128
TOK = 256
SUMM = 128
STRIDE = 16
REACH = TOK // STRIDE
ROWS = 16
GROUP = 4
ALL = GROUP * TOK
KEYS = ROWS * SUMM
TILE = 256
STAT = 64
FAR = 6 * REACH
SCALE = HEAD ** (-0.5)
LOG2E = 1.4426950408889634
SCALE2 = SCALE * LOG2E
NEG = -1e30
F32 = jnp.float32
BF = jnp.bfloat16

VM = pl.BlockSpec(memory_space=pltpu.VMEM)
SM = pl.BlockSpec(memory_space=pltpu.SMEM)


def nn(a, b):
    return lax.dot_general(a, b, (((1,), (0,)), ((), ())), preferred_element_type=F32)


def nt(a, b):
    return lax.dot_general(a, b, (((1,), (1,)), ((), ())), preferred_element_type=F32)


def tn(a, b):
    return lax.dot_general(a, b, (((0,), (0,)), ((), ())), preferred_element_type=F32)


def iota(shape, dim):
    return lax.broadcasted_iota(jnp.int32, shape, dim)


def ones_where(condition):
    return condition.astype(F32).astype(BF)


def summary_select(sidx):
    return ones_where(iota((TOK, SUMM), 0) == sidx)


def stride_select(soff_t, shard):
    there = jnp.minimum(shard + 1 + iota((4, ROWS * GROUP), 0), ROWS * GROUP - 1)
    offset = jnp.where(iota((4, ROWS * GROUP), 1) == there, soff_t, 0)
    offset = jnp.sum(offset.astype(F32), axis=1, keepdims=True).astype(jnp.int32)
    row, col = iota((4 * REACH, TOK), 0), iota((4 * REACH, TOK), 1)
    slot = row // REACH
    want = (row % REACH) * STRIDE
    for u in range(4):
        want = want + jnp.where(slot == u, offset[u : u + 1], 0)
    return ones_where(want == col)


def call(kernel, outs, ins, scratch=(), name=None, vmem=24, fetch=(), raw=(), store=()):
    fetch, raw, store = sorted(fetch), set(raw), sorted(store)
    n_in, n_out, n_own = len(ins), len(outs), len(scratch)
    hbm = pl.BlockSpec(memory_space=pltpu.HBM)

    def body(*refs):
        given = list(refs[:n_in])
        made = list(refs[n_in : n_in + n_out])
        own = list(refs[n_in + n_out : n_in + n_out + n_own])
        rest = list(refs[n_in + n_out + n_own :])
        here = rest[: len(fetch)]
        there = rest[len(fetch) : len(fetch) + len(store)]
        sems = rest[-1] if fetch or store else None
        copies = []
        for n, (i, ref) in enumerate(zip(fetch, here)):
            copies.append(pltpu.make_async_copy(given[i], ref, sems.at[n]))
            given[i] = ref
        for copy in copies:
            copy.start()
        for copy in copies:
            copy.wait()
        copies = []
        for n, (i, ref) in enumerate(zip(store, there)):
            copies.append(
                pltpu.make_async_copy(ref, made[i], sems.at[len(fetch) + n])
            )
            made[i] = ref
        kernel(*given, *made, *own)
        for copy in copies:
            copy.start()
        for copy in copies:
            copy.wait()

    extra = [pltpu.VMEM(ins[i].shape, ins[i].dtype) for i in fetch]
    extra += [pltpu.VMEM(outs[i].shape, outs[i].dtype) for i in store]
    if extra:
        extra.append(dma(len(extra)))
    return pl.pallas_call(
        body,
        out_shape=tuple(
            pltpu.HBM(s.shape, s.dtype) if i in store else s
            for i, s in enumerate(outs)
        ),
        in_specs=[SM]
        + [hbm if i in fetch or i in raw else VM for i in range(1, n_in)],
        out_specs=tuple(hbm if i in store else VM for i in range(n_out)),
        scratch_shapes=list(scratch) + extra,
        compiler_params=pltpu.CompilerParams(vmem_limit_bytes=vmem * 2**20),
        cost_estimate=pl.CostEstimate(flops=1, bytes_accessed=1, transcendentals=0),
        name=name,
    )(
        *(
            pltpu.with_memory_space_constraint(x, pltpu.HBM)
            if i in fetch or i in raw
            else x
            for i, x in enumerate(ins)
        )
    )


def sds(shape, dtype=BF):
    return jax.ShapeDtypeStruct(shape, dtype)


def prep_kernel(
    meta, soff_t, sidx, q, k, v, kvb, q0, picks, q0_own, kv0, picks_own
):
    q0[...] = q[:, :HEAD]
    q0_own[...] = q[:, :HEAD]
    pick = summary_select(sidx[...])
    kv = jnp.concatenate([k[:, :HEAD], v[:, :HEAD]], 1)
    kv0[...] = kv
    kv = tn(pick, kv).astype(BF)
    for i in range(ROWS):
        kvb[i] = kv
    sel = stride_select(soff_t[...], GROUP * meta[0] + meta[1])
    got = nn(sel, jnp.concatenate([k[:, HEAD:], v[:, HEAD:]], 1)).astype(BF)
    for u in range(4):
        for h in range(6):
            part = got[u * REACH : (u + 1) * REACH, h * HEAD : (h + 1) * HEAD]
            picks[u, h * REACH : (h + 1) * REACH, :] = part
            picks_own[u, h * REACH : (h + 1) * REACH, :] = part


def grad_near_kernel(meta, up, up_c, w, order, acc, far_w, near_w, sems):
    zl, c = meta[2], meta[3]
    wide = up.shape[1]
    copies = []
    for i, (z, core) in enumerate(
        ((zl, c), (zl, 1 - c), (1 - zl, c), (1 - zl, 1 - c))
    ):
        at = pl.ds(pl.multiple_of((2 * z + core) * wide, wide), wide)
        to = near_w.at[i] if i < 2 else far_w.at[i - 2]
        copies.append(pltpu.make_async_copy(w.at[:, at], to, sems.at[i]))
    for copy in copies:
        copy.start()
    copies[0].wait()
    total = nt(up[...], near_w[0])
    copies[1].wait()
    acc[...] = total + nt(up_c[...], near_w[1])
    copies[2].wait()
    copies[3].wait()


def grad_far_kernel(meta, up_z, up_zc, far_w, acc, picks, before, g, last, *sent):
    zh = meta[1]
    full = acc[...] + nt(up_z[...], far_w[0])
    full = (full + nt(up_zc[...], far_w[1])).astype(BF)
    g[...] = full
    last[...] = before[3]
    for d in (1, 2, 3):
        ref = sent[d - 1]
        ref[:TOK, :] = full[:, :HEAD]

        @pl.when(zh + d < GROUP)
        def _(d=d, ref=ref):
            ref[TOK:, :] = picks[d - 1]

        @pl.when(zh + d >= GROUP)
        def _(d=d, ref=ref):
            ref[TOK:, :] = before[d - 1]


def fold8(a, how):
    return how(a.reshape(a.shape[0] // 8, 8, a.shape[1]), axis=0)


def causal_t():
    return iota((TOK, TOK), 0) <= iota((TOK, TOK), 1)


def block_masks(row, zh):
    slot = iota((1, ALL), 1) // TOK
    edge = jnp.where(slot > zh, 0.0, NEG)
    none = jnp.full((1, ALL), NEG, F32)
    return [
        jnp.where(jnp.full((1, ALL), b, jnp.int32) < row, 0.0,
                  jnp.where(jnp.full((1, ALL), b, jnp.int32) == row, edge, none))
        for b in range(ROWS)
    ]


def split3(a):
    hi = a.astype(BF).astype(F32)
    mid = (a - hi).astype(BF).astype(F32)
    return [hi, mid, (a - hi - mid).astype(BF).astype(F32)]


def halves(a):
    return jnp.concatenate([a[:, :HEAD], a[:, HEAD:]], 0)


def whole(a):
    n = a.shape[0] // 2
    return jnp.concatenate([a[:n], a[n:]], 1)


def forward_kernel(
    meta, q0, q1, q2, q3, g0, g1, g2, g3, kva, kv0, ob, q_all, g_all, kv_all, near, s_ref
):
    row, zh = meta[0], meta[1]
    q = jnp.concatenate([q0[...], q1[...], q2[...], q3[...]], 0)
    g = jnp.concatenate([g0[:, :HEAD], g1[:TOK], g2[:TOK], g3[:TOK]], 0)
    q_all[...] = q
    g_all[...] = g
    for d, ref in ((1, g1), (2, g2), (3, g3)):
        near[d - 1] = ref[TOK:]
    masks = block_masks(row, zh)
    per = TILE // SUMM
    top = jnp.full((8, ALL), NEG, F32)
    for j in range(KEYS // TILE):
        s = nt(kva[j * TILE : (j + 1) * TILE, :HEAD], q)
        kv_all[j * TILE : (j + 1) * TILE, :] = kva[j * TILE : (j + 1) * TILE, :]
        s_ref[j * TILE : (j + 1) * TILE, :] = s
        for i in range(per):
            most = fold8(s[i * SUMM : (i + 1) * SUMM], jnp.max)
            top = jnp.maximum(top, most + masks[per * j + i])
    top = jnp.max(top, axis=0, keepdims=True) * SCALE2
    sums = jnp.zeros((8, ALL), F32)
    dots = jnp.zeros((8, ALL), F32)
    out = jnp.zeros((HEAD, ALL), F32)
    for j in range(KEYS // TILE):
        at = slice(j * TILE, (j + 1) * TILE)
        value = kva[at, HEAD:]
        parts = []
        for i in range(per):
            b = per * j + i
            shift = jnp.where(masks[b] < 0, -NEG, top)
            parts.append(
                jnp.exp2(s_ref[b * SUMM : (b + 1) * SUMM, :] * SCALE2 - shift)
            )
        e = jnp.concatenate(parts, 0)
        sums = sums + fold8(e, jnp.sum)
        dots = dots + fold8(e * nt(value, g), jnp.sum)
        out = out + tn(value, e.astype(BF))
    sums = jnp.sum(sums, axis=0, keepdims=True)
    dots = jnp.sum(dots, axis=0, keepdims=True)
    some = sums > 0
    safe = jnp.where(some, sums, 1.0)
    inv = 1.0 / safe
    log_sum = jnp.where(some, top + jnp.log(safe) * LOG2E, NEG)
    dots = dots * inv
    out = out * inv

    key, value = kv0[:, :HEAD], kv0[:, HEAD:]
    s = jnp.where(causal_t(), nt(key, q0[...]) * SCALE2, NEG)
    own_top = jnp.max(s, axis=0, keepdims=True)
    e = jnp.exp2(s - own_top)
    own_sum = jnp.sum(e, axis=0, keepdims=True)
    own_dot = jnp.sum(e * nt(value, g0[:, :HEAD]), axis=0, keepdims=True)
    own_out = tn(value, e.astype(BF))
    own_log = own_top + jnp.log(own_sum) * LOG2E
    near = log_sum[:, :TOK]
    most = jnp.maximum(near, own_log)
    wa, wb = jnp.exp2(near - most), jnp.exp2(own_log - most)
    inv = 1.0 / (wa + wb)
    wa, wb = wa * inv, wb * inv / own_sum
    log_sum = jnp.concatenate(
        [most - jnp.log(inv) * LOG2E, log_sum[:, TOK:]], 1
    )
    dots = jnp.concatenate(
        [wa * dots[:, :TOK] + wb * own_dot, dots[:, TOK:]], 1
    )

    stats = jnp.concatenate(
        split3(log_sum) + split3(dots) + [jnp.zeros((2, ALL), F32)], 0
    )
    stats = jnp.concatenate(
        [stats[:, i * HEAD : (i + 1) * HEAD] for i in range(ALL // HEAD)], 0
    ).astype(BF)
    for d in range(GROUP):
        part = out[:, d * TOK : (d + 1) * TOK]
        if d == 0:
            part = wa * part + wb * own_out
        to = lax.rem(zh - d + GROUP, GROUP)
        ob[to, :TOK, :] = halves(part).astype(BF)
        ob[to, TOK:, :] = stats


def combine_kernel(meta, oa, o_sc, o, stat, o_own, o_beside):
    o_beside[...] = o_sc[...]
    zh = meta[1]
    got = []
    for f in range(GROUP):
        rows = oa[lax.rem(zh - f + GROUP, GROUP), TOK:, :].astype(F32)
        got.append(
            jnp.concatenate([rows[8 * i : 8 * i + 8] for i in range(STAT // 8)], 1)
        )
    for d in range(GROUP):
        logs, dots = [], []
        for f in range(GROUP):
            e = (d - f) % GROUP
            part = got[f][:, e * TOK : (e + 1) * TOK]
            logs.append(part[0:1] + part[1:2] + part[2:3])
            dots.append(part[3:4] + part[4:5] + part[5:6])
        most = functools.reduce(jnp.maximum, logs)
        shares = [jnp.exp2(x - most) for x in logs]
        both = functools.reduce(jnp.add, shares)
        shares = [x / both for x in shares]
        at = slice(d * TOK, (d + 1) * TOK)
        stat[0:1, at] = most + jnp.log(both) * LOG2E
        stat[1:2, at] = functools.reduce(
            jnp.add, [x * y for x, y in zip(shares, dots)]
        )
        if d == 0:
            full = functools.reduce(
                jnp.add,
                [
                    shares[f]
                    * whole(oa[lax.rem(zh - f + GROUP, GROUP), :TOK, :].astype(F32))
                    for f in range(GROUP)
                ],
            )
            eye = ones_where(iota((HEAD, HEAD), 0) == iota((HEAD, HEAD), 1))
            full = tn(full.astype(BF), eye).astype(BF)
            o[...] = full
            o_own[...] = full
    stat[2:8, :] = jnp.zeros((6, ALL), F32)


def backward_kernel(
    meta, q_all, g_all, kva, kv0, stat, far, dkv, dq1, dq2, dq3, own, dq0
):
    row, zh = meta[0], meta[1]
    q, g = q_all[...], g_all[...]
    q0, g0 = q[:TOK], g[:TOK]
    masks = block_masks(row, zh)
    log_sum, dot = stat[0:1, :], stat[1:2, :]
    per = TILE // SUMM
    dq = jnp.zeros((HEAD, ALL), F32)
    for j in range(KEYS // TILE):
        at = slice(j * TILE, (j + 1) * TILE)
        key, value = kva[at, :HEAD], kva[at, HEAD:]
        s = nt(key, q)
        parts = []
        for i in range(per):
            shift = jnp.where(masks[per * j + i] < 0, -NEG, log_sum)
            parts.append(
                jnp.exp2(s[i * SUMM : (i + 1) * SUMM] * SCALE2 - shift)
            )
        p = jnp.concatenate(parts, 0)
        dkv[at, HEAD:] = nn(p.astype(BF), g).astype(BF)
        ds = (p * (nt(value, g) - dot)).astype(BF)
        dkv[at, :HEAD] = (nn(ds, q) * SCALE).astype(BF)
        dq = dq + tn(key, ds)
    key, value = kv0[:, :HEAD], kv0[:, HEAD:]
    s = jnp.where(causal_t(), nt(key, q0) * SCALE2, NEG)
    p = jnp.exp2(s - log_sum[:, :TOK])
    own[:, HEAD:] = nn(p.astype(BF), g0)
    ds = (p * (nt(value, g0) - dot[:, :TOK])).astype(BF)
    own[:, :HEAD] = nn(ds, q0) * SCALE
    dq0[...] = (dq[:, :TOK] + tn(key, ds)) * SCALE
    for d, ref in ((1, dq1), (2, dq2), (3, dq3)):
        ref[:TOK, :] = (halves(dq[:, d * TOK : (d + 1) * TOK]) * SCALE).astype(BF)
        ref[TOK:, :] = far[d - 1]


def strided_kernel(meta, q, k, v, g, near, last, o, dq, dkv, far, o_own):
    row, zh = meta[0], meta[1]
    slot = iota((TOK, 4 * REACH), 1) // REACH
    far_ok = (slot < zh) | (jnp.full((TOK, 4 * REACH), row, jnp.int32) > 0)
    near_ok = iota((TOK, TOK), 0) >= iota((TOK, TOK), 1)

    def far_rows(i):
        at = slice(i * REACH, (i + 1) * REACH)
        return jnp.concatenate([near[0, at], near[1, at], near[2, at], last[at]], 0)

    for h in range(3):
        at = slice((h + 1) * HEAD, (h + 2) * HEAD)
        to = slice(h * HEAD, (h + 1) * HEAD)
        qh, kh, vh, gh = q[:, at], k[:, at], v[:, at], g[:, at]
        kf, vf = far_rows(h), far_rows(h + 3)
        s = jnp.where(near_ok, nt(qh, kh) * SCALE, NEG)
        sf = jnp.where(far_ok, nt(qh, kf) * SCALE, NEG)
        top = jnp.maximum(
            jnp.max(s, axis=1, keepdims=True), jnp.max(sf, axis=1, keepdims=True)
        )
        e, ef = jnp.exp(s - top), jnp.exp(sf - top)
        inv = 1.0 / (
            jnp.sum(e, axis=1, keepdims=True) + jnp.sum(ef, axis=1, keepdims=True)
        )
        p, pf = e * inv, ef * inv
        w, wf = p.astype(BF), pf.astype(BF)
        out = (nn(w, vh) + nn(wf, vf)).astype(BF)
        o[:, to] = out
        o_own[:, to] = out
        delta = jnp.sum(gh.astype(F32) * out.astype(F32), axis=1, keepdims=True)
        ds = (p * (nt(gh, vh) - delta) * SCALE).astype(BF)
        dsf = (pf * (nt(gh, vf) - delta) * SCALE).astype(BF)
        dq[:, to] = (nn(ds, kh) + nn(dsf, kf)).astype(BF)
        dkv[:, to] = tn(ds, qh)
        dkv[:, 3 * HEAD + h * HEAD : 3 * HEAD + (h + 1) * HEAD] = tn(w, gh)
        dkf = tn(dsf, qh).astype(BF)
        dvf = tn(wf, gh).astype(BF)
        for u in range(4):
            rows = slice(u * REACH, (u + 1) * REACH)
            far[u, h * REACH : (h + 1) * REACH, :] = dkf[rows]
            far[u, (h + 3) * REACH : (h + 4) * REACH, :] = dvf[rows]


def project_kernel(meta, o_f, o_fc, o, o_c, w, w_c, order, send, keep, wa, wb, sems):
    zl, c = meta[2], meta[3]
    wide = wa.shape[2]
    copies = []
    for i, z in enumerate((1 - zl, zl)):
        at = pl.ds(pl.multiple_of((2 * z + c) * wide, wide), wide)
        copies.append(
            (
                pltpu.make_async_copy(w.at[:, at], wa.at[i], sems.at[2 * i]),
                pltpu.make_async_copy(w_c.at[:, at], wb.at[i], sems.at[2 * i + 1]),
            )
        )
    for pair in copies:
        for copy in pair:
            copy.start()
    here = jnp.concatenate([o_f[...], o[...]], 1)
    beside = jnp.concatenate([o_fc[...], o_c[...]], 1)
    for i, ref in ((0, send), (1, keep)):
        copies[i][0].wait()
        total = nn(here, wa[i])
        copies[i][1].wait()
        ref[...] = (total + nn(beside, wb[i])).astype(ref.dtype)


def back_kernel(meta, dq0, b1, b2, b3, far, sent, here, dq):
    for u, ref in ((0, b1), (1, b2), (2, b3)):
        sent[u] = ref[TOK:, :]
        here[u] = ref[TOK:, :]
    sent[3] = far[3]
    total = dq0[...]
    for ref in (b1, b2, b3):
        total = total + whole(ref[:TOK, :].astype(F32))
    eye = ones_where(iota((HEAD, HEAD), 0) == iota((HEAD, HEAD), 1))
    dq[...] = tn(total.astype(BF), eye).astype(BF)


def final_kernel(
    meta,
    soff_t,
    sidx,
    dkv,
    own,
    dq,
    here,
    after,
    strided_dq,
    strided,
    keep,
    over,
    out,
    qg,
    kg,
    vg,
):
    zh = meta[1]
    shard = GROUP * meta[0] + meta[1]
    out[...] = (keep[...].astype(F32) + over[...].astype(F32)).astype(BF)
    pick = summary_select(sidx[...])
    fixed = own[...] + nn(jnp.concatenate([pick] * ROWS, 1), dkv[...])
    kg[:, :HEAD] = fixed[:, :HEAD].astype(BF)
    vg[:, :HEAD] = fixed[:, HEAD:].astype(BF)
    qg[:, :HEAD] = dq[...]
    qg[:, HEAD:] = strided_dq[...]
    sel = stride_select(soff_t[...], shard)
    slots = []
    for u in range(4):
        block = after[u]
        if u < 3:
            block = jnp.where(
                zh + 1 + u < GROUP, here[u].astype(F32), block.astype(F32)
            ).astype(BF)
        slots.append(
            jnp.concatenate(
                [block[h * REACH : (h + 1) * REACH] for h in range(6)], 1
            )
        )
    total = strided[...] + tn(sel, jnp.concatenate(slots, 0))
    kg[:, HEAD:] = total[:, : 3 * HEAD].astype(BF)
    vg[:, HEAD:] = total[:, 3 * HEAD :].astype(BF)


def swap(a, axis):
    return lax.ppermute(a, axis, [(0, 1), (1, 0)])


def turn(a, by):
    return lax.ppermute(a, "zh", [(i, (i + by) % GROUP) for i in range(GROUP)])


def after(a, other):
    return lax.optimization_barrier((a, other))[0]


def dma(n):
    return pltpu.SemaphoreType.DMA((n,))


def shards(queries, key_rows, value_rows, out_weight, upstream, summary_index, soff):
    row = lax.axis_index(("x", "y"))
    zh, zl, c = lax.axis_index("zh"), lax.axis_index("zl"), lax.axis_index("c")
    meta = jnp.stack([row, zh, zl, c]).astype(jnp.int32)
    soff_t = soff.T
    width = queries.shape[1]
    quarter = upstream.shape[1]
    plane = ("x", "y")

    up_z = swap(upstream, "zl")
    up_c = swap(upstream, "c")
    block = sds((4, FAR, HEAD))
    kvb, q0, picks, q0_own, kv0, picks_own = call(
        prep_kernel,
        [
            sds((ROWS, SUMM, 2 * HEAD)),
            sds((TOK, HEAD)),
            block,
            sds((TOK, HEAD)),
            sds((TOK, 2 * HEAD)),
            block,
        ],
        [meta, soff_t, summary_index, queries, key_rows, value_rows],
        name="pick_rows",
        fetch=range(1, 6),
        store=[3, 4, 5],
    )
    kva = lax.all_to_all(kvb, plane, 0, 0, tiled=True).reshape(KEYS, 2 * HEAD)
    before = lax.ppermute(picks, plane, [(i, i + 1) for i in range(ROWS - 1)])
    acc, far_w = call(
        grad_near_kernel,
        [sds((TOK, width), F32), sds((2, width, quarter))],
        [meta, upstream, up_c, out_weight, kv0],
        [pltpu.VMEM((2, width, quarter), BF), dma(4)],
        name="attention_grad_near",
        fetch=[1],
        raw=[3, 4],
    )
    up_zc = swap(after(up_z, kv0), "c")
    qs = [q0_own] + [turn(q0, d) for d in (1, 2, 3)]
    g, last, *gs = call(
        grad_far_kernel,
        [sds((TOK, width)), sds((FAR, HEAD))] + [sds((TOK + FAR, HEAD))] * 3,
        [meta, up_z, up_zc, far_w, acc, picks_own, before],
        name="attention_grad_far",
        fetch=[5],
        store=[0, 1],
    )
    gs = [g] + [turn(gs[d - 1], d) for d in (1, 2, 3)]
    ob, q_all, g_all, kv_all, near = call(
        forward_kernel,
        [
            sds((GROUP, TOK + STAT, HEAD)),
            sds((ALL, HEAD)),
            sds((ALL, HEAD)),
            sds((KEYS, 2 * HEAD)),
            sds((3, FAR, HEAD)),
        ],
        [meta, *qs, *gs, kva, kv0],
        [pltpu.VMEM((KEYS, ALL), F32)],
        name="fixed_forward",
        fetch=[1, 5, 10],
        store=[1, 2, 3, 4],
    )
    weight_c = swap(after(out_weight, near), "c")
    oa = lax.all_to_all(ob, "zh", 0, 0, tiled=True)
    o_s, dq_s, dkv_s, far, o_own = call(
        strided_kernel,
        [
            sds((TOK, 3 * HEAD)),
            sds((TOK, 3 * HEAD)),
            sds((TOK, 6 * HEAD), F32),
            block,
            sds((TOK, 3 * HEAD)),
        ],
        [meta, queries, key_rows, value_rows, g, near, last],
        name="strided_heads",
        fetch=range(1, 7),
        store=[1, 2, 3, 4],
    )
    o_sc = swap(o_s, "c")
    o_f, stat, o_f_own, o_beside = call(
        combine_kernel,
        [
            sds((TOK, HEAD)),
            sds((8, ALL), F32),
            sds((TOK, HEAD)),
            sds((TOK, 3 * HEAD)),
        ],
        [meta, oa, o_sc],
        name="combine",
        store=[2, 3],
    )
    o_fc = swap(o_f, "c")
    dkv, *dqs, own, dq0 = call(
        backward_kernel,
        [sds((KEYS, 2 * HEAD))]
        + [sds((TOK + FAR, HEAD))] * 3
        + [sds((TOK, 2 * HEAD), F32), sds((HEAD, TOK), F32)],
        [meta, q_all, g_all, kv_all, kv0, stat, far],
        name="fixed_backward",
        fetch=[1, 2, 3, 4, 6],
        store=[4, 5],
    )
    dkva = lax.all_to_all(
        after(dkv, o_fc).reshape(ROWS, SUMM, 2 * HEAD), plane, 0, 0, tiled=True
    ).reshape(KEYS, 2 * HEAD)
    send, keep = call(
        project_kernel,
        [sds((TOK, quarter))] * 2,
        [meta, o_f_own, o_fc, o_own, o_beside, out_weight, weight_c, dq0],
        [
            pltpu.VMEM((2, width, quarter), BF),
            pltpu.VMEM((2, width, quarter), BF),
            dma(4),
        ],
        name="project",
        fetch=[1, 3, 4],
        raw=[5, 6, 7],
        store=[1],
    )
    over = swap(send, "zl")
    dqs = [turn(dqs[d - 1], -d) for d in (1, 2, 3)]
    sent, here, dq_f = call(
        back_kernel,
        [block, sds((3, FAR, HEAD)), sds((TOK, HEAD))],
        [meta, dq0, *dqs, far],
        name="bundle_back",
        fetch=[1, 5],
        store=[1, 2],
    )
    back = lax.ppermute(sent, plane, [(i + 1, i) for i in range(ROWS - 1)])
    return call(
        final_kernel,
        [sds((TOK, quarter))] + [sds((TOK, width))] * 3,
        [meta, soff_t, summary_index, dkva, own, dq_f, here, back, dq_s, dkv_s]
        + [keep, over],
        name="join_results",
        fetch=[1, 2, 4, 5, 6, 8, 9, 10],
    )


def solution(mesh):
    grid = Mesh(mesh.devices.reshape(4, 4, 4, 2, 2), ("x", "y", "zh", "zl", "c"))
    ctx, head = ("x", "y", "zh"), ("zl", "c")
    return jax.shard_map(
        shards,
        mesh=grid,
        in_specs=(
            P(ctx, head),
            P(ctx, head),
            P(ctx, head),
            P(head, None),
            P(ctx, head),
            P(ctx, None),
            P(),
        ),
        out_specs=(P(ctx, head),) * 4,
        check_vma=False,
    )
```

time: 159 us -> 139 us (0.87)
  local copies, waits for them, and re-layouts: 19.4 us -> 0 us
  blocking collectives: 15.6 us -> 0 us
  Pallas kernels: 34.2 us -> 45.6 us
  waiting for transfers between devices: 37.4 us -> 40.1 us
    unnamed x80 -> x0, local copies, waits for them, and re-layouts: 19.3 us -> none
    all_to_all x1 -> x0, blocking collectives: 15.6 us -> none  [shards(): oa = lax.all_to_all(ob, 'zh', 0, 0, tiled=True)]
    pallas_call x11 -> x10, Pallas kernels: 34.2 us -> 45.6 us  [call(): pl.pallas_call(body, out_shape=tuple((pltpu.HBM(s.shape, s.dtype) if i in...]
    ppermute x9, waiting for transfers between devices: 14.1 us -> 25.3 us  [turn(): return lax.ppermute(a, 'zh', [(i, (i + by) % GROUP) for i in range(GROUP)])]
    ppermute x7, waiting for transfers between devices: 13.1 us -> 2.25 us  [swap(): return lax.ppermute(a, axis, [(0, 1), (1, 0)])]
    ppermute x1, waiting for transfers between devices: 10.2 us -> 0.89 us  [shards(): before = lax.ppermute(picks, plane, [(i, i + 1) for i in range(ROWS - 1)])]
    ppermute x1, waiting for transfers between devices: 0.01 us -> 5.85 us  [shards(): back = lax.ppermute(sent, plane, [(i + 1, i) for i in range(ROWS - 1)])]
    all_to_all x1 -> x2, waiting for transfers between devices: 0.01 us -> 5.82 us  [the longest x1 5.82 us: shards(): oa = lax.all_to_all(ob, 'zh', 0, 0, tiled=True)]
  transfers between devices with their start and end apart: 20 -> 21, of which waited for: 6 -> 9; matrix products, arithmetic and copies ran while one was open for 0% -> 0% of each run, Pallas kernels for 18% -> 25%
where the time goes in v3:
time: 139 us; the launch traced here: 138 us
  starting transfers between devices  51.3 us (37%)
  Pallas kernels  45.6 us (33%)
  waiting for transfers between devices  40.1 us (29%)
    pallas_call x10, Pallas kernels, call(): pl.pallas_call(body, out_shape=tuple((pltpu.HBM(s.shape, s.dtype) if i in...  45.6 us
    ppermute x9, waiting for transfers between devices, turn(): return lax.ppermute(a, 'zh', [(i, (i + by) % GROUP) for i in range(GROUP)])  25.3 us
    ppermute x9, starting transfers between devices, turn(): return lax.ppermute(a, 'zh', [(i, (i + by) % GROUP) for i in range(GROUP)])  23.5 us
    all_to_all x1, starting transfers between devices, shards(): kva = lax.all_to_all(kvb, plane, 0, 0, tiled=True).reshape(KEYS, 2 * HEAD)  7.18 us
    all_to_all x1, starting transfers between devices, shards(): lax.all_to_all(after(dkv, o_fc).reshape(ROWS, SUMM, 2 * HEAD), plane, 0,...  6.27 us
    ppermute x1, waiting for transfers between devices, shards(): back = lax.ppermute(sent, plane, [(i + 1, i) for i in range(ROWS - 1)])  5.85 us
    all_to_all x1, waiting for transfers between devices, shards(): oa = lax.all_to_all(ob, 'zh', 0, 0, tiled=True)  5.82 us
    ppermute x7, starting transfers between devices, swap(): return lax.ppermute(a, axis, [(0, 1), (1, 0)])  5.02 us
  transfers between devices with their start and end apart: 21, of which 9 were waited for; matrix products, arithmetic and copies ran while one was open for 0% of the time, Pallas kernels for 25%

profile of v3, /device:TPU:24, one launch (start us, length us, event | category | flops | bytes accessed | tf_op | source)
XLA Modules:
  0.0 138.1 jit_solution(3547001262032139248)
XLA Ops:
  0.6 2.0 %collective-permute-start.3 = (bf16[256,1024]{1,0:T(8,128)(2,1)}, bf16[256,1024]{1,0:T(8,128)(2,1)S(1)}, u32[]{:S(2)}, u32[]{:S(2)}) collective-permute-start(bf16[256,1024]{1,0:T(8,128)(2,1)} %refs_1_.2), channel_id=1, source_target_pairs={{0,2},{2,0},{1,3},{3,1},{4,6},{6,4},{5,7},{7,5},{8,10},{10,8},{9,1... | collective-permute-start | bytes 1572872 | tf_op jit(solution)/shard_map/ppermute | solution.py:512
  2.7 3.7 %pick_rows.1 = (bf16[16,128,256]{2,1,0:T(8,128)(2,1)}, bf16[256,128]{1,0:T(8,128)(2,1)S(1)}, bf16[4,96,128]{2,1,0:T(8,128)(2,1)S(1)}, bf16[256,128]{1,0:T(8,128)...) custom-call(s32[4]{0:T(128)S(1)} %pad_add_fusion.refs_0_, s32[4,64]{1,0:T(4,128)} %bitcast.10, ...), custom_call_target="tpu_custom_call" | custom-call | flops 1 | bytes 1 | tf_op jit(solution)/shard_map/pick_rows/pallas_call | solution.py:107
  6.4 7.2 %all-to-all-start = ((bf16[16,128,256]{2,1,0:T(8,128)(2,1)}), bf16[16,128,256]{2,1,0:T(8,128)(2,1)S(1)}, u32[]{:S(2)}, u32[]{:S(2)}) async-start(bf16[16,128,256]{2,1,0:T(8,128)(2,1)} %get-tuple-element.57), calls=%async_computation | async-start | bytes 2097152 | tf_op jit(solution)/shard_map/all_to_all | solution.py:554
  13.6 1.2 collective-permute-done.3.refs_1_
  14.8 3.0 %collective-permute-start.6 = (bf16[4,96,128]{2,1,0:T(8,128)(2,1)S(1)}, bf16[4,96,128]{2,1,0:T(8,128)(2,1)S(1)}, u32[]{:S(2)}, u32[]{:S(2)}) collective-permute-start(bf16[4,96,128]{2,1,0:T(8,128)(2,1)S(1)} %get-tuple-element.52), channel_id=1, source_target_pairs={{0,16},{16,32},{32,48},{48,64},{64,80},{80,96},{96,112},{112,128},... | collective-permute-start | bytes 294920 | tf_op jit(solution)/shard_map/ppermute | solution.py:555
  17.8 6.2 %collective-permute-start.2 = (bf16[256,128]{1,0:T(8,128)(2,1)S(1)}, bf16[256,128]{1,0:T(8,128)(2,1)S(1)}, u32[]{:S(2)}, u32[]{:S(2)}) collective-permute-start(bf16[256,128]{1,0:T(8,128)(2,1)S(1)} %get-tuple-element.46), channel_id=1, source_target_pairs={{0,12},{4,0},{8,4},{12,8},{1,13},{5,1},{9,5},{13,9},{2,14},{6,2},{... | collective-permute-start | bytes 196616 | tf_op jit(solution)/shard_map/ppermute | solution.py:516
  24.0 3.9 %attention_grad_near.1 = (f32[256,512]{1,0:T(8,128)S(1)}, bf16[2,512,1024]{2,1,0:T(8,128)(2,1)S(1)}) custom-call(s32[4]{0:T(128)S(1)} %pad_add_fusion.refs_0_, bf16[256,1024]{1,0:T(8,128)(2,1)} %refs_1_.2, bf16[256,1024]{1,0:T(8,128)(2,1)S(1)} %collective-permute-done.5.refs_2_, bf16[512,4096]{1,0:T(8,128)(2,1)} %refs_5_.3, ...), custom_call_target="tpu_custom_call" | custom-call | flops 1 | bytes 1 | tf_op jit(solution)/shard_map/attention_grad_near/pallas_call | solution.py:107
  28.8 2.9 %attention_grad_far.1 = (bf16[256,512]{1,0:T(8,128)(2,1)}, bf16[96,128]{1,0:T(8,128)(2,1)}, bf16[352,128]{1,0:T(8,128)(2,1)S(1)}, bf16[352,128]{1,0:T(8,128)(2,1)S(1)}, bf16[352,128]{1,0:T(8,128)(2,1)S(1)}) custom-call(s32[4]{0:T(128)S(1)} %pad_add_fusion.refs_0_, bf16[256,1024]{1,0:T(8,128)(2,1)S(1)} %collective-permute-done.3.refs_1_, ...), custom_call_target="tpu_custom_call" | custom-call | flops 1 | bytes 1 | tf_op jit(solution)/shard_map/attention_grad_far/pallas_call | solution.py:107
  31.8 3.3 %collective-permute-start.7 = (bf16[352,128]{1,0:T(8,128)(2,1)S(1)}, bf16[352,128]{1,0:T(8,128)(2,1)S(1)}, u32[]{:S(2)}, u32[]{:S(2)}) collective-permute-start(bf16[352,128]{1,0:T(8,128)(2,1)S(1)} %get-tuple-element.54), channel_id=1, source_target_pairs={{0,4},{4,8},{8,12},{12,0},{1,5},{5,9},{9,13},{13,1},{2,6},{6,10},{... | collective-permute-start | bytes 270344 | tf_op jit(solution)/shard_map/ppermute | solution.py:516
  35.1 4.6 %collective-permute-start.8 = (bf16[352,128]{1,0:T(8,128)(2,1)S(1)}, bf16[352,128]{1,0:T(8,128)(2,1)S(1)}, u32[]{:S(2)}, u32[]{:S(2)}) collective-permute-start(bf16[352,128]{1,0:T(8,128)(2,1)S(1)} %get-tuple-element.55), channel_id=1, source_target_pairs={{0,8},{4,12},{8,0},{12,4},{1,9},{5,13},{9,1},{13,5},{2,10},{6,14},... | collective-permute-start | bytes 270344 | tf_op jit(solution)/shard_map/ppermute | solution.py:516
  39.7 2.7 %collective-permute-start.9 = (bf16[352,128]{1,0:T(8,128)(2,1)S(1)}, bf16[352,128]{1,0:T(8,128)(2,1)S(1)}, u32[]{:S(2)}, u32[]{:S(2)}) collective-permute-start(bf16[352,128]{1,0:T(8,128)(2,1)S(1)} %get-tuple-element.56), channel_id=1, source_target_pairs={{0,12},{4,0},{8,4},{12,8},{1,13},{5,1},{9,5},{13,9},{2,14},{6,2},{... | collective-permute-start | bytes 270344 | tf_op jit(solution)/shard_map/ppermute | solution.py:516
  43.4 1.4 collective-permute-start
  44.8 8.8 %collective-permute-done.1.refs_3_ = bf16[256,128]{1,0:T(8,128)(2,1)S(1)} collective-permute-done((bf16[256,128]{1,0:T(8,128)(2,1)S(1)}, bf16[256,128]{1,0:T(8,128)(2,1)S(1)}, u32[]{:S(2)}, u32[]{:S(2)}) %collective-permute-start.1) | collective-permute-done | bytes 65568 | tf_op jit(solution)/shard_map/ppermute | solution.py:516
  53.6 7.4 %fixed_forward.1 = (bf16[4,320,128]{2,1,0:T(8,128)(2,1)}, bf16[1024,128]{1,0:T(8,128)(2,1)}, bf16[1024,128]{1,0:T(8,128)(2,1)}, bf16[2048,256]{1,0:T(8,128)(2,1)}, bf16[3,96,128]{2,1,0:T(8,128)(2,1)}) custom-call(s32[4]{0:T(128)S(1)} %pad_add_fusion.refs_0_, bf16[256,128]{1,0:T(8,128)(2,1)} %get-tuple-element.45.refs_1_, ...), custom_call_target="tpu_custom_call" | custom-call | flops 1 | bytes 1 | tf_op jit(solution)/shard_map/fixed_forward/pallas_call | solution.py:107
  61.3 3.5 %all-to-all-start.1 = ((bf16[4,320,128]{2,1,0:T(8,128)(2,1)}), bf16[4,320,128]{2,1,0:T(8,128)(2,1)S(1)}, u32[]{:S(2)}, u32[]{:S(2)}) async-start(bf16[4,320,128]{2,1,0:T(8,128)(2,1)} %get-tuple-element.61), calls=%async_computation.1 | async-start | bytes 655360 | tf_op jit(solution)/shard_map/all_to_all | solution.py:592
  64.8 5.3 %strided_heads.1 = (bf16[256,384]{1,0:T(8,128)(2,1)S(1)}, bf16[256,384]{1,0:T(8,128)(2,1)}, f32[256,768]{1,0:T(8,128)}, bf16[4,96,128]{2,1,0:T(8,128)(2,1)}, bf16[256,384]{1,0:T(8,128)(2,1)}) custom-call(s32[4]{0:T(128)S(1)} %pad_add_fusion.refs_0_, bf16[256,512]{1,0:T(8,128)(2,1)} %refs_1_.3, bf16[256,512]{1,0:T(8,128)(2,1)} %refs_2_.4, ...), custom_call_target="tpu_custom_call" | custom-call | flops 1 | bytes 1 | tf_op jit(solution)/shard_map/strided_heads/pallas_call | solution.py:107
  70.7 1.1 collective-permute-done.10.refs_2_
  71.7 5.8 %all-to-all-done.1.refs_1_ = bf16[4,320,128]{2,1,0:T(8,128)(2,1)S(1)} async-done(((bf16[4,320,128]{2,1,0:T(8,128)(2,1)}), bf16[4,320,128]{2,1,0:T(8,128)(2,1)S(1)}, u32[]{:S(2)}, u32[]{:S(2)}) %all-to-all-start.1) | async-done | bytes 327712 | tf_op jit(solution)/shard_map/all_to_all | solution.py:592
  77.6 1.5 %combine.1 = (bf16[256,128]{1,0:T(8,128)(2,1)S(1)}, f32[8,1024]{1,0:T(8,128)S(1)}, bf16[256,128]{1,0:T(8,128)(2,1)}, bf16[256,384]{1,0:T(8,128)(2,1)}) custom-call(s32[4]{0:T(128)S(1)} %pad_add_fusion.refs_0_, bf16[4,320,128]{2,1,0:T(8,128)(2,1)S(1)} %all-to-all-done.1.refs_1_, bf16[256,384]{1,0:T(8,128)(2,1)S(1)} %collective-permute-done.10.refs_2_), custom_call_target="tpu_custom_call" | custom-call | flops 1 | bytes 1 | tf_op jit(solution)/shard_map/combine/pallas_call | solution.py:107
  79.2 9.2 %fixed_backward.1 = (bf16[2048,256]{1,0:T(8,128)(2,1)}, bf16[352,128]{1,0:T(8,128)(2,1)S(1)}, bf16[352,128]{1,0:T(8,128)(2,1)S(1)}, bf16[352,128]{1,0:T(8,128)(2...) custom-call(s32[4]{0:T(128)S(1)} %pad_add_fusion.refs_0_, bf16[1024,128]{1,0:T(8,128)(2,1)} %get-tuple-element.58.refs_1_, ...), custom_call_target="tpu_custom_call" | custom-call | flops 1 | bytes 1 | tf_op jit(solution)/shard_map/fixed_backward/pallas_call | solution.py:107
  88.4 6.3 %all-to-all-start.2 = ((bf16[16,128,256]{2,1,0:T(8,128)(2,1)}), bf16[16,128,256]{2,1,0:T(8,128)(2,1)S(1)}, u32[]{:S(2)}, u32[]{:S(2)}) async-start(bf16[16,128,256]{2,1,0:T(8,128)(2,1)} %bitcast.6), calls=%async_computation.2 | async-start | bytes 2097152 | tf_op jit(solution)/shard_map/all_to_all | solution.py:631
  94.7 5.5 %project.1 = (bf16[256,1024]{1,0:T(8,128)(2,1)S(1)}, bf16[256,1024]{1,0:T(8,128)(2,1)}) custom-call(s32[4]{0:T(128)S(1)} %pad_add_fusion.refs_0_, bf16[256,128]{1,0:T(8,128)(2,1)} %get-tuple-element.80.refs_1_, bf16[256,128]{1,0:T(8,128)(2,1)S(1)} %collective-permute-done.11.refs_2_, bf16[256,384]{1,0:T(8,128)(2,1)} %get-tuple-element.81.refs_3_, ...), custom_call_target="tpu_custom_call" | custom-call | flops 1 | bytes 1 | tf_op jit(solution)/shard_map/project/pallas_call | solution.py:107
  100.2 2.1 %collective-permute-start.17 = (bf16[256,1024]{1,0:T(8,128)(2,1)S(1)}, bf16[256,1024]{1,0:T(8,128)(2,1)S(1)}, u32[]{:S(2)}, u32[]{:S(2)}) collective-permute-start(bf16[256,1024]{1,0:T(8,128)(2,1)S(1)} %get-tuple-element.85), channel_id=1, source_target_pairs={{0,2},{2,0},{1,3},{3,1},{4,6},{6,4},{5,7},{7,5},{8,10},{10,8},{9,1... | collective-permute-start | bytes 1572872 | tf_op jit(solution)/shard_map/ppermute | solution.py:512
  102.3 1.4 %collective-permute-start.12 = (bf16[352,128]{1,0:T(8,128)(2,1)S(1)}, bf16[352,128]{1,0:T(8,128)(2,1)S(1)}, u32[]{:S(2)}, u32[]{:S(2)}) collective-permute-start(bf16[352,128]{1,0:T(8,128)(2,1)S(1)} %get-tuple-element.72), channel_id=1, source_target_pairs={{0,12},{4,0},{8,4},{12,8},{1,13},{5,1},{9,5},{13,9},{2,14},{6,2},{... | collective-permute-start | bytes 270344 | tf_op jit(solution)/shard_map/ppermute | solution.py:516
  103.7 2.3 %collective-permute-start.13 = (bf16[352,128]{1,0:T(8,128)(2,1)S(1)}, bf16[352,128]{1,0:T(8,128)(2,1)S(1)}, u32[]{:S(2)}, u32[]{:S(2)}) collective-permute-start(bf16[352,128]{1,0:T(8,128)(2,1)S(1)} %get-tuple-element.73), channel_id=1, source_target_pairs={{0,8},{4,12},{8,0},{12,4},{1,9},{5,13},{9,1},{13,5},{2,10},{6,14},... | collective-permute-start | bytes 270344 | tf_op jit(solution)/shard_map/ppermute | solution.py:516
  106.6 1.1 collective-permute-done.12.refs_2_
  107.8 14.0 %collective-permute-done.13.refs_3_ = bf16[352,128]{1,0:T(8,128)(2,1)S(1)} collective-permute-done((bf16[352,128]{1,0:T(8,128)(2,1)S(1)}, bf16[352,128]{1,0:T(8,128)(2,1)S(1)}, u32[]{:S(2)}, u32[]{:S(2)}) %collective-permute-start.13) | collective-permute-done | bytes 90144 | tf_op jit(solution)/shard_map/ppermute | solution.py:516
  121.8 1.4 %collective-permute-done.14.refs_4_ = bf16[352,128]{1,0:T(8,128)(2,1)S(1)} collective-permute-done((bf16[352,128]{1,0:T(8,128)(2,1)S(1)}, bf16[352,128]{1,0:T(8,128)(2,1)S(1)}, u32[]{:S(2)}, u32[]{:S(2)}) %collective-permute-start.14) | collective-permute-done | bytes 90144 | tf_op jit(solution)/shard_map/ppermute | solution.py:516
  123.2 2.4 %bundle_back.1 = (bf16[4,96,128]{2,1,0:T(8,128)(2,1)S(1)}, bf16[3,96,128]{2,1,0:T(8,128)(2,1)}, bf16[256,128]{1,0:T(8,128)(2,1)}) custom-call(s32[4]{0:T(128)S(1)} %pad_add_fusion.refs_0_, f32[128,256]{1,0:T(8,128)} %get-tuple-element.71.refs_1_.refs_7_, bf16[352,128]{1,0:T(8,128)(2,1)S(1)} %collective-permute-done.12.refs_2_, ...), custom_call_target="tpu_custom_call" | custom-call | flops 1 | bytes 1 | tf_op jit(solution)/shard_map/bundle_back/pallas_call | solution.py:107
  125.5 2.8 %collective-permute-start.15 = (bf16[4,96,128]{2,1,0:T(8,128)(2,1)S(1)}, bf16[4,96,128]{2,1,0:T(8,128)(2,1)S(1)}, u32[]{:S(2)}, u32[]{:S(2)}) collective-permute-start(bf16[4,96,128]{2,1,0:T(8,128)(2,1)S(1)} %get-tuple-element.77), channel_id=1, source_target_pairs={{16,0},{32,16},{48,32},{64,48},{80,64},{96,80},{112,96},{128,112},... | collective-permute-start | bytes 294920 | tf_op jit(solution)/shard_map/ppermute | solution.py:658
  128.3 5.8 %collective-permute-done.15.refs_7_ = bf16[4,96,128]{2,1,0:T(8,128)(2,1)S(1)} collective-permute-done((bf16[4,96,128]{2,1,0:T(8,128)(2,1)S(1)}, bf16[4,96,128]{2,1,0:T(8,128)(2,1)S(1)}, u32[]{:S(2)}, u32[]{:S(2)}) %collective-permute-start.15) | collective-permute-done | bytes 98336 | tf_op jit(solution)/shard_map/ppermute | solution.py:658
  134.2 3.7 %join_results.1 = (bf16[256,1024]{1,0:T(8,128)(2,1)}, bf16[256,512]{1,0:T(8,128)(2,1)}, bf16[256,512]{1,0:T(8,128)(2,1)}, bf16[256,512]{1,0:T(8,128)(2,1)}) custom-call(s32[4]{0:T(128)S(1)} %pad_add_fusion.refs_0_, s32[4,64]{1,0:T(4,128)} %bitcast.11, s32[1,128]{1,0:T(1,128)} %refs_2_.5, bf16[2048,256]{1,0:T(8,128)(2,1)S(1)} %bitcast.8, ...), custom_call_target="tpu_custom_call" | custom-call | flops 1 | bytes 1 | tf_op jit(solution)/shard_map/join_results/pallas_call | solution.py:107
  (21 shorter events, 3.6 us)
Async XLA Ops:
  0.6 14.1 %collective-permute-start.3 = (bf16[256,1024]{1,0:T(8,128)(2,1)}, bf16[256,1024]{1,0:T(8,128)(2,1)S(1)}, u32[]{:S(2)}, u32[]{:S(2)}) collective-permute-start(bf16[256,1024]{1,0:T(8,128)(2,1)} %refs_1_.2), channel_id=1, source_target_pairs={{0,2},{2,0},{1,3},{3,1},{4,6},{6,4},{5,7},{7,5},{8,10},{10,8},{9,1... | collective-permute-start | bytes 1572872 | tf_op jit(solution)/shard_map/ppermute | solution.py:512
  6.4 47.1 %all-to-all-start = ((bf16[16,128,256]{2,1,0:T(8,128)(2,1)}), bf16[16,128,256]{2,1,0:T(8,128)(2,1)S(1)}, u32[]{:S(2)}, u32[]{:S(2)}) async-start(bf16[16,128,256]{2,1,0:T(8,128)(2,1)} %get-tuple-element.57), calls=%async_computation | async-start | bytes 2097152 | tf_op jit(solution)/shard_map/all_to_all | solution.py:554
  13.6 10.4 %collective-permute-start.5 = (bf16[256,1024]{1,0:T(8,128)(2,1)}, bf16[256,1024]{1,0:T(8,128)(2,1)S(1)}, u32[]{:S(2)}, u32[]{:S(2)}) collective-permute-start(bf16[256,1024]{1,0:T(8,128)(2,1)} %refs_1_.2), channel_id=1, source_target_pairs={{0,1},{1,0},{2,3},{3,2},{4,5},{5,4},{6,7},{7,6},{8,9},{9,8},{10,11... | collective-permute-start | bytes 1572872 | tf_op jit(solution)/shard_map/ppermute | solution.py:512
  14.8 14.1 %collective-permute-start.4 = (bf16[256,1024]{1,0:T(8,128)(2,1)S(1)}, bf16[256,1024]{1,0:T(8,128)(2,1)S(1)}, u32[]{:S(2)}, u32[]{:S(2)}) collective-permute-start(bf16[256,1024]{1,0:T(8,128)(2,1)S(1)} %collective-permute-done.3.refs_1_), channel_id=1, source_target_pairs={{0,1},{1,0},{2,3},{3,2},{4,5},{5,4},{6,7},{7,6},{8,9},{9,8},{10,11... | collective-permute-start | bytes 1572872 | tf_op jit(solution)/shard_map/ppermute | solution.py:512
  14.8 14.1 %collective-permute-start.6 = (bf16[4,96,128]{2,1,0:T(8,128)(2,1)S(1)}, bf16[4,96,128]{2,1,0:T(8,128)(2,1)S(1)}, u32[]{:S(2)}, u32[]{:S(2)}) collective-permute-start(bf16[4,96,128]{2,1,0:T(8,128)(2,1)S(1)} %get-tuple-element.52), channel_id=1, source_target_pairs={{0,16},{16,32},{32,48},{48,64},{64,80},{80,96},{96,112},{112,128},... | collective-permute-start | bytes 294920 | tf_op jit(solution)/shard_map/ppermute | solution.py:555
  17.8 25.6 %collective-permute-start.2 = (bf16[256,128]{1,0:T(8,128)(2,1)S(1)}, bf16[256,128]{1,0:T(8,128)(2,1)S(1)}, u32[]{:S(2)}, u32[]{:S(2)}) collective-permute-start(bf16[256,128]{1,0:T(8,128)(2,1)S(1)} %get-tuple-element.46), channel_id=1, source_target_pairs={{0,12},{4,0},{8,4},{12,8},{1,13},{5,1},{9,5},{13,9},{2,14},{6,2},{... | collective-permute-start | bytes 196616 | tf_op jit(solution)/shard_map/ppermute | solution.py:516
  31.8 21.8 %collective-permute-start.7 = (bf16[352,128]{1,0:T(8,128)(2,1)S(1)}, bf16[352,128]{1,0:T(8,128)(2,1)S(1)}, u32[]{:S(2)}, u32[]{:S(2)}) collective-permute-start(bf16[352,128]{1,0:T(8,128)(2,1)S(1)} %get-tuple-element.54), channel_id=1, source_target_pairs={{0,4},{4,8},{8,12},{12,0},{1,5},{5,9},{9,13},{13,1},{2,6},{6,10},{... | collective-permute-start | bytes 270344 | tf_op jit(solution)/shard_map/ppermute | solution.py:516
  35.1 18.4 %collective-permute-start.8 = (bf16[352,128]{1,0:T(8,128)(2,1)S(1)}, bf16[352,128]{1,0:T(8,128)(2,1)S(1)}, u32[]{:S(2)}, u32[]{:S(2)}) collective-permute-start(bf16[352,128]{1,0:T(8,128)(2,1)S(1)} %get-tuple-element.55), channel_id=1, source_target_pairs={{0,8},{4,12},{8,0},{12,4},{1,9},{5,13},{9,1},{13,5},{2,10},{6,14},... | collective-permute-start | bytes 270344 | tf_op jit(solution)/shard_map/ppermute | solution.py:516
  39.7 13.8 %collective-permute-start.9 = (bf16[352,128]{1,0:T(8,128)(2,1)S(1)}, bf16[352,128]{1,0:T(8,128)(2,1)S(1)}, u32[]{:S(2)}, u32[]{:S(2)}) collective-permute-start(bf16[352,128]{1,0:T(8,128)(2,1)S(1)} %get-tuple-element.56), channel_id=1, source_target_pairs={{0,12},{4,0},{8,4},{12,8},{1,13},{5,1},{9,5},{13,9},{2,14},{6,2},{... | collective-permute-start | bytes 270344 | tf_op jit(solution)/shard_map/ppermute | solution.py:516
  42.4 11.1 %collective-permute-start.1 = (bf16[256,128]{1,0:T(8,128)(2,1)S(1)}, bf16[256,128]{1,0:T(8,128)(2,1)S(1)}, u32[]{:S(2)}, u32[]{:S(2)}) collective-permute-start(bf16[256,128]{1,0:T(8,128)(2,1)S(1)} %get-tuple-element.46), channel_id=1, source_target_pairs={{0,8},{4,12},{8,0},{12,4},{1,9},{5,13},{9,1},{13,5},{2,10},{6,14},... | collective-permute-start | bytes 196616 | tf_op jit(solution)/shard_map/ppermute | solution.py:516
  43.4 10.1 %collective-permute-start = (bf16[256,128]{1,0:T(8,128)(2,1)S(1)}, bf16[256,128]{1,0:T(8,128)(2,1)S(1)}, u32[]{:S(2)}, u32[]{:S(2)}) collective-permute-start(bf16[256,128]{1,0:T(8,128)(2,1)S(1)} %get-tuple-element.46), channel_id=1, source_target_pairs={{0,4},{4,8},{8,12},{12,0},{1,5},{5,9},{9,13},{13,1},{2,6},{6,10},{... | collective-permute-start | bytes 196616 | tf_op jit(solution)/shard_map/ppermute | solution.py:516
  61.0 33.6 %collective-permute-start.16 = (bf16[512,4096]{1,0:T(8,128)(2,1)}, bf16[512,4096]{1,0:T(8,128)(2,1)}, u32[]{:S(2)}, u32[]{:S(2)}) collective-permute-start(bf16[512,4096]{1,0:T(8,128)(2,1)} %refs_5_.3), channel_id=1, source_target_pairs={{0,1},{1,0},{2,3},{3,2},{4,5},{5,4},{6,7},{7,6},{8,9},{9,8},{10,11... | collective-permute-start | bytes 12582920 | tf_op jit(solution)/shard_map/ppermute | solution.py:512
  61.3 16.3 %all-to-all-start.1 = ((bf16[4,320,128]{2,1,0:T(8,128)(2,1)}), bf16[4,320,128]{2,1,0:T(8,128)(2,1)S(1)}, u32[]{:S(2)}, u32[]{:S(2)}) async-start(bf16[4,320,128]{2,1,0:T(8,128)(2,1)} %get-tuple-element.61), calls=%async_computation.1 | async-start | bytes 655360 | tf_op jit(solution)/shard_map/all_to_all | solution.py:592
  70.1 1.6 %collective-permute-start.10 = (bf16[256,384]{1,0:T(8,128)(2,1)S(1)}, bf16[256,384]{1,0:T(8,128)(2,1)S(1)}, u32[]{:S(2)}, u32[]{:S(2)}) collective-permute-start(bf16[256,384]{1,0:T(8,128)(2,1)S(1)} %get-tuple-element.64), channel_id=1, source_target_pairs={{0,1},{1,0},{2,3},{3,2},{4,5},{5,4},{6,7},{7,6},{8,9},{9,8},{10,11... | collective-permute-start | bytes 589832 | tf_op jit(solution)/shard_map/ppermute | solution.py:512
  79.1 9.3 %collective-permute-start.11 = (bf16[256,128]{1,0:T(8,128)(2,1)S(1)}, bf16[256,128]{1,0:T(8,128)(2,1)S(1)}, u32[]{:S(2)}, u32[]{:S(2)}) collective-permute-start(bf16[256,128]{1,0:T(8,128)(2,1)S(1)} %get-tuple-element.68), channel_id=1, source_target_pairs={{0,1},{1,0},{2,3},{3,2},{4,5},{5,4},{6,7},{7,6},{8,9},{9,8},{10,11... | collective-permute-start | bytes 196616 | tf_op jit(solution)/shard_map/ppermute | solution.py:512
  88.4 45.8 %all-to-all-start.2 = ((bf16[16,128,256]{2,1,0:T(8,128)(2,1)}), bf16[16,128,256]{2,1,0:T(8,128)(2,1)S(1)}, u32[]{:S(2)}, u32[]{:S(2)}) async-start(bf16[16,128,256]{2,1,0:T(8,128)(2,1)} %bitcast.6), calls=%async_computation.2 | async-start | bytes 2097152 | tf_op jit(solution)/shard_map/all_to_all | solution.py:631
  100.2 34.0 %collective-permute-start.17 = (bf16[256,1024]{1,0:T(8,128)(2,1)S(1)}, bf16[256,1024]{1,0:T(8,128)(2,1)S(1)}, u32[]{:S(2)}, u32[]{:S(2)}) collective-permute-start(bf16[256,1024]{1,0:T(8,128)(2,1)S(1)} %get-tuple-element.85), channel_id=1, source_target_pairs={{0,2},{2,0},{1,3},{3,1},{4,6},{6,4},{5,7},{7,5},{8,10},{10,8},{9,1... | collective-permute-start | bytes 1572872 | tf_op jit(solution)/shard_map/ppermute | solution.py:512
  102.3 5.5 %collective-permute-start.12 = (bf16[352,128]{1,0:T(8,128)(2,1)S(1)}, bf16[352,128]{1,0:T(8,128)(2,1)S(1)}, u32[]{:S(2)}, u32[]{:S(2)}) collective-permute-start(bf16[352,128]{1,0:T(8,128)(2,1)S(1)} %get-tuple-element.72), channel_id=1, source_target_pairs={{0,12},{4,0},{8,4},{12,8},{1,13},{5,1},{9,5},{13,9},{2,14},{6,2},{... | collective-permute-start | bytes 270344 | tf_op jit(solution)/shard_map/ppermute | solution.py:516
  103.7 18.1 %collective-permute-start.13 = (bf16[352,128]{1,0:T(8,128)(2,1)S(1)}, bf16[352,128]{1,0:T(8,128)(2,1)S(1)}, u32[]{:S(2)}, u32[]{:S(2)}) collective-permute-start(bf16[352,128]{1,0:T(8,128)(2,1)S(1)} %get-tuple-element.73), channel_id=1, source_target_pairs={{0,8},{4,12},{8,0},{12,4},{1,9},{5,13},{9,1},{13,5},{2,10},{6,14},... | collective-permute-start | bytes 270344 | tf_op jit(solution)/shard_map/ppermute | solution.py:516
  106.0 17.2 %collective-permute-start.14 = (bf16[352,128]{1,0:T(8,128)(2,1)S(1)}, bf16[352,128]{1,0:T(8,128)(2,1)S(1)}, u32[]{:S(2)}, u32[]{:S(2)}) collective-permute-start(bf16[352,128]{1,0:T(8,128)(2,1)S(1)} %get-tuple-element.74), channel_id=1, source_target_pairs={{0,4},{4,8},{8,12},{12,0},{1,5},{5,9},{9,13},{13,1},{2,6},{6,10},{... | collective-permute-start | bytes 270344 | tf_op jit(solution)/shard_map/ppermute | solution.py:516
  125.5 8.6 %collective-permute-start.15 = (bf16[4,96,128]{2,1,0:T(8,128)(2,1)S(1)}, bf16[4,96,128]{2,1,0:T(8,128)(2,1)S(1)}, u32[]{:S(2)}, u32[]{:S(2)}) collective-permute-start(bf16[4,96,128]{2,1,0:T(8,128)(2,1)S(1)} %get-tuple-element.77), channel_id=1, source_target_pairs={{16,0},{32,16},{48,32},{64,48},{80,64},{96,80},{112,96},{128,112},... | collective-permute-start | bytes 294920 | tf_op jit(solution)/shard_map/ppermute | solution.py:658

commit v4 on v3

--- a/solution.py
+++ b/solution.py
@@ -67,8 +67,12 @@
     return ones_where(want == col)
 
 
-def call(kernel, outs, ins, scratch=(), name=None, vmem=24, fetch=(), raw=(), store=()):
+def call(
+    kernel, outs, ins, scratch=(), name=None, vmem=24, fetch=(), raw=(), store=(),
+    direct=(), flops=1,
+):
     fetch, raw, store = sorted(fetch), set(raw), sorted(store)
+    pinned = set(store) | set(direct)
     n_in, n_out, n_own = len(ins), len(outs), len(scratch)
     hbm = pl.BlockSpec(memory_space=pltpu.HBM)
 
@@ -107,15 +111,17 @@
     return pl.pallas_call(
         body,
         out_shape=tuple(
-            pltpu.HBM(s.shape, s.dtype) if i in store else s
+            pltpu.HBM(s.shape, s.dtype) if i in pinned else s
             for i, s in enumerate(outs)
         ),
         in_specs=[SM]
         + [hbm if i in fetch or i in raw else VM for i in range(1, n_in)],
-        out_specs=tuple(hbm if i in store else VM for i in range(n_out)),
+        out_specs=tuple(hbm if i in pinned else VM for i in range(n_out)),
         scratch_shapes=list(scratch) + extra,
         compiler_params=pltpu.CompilerParams(vmem_limit_bytes=vmem * 2**20),
-        cost_estimate=pl.CostEstimate(flops=1, bytes_accessed=1, transcendentals=0),
+        cost_estimate=pl.CostEstimate(
+            flops=flops, bytes_accessed=1, transcendentals=0
+        ),
         name=name,
     )(
         *(
@@ -131,50 +137,55 @@
     return jax.ShapeDtypeStruct(shape, dtype)
 
 
-def prep_kernel(
-    meta, soff_t, sidx, q, k, v, kvb, q0, picks, q0_own, kv0, picks_own
-):
-    q0[...] = q[:, :HEAD]
-    q0_own[...] = q[:, :HEAD]
+def prep_kernel(meta, soff_t, sidx, k, v, q, kvb, q0, picks, sem):
+    copy = pltpu.make_async_copy(q.at[:, pl.ds(0, HEAD)], q0, sem.at[0])
+    copy.start()
     pick = summary_select(sidx[...])
-    kv = jnp.concatenate([k[:, :HEAD], v[:, :HEAD]], 1)
-    kv0[...] = kv
-    kv = tn(pick, kv).astype(BF)
+    kv = tn(pick, jnp.concatenate([k[:, :HEAD], v[:, :HEAD]], 1)).astype(BF)
     for i in range(ROWS):
         kvb[i] = kv
     sel = stride_select(soff_t[...], GROUP * meta[0] + meta[1])
     got = nn(sel, jnp.concatenate([k[:, HEAD:], v[:, HEAD:]], 1)).astype(BF)
     for u in range(4):
         for h in range(6):
-            part = got[u * REACH : (u + 1) * REACH, h * HEAD : (h + 1) * HEAD]
-            picks[u, h * REACH : (h + 1) * REACH, :] = part
-            picks_own[u, h * REACH : (h + 1) * REACH, :] = part
-
-
-def grad_near_kernel(meta, up, up_c, w, order, acc, far_w, near_w, sems):
-    zl, c = meta[2], meta[3]
-    wide = up.shape[1]
+            picks[u, h * REACH : (h + 1) * REACH, :] = got[
+                u * REACH : (u + 1) * REACH, h * HEAD : (h + 1) * HEAD
+            ]
+    copy.wait()
+
+
+def weight_blocks(w, blocks, places, sems):
+    wide = blocks.shape[2]
     copies = []
-    for i, (z, core) in enumerate(
-        ((zl, c), (zl, 1 - c), (1 - zl, c), (1 - zl, 1 - c))
-    ):
+    for i, (z, core) in enumerate(places):
         at = pl.ds(pl.multiple_of((2 * z + core) * wide, wide), wide)
-        to = near_w.at[i] if i < 2 else far_w.at[i - 2]
-        copies.append(pltpu.make_async_copy(w.at[:, at], to, sems.at[i]))
+        copies.append(pltpu.make_async_copy(w.at[:, at], blocks.at[i], sems.at[i]))
     for copy in copies:
         copy.start()
+    return copies
+
+
+def grad_near_kernel(meta, up, up_c, w, order, acc, blocks, sems):
+    zl, c = meta[2], meta[3]
+    copies = weight_blocks(w, blocks, ((zl, c), (zl, 1 - c)), sems)
     copies[0].wait()
-    total = nt(up[...], near_w[0])
+    total = nt(up[...], blocks[0])
     copies[1].wait()
-    acc[...] = total + nt(up_c[...], near_w[1])
-    copies[2].wait()
-    copies[3].wait()
-
-
-def grad_far_kernel(meta, up_z, up_zc, far_w, acc, picks, before, g, last, *sent):
-    zh = meta[1]
-    full = acc[...] + nt(up_z[...], far_w[0])
-    full = (full + nt(up_zc[...], far_w[1])).astype(BF)
+    acc[...] = total + nt(up_c[...], blocks[1])
+
+
+def grad_far_kernel(
+    meta, up_z, up_zc, w, acc, picks, before, q0, q1, q2, q3, g, last, q_all, *rest
+):
+    sent, blocks, sems = rest[:3], rest[3], rest[4]
+    zh, zl, c = meta[1], meta[2], meta[3]
+    copies = weight_blocks(w, blocks, ((1 - zl, c), (1 - zl, 1 - c)), sems)
+    for d, ref in enumerate((q0, q1, q2, q3)):
+        q_all[d * TOK : (d + 1) * TOK, :] = ref[...]
+    copies[0].wait()
+    full = acc[...] + nt(up_z[...], blocks[0])
+    copies[1].wait()
+    full = (full + nt(up_zc[...], blocks[1])).astype(BF)
     g[...] = full
     last[...] = before[3]
     for d in (1, 2, 3):
@@ -225,21 +236,40 @@
 
 
 def forward_kernel(
-    meta, q0, q1, q2, q3, g0, g1, g2, g3, kva, kv0, ob, q_all, g_all, kv_all, near, s_ref
+    meta, q_all, g0, g1, g2, g3, kva, k, v, ob, g_all, kv_all, near, s_ref, gs, kv0, sems
 ):
     row, zh = meta[0], meta[1]
-    q = jnp.concatenate([q0[...], q1[...], q2[...], q3[...]], 0)
-    g = jnp.concatenate([g0[:, :HEAD], g1[:TOK], g2[:TOK], g3[:TOK]], 0)
-    q_all[...] = q
-    g_all[...] = g
+    first = pl.ds(0, HEAD)
+    brought = [
+        pltpu.make_async_copy(g0.at[:, first], gs.at[pl.ds(0, TOK)], sems.at[0]),
+        pltpu.make_async_copy(k.at[:, first], kv0.at[:, first], sems.at[1]),
+        pltpu.make_async_copy(
+            v.at[:, first], kv0.at[:, pl.ds(HEAD, HEAD)], sems.at[2]
+        ),
+    ]
+    for copy in brought:
+        copy.start()
     for d, ref in ((1, g1), (2, g2), (3, g3)):
-        near[d - 1] = ref[TOK:]
+        gs[d * TOK : (d + 1) * TOK, :] = ref[:TOK, :]
+    kept = [pltpu.make_async_copy(kva, kv_all, sems.at[3])]
+    for d, ref in ((1, g1), (2, g2), (3, g3)):
+        kept.append(
+            pltpu.make_async_copy(
+                ref.at[pl.ds(TOK, FAR)], near.at[d - 1], sems.at[3 + d]
+            )
+        )
+    for copy in brought:
+        copy.wait()
+    kept.append(pltpu.make_async_copy(gs, g_all, sems.at[7]))
+    for copy in kept:
+        copy.start()
+    q, g = q_all[...], gs[...]
+    q0, g0 = q[:TOK], g[:TOK]
     masks = block_masks(row, zh)
     per = TILE // SUMM
     top = jnp.full((8, ALL), NEG, F32)
     for j in range(KEYS // TILE):
         s = nt(kva[j * TILE : (j + 1) * TILE, :HEAD], q)
-        kv_all[j * TILE : (j + 1) * TILE, :] = kva[j * TILE : (j + 1) * TILE, :]
         s_ref[j * TILE : (j + 1) * TILE, :] = s
         for i in range(per):
             most = fold8(s[i * SUMM : (i + 1) * SUMM], jnp.max)
@@ -272,11 +302,11 @@
     out = out * inv
 
     key, value = kv0[:, :HEAD], kv0[:, HEAD:]
-    s = jnp.where(causal_t(), nt(key, q0[...]) * SCALE2, NEG)
+    s = jnp.where(causal_t(), nt(key, q0) * SCALE2, NEG)
     own_top = jnp.max(s, axis=0, keepdims=True)
     e = jnp.exp2(s - own_top)
     own_sum = jnp.sum(e, axis=0, keepdims=True)
-    own_dot = jnp.sum(e * nt(value, g0[:, :HEAD]), axis=0, keepdims=True)
+    own_dot = jnp.sum(e * nt(value, g0), axis=0, keepdims=True)
     own_out = tn(value, e.astype(BF))
     own_log = own_top + jnp.log(own_sum) * LOG2E
     near = log_sum[:, :TOK]
@@ -304,6 +334,8 @@
         to = lax.rem(zh - d + GROUP, GROUP)
         ob[to, :TOK, :] = halves(part).astype(BF)
         ob[to, TOK:, :] = stats
+    for copy in kept:
+        copy.wait()
 
 
 def combine_kernel(meta, oa, o_sc, o, stat, o_own, o_beside):
@@ -348,9 +380,27 @@
 
 
 def backward_kernel(
-    meta, q_all, g_all, kva, kv0, stat, far, dkv, dq1, dq2, dq3, own, dq0
+    meta, q_all, g_all, kv_all, k, v, stat, far, dkv, dq1, dq2, dq3, own, dq0,
+    kva, kv0, sems
 ):
     row, zh = meta[0], meta[1]
+    first = pl.ds(0, HEAD)
+    half = KEYS // 2
+    brought = [
+        pltpu.make_async_copy(
+            kv_all.at[pl.ds(i * half, half)], kva.at[pl.ds(i * half, half)], sems.at[i]
+        )
+        for i in range(2)
+    ]
+    brought += [
+        pltpu.make_async_copy(k.at[:, first], kv0.at[:, first], sems.at[2]),
+        pltpu.make_async_copy(
+            v.at[:, first], kv0.at[:, pl.ds(HEAD, HEAD)], sems.at[3]
+        ),
+    ]
+    for copy in brought:
+        copy.start()
+    brought[0].wait()
     q, g = q_all[...], g_all[...]
     q0, g0 = q[:TOK], g[:TOK]
     masks = block_masks(row, zh)
@@ -358,6 +408,8 @@
     per = TILE // SUMM
     dq = jnp.zeros((HEAD, ALL), F32)
     for j in range(KEYS // TILE):
+        if j * TILE == half:
+            brought[1].wait()
         at = slice(j * TILE, (j + 1) * TILE)
         key, value = kva[at, :HEAD], kva[at, HEAD:]
         s = nt(key, q)
@@ -372,6 +424,8 @@
         ds = (p * (nt(value, g) - dot)).astype(BF)
         dkv[at, :HEAD] = (nn(ds, q) * SCALE).astype(BF)
         dq = dq + tn(key, ds)
+    for copy in brought[2:4]:
+        copy.wait()
     key, value = kv0[:, :HEAD], kv0[:, HEAD:]
     s = jnp.where(causal_t(), nt(key, q0) * SCALE2, NEG)
     p = jnp.exp2(s - log_sum[:, :TOK])
@@ -427,28 +481,20 @@
             far[u, (h + 3) * REACH : (h + 4) * REACH, :] = dvf[rows]
 
 
-def project_kernel(meta, o_f, o_fc, o, o_c, w, w_c, order, send, keep, wa, wb, sems):
+def project_kernel(
+    meta, o_f, o_fc, o, o_c, w, w_c, send, keep, here_w, beside_w, here_s, beside_s
+):
     zl, c = meta[2], meta[3]
-    wide = wa.shape[2]
-    copies = []
-    for i, z in enumerate((1 - zl, zl)):
-        at = pl.ds(pl.multiple_of((2 * z + c) * wide, wide), wide)
-        copies.append(
-            (
-                pltpu.make_async_copy(w.at[:, at], wa.at[i], sems.at[2 * i]),
-                pltpu.make_async_copy(w_c.at[:, at], wb.at[i], sems.at[2 * i + 1]),
-            )
-        )
-    for pair in copies:
-        for copy in pair:
-            copy.start()
+    places = ((1 - zl, c), (zl, c))
+    copies = weight_blocks(w, here_w, places, here_s)
+    beside_copies = weight_blocks(w_c, beside_w, places, beside_s)
     here = jnp.concatenate([o_f[...], o[...]], 1)
     beside = jnp.concatenate([o_fc[...], o_c[...]], 1)
     for i, ref in ((0, send), (1, keep)):
-        copies[i][0].wait()
-        total = nn(here, wa[i])
-        copies[i][1].wait()
-        ref[...] = (total + nn(beside, wb[i])).astype(ref.dtype)
+        copies[i].wait()
+        total = nn(here, here_w[i])
+        beside_copies[i].wait()
+        ref[...] = (total + nn(beside, beside_w[i])).astype(ref.dtype)
 
 
 def back_kernel(meta, dq0, b1, b2, b3, far, sent, here, dq):
@@ -536,57 +582,62 @@
     up_z = swap(upstream, "zl")
     up_c = swap(upstream, "c")
     block = sds((4, FAR, HEAD))
-    kvb, q0, picks, q0_own, kv0, picks_own = call(
+    kvb, q0, picks = call(
         prep_kernel,
-        [
-            sds((ROWS, SUMM, 2 * HEAD)),
-            sds((TOK, HEAD)),
-            block,
-            sds((TOK, HEAD)),
-            sds((TOK, 2 * HEAD)),
-            block,
-        ],
-        [meta, soff_t, summary_index, queries, key_rows, value_rows],
+        [sds((ROWS, SUMM, 2 * HEAD)), sds((TOK, HEAD)), block],
+        [meta, soff_t, summary_index, key_rows, value_rows, queries],
+        [dma(1)],
         name="pick_rows",
-        fetch=range(1, 6),
-        store=[3, 4, 5],
-    )
-    kva = lax.all_to_all(kvb, plane, 0, 0, tiled=True).reshape(KEYS, 2 * HEAD)
+        fetch=range(1, 5),
+        raw=[5],
+    )
     before = lax.ppermute(picks, plane, [(i, i + 1) for i in range(ROWS - 1)])
-    acc, far_w = call(
+    two_blocks = [pltpu.VMEM((2, width, quarter), BF), dma(2)]
+    (acc,) = call(
         grad_near_kernel,
-        [sds((TOK, width), F32), sds((2, width, quarter))],
-        [meta, upstream, up_c, out_weight, kv0],
-        [pltpu.VMEM((2, width, quarter), BF), dma(4)],
+        [sds((TOK, width), F32)],
+        [meta, upstream, up_c, out_weight, picks],
+        two_blocks,
         name="attention_grad_near",
         fetch=[1],
-        raw=[3, 4],
-    )
-    up_zc = swap(after(up_z, kv0), "c")
-    qs = [q0_own] + [turn(q0, d) for d in (1, 2, 3)]
-    g, last, *gs = call(
+        raw=[3],
+        store=[0],
+    )
+    kvb = after(after(kvb, before), acc)
+    kva = lax.all_to_all(kvb, plane, 0, 0, tiled=True).reshape(KEYS, 2 * HEAD)
+    up_zc = swap(after(up_z, picks), "c")
+    qs = [q0] + [turn(q0, d) for d in (1, 2, 3)]
+    g, last, q_all, *gs = call(
         grad_far_kernel,
-        [sds((TOK, width)), sds((FAR, HEAD))] + [sds((TOK + FAR, HEAD))] * 3,
-        [meta, up_z, up_zc, far_w, acc, picks_own, before],
+        [sds((TOK, width)), sds((FAR, HEAD)), sds((ALL, HEAD))]
+        + [sds((TOK + FAR, HEAD))] * 3,
+        [meta, up_z, up_zc, out_weight, acc, picks, before, *qs],
+        two_blocks,
         name="attention_grad_far",
-        fetch=[5],
-        store=[0, 1],
-    )
-    gs = [g] + [turn(gs[d - 1], d) for d in (1, 2, 3)]
-    ob, q_all, g_all, kv_all, near = call(
+        fetch=[4],
+        raw=[3],
+        store=[0, 1, 2],
+    )
+    gs = [turn(gs[d - 1], d) for d in (1, 2, 3)]
+    ob, g_all, kv_all, near = call(
         forward_kernel,
         [
             sds((GROUP, TOK + STAT, HEAD)),
             sds((ALL, HEAD)),
-            sds((ALL, HEAD)),
             sds((KEYS, 2 * HEAD)),
             sds((3, FAR, HEAD)),
         ],
-        [meta, *qs, *gs, kva, kv0],
-        [pltpu.VMEM((KEYS, ALL), F32)],
+        [meta, q_all, g, *gs, kva, key_rows, value_rows],
+        [
+            pltpu.VMEM((KEYS, ALL), F32),
+            pltpu.VMEM((ALL, HEAD), BF),
+            pltpu.VMEM((TOK, 2 * HEAD), BF),
+            dma(8),
+        ],
         name="fixed_forward",
-        fetch=[1, 5, 10],
-        store=[1, 2, 3, 4],
+        fetch=[1],
+        raw=[2, 7, 8],
+        direct=[1, 2, 3],
     )
     weight_c = swap(after(out_weight, near), "c")
     oa = lax.all_to_all(ob, "zh", 0, 0, tiled=True)
@@ -623,9 +674,15 @@
         [sds((KEYS, 2 * HEAD))]
         + [sds((TOK + FAR, HEAD))] * 3
         + [sds((TOK, 2 * HEAD), F32), sds((HEAD, TOK), F32)],
-        [meta, q_all, g_all, kv_all, kv0, stat, far],
+        [meta, q_all, g_all, kv_all, key_rows, value_rows, stat, far],
+        [
+            pltpu.VMEM((KEYS, 2 * HEAD), BF),
+            pltpu.VMEM((TOK, 2 * HEAD), BF),
+            dma(4),
+        ],
         name="fixed_backward",
-        fetch=[1, 2, 3, 4, 6],
+        fetch=[1, 2, 7],
+        raw=[3, 4, 5],
         store=[4, 5],
     )
     dkva = lax.all_to_all(
@@ -634,15 +691,11 @@
     send, keep = call(
         project_kernel,
         [sds((TOK, quarter))] * 2,
-        [meta, o_f_own, o_fc, o_own, o_beside, out_weight, weight_c, dq0],
-        [
-            pltpu.VMEM((2, width, quarter), BF),
-            pltpu.VMEM((2, width, quarter), BF),
-            dma(4),
-        ],
+        [meta, o_f_own, o_fc, o_own, o_beside, out_weight, weight_c],
+        two_blocks[:1] * 2 + two_blocks[1:] * 2,
         name="project",
         fetch=[1, 3, 4],
-        raw=[5, 6, 7],
+        raw=[5, 6],
         store=[1],
     )
     over = swap(send, "zl")
@@ -654,6 +707,7 @@
         name="bundle_back",
         fetch=[1, 5],
         store=[1, 2],
+        flops=5 * 10**9,
     )
     back = lax.ppermute(sent, plane, [(i + 1, i) for i in range(ROWS - 1)])
     return call(

time: 139 us -> 133 us (0.957)
  waiting for transfers between devices: 40.1 us -> 31.8 us
  Pallas kernels: 45.6 us -> 48.8 us
    ppermute x9, waiting for transfers between devices: 25.3 us -> 15.9 us  [turn(): return lax.ppermute(a, 'zh', [(i, (i + by) % GROUP) for i in range(GROUP)])]
    pallas_call x10, Pallas kernels: 45.6 us -> 48.8 us  [call(): pl.pallas_call(body, out_shape=tuple((pltpu.HBM(s.shape, s.dtype) if i in...]
    ppermute x1, waiting for transfers between devices: 0.89 us -> 3.68 us  [shards(): before = lax.ppermute(picks, plane, [(i, i + 1) for i in range(ROWS - 1)])]
    ppermute x9, starting transfers between devices: 23.5 us -> 21.9 us  [turn(): return lax.ppermute(a, 'zh', [(i, (i + by) % GROUP) for i in range(GROUP)])]
  transfers between devices with their start and end apart: 21 -> 21, of which waited for: 9 -> 11; matrix products, arithmetic and copies ran while one was open for 0% -> 0% of each run, Pallas kernels for 25% -> 28%
where the time goes in v4:
time: 133 us; the launch traced here: 132 us
  starting transfers between devices  50.5 us (38%)
  Pallas kernels  48.8 us (37%)
  waiting for transfers between devices  31.8 us (24%)
    pallas_call x10, Pallas kernels, call(): pl.pallas_call(body, out_shape=tuple((pltpu.HBM(s.shape, s.dtype) if i in...  48.8 us
    ppermute x9, starting transfers between devices, turn(): return lax.ppermute(a, 'zh', [(i, (i + by) % GROUP) for i in range(GROUP)])  21.9 us
    ppermute x9, waiting for transfers between devices, turn(): return lax.ppermute(a, 'zh', [(i, (i + by) % GROUP) for i in range(GROUP)])  15.9 us
    all_to_all x1, starting transfers between devices, shards(): lax.all_to_all(after(dkv, o_fc).reshape(ROWS, SUMM, 2 * HEAD), plane, 0,...  7.23 us
    all_to_all x1, starting transfers between devices, shards(): kva = lax.all_to_all(kvb, plane, 0, 0, tiled=True).reshape(KEYS, 2 * HEAD)  7.18 us
    ppermute x1, waiting for transfers between devices, shards(): back = lax.ppermute(sent, plane, [(i + 1, i) for i in range(ROWS - 1)])  5.85 us
    all_to_all x1, waiting for transfers between devices, shards(): oa = lax.all_to_all(ob, 'zh', 0, 0, tiled=True)  5.15 us
    all_to_all x1, starting transfers between devices, shards(): oa = lax.all_to_all(ob, 'zh', 0, 0, tiled=True)  4.72 us
  transfers between devices with their start and end apart: 21, of which 11 were waited for; matrix products, arithmetic and copies ran while one was open for 0% of the time, Pallas kernels for 28%

profile of v4, /device:TPU:24, one launch (start us, length us, event | category | flops | bytes accessed | tf_op | source)
XLA Modules:
  0.0 132.1 jit_solution(9293555536163600385)
XLA Ops:
  0.7 2.0 %collective-permute-start = (bf16[256,1024]{1,0:T(8,128)(2,1)}, bf16[256,1024]{1,0:T(8,128)(2,1)S(1)}, u32[]{:S(2)}, u32[]{:S(2)}) collective-permute-start(bf16[256,1024]{1,0:T(8,128)(2,1)} %refs_1_.2), channel_id=1, source_target_pairs={{0,2},{2,0},{1,3},{3,1},{4,6},{6,4},{5,7},{7,5},{8,10},{10,8},{9,1... | collective-permute-start | bytes 1572872 | tf_op jit(solution)/shard_map/ppermute | solution.py:558
  2.8 3.5 %pick_rows.1 = (bf16[16,128,256]{2,1,0:T(8,128)(2,1)}, bf16[256,128]{1,0:T(8,128)(2,1)S(1)}, bf16[4,96,128]{2,1,0:T(8,128)(2,1)S(1)}) custom-call(s32[4]{0:T(128)S(1)} %pad_add_fusion.refs_0_, s32[4,64]{1,0:T(4,128)} %bitcast.10, s32[1,128]{1,0:T(1,128)} %refs_2_.5, bf16[256,512]{1,0:T(8,128)(2,1)} %refs_4_.3, bf16[256,512]{1,0:T(8,128)(2,1)} %refs_5_.4, ...), custom_call_target="tpu_custom_call" | custom-call | flops 1 | bytes 1 | tf_op jit(solution)/shard_map/pick_rows/pallas_call | solution.py:111
  6.3 3.1 %collective-permute-start.3 = (bf16[4,96,128]{2,1,0:T(8,128)(2,1)S(1)}, bf16[4,96,128]{2,1,0:T(8,128)(2,1)S(1)}, u32[]{:S(2)}, u32[]{:S(2)}) collective-permute-start(bf16[4,96,128]{2,1,0:T(8,128)(2,1)S(1)} %get-tuple-element.42.refs_4_.refs_5_), channel_id=1, source_target_pairs={{0,16},{16,32},{32,48},{48,64},{64,80},{80,96},{96,112},{112,128},... | collective-permute-start | bytes 294920 | tf_op jit(solution)/shard_map/ppermute | solution.py:594
  9.4 3.7 %collective-permute-done.3.refs_6_ = bf16[4,96,128]{2,1,0:T(8,128)(2,1)S(1)} collective-permute-done((bf16[4,96,128]{2,1,0:T(8,128)(2,1)S(1)}, bf16[4,96,128]{2,1,0:T(8,128)(2,1)S(1)}, u32[]{:S(2)}, u32[]{:S(2)}) %collective-permute-start.3) | collective-permute-done | bytes 98336 | tf_op jit(solution)/shard_map/ppermute | solution.py:594
  13.1 4.7 %attention_grad_near.1.refs_4_ = f32[256,512]{1,0:T(8,128)} custom-call(s32[4]{0:T(128)S(1)} %pad_add_fusion.refs_0_, bf16[256,1024]{1,0:T(8,128)(2,1)} %refs_1_.2, bf16[256,1024]{1,0:T(8,128)(2,1)S(1)} %collective-permute-done.2.refs_2_, bf16[512,4096]{1,0:T(8,128)(2,1)} %refs_5_.5, bf16[4,96,128]{2,1,0:T(8,128)(2,1)S(1)} %get-tuple-element.42.refs_4_.refs_5_), custom_call_target="tpu_custom_call" | custom-call | flops 1 | bytes 1 | tf_op jit(solution)/shard_map/attention_grad_near/pallas_call | solution.py:111
  17.8 7.2 %all-to-all-start = ((bf16[16,128,256]{2,1,0:T(8,128)(2,1)}), bf16[16,128,256]{2,1,0:T(8,128)(2,1)S(1)}, u32[]{:S(2)}, u32[]{:S(2)}) async-start(bf16[16,128,256]{2,1,0:T(8,128)(2,1)} %get-tuple-element.52), calls=%async_computation | async-start | bytes 2097152 | tf_op jit(solution)/shard_map/all_to_all | solution.py:607
  25.0 5.5 %collective-permute-start.6 = (bf16[256,128]{1,0:T(8,128)(2,1)S(1)}, bf16[256,128]{1,0:T(8,128)(2,1)S(1)}, u32[]{:S(2)}, u32[]{:S(2)}) collective-permute-start(bf16[256,128]{1,0:T(8,128)(2,1)S(1)} %get-tuple-element.44.refs_7_), channel_id=1, source_target_pairs={{0,12},{4,0},{8,4},{12,8},{1,13},{5,1},{9,5},{13,9},{2,14},{6,2},{... | collective-permute-start | bytes 196616 | tf_op jit(solution)/shard_map/ppermute | solution.py:562
  30.5 1.4 %collective-permute-start.5 = (bf16[256,128]{1,0:T(8,128)(2,1)S(1)}, bf16[256,128]{1,0:T(8,128)(2,1)S(1)}, u32[]{:S(2)}, u32[]{:S(2)}) collective-permute-start(bf16[256,128]{1,0:T(8,128)(2,1)S(1)} %get-tuple-element.44.refs_7_), channel_id=1, source_target_pairs={{0,8},{4,12},{8,0},{12,4},{1,9},{5,13},{9,1},{13,5},{2,10},{6,14},... | collective-permute-start | bytes 196616 | tf_op jit(solution)/shard_map/ppermute | solution.py:562
  32.0 2.4 %collective-permute-start.4 = (bf16[256,128]{1,0:T(8,128)(2,1)S(1)}, bf16[256,128]{1,0:T(8,128)(2,1)S(1)}, u32[]{:S(2)}, u32[]{:S(2)}) collective-permute-start(bf16[256,128]{1,0:T(8,128)(2,1)S(1)} %get-tuple-element.44.refs_7_), channel_id=1, source_target_pairs={{0,4},{4,8},{8,12},{12,0},{1,5},{5,9},{9,13},{13,1},{2,6},{6,10},{... | collective-permute-start | bytes 196616 | tf_op jit(solution)/shard_map/ppermute | solution.py:562
  34.3 2.4 %collective-permute-done.6.refs_10_ = bf16[256,128]{1,0:T(8,128)(2,1)S(1)} collective-permute-done((bf16[256,128]{1,0:T(8,128)(2,1)S(1)}, bf16[256,128]{1,0:T(8,128)(2,1)S(1)}, u32[]{:S(2)}, u32[]{:S(2)}) %collective-permute-start.6) | collective-permute-done | bytes 65568 | tf_op jit(solution)/shard_map/ppermute | solution.py:562
  36.7 3.9 %collective-permute-done.5.refs_9_ = bf16[256,128]{1,0:T(8,128)(2,1)S(1)} collective-permute-done((bf16[256,128]{1,0:T(8,128)(2,1)S(1)}, bf16[256,128]{1,0:T(8,128)(2,1)S(1)}, u32[]{:S(2)}, u32[]{:S(2)}) %collective-permute-start.5) | collective-permute-done | bytes 65568 | tf_op jit(solution)/shard_map/ppermute | solution.py:562
  40.6 4.5 %attention_grad_far.1 = (bf16[256,512]{1,0:T(8,128)(2,1)}, bf16[96,128]{1,0:T(8,128)(2,1)}, bf16[1024,128]{1,0:T(8,128)(2,1)}, bf16[352,128]{1,0:T(8,128)(2,1)S(...) custom-call(s32[4]{0:T(128)S(1)} %pad_add_fusion.refs_0_, ...), custom_call_target="tpu_custom_call" | custom-call | flops 1 | bytes 1 | tf_op jit(solution)/shard_map/attention_grad_far/pallas_call | solution.py:111
  45.4 4.7 %collective-permute-start.8 = (bf16[352,128]{1,0:T(8,128)(2,1)S(1)}, bf16[352,128]{1,0:T(8,128)(2,1)S(1)}, u32[]{:S(2)}, u32[]{:S(2)}) collective-permute-start(bf16[352,128]{1,0:T(8,128)(2,1)S(1)} %get-tuple-element.48), channel_id=1, source_target_pairs={{0,8},{4,12},{8,0},{12,4},{1,9},{5,13},{9,1},{13,5},{2,10},{6,14},... | collective-permute-start | bytes 270344 | tf_op jit(solution)/shard_map/ppermute | solution.py:562
  50.1 2.9 %collective-permute-start.9 = (bf16[352,128]{1,0:T(8,128)(2,1)S(1)}, bf16[352,128]{1,0:T(8,128)(2,1)S(1)}, u32[]{:S(2)}, u32[]{:S(2)}) collective-permute-start(bf16[352,128]{1,0:T(8,128)(2,1)S(1)} %get-tuple-element.49), channel_id=1, source_target_pairs={{0,12},{4,0},{8,4},{12,8},{1,13},{5,1},{9,5},{13,9},{2,14},{6,2},{... | collective-permute-start | bytes 270344 | tf_op jit(solution)/shard_map/ppermute | solution.py:562
  53.0 1.7 %collective-permute-done.7.refs_3_ = bf16[352,128]{1,0:T(8,128)(2,1)S(1)} collective-permute-done((bf16[352,128]{1,0:T(8,128)(2,1)S(1)}, bf16[352,128]{1,0:T(8,128)(2,1)S(1)}, u32[]{:S(2)}, u32[]{:S(2)}) %collective-permute-start.7) | collective-permute-done | bytes 90144 | tf_op jit(solution)/shard_map/ppermute | solution.py:562
  54.8 1.7 %collective-permute-done.8.refs_4_ = bf16[352,128]{1,0:T(8,128)(2,1)S(1)} collective-permute-done((bf16[352,128]{1,0:T(8,128)(2,1)S(1)}, bf16[352,128]{1,0:T(8,128)(2,1)S(1)}, u32[]{:S(2)}, u32[]{:S(2)}) %collective-permute-start.8) | collective-permute-done | bytes 90144 | tf_op jit(solution)/shard_map/ppermute | solution.py:562
  56.4 2.9 %collective-permute-done.9.refs_5_ = bf16[352,128]{1,0:T(8,128)(2,1)S(1)} collective-permute-done((bf16[352,128]{1,0:T(8,128)(2,1)S(1)}, bf16[352,128]{1,0:T(8,128)(2,1)S(1)}, u32[]{:S(2)}, u32[]{:S(2)}) %collective-permute-start.9) | collective-permute-done | bytes 90144 | tf_op jit(solution)/shard_map/ppermute | solution.py:562
  59.4 7.4 %fixed_forward.1 = (bf16[4,320,128]{2,1,0:T(8,128)(2,1)}, bf16[1024,128]{1,0:T(8,128)(2,1)}, bf16[2048,256]{1,0:T(8,128)(2,1)}, bf16[3,96,128]{2,1,0:T(8,128)(2,1)}) custom-call(s32[4]{0:T(128)S(1)} %pad_add_fusion.refs_0_, bf16[1024,128]{1,0:T(8,128)(2,1)} %get-tuple-element.45.refs_1_, bf16[256,512]{1,0:T(8,128)(2,1)} %get-tuple-element.46.refs_2_.refs_4_, ...), custom_call_target="tpu_custom_call" | custom-call | flops 1 | bytes 1 | tf_op jit(solution)/shard_map/fixed_forward/pallas_call | solution.py:111
  67.1 4.7 %all-to-all-start.1 = ((bf16[4,320,128]{2,1,0:T(8,128)(2,1)}), bf16[4,320,128]{2,1,0:T(8,128)(2,1)S(1)}, u32[]{:S(2)}, u32[]{:S(2)}) async-start(bf16[4,320,128]{2,1,0:T(8,128)(2,1)} %get-tuple-element.55), calls=%async_computation.1 | async-start | bytes 655360 | tf_op jit(solution)/shard_map/all_to_all | solution.py:643
  71.8 5.3 %strided_heads.1 = (bf16[256,384]{1,0:T(8,128)(2,1)S(1)}, bf16[256,384]{1,0:T(8,128)(2,1)}, f32[256,768]{1,0:T(8,128)}, bf16[4,96,128]{2,1,0:T(8,128)(2,1)}, bf16[256,384]{1,0:T(8,128)(2,1)}) custom-call(s32[4]{0:T(128)S(1)} %pad_add_fusion.refs_0_, bf16[256,512]{1,0:T(8,128)(2,1)} %refs_1_.3, bf16[256,512]{1,0:T(8,128)(2,1)} %refs_4_.3, ...), custom_call_target="tpu_custom_call" | custom-call | flops 1 | bytes 1 | tf_op jit(solution)/shard_map/strided_heads/pallas_call | solution.py:111
  78.7 5.2 %all-to-all-done.1.refs_1_ = bf16[4,320,128]{2,1,0:T(8,128)(2,1)S(1)} async-done(((bf16[4,320,128]{2,1,0:T(8,128)(2,1)}), bf16[4,320,128]{2,1,0:T(8,128)(2,1)S(1)}, u32[]{:S(2)}, u32[]{:S(2)}) %all-to-all-start.1) | async-done | bytes 327712 | tf_op jit(solution)/shard_map/all_to_all | solution.py:643
  83.8 1.5 %combine.1 = (bf16[256,128]{1,0:T(8,128)(2,1)S(1)}, f32[8,1024]{1,0:T(8,128)S(1)}, bf16[256,128]{1,0:T(8,128)(2,1)}, bf16[256,384]{1,0:T(8,128)(2,1)}) custom-call(s32[4]{0:T(128)S(1)} %pad_add_fusion.refs_0_, bf16[4,320,128]{2,1,0:T(8,128)(2,1)S(1)} %all-to-all-done.1.refs_1_, bf16[256,384]{1,0:T(8,128)(2,1)S(1)} %collective-permute-done.10.refs_2_), custom_call_target="tpu_custom_call" | custom-call | flops 1 | bytes 1 | tf_op jit(solution)/shard_map/combine/pallas_call | solution.py:111
  85.5 10.1 %fixed_backward.1 = (bf16[2048,256]{1,0:T(8,128)(2,1)}, bf16[352,128]{1,0:T(8,128)(2,1)S(1)}, bf16[352,128]{1,0:T(8,128)(2,1)S(1)}, bf16[352,128]{1,0:T(8,128)(2...) custom-call(s32[4]{0:T(128)S(1)} %pad_add_fusion.refs_0_, bf16[1024,128]{1,0:T(8,128)(2,1)} %get-tuple-element.45.refs_1_, ...), custom_call_target="tpu_custom_call" | custom-call | flops 1 | bytes 1 | tf_op jit(solution)/shard_map/fixed_backward/pallas_call | solution.py:111
  95.6 7.2 %all-to-all-start.2 = ((bf16[16,128,256]{2,1,0:T(8,128)(2,1)}), bf16[16,128,256]{2,1,0:T(8,128)(2,1)S(1)}, u32[]{:S(2)}, u32[]{:S(2)}) async-start(bf16[16,128,256]{2,1,0:T(8,128)(2,1)} %bitcast.6), calls=%async_computation.2 | async-start | bytes 2097152 | tf_op jit(solution)/shard_map/all_to_all | solution.py:688
  103.6 3.9 %collective-permute-start.13 = (bf16[352,128]{1,0:T(8,128)(2,1)S(1)}, bf16[352,128]{1,0:T(8,128)(2,1)S(1)}, u32[]{:S(2)}, u32[]{:S(2)}) collective-permute-start(bf16[352,128]{1,0:T(8,128)(2,1)S(1)} %get-tuple-element.67), channel_id=1, source_target_pairs={{0,8},{4,12},{8,0},{12,4},{1,9},{5,13},{9,1},{13,5},{2,10},{6,14},... | collective-permute-start | bytes 270344 | tf_op jit(solution)/shard_map/ppermute | solution.py:562
  107.5 5.5 %project.1 = (bf16[256,1024]{1,0:T(8,128)(2,1)S(1)}, bf16[256,1024]{1,0:T(8,128)(2,1)}) custom-call(s32[4]{0:T(128)S(1)} %pad_add_fusion.refs_0_, bf16[256,128]{1,0:T(8,128)(2,1)} %get-tuple-element.74.refs_1_, bf16[256,128]{1,0:T(8,128)(2,1)S(1)} %collective-permute-done.11.refs_2_, bf16[256,384]{1,0:T(8,128)(2,1)} %get-tuple-element.75.refs_3_, ...), custom_call_target="tpu_custom_call" | custom-call | flops 1 | bytes 1 | tf_op jit(solution)/shard_map/project/pallas_call | solution.py:111
  113.9 1.5 %collective-permute-done.13.refs_3_ = bf16[352,128]{1,0:T(8,128)(2,1)S(1)} collective-permute-done((bf16[352,128]{1,0:T(8,128)(2,1)S(1)}, bf16[352,128]{1,0:T(8,128)(2,1)S(1)}, u32[]{:S(2)}, u32[]{:S(2)}) %collective-permute-start.13) | collective-permute-done | bytes 90144 | tf_op jit(solution)/shard_map/ppermute | solution.py:562
  115.4 1.8 %collective-permute-done.14.refs_4_ = bf16[352,128]{1,0:T(8,128)(2,1)S(1)} collective-permute-done((bf16[352,128]{1,0:T(8,128)(2,1)S(1)}, bf16[352,128]{1,0:T(8,128)(2,1)S(1)}, u32[]{:S(2)}, u32[]{:S(2)}) %collective-permute-start.14) | collective-permute-done | bytes 90144 | tf_op jit(solution)/shard_map/ppermute | solution.py:562
  117.2 2.4 %bundle_back.1 = (bf16[4,96,128]{2,1,0:T(8,128)(2,1)S(1)}, bf16[3,96,128]{2,1,0:T(8,128)(2,1)}, bf16[256,128]{1,0:T(8,128)(2,1)}) custom-call(s32[4]{0:T(128)S(1)} %pad_add_fusion.refs_0_, f32[128,256]{1,0:T(8,128)} %get-tuple-element.65.refs_1_, bf16[352,128]{1,0:T(8,128)(2,1)S(1)} %collective-permute-done.12.refs_2_, ...), custom_call_target="tpu_custom_call" | custom-call | flops 5000000000 | bytes 1 | tf_op jit(solution)/shard_map/bundle_back/pallas_call | solution.py:111
  119.6 2.8 %collective-permute-start.15 = (bf16[4,96,128]{2,1,0:T(8,128)(2,1)S(1)}, bf16[4,96,128]{2,1,0:T(8,128)(2,1)S(1)}, u32[]{:S(2)}, u32[]{:S(2)}) collective-permute-start(bf16[4,96,128]{2,1,0:T(8,128)(2,1)S(1)} %get-tuple-element.71), channel_id=1, source_target_pairs={{16,0},{32,16},{48,32},{64,48},{80,64},{96,80},{112,96},{128,112},... | collective-permute-start | bytes 294920 | tf_op jit(solution)/shard_map/ppermute | solution.py:712
  122.4 5.8 %collective-permute-done.15.refs_7_ = bf16[4,96,128]{2,1,0:T(8,128)(2,1)S(1)} collective-permute-done((bf16[4,96,128]{2,1,0:T(8,128)(2,1)S(1)}, bf16[4,96,128]{2,1,0:T(8,128)(2,1)S(1)}, u32[]{:S(2)}, u32[]{:S(2)}) %collective-permute-start.15) | collective-permute-done | bytes 98336 | tf_op jit(solution)/shard_map/ppermute | solution.py:712
  128.2 3.7 %join_results.1 = (bf16[256,1024]{1,0:T(8,128)(2,1)}, bf16[256,512]{1,0:T(8,128)(2,1)}, bf16[256,512]{1,0:T(8,128)(2,1)}, bf16[256,512]{1,0:T(8,128)(2,1)}) custom-call(s32[4]{0:T(128)S(1)} %pad_add_fusion.refs_0_, s32[4,64]{1,0:T(4,128)} %bitcast.11, s32[1,128]{1,0:T(1,128)} %refs_2_.5, bf16[2048,256]{1,0:T(8,128)(2,1)S(1)} %bitcast.8, ...), custom_call_target="tpu_custom_call" | custom-call | flops 1 | bytes 1 | tf_op jit(solution)/shard_map/join_results/pallas_call | solution.py:111
  (21 shorter events, 4.0 us)
Async XLA Ops:
  0.6 12.4 %collective-permute-start.2 = (bf16[256,1024]{1,0:T(8,128)(2,1)}, bf16[256,1024]{1,0:T(8,128)(2,1)S(1)}, u32[]{:S(2)}, u32[]{:S(2)}) collective-permute-start(bf16[256,1024]{1,0:T(8,128)(2,1)} %refs_1_.2), channel_id=1, source_target_pairs={{0,1},{1,0},{2,3},{3,2},{4,5},{5,4},{6,7},{7,6},{8,9},{9,8},{10,11... | collective-permute-start | bytes 1572872 | tf_op jit(solution)/shard_map/ppermute | solution.py:558
  0.7 24.2 %collective-permute-start = (bf16[256,1024]{1,0:T(8,128)(2,1)}, bf16[256,1024]{1,0:T(8,128)(2,1)S(1)}, u32[]{:S(2)}, u32[]{:S(2)}) collective-permute-start(bf16[256,1024]{1,0:T(8,128)(2,1)} %refs_1_.2), channel_id=1, source_target_pairs={{0,2},{2,0},{1,3},{3,1},{4,6},{6,4},{5,7},{7,5},{8,10},{10,8},{9,1... | collective-permute-start | bytes 1572872 | tf_op jit(solution)/shard_map/ppermute | solution.py:558
  6.3 6.7 %collective-permute-start.3 = (bf16[4,96,128]{2,1,0:T(8,128)(2,1)S(1)}, bf16[4,96,128]{2,1,0:T(8,128)(2,1)S(1)}, u32[]{:S(2)}, u32[]{:S(2)}) collective-permute-start(bf16[4,96,128]{2,1,0:T(8,128)(2,1)S(1)} %get-tuple-element.42.refs_4_.refs_5_), channel_id=1, source_target_pairs={{0,16},{16,32},{32,48},{48,64},{64,80},{80,96},{96,112},{112,128},... | collective-permute-start | bytes 294920 | tf_op jit(solution)/shard_map/ppermute | solution.py:594
  17.8 41.6 %all-to-all-start = ((bf16[16,128,256]{2,1,0:T(8,128)(2,1)}), bf16[16,128,256]{2,1,0:T(8,128)(2,1)S(1)}, u32[]{:S(2)}, u32[]{:S(2)}) async-start(bf16[16,128,256]{2,1,0:T(8,128)(2,1)} %get-tuple-element.52), calls=%async_computation | async-start | bytes 2097152 | tf_op jit(solution)/shard_map/all_to_all | solution.py:607
  24.9 15.7 %collective-permute-start.1 = (bf16[256,1024]{1,0:T(8,128)(2,1)S(1)}, bf16[256,1024]{1,0:T(8,128)(2,1)S(1)}, u32[]{:S(2)}, u32[]{:S(2)}) collective-permute-start(bf16[256,1024]{1,0:T(8,128)(2,1)S(1)} %collective-permute-done.refs_1_), channel_id=1, source_target_pairs={{0,1},{1,0},{2,3},{3,2},{4,5},{5,4},{6,7},{7,6},{8,9},{9,8},{10,11... | collective-permute-start | bytes 1572872 | tf_op jit(solution)/shard_map/ppermute | solution.py:558
  25.0 11.7 %collective-permute-start.6 = (bf16[256,128]{1,0:T(8,128)(2,1)S(1)}, bf16[256,128]{1,0:T(8,128)(2,1)S(1)}, u32[]{:S(2)}, u32[]{:S(2)}) collective-permute-start(bf16[256,128]{1,0:T(8,128)(2,1)S(1)} %get-tuple-element.44.refs_7_), channel_id=1, source_target_pairs={{0,12},{4,0},{8,4},{12,8},{1,13},{5,1},{9,5},{13,9},{2,14},{6,2},{... | collective-permute-start | bytes 196616 | tf_op jit(solution)/shard_map/ppermute | solution.py:562
  30.5 10.1 %collective-permute-start.5 = (bf16[256,128]{1,0:T(8,128)(2,1)S(1)}, bf16[256,128]{1,0:T(8,128)(2,1)S(1)}, u32[]{:S(2)}, u32[]{:S(2)}) collective-permute-start(bf16[256,128]{1,0:T(8,128)(2,1)S(1)} %get-tuple-element.44.refs_7_), channel_id=1, source_target_pairs={{0,8},{4,12},{8,0},{12,4},{1,9},{5,13},{9,1},{13,5},{2,10},{6,14},... | collective-permute-start | bytes 196616 | tf_op jit(solution)/shard_map/ppermute | solution.py:562
  32.0 8.7 %collective-permute-start.4 = (bf16[256,128]{1,0:T(8,128)(2,1)S(1)}, bf16[256,128]{1,0:T(8,128)(2,1)S(1)}, u32[]{:S(2)}, u32[]{:S(2)}) collective-permute-start(bf16[256,128]{1,0:T(8,128)(2,1)S(1)} %get-tuple-element.44.refs_7_), channel_id=1, source_target_pairs={{0,4},{4,8},{8,12},{12,0},{1,5},{5,9},{9,13},{13,1},{2,6},{6,10},{... | collective-permute-start | bytes 196616 | tf_op jit(solution)/shard_map/ppermute | solution.py:562
  45.2 9.6 %collective-permute-start.7 = (bf16[352,128]{1,0:T(8,128)(2,1)S(1)}, bf16[352,128]{1,0:T(8,128)(2,1)S(1)}, u32[]{:S(2)}, u32[]{:S(2)}) collective-permute-start(bf16[352,128]{1,0:T(8,128)(2,1)S(1)} %get-tuple-element.47), channel_id=1, source_target_pairs={{0,4},{4,8},{8,12},{12,0},{1,5},{5,9},{9,13},{13,1},{2,6},{6,10},{... | collective-permute-start | bytes 270344 | tf_op jit(solution)/shard_map/ppermute | solution.py:562
  45.4 11.0 %collective-permute-start.8 = (bf16[352,128]{1,0:T(8,128)(2,1)S(1)}, bf16[352,128]{1,0:T(8,128)(2,1)S(1)}, u32[]{:S(2)}, u32[]{:S(2)}) collective-permute-start(bf16[352,128]{1,0:T(8,128)(2,1)S(1)} %get-tuple-element.48), channel_id=1, source_target_pairs={{0,8},{4,12},{8,0},{12,4},{1,9},{5,13},{9,1},{13,5},{2,10},{6,14},... | collective-permute-start | bytes 270344 | tf_op jit(solution)/shard_map/ppermute | solution.py:562
  50.1 9.2 %collective-permute-start.9 = (bf16[352,128]{1,0:T(8,128)(2,1)S(1)}, bf16[352,128]{1,0:T(8,128)(2,1)S(1)}, u32[]{:S(2)}, u32[]{:S(2)}) collective-permute-start(bf16[352,128]{1,0:T(8,128)(2,1)S(1)} %get-tuple-element.49), channel_id=1, source_target_pairs={{0,12},{4,0},{8,4},{12,8},{1,13},{5,1},{9,5},{13,9},{2,14},{6,2},{... | collective-permute-start | bytes 270344 | tf_op jit(solution)/shard_map/ppermute | solution.py:562
  66.8 40.7 %collective-permute-start.16 = (bf16[512,4096]{1,0:T(8,128)(2,1)}, bf16[512,4096]{1,0:T(8,128)(2,1)}, u32[]{:S(2)}, u32[]{:S(2)}) collective-permute-start(bf16[512,4096]{1,0:T(8,128)(2,1)} %refs_5_.5), channel_id=1, source_target_pairs={{0,1},{1,0},{2,3},{3,2},{4,5},{5,4},{6,7},{7,6},{8,9},{9,8},{10,11... | collective-permute-start | bytes 12582920 | tf_op jit(solution)/shard_map/ppermute | solution.py:558
  67.1 16.7 %all-to-all-start.1 = ((bf16[4,320,128]{2,1,0:T(8,128)(2,1)}), bf16[4,320,128]{2,1,0:T(8,128)(2,1)S(1)}, u32[]{:S(2)}, u32[]{:S(2)}) async-start(bf16[4,320,128]{2,1,0:T(8,128)(2,1)} %get-tuple-element.55), calls=%async_computation.1 | async-start | bytes 655360 | tf_op jit(solution)/shard_map/all_to_all | solution.py:643
  77.2 1.5 %collective-permute-start.10 = (bf16[256,384]{1,0:T(8,128)(2,1)S(1)}, bf16[256,384]{1,0:T(8,128)(2,1)S(1)}, u32[]{:S(2)}, u32[]{:S(2)}) collective-permute-start(bf16[256,384]{1,0:T(8,128)(2,1)S(1)} %get-tuple-element.58), channel_id=1, source_target_pairs={{0,1},{1,0},{2,3},{3,2},{4,5},{5,4},{6,7},{7,6},{8,9},{9,8},{10,11... | collective-permute-start | bytes 589832 | tf_op jit(solution)/shard_map/ppermute | solution.py:558
  85.4 10.2 %collective-permute-start.11 = (bf16[256,128]{1,0:T(8,128)(2,1)S(1)}, bf16[256,128]{1,0:T(8,128)(2,1)S(1)}, u32[]{:S(2)}, u32[]{:S(2)}) collective-permute-start(bf16[256,128]{1,0:T(8,128)(2,1)S(1)} %get-tuple-element.62), channel_id=1, source_target_pairs={{0,1},{1,0},{2,3},{3,2},{4,5},{5,4},{6,7},{7,6},{8,9},{9,8},{10,11... | collective-permute-start | bytes 196616 | tf_op jit(solution)/shard_map/ppermute | solution.py:558
  95.6 32.6 %all-to-all-start.2 = ((bf16[16,128,256]{2,1,0:T(8,128)(2,1)}), bf16[16,128,256]{2,1,0:T(8,128)(2,1)S(1)}, u32[]{:S(2)}, u32[]{:S(2)}) async-start(bf16[16,128,256]{2,1,0:T(8,128)(2,1)} %bitcast.6), calls=%async_computation.2 | async-start | bytes 2097152 | tf_op jit(solution)/shard_map/all_to_all | solution.py:688
  102.9 11.1 %collective-permute-start.12 = (bf16[352,128]{1,0:T(8,128)(2,1)S(1)}, bf16[352,128]{1,0:T(8,128)(2,1)S(1)}, u32[]{:S(2)}, u32[]{:S(2)}) collective-permute-start(bf16[352,128]{1,0:T(8,128)(2,1)S(1)} %get-tuple-element.66), channel_id=1, source_target_pairs={{0,12},{4,0},{8,4},{12,8},{1,13},{5,1},{9,5},{13,9},{2,14},{6,2},{... | collective-permute-start | bytes 270344 | tf_op jit(solution)/shard_map/ppermute | solution.py:562
  103.6 11.8 %collective-permute-start.13 = (bf16[352,128]{1,0:T(8,128)(2,1)S(1)}, bf16[352,128]{1,0:T(8,128)(2,1)S(1)}, u32[]{:S(2)}, u32[]{:S(2)}) collective-permute-start(bf16[352,128]{1,0:T(8,128)(2,1)S(1)} %get-tuple-element.67), channel_id=1, source_target_pairs={{0,8},{4,12},{8,0},{12,4},{1,9},{5,13},{9,1},{13,5},{2,10},{6,14},... | collective-permute-start | bytes 270344 | tf_op jit(solution)/shard_map/ppermute | solution.py:562
  107.5 9.7 %collective-permute-start.14 = (bf16[352,128]{1,0:T(8,128)(2,1)S(1)}, bf16[352,128]{1,0:T(8,128)(2,1)S(1)}, u32[]{:S(2)}, u32[]{:S(2)}) collective-permute-start(bf16[352,128]{1,0:T(8,128)(2,1)S(1)} %get-tuple-element.68), channel_id=1, source_target_pairs={{0,4},{4,8},{8,12},{12,0},{1,5},{5,9},{9,13},{13,1},{2,6},{6,10},{... | collective-permute-start | bytes 270344 | tf_op jit(solution)/shard_map/ppermute | solution.py:562
  113.1 15.1 %collective-permute-start.17 = (bf16[256,1024]{1,0:T(8,128)(2,1)S(1)}, bf16[256,1024]{1,0:T(8,128)(2,1)S(1)}, u32[]{:S(2)}, u32[]{:S(2)}) collective-permute-start(bf16[256,1024]{1,0:T(8,128)(2,1)S(1)} %get-tuple-element.79), channel_id=1, source_target_pairs={{0,2},{2,0},{1,3},{3,1},{4,6},{6,4},{5,7},{7,5},{8,10},{10,8},{9,1... | collective-permute-start | bytes 1572872 | tf_op jit(solution)/shard_map/ppermute | solution.py:558
  119.6 8.6 %collective-permute-start.15 = (bf16[4,96,128]{2,1,0:T(8,128)(2,1)S(1)}, bf16[4,96,128]{2,1,0:T(8,128)(2,1)S(1)}, u32[]{:S(2)}, u32[]{:S(2)}) collective-permute-start(bf16[4,96,128]{2,1,0:T(8,128)(2,1)S(1)} %get-tuple-element.71), channel_id=1, source_target_pairs={{16,0},{32,16},{48,32},{64,48},{80,64},{96,80},{112,96},{128,112},... | collective-permute-start | bytes 294920 | tf_op jit(solution)/shard_map/ppermute | solution.py:712

commit v5 on v4

--- a/solution.py
+++ b/solution.py
@@ -165,32 +165,12 @@
     return copies
 
 
-def grad_near_kernel(meta, up, up_c, w, order, acc, blocks, sems):
-    zl, c = meta[2], meta[3]
-    copies = weight_blocks(w, blocks, ((zl, c), (zl, 1 - c)), sems)
-    copies[0].wait()
-    total = nt(up[...], blocks[0])
-    copies[1].wait()
-    acc[...] = total + nt(up_c[...], blocks[1])
-
-
-def grad_far_kernel(
-    meta, up_z, up_zc, w, acc, picks, before, q0, q1, q2, q3, g, last, q_all, *rest
-):
-    sent, blocks, sems = rest[:3], rest[3], rest[4]
-    zh, zl, c = meta[1], meta[2], meta[3]
-    copies = weight_blocks(w, blocks, ((1 - zl, c), (1 - zl, 1 - c)), sems)
-    for d, ref in enumerate((q0, q1, q2, q3)):
-        q_all[d * TOK : (d + 1) * TOK, :] = ref[...]
-    copies[0].wait()
-    full = acc[...] + nt(up_z[...], blocks[0])
-    copies[1].wait()
-    full = (full + nt(up_zc[...], blocks[1])).astype(BF)
-    g[...] = full
+def bundle_kernel(meta, q0, picks, before, last, *sent):
+    zh = meta[1]
     last[...] = before[3]
     for d in (1, 2, 3):
         ref = sent[d - 1]
-        ref[:TOK, :] = full[:, :HEAD]
+        ref[:TOK, :] = q0[...]
 
         @pl.when(zh + d < GROUP)
         def _(d=d, ref=ref):
@@ -199,6 +179,25 @@
         @pl.when(zh + d >= GROUP)
         def _(d=d, ref=ref):
             ref[TOK:, :] = before[d - 1]
+
+
+def grad_near_kernel(meta, up, up_c, w, order, acc, far_w, near_w, sems, far_sems):
+    zl, c = meta[2], meta[3]
+    copies = weight_blocks(w, near_w, ((zl, c), (zl, 1 - c)), sems)
+    far_copies = weight_blocks(w, far_w, ((1 - zl, c), (1 - zl, 1 - c)), far_sems)
+    copies[0].wait()
+    total = nt(up[...], near_w[0])
+    copies[1].wait()
+    acc[...] = total + nt(up_c[...], near_w[1])
+    for copy in far_copies:
+        copy.wait()
+
+
+def grad_far_kernel(meta, up_z, up_zc, far_w, acc, g0, g):
+    full = acc[...] + nt(up_z[...], far_w[0])
+    full = (full + nt(up_zc[...], far_w[1])).astype(BF)
+    g0[...] = full[:, :HEAD]
+    g[...] = full
 
 
 def fold8(a, how):
@@ -236,35 +235,27 @@
 
 
 def forward_kernel(
-    meta, q_all, g0, g1, g2, g3, kva, k, v, ob, g_all, kv_all, near, s_ref, gs, kv0, sems
+    meta, q0, q1, q2, q3, g0, g1, g2, g3, kva, k, v, far, ob, q_all, g_all, kv_all,
+    s_ref, kv0, sems
 ):
     row, zh = meta[0], meta[1]
     first = pl.ds(0, HEAD)
-    brought = [
-        pltpu.make_async_copy(g0.at[:, first], gs.at[pl.ds(0, TOK)], sems.at[0]),
-        pltpu.make_async_copy(k.at[:, first], kv0.at[:, first], sems.at[1]),
+    kept = [
+        pltpu.make_async_copy(k.at[:, first], kv0.at[:, first], sems.at[0]),
         pltpu.make_async_copy(
-            v.at[:, first], kv0.at[:, pl.ds(HEAD, HEAD)], sems.at[2]
+            v.at[:, first], kv0.at[:, pl.ds(HEAD, HEAD)], sems.at[1]
         ),
+        pltpu.make_async_copy(kva, kv_all, sems.at[2]),
     ]
-    for copy in brought:
-        copy.start()
-    for d, ref in ((1, g1), (2, g2), (3, g3)):
-        gs[d * TOK : (d + 1) * TOK, :] = ref[:TOK, :]
-    kept = [pltpu.make_async_copy(kva, kv_all, sems.at[3])]
-    for d, ref in ((1, g1), (2, g2), (3, g3)):
-        kept.append(
-            pltpu.make_async_copy(
-                ref.at[pl.ds(TOK, FAR)], near.at[d - 1], sems.at[3 + d]
-            )
-        )
-    for copy in brought:
-        copy.wait()
-    kept.append(pltpu.make_async_copy(gs, g_all, sems.at[7]))
+    for d, (q, g) in enumerate(((q0, g0), (q1, g1), (q2, g2), (q3, g3))):
+        at = pl.ds(d * TOK, TOK)
+        source = q.at[pl.ds(0, TOK)]
+        kept.append(pltpu.make_async_copy(source, q_all.at[at], sems.at[3 + d]))
+        kept.append(pltpu.make_async_copy(g, g_all.at[at], sems.at[7 + d]))
     for copy in kept:
         copy.start()
-    q, g = q_all[...], gs[...]
-    q0, g0 = q[:TOK], g[:TOK]
+    q = jnp.concatenate([q0[...], q1[:TOK], q2[:TOK], q3[:TOK]], 0)
+    g = jnp.concatenate([g0[...], g1[...], g2[...], g3[...]], 0)
     masks = block_masks(row, zh)
     per = TILE // SUMM
     top = jnp.full((8, ALL), NEG, F32)
@@ -301,12 +292,14 @@
     dots = dots * inv
     out = out * inv
 
+    for copy in kept:
+        copy.wait()
     key, value = kv0[:, :HEAD], kv0[:, HEAD:]
-    s = jnp.where(causal_t(), nt(key, q0) * SCALE2, NEG)
+    s = jnp.where(causal_t(), nt(key, q0[...]) * SCALE2, NEG)
     own_top = jnp.max(s, axis=0, keepdims=True)
     e = jnp.exp2(s - own_top)
     own_sum = jnp.sum(e, axis=0, keepdims=True)
-    own_dot = jnp.sum(e * nt(value, g0), axis=0, keepdims=True)
+    own_dot = jnp.sum(e * nt(value, g0[...]), axis=0, keepdims=True)
     own_out = tn(value, e.astype(BF))
     own_log = own_top + jnp.log(own_sum) * LOG2E
     near = log_sum[:, :TOK]
@@ -333,17 +326,19 @@
             part = wa * part + wb * own_out
         to = lax.rem(zh - d + GROUP, GROUP)
         ob[to, :TOK, :] = halves(part).astype(BF)
-        ob[to, TOK:, :] = stats
-    for copy in kept:
-        copy.wait()
-
-
-def combine_kernel(meta, oa, o_sc, o, stat, o_own, o_beside):
-    o_beside[...] = o_sc[...]
+        ob[to, TOK : TOK + STAT, :] = stats
+        ob[to, TOK + STAT :, :] = far[(d + 3) % 4]
+
+
+def combine_kernel(meta, oa, order, o, stat, sent, here):
     zh = meta[1]
+    for u in range(4):
+        block = oa[lax.rem(zh + 1 + u, GROUP), TOK + STAT :, :]
+        sent[u] = block
+        here[u] = block
     got = []
     for f in range(GROUP):
-        rows = oa[lax.rem(zh - f + GROUP, GROUP), TOK:, :].astype(F32)
+        rows = oa[lax.rem(zh - f + GROUP, GROUP), TOK : TOK + STAT, :].astype(F32)
         got.append(
             jnp.concatenate([rows[8 * i : 8 * i + 8] for i in range(STAT // 8)], 1)
         )
@@ -373,44 +368,54 @@
                 ],
             )
             eye = ones_where(iota((HEAD, HEAD), 0) == iota((HEAD, HEAD), 1))
-            full = tn(full.astype(BF), eye).astype(BF)
-            o[...] = full
-            o_own[...] = full
+            o[...] = tn(full.astype(BF), eye).astype(BF)
     stat[2:8, :] = jnp.zeros((6, ALL), F32)
 
 
 def backward_kernel(
-    meta, q_all, g_all, kv_all, k, v, stat, far, dkv, dq1, dq2, dq3, own, dq0,
-    kva, kv0, sems
+    meta, q_all, g_all, kv_all, k, v, stat, dkv, dq1, dq2, dq3, own, dq0,
+    qs, gs, kva, kv0, mine, made, sems
 ):
     row, zh = meta[0], meta[1]
     first = pl.ds(0, HEAD)
-    half = KEYS // 2
+    steps = KEYS // TILE
     brought = [
-        pltpu.make_async_copy(
-            kv_all.at[pl.ds(i * half, half)], kva.at[pl.ds(i * half, half)], sems.at[i]
-        )
-        for i in range(2)
-    ]
-    brought += [
+        pltpu.make_async_copy(q_all, qs, sems.at[0]),
+        pltpu.make_async_copy(g_all, gs, sems.at[1]),
         pltpu.make_async_copy(k.at[:, first], kv0.at[:, first], sems.at[2]),
         pltpu.make_async_copy(
             v.at[:, first], kv0.at[:, pl.ds(HEAD, HEAD)], sems.at[3]
         ),
     ]
+    tiles, sent = [], []
+    for j in range(steps):
+        at = pl.ds(j * TILE, TILE)
+        tiles.append(pltpu.make_async_copy(kv_all.at[at], kva.at[at], sems.at[4 + j]))
+        sent.append(
+            pltpu.make_async_copy(made.at[at], dkv.at[at], sems.at[4 + steps + j])
+        )
+    sent.append(pltpu.make_async_copy(mine, own, sems.at[4 + 2 * steps]))
+    for copy in brought + tiles:
+        copy.start()
     for copy in brought:
-        copy.start()
-    brought[0].wait()
-    q, g = q_all[...], g_all[...]
+        copy.wait()
+    log_sum, dot = stat[0:1, :], stat[1:2, :]
+    q, g = qs[...], gs[...]
     q0, g0 = q[:TOK], g[:TOK]
+    key, value = kv0[:, :HEAD], kv0[:, HEAD:]
+    s = jnp.where(causal_t(), nt(key, q0) * SCALE2, NEG)
+    p = jnp.exp2(s - log_sum[:, :TOK])
+    mine[:, HEAD:] = nn(p.astype(BF), g0)
+    ds = (p * (nt(value, g0) - dot[:, :TOK])).astype(BF)
+    mine[:, :HEAD] = nn(ds, q0) * SCALE
+    dq_own = tn(key, ds)
+    sent[-1].start()
     masks = block_masks(row, zh)
-    log_sum, dot = stat[0:1, :], stat[1:2, :]
     per = TILE // SUMM
     dq = jnp.zeros((HEAD, ALL), F32)
-    for j in range(KEYS // TILE):
-        if j * TILE == half:
-            brought[1].wait()
+    for j in range(steps):
         at = slice(j * TILE, (j + 1) * TILE)
+        tiles[j].wait()
         key, value = kva[at, :HEAD], kva[at, HEAD:]
         s = nt(key, q)
         parts = []
@@ -420,33 +425,28 @@
                 jnp.exp2(s[i * SUMM : (i + 1) * SUMM] * SCALE2 - shift)
             )
         p = jnp.concatenate(parts, 0)
-        dkv[at, HEAD:] = nn(p.astype(BF), g).astype(BF)
+        made[at, HEAD:] = nn(p.astype(BF), g).astype(BF)
         ds = (p * (nt(value, g) - dot)).astype(BF)
-        dkv[at, :HEAD] = (nn(ds, q) * SCALE).astype(BF)
+        made[at, :HEAD] = (nn(ds, q) * SCALE).astype(BF)
+        sent[j].start()
         dq = dq + tn(key, ds)
-    for copy in brought[2:4]:
+    dq0[...] = (dq[:, :TOK] + dq_own) * SCALE
+    for d, ref in ((1, dq1), (2, dq2), (3, dq3)):
+        ref[...] = (halves(dq[:, d * TOK : (d + 1) * TOK]) * SCALE).astype(BF)
+    for copy in sent:
         copy.wait()
-    key, value = kv0[:, :HEAD], kv0[:, HEAD:]
-    s = jnp.where(causal_t(), nt(key, q0) * SCALE2, NEG)
-    p = jnp.exp2(s - log_sum[:, :TOK])
-    own[:, HEAD:] = nn(p.astype(BF), g0)
-    ds = (p * (nt(value, g0) - dot[:, :TOK])).astype(BF)
-    own[:, :HEAD] = nn(ds, q0) * SCALE
-    dq0[...] = (dq[:, :TOK] + tn(key, ds)) * SCALE
-    for d, ref in ((1, dq1), (2, dq2), (3, dq3)):
-        ref[:TOK, :] = (halves(dq[:, d * TOK : (d + 1) * TOK]) * SCALE).astype(BF)
-        ref[TOK:, :] = far[d - 1]
-
-
-def strided_kernel(meta, q, k, v, g, near, last, o, dq, dkv, far, o_own):
+
+
+def strided_kernel(meta, q, k, v, g, f1, f2, f3, last, o, dq, dkv, far, o_own):
     row, zh = meta[0], meta[1]
     slot = iota((TOK, 4 * REACH), 1) // REACH
     far_ok = (slot < zh) | (jnp.full((TOK, 4 * REACH), row, jnp.int32) > 0)
     near_ok = iota((TOK, TOK), 0) >= iota((TOK, TOK), 1)
 
     def far_rows(i):
-        at = slice(i * REACH, (i + 1) * REACH)
-        return jnp.concatenate([near[0, at], near[1, at], near[2, at], last[at]], 0)
+        at = slice(TOK + i * REACH, TOK + (i + 1) * REACH)
+        to = slice(i * REACH, (i + 1) * REACH)
+        return jnp.concatenate([f1[at], f2[at], f3[at], last[to]], 0)
 
     for h in range(3):
         at = slice((h + 1) * HEAD, (h + 2) * HEAD)
@@ -481,32 +481,38 @@
             far[u, (h + 3) * REACH : (h + 4) * REACH, :] = dvf[rows]
 
 
-def project_kernel(
-    meta, o_f, o_fc, o, o_c, w, w_c, send, keep, here_w, beside_w, here_s, beside_s
-):
+def project_blocks(meta, w, w_c, first, here_w, beside_w, here_s, beside_s):
     zl, c = meta[2], meta[3]
     places = ((1 - zl, c), (zl, c))
-    copies = weight_blocks(w, here_w, places, here_s)
-    beside_copies = weight_blocks(w_c, beside_w, places, beside_s)
-    here = jnp.concatenate([o_f[...], o[...]], 1)
-    beside = jnp.concatenate([o_fc[...], o_c[...]], 1)
+    rows = pl.ds(first, here_w.shape[1])
+    return (
+        weight_blocks(w.at[rows], here_w, places, here_s),
+        weight_blocks(w_c.at[rows], beside_w, places, beside_s),
+    )
+
+
+def project_strided_kernel(meta, o, o_c, w, w_c, acc, *space):
+    here_w, beside_w = space[:2]
+    copies, beside_copies = project_blocks(meta, w, w_c, HEAD, *space)
+    for i in range(2):
+        copies[i].wait()
+        total = nn(o[...], here_w[i])
+        beside_copies[i].wait()
+        acc[i] = total + nn(o_c[...], beside_w[i])
+
+
+def project_fixed_kernel(meta, o, o_c, acc, w, w_c, send, keep, got, sems, *space):
+    here_w, beside_w = space[:2]
+    before = [pltpu.make_async_copy(acc.at[i], got.at[i], sems.at[i]) for i in range(2)]
+    for copy in before:
+        copy.start()
+    copies, beside_copies = project_blocks(meta, w, w_c, 0, *space)
     for i, ref in ((0, send), (1, keep)):
         copies[i].wait()
-        total = nn(here, here_w[i])
         beside_copies[i].wait()
-        ref[...] = (total + nn(beside, beside_w[i])).astype(ref.dtype)
-
-
-def back_kernel(meta, dq0, b1, b2, b3, far, sent, here, dq):
-    for u, ref in ((0, b1), (1, b2), (2, b3)):
-        sent[u] = ref[TOK:, :]
-        here[u] = ref[TOK:, :]
-    sent[3] = far[3]
-    total = dq0[...]
-    for ref in (b1, b2, b3):
-        total = total + whole(ref[:TOK, :].astype(F32))
-    eye = ones_where(iota((HEAD, HEAD), 0) == iota((HEAD, HEAD), 1))
-    dq[...] = tn(total.astype(BF), eye).astype(BF)
+        total = nn(o[...], here_w[i]) + nn(o_c[...], beside_w[i])
+        before[i].wait()
+        ref[...] = (total + got[i]).astype(ref.dtype)
 
 
 def final_kernel(
@@ -515,7 +521,10 @@
     sidx,
     dkv,
     own,
-    dq,
+    dq0,
+    dq1,
+    dq2,
+    dq3,
     here,
     after,
     strided_dq,
@@ -534,7 +543,11 @@
     fixed = own[...] + nn(jnp.concatenate([pick] * ROWS, 1), dkv[...])
     kg[:, :HEAD] = fixed[:, :HEAD].astype(BF)
     vg[:, :HEAD] = fixed[:, HEAD:].astype(BF)
-    qg[:, :HEAD] = dq[...]
+    total = dq0[...]
+    for ref in (dq1, dq2, dq3):
+        total = total + whole(ref[...].astype(F32))
+    eye = ones_where(iota((HEAD, HEAD), 0) == iota((HEAD, HEAD), 1))
+    qg[:, :HEAD] = tn(total.astype(BF), eye).astype(BF)
     qg[:, HEAD:] = strided_dq[...]
     sel = stride_select(soff_t[...], shard)
     slots = []
@@ -592,55 +605,33 @@
         raw=[5],
     )
     before = lax.ppermute(picks, plane, [(i, i + 1) for i in range(ROWS - 1)])
+    last, *sent = call(
+        bundle_kernel,
+        [sds((FAR, HEAD))] + [sds((TOK + FAR, HEAD))] * 3,
+        [meta, q0, picks, before],
+        name="bundle_queries",
+    )
+    kvb = after(kvb, last)
+    kva = lax.all_to_all(kvb, plane, 0, 0, tiled=True).reshape(KEYS, 2 * HEAD)
+    qs = [q0] + [turn(sent[d - 1], d) for d in (1, 2, 3)]
     two_blocks = [pltpu.VMEM((2, width, quarter), BF), dma(2)]
-    (acc,) = call(
+    acc, far_w = call(
         grad_near_kernel,
-        [sds((TOK, width), F32)],
-        [meta, upstream, up_c, out_weight, picks],
-        two_blocks,
+        [sds((TOK, width), F32), sds((2, width, quarter))],
+        [meta, upstream, up_c, out_weight, last],
+        two_blocks + [dma(2)],
         name="attention_grad_near",
         fetch=[1],
         raw=[3],
-        store=[0],
-    )
-    kvb = after(after(kvb, before), acc)
-    kva = lax.all_to_all(kvb, plane, 0, 0, tiled=True).reshape(KEYS, 2 * HEAD)
-    up_zc = swap(after(up_z, picks), "c")
-    qs = [q0] + [turn(q0, d) for d in (1, 2, 3)]
-    g, last, q_all, *gs = call(
+    )
+    up_zc = swap(after(up_z, last), "c")
+    g0, g = call(
         grad_far_kernel,
-        [sds((TOK, width)), sds((FAR, HEAD)), sds((ALL, HEAD))]
-        + [sds((TOK + FAR, HEAD))] * 3,
-        [meta, up_z, up_zc, out_weight, acc, picks, before, *qs],
-        two_blocks,
+        [sds((TOK, HEAD)), sds((TOK, width))],
+        [meta, up_z, up_zc, far_w, acc],
         name="attention_grad_far",
-        fetch=[4],
-        raw=[3],
-        store=[0, 1, 2],
-    )
-    gs = [turn(gs[d - 1], d) for d in (1, 2, 3)]
-    ob, g_all, kv_all, near = call(
-        forward_kernel,
-        [
-            sds((GROUP, TOK + STAT, HEAD)),
-            sds((ALL, HEAD)),
-            sds((KEYS, 2 * HEAD)),
-            sds((3, FAR, HEAD)),
-        ],
-        [meta, q_all, g, *gs, kva, key_rows, value_rows],
-        [
-            pltpu.VMEM((KEYS, ALL), F32),
-            pltpu.VMEM((ALL, HEAD), BF),
-            pltpu.VMEM((TOK, 2 * HEAD), BF),
-            dma(8),
-        ],
-        name="fixed_forward",
-        fetch=[1],
-        raw=[2, 7, 8],
-        direct=[1, 2, 3],
-    )
-    weight_c = swap(after(out_weight, near), "c")
-    oa = lax.all_to_all(ob, "zh", 0, 0, tiled=True)
+    )
+    gs = [g0] + [turn(g0, d) for d in (1, 2, 3)]
     o_s, dq_s, dkv_s, far, o_own = call(
         strided_kernel,
         [
@@ -650,73 +641,95 @@
             block,
             sds((TOK, 3 * HEAD)),
         ],
-        [meta, queries, key_rows, value_rows, g, near, last],
+        [meta, queries, key_rows, value_rows, g, *qs[1:], last],
         name="strided_heads",
-        fetch=range(1, 7),
-        store=[1, 2, 3, 4],
+        fetch=range(1, 4),
+        store=[1, 2, 4],
     )
     o_sc = swap(o_s, "c")
-    o_f, stat, o_f_own, o_beside = call(
+    ob, q_all, g_all, kv_all = call(
+        forward_kernel,
+        [
+            sds((GROUP, TOK + STAT + FAR, HEAD)),
+            sds((ALL, HEAD)),
+            sds((ALL, HEAD)),
+            sds((KEYS, 2 * HEAD)),
+        ],
+        [meta, *qs, *gs, kva, key_rows, value_rows, far],
+        [
+            pltpu.VMEM((KEYS, ALL), F32),
+            pltpu.VMEM((TOK, 2 * HEAD), BF),
+            dma(11),
+        ],
+        name="fixed_forward",
+        raw=[10, 11],
+        direct=[1, 2, 3],
+    )
+    weight_c = swap(after(out_weight, q_all), "c")
+    oa = lax.all_to_all(ob, "zh", 0, 0, tiled=True)
+    (acc_out,) = call(
+        project_strided_kernel,
+        [sds((2, TOK, quarter), F32)],
+        [meta, o_own, o_sc, out_weight, weight_c],
+        [pltpu.VMEM((2, 3 * HEAD, quarter), BF)] * 2 + [dma(2)] * 2,
+        name="project_strided",
+        fetch=[1],
+        raw=[3, 4],
+        store=[0],
+    )
+    o_f, stat, sent, here = call(
         combine_kernel,
-        [
-            sds((TOK, HEAD)),
-            sds((8, ALL), F32),
-            sds((TOK, HEAD)),
-            sds((TOK, 3 * HEAD)),
-        ],
-        [meta, oa, o_sc],
+        [sds((TOK, HEAD)), sds((8, ALL), F32), block, block],
+        [meta, oa, acc_out],
         name="combine",
-        store=[2, 3],
+        raw=[2],
+        store=[3],
     )
     o_fc = swap(o_f, "c")
+    back = lax.ppermute(sent, plane, [(i + 1, i) for i in range(ROWS - 1)])
     dkv, *dqs, own, dq0 = call(
         backward_kernel,
         [sds((KEYS, 2 * HEAD))]
-        + [sds((TOK + FAR, HEAD))] * 3
+        + [sds((TOK, HEAD))] * 3
         + [sds((TOK, 2 * HEAD), F32), sds((HEAD, TOK), F32)],
-        [meta, q_all, g_all, kv_all, key_rows, value_rows, stat, far],
+        [meta, q_all, g_all, kv_all, key_rows, value_rows, stat],
         [
+            pltpu.VMEM((ALL, HEAD), BF),
+            pltpu.VMEM((ALL, HEAD), BF),
             pltpu.VMEM((KEYS, 2 * HEAD), BF),
             pltpu.VMEM((TOK, 2 * HEAD), BF),
-            dma(4),
+            pltpu.VMEM((TOK, 2 * HEAD), F32),
+            pltpu.VMEM((KEYS, 2 * HEAD), BF),
+            dma(5 + 2 * (KEYS // TILE)),
         ],
         name="fixed_backward",
-        fetch=[1, 2, 7],
+        raw=range(1, 6),
+        store=[5],
+        direct=[0, 4],
+    )
+    send, keep = call(
+        project_fixed_kernel,
+        [sds((TOK, quarter))] * 2,
+        [meta, o_f, o_fc, acc_out, out_weight, weight_c],
+        [pltpu.VMEM((2, TOK, quarter), F32), dma(2)]
+        + [pltpu.VMEM((2, HEAD, quarter), BF)] * 2
+        + [dma(2)] * 2,
+        name="project_fixed",
         raw=[3, 4, 5],
-        store=[4, 5],
-    )
+        store=[1],
+    )
+    over = swap(send, "zl")
     dkva = lax.all_to_all(
         after(dkv, o_fc).reshape(ROWS, SUMM, 2 * HEAD), plane, 0, 0, tiled=True
     ).reshape(KEYS, 2 * HEAD)
-    send, keep = call(
-        project_kernel,
-        [sds((TOK, quarter))] * 2,
-        [meta, o_f_own, o_fc, o_own, o_beside, out_weight, weight_c],
-        two_blocks[:1] * 2 + two_blocks[1:] * 2,
-        name="project",
-        fetch=[1, 3, 4],
-        raw=[5, 6],
-        store=[1],
-    )
-    over = swap(send, "zl")
     dqs = [turn(dqs[d - 1], -d) for d in (1, 2, 3)]
-    sent, here, dq_f = call(
-        back_kernel,
-        [block, sds((3, FAR, HEAD)), sds((TOK, HEAD))],
-        [meta, dq0, *dqs, far],
-        name="bundle_back",
-        fetch=[1, 5],
-        store=[1, 2],
-        flops=5 * 10**9,
-    )
-    back = lax.ppermute(sent, plane, [(i + 1, i) for i in range(ROWS - 1)])
     return call(
         final_kernel,
         [sds((TOK, quarter))] + [sds((TOK, width))] * 3,
-        [meta, soff_t, summary_index, dkva, own, dq_f, here, back, dq_s, dkv_s]
+        [meta, soff_t, summary_index, dkva, own, dq0, *dqs, here, back, dq_s, dkv_s]
         + [keep, over],
         name="join_results",
-        fetch=[1, 2, 4, 5, 6, 8, 9, 10],
+        fetch=[1, 2, 4, 5, 9, 11, 12, 13],
     )
 
 

time: 133 us -> 123 us (0.925)
  waiting for transfers between devices: 31.8 us -> 26 us
  Pallas kernels: 48.8 us -> 45.7 us
  starting transfers between devices: 50.5 us -> 49 us
    ppermute x1, waiting for transfers between devices: 5.85 us -> 0.01 us  [shards(): back = lax.ppermute(sent, plane, [(i + 1, i) for i in range(ROWS - 1)])]
    pallas_call x10 -> x11, Pallas kernels: 48.8 us -> 45.7 us  [call(): pl.pallas_call(body, out_shape=tuple((pltpu.HBM(s.shape, s.dtype) if i in...]
    ppermute x9, waiting for transfers between devices: 15.9 us -> 12.8 us  [turn(): return lax.ppermute(a, 'zh', [(i, (i + by) % GROUP) for i in range(GROUP)])]
    ppermute x9, starting transfers between devices: 21.9 us -> 19.7 us  [turn(): return lax.ppermute(a, 'zh', [(i, (i + by) % GROUP) for i in range(GROUP)])]
    all_to_all x1, waiting for transfers between devices: 5.15 us -> 7.3 us  [shards(): oa = lax.all_to_all(ob, 'zh', 0, 0, tiled=True)]
  transfers between devices with their start and end apart: 21 -> 21, of which waited for: 11 -> 8; matrix products, arithmetic and copies ran while one was open for 0% -> 0% of each run, Pallas kernels for 28% -> 28%
where the time goes in v5:
time: 123 us; the launch traced here: 122 us
  starting transfers between devices  49 us (40%)
  Pallas kernels  45.7 us (37%)
  waiting for transfers between devices  26 us (21%)
    pallas_call x11, Pallas kernels, call(): pl.pallas_call(body, out_shape=tuple((pltpu.HBM(s.shape, s.dtype) if i in...  45.7 us
    ppermute x9, starting transfers between devices, turn(): return lax.ppermute(a, 'zh', [(i, (i + by) % GROUP) for i in range(GROUP)])  19.7 us
    ppermute x9, waiting for transfers between devices, turn(): return lax.ppermute(a, 'zh', [(i, (i + by) % GROUP) for i in range(GROUP)])  12.8 us
    all_to_all x1, waiting for transfers between devices, shards(): oa = lax.all_to_all(ob, 'zh', 0, 0, tiled=True)  7.3 us
    all_to_all x1, starting transfers between devices, shards(): lax.all_to_all(after(dkv, o_fc).reshape(ROWS, SUMM, 2 * HEAD), plane, 0,...  7.24 us
    all_to_all x1, starting transfers between devices, shards(): kva = lax.all_to_all(kvb, plane, 0, 0, tiled=True).reshape(KEYS, 2 * HEAD)  7.18 us
    all_to_all x1, starting transfers between devices, shards(): oa = lax.all_to_all(ob, 'zh', 0, 0, tiled=True)  4.93 us
    ppermute x7, starting transfers between devices, swap(): return lax.ppermute(a, axis, [(0, 1), (1, 0)])  4.17 us
  transfers between devices with their start and end apart: 21, of which 8 were waited for; matrix products, arithmetic and copies ran while one was open for 0% of the time, Pallas kernels for 28%

profile of v5, /device:TPU:24, one launch (start us, length us, event | category | flops | bytes accessed | tf_op | source)
XLA Modules:
  0.0 121.7 jit_solution(9522786178919048459)
XLA Ops:
  0.6 2.0 %collective-permute-start.4 = (bf16[256,1024]{1,0:T(8,128)(2,1)}, bf16[256,1024]{1,0:T(8,128)(2,1)S(1)}, u32[]{:S(2)}, u32[]{:S(2)}) collective-permute-start(bf16[256,1024]{1,0:T(8,128)(2,1)} %refs_1_.2), channel_id=1, source_target_pairs={{0,2},{2,0},{1,3},{3,1},{4,6},{6,4},{5,7},{7,5},{8,10},{10,8},{9,1... | collective-permute-start | bytes 1572872 | tf_op jit(solution)/shard_map/ppermute | solution.py:571
  2.7 3.5 %pick_rows.1 = (bf16[16,128,256]{2,1,0:T(8,128)(2,1)}, bf16[256,128]{1,0:T(8,128)(2,1)S(1)}, bf16[4,96,128]{2,1,0:T(8,128)(2,1)S(1)}) custom-call(s32[4]{0:T(128)S(1)} %pad_add_fusion.refs_0_, s32[4,64]{1,0:T(4,128)} %bitcast.11, s32[1,128]{1,0:T(1,128)} %refs_2_.5, bf16[256,512]{1,0:T(8,128)(2,1)} %refs_4_.4, bf16[256,512]{1,0:T(8,128)(2,1)} %refs_5_.3, ...), custom_call_target="tpu_custom_call" | custom-call | flops 1 | bytes 1 | tf_op jit(solution)/shard_map/pick_rows/pallas_call | solution.py:111
  6.2 3.1 %collective-permute-start = (bf16[4,96,128]{2,1,0:T(8,128)(2,1)S(1)}, bf16[4,96,128]{2,1,0:T(8,128)(2,1)S(1)}, u32[]{:S(2)}, u32[]{:S(2)}) collective-permute-start(bf16[4,96,128]{2,1,0:T(8,128)(2,1)S(1)} %get-tuple-element.41.refs_2_), channel_id=1, source_target_pairs={{0,16},{16,32},{32,48},{48,64},{64,80},{80,96},{96,112},{112,128},... | collective-permute-start | bytes 294920 | tf_op jit(solution)/shard_map/ppermute | solution.py:607
  9.3 3.4 %collective-permute-done.refs_3_ = bf16[4,96,128]{2,1,0:T(8,128)(2,1)S(1)} collective-permute-done((bf16[4,96,128]{2,1,0:T(8,128)(2,1)S(1)}, bf16[4,96,128]{2,1,0:T(8,128)(2,1)S(1)}, u32[]{:S(2)}, u32[]{:S(2)}) %collective-permute-start) | collective-permute-done | bytes 98336 | tf_op jit(solution)/shard_map/ppermute | solution.py:607
  12.7 0.6 bundle_queries.1
  13.3 7.2 %all-to-all-start = ((bf16[16,128,256]{2,1,0:T(8,128)(2,1)}), bf16[16,128,256]{2,1,0:T(8,128)(2,1)S(1)}, u32[]{:S(2)}, u32[]{:S(2)}) async-start(bf16[16,128,256]{2,1,0:T(8,128)(2,1)} %get-tuple-element.51), calls=%async_computation | async-start | bytes 2097152 | tf_op jit(solution)/shard_map/all_to_all | solution.py:615
  21.0 3.3 %collective-permute-start.1 = (bf16[352,128]{1,0:T(8,128)(2,1)S(1)}, bf16[352,128]{1,0:T(8,128)(2,1)S(1)}, u32[]{:S(2)}, u32[]{:S(2)}) collective-permute-start(bf16[352,128]{1,0:T(8,128)(2,1)S(1)} %get-tuple-element.42), channel_id=1, source_target_pairs={{0,4},{4,8},{8,12},{12,0},{1,5},{5,9},{9,13},{13,1},{2,6},{6,10},{... | collective-permute-start | bytes 270344 | tf_op jit(solution)/shard_map/ppermute | solution.py:575
  24.3 4.5 %collective-permute-start.2 = (bf16[352,128]{1,0:T(8,128)(2,1)S(1)}, bf16[352,128]{1,0:T(8,128)(2,1)S(1)}, u32[]{:S(2)}, u32[]{:S(2)}) collective-permute-start(bf16[352,128]{1,0:T(8,128)(2,1)S(1)} %get-tuple-element.43), channel_id=1, source_target_pairs={{0,8},{4,12},{8,0},{12,4},{1,9},{5,13},{9,1},{13,5},{2,10},{6,14},... | collective-permute-start | bytes 270344 | tf_op jit(solution)/shard_map/ppermute | solution.py:575
  28.7 2.7 %collective-permute-start.3 = (bf16[352,128]{1,0:T(8,128)(2,1)S(1)}, bf16[352,128]{1,0:T(8,128)(2,1)S(1)}, u32[]{:S(2)}, u32[]{:S(2)}) collective-permute-start(bf16[352,128]{1,0:T(8,128)(2,1)S(1)} %get-tuple-element.44), channel_id=1, source_target_pairs={{0,12},{4,0},{8,4},{12,8},{1,13},{5,1},{9,5},{13,9},{2,14},{6,2},{... | collective-permute-start | bytes 270344 | tf_op jit(solution)/shard_map/ppermute | solution.py:575
  31.4 4.2 %attention_grad_near.1 = (f32[256,512]{1,0:T(8,128)S(1)}, bf16[2,512,1024]{2,1,0:T(8,128)(2,1)S(1)}) custom-call(s32[4]{0:T(128)S(1)} %pad_add_fusion.refs_0_, bf16[256,1024]{1,0:T(8,128)(2,1)} %refs_1_.2, bf16[256,1024]{1,0:T(8,128)(2,1)S(1)} %collective-permute-done.6.refs_2_, bf16[512,4096]{1,0:T(8,128)(2,1)} %refs_4_.5, ...), custom_call_target="tpu_custom_call" | custom-call | flops 1 | bytes 1 | tf_op jit(solution)/shard_map/attention_grad_near/pallas_call | solution.py:111
  35.7 1.3 %attention_grad_far.1 = (bf16[256,128]{1,0:T(8,128)(2,1)S(1)}, bf16[256,512]{1,0:T(8,128)(2,1)S(1)}) custom-call(s32[4]{0:T(128)S(1)} %pad_add_fusion.refs_0_, bf16[256,1024]{1,0:T(8,128)(2,1)S(1)} %collective-permute-done.4.refs_1_, bf16[256,1024]{1,0:T(8,128)(2,1)S(1)} %collective-permute-done.5.refs_2_, ...), custom_call_target="tpu_custom_call" | custom-call | flops 1 | bytes 1 | tf_op jit(solution)/shard_map/attention_grad_far/pallas_call | solution.py:111
  37.3 2.1 %collective-permute-start.8 = (bf16[256,128]{1,0:T(8,128)(2,1)S(1)}, bf16[256,128]{1,0:T(8,128)(2,1)S(1)}, u32[]{:S(2)}, u32[]{:S(2)}) collective-permute-start(bf16[256,128]{1,0:T(8,128)(2,1)S(1)} %get-tuple-element.49.refs_5_), channel_id=1, source_target_pairs={{0,8},{4,12},{8,0},{12,4},{1,9},{5,13},{9,1},{13,5},{2,10},{6,14},... | collective-permute-start | bytes 196616 | tf_op jit(solution)/shard_map/ppermute | solution.py:575
  39.4 2.7 %collective-permute-start.9 = (bf16[256,128]{1,0:T(8,128)(2,1)S(1)}, bf16[256,128]{1,0:T(8,128)(2,1)S(1)}, u32[]{:S(2)}, u32[]{:S(2)}) collective-permute-start(bf16[256,128]{1,0:T(8,128)(2,1)S(1)} %get-tuple-element.49.refs_5_), channel_id=1, source_target_pairs={{0,12},{4,0},{8,4},{12,8},{1,13},{5,1},{9,5},{13,9},{2,14},{6,2},{... | collective-permute-start | bytes 196616 | tf_op jit(solution)/shard_map/ppermute | solution.py:575
  42.1 5.2 %strided_heads.1 = (bf16[256,384]{1,0:T(8,128)(2,1)S(1)}, bf16[256,384]{1,0:T(8,128)(2,1)}, f32[256,768]{1,0:T(8,128)}, bf16[4,96,128]{2,1,0:T(8,128)(2,1)S(1)}, bf16[256,384]{1,0:T(8,128)(2,1)}) custom-call(s32[4]{0:T(128)S(1)} %pad_add_fusion.refs_0_, bf16[256,512]{1,0:T(8,128)(2,1)} %refs_1_.3, bf16[256,512]{1,0:T(8,128)(2,1)} %refs_4_.4, ...), custom_call_target="tpu_custom_call" | custom-call | flops 1 | bytes 1 | tf_op jit(solution)/shard_map/strided_heads/pallas_call | solution.py:111
  47.3 1.4 %collective-permute-done.9.refs_8_ = bf16[256,128]{1,0:T(8,128)(2,1)S(1)} collective-permute-done((bf16[256,128]{1,0:T(8,128)(2,1)S(1)}, bf16[256,128]{1,0:T(8,128)(2,1)S(1)}, u32[]{:S(2)}, u32[]{:S(2)}) %collective-permute-start.9) | collective-permute-done | bytes 65568 | tf_op jit(solution)/shard_map/ppermute | solution.py:575
  48.7 6.8 %fixed_forward.1 = (bf16[4,416,128]{2,1,0:T(8,128)(2,1)}, bf16[1024,128]{1,0:T(8,128)(2,1)}, bf16[1024,128]{1,0:T(8,128)(2,1)}, bf16[2048,256]{1,0:T(8,128)(2,1)}) custom-call(s32[4]{0:T(128)S(1)} %pad_add_fusion.refs_0_, bf16[256,128]{1,0:T(8,128)(2,1)S(1)} %get-tuple-element.40.refs_1_, bf16[352,128]{1,0:T(8,128)(2,1)S(1)} %collective-permute-done.1.refs_5_.refs_2_, ...), custom_call_target="tpu_custom_call" | custom-call | flops 1 | bytes 1 | tf_op jit(solution)/shard_map/fixed_forward/pallas_call | solution.py:111
  55.6 4.9 %all-to-all-start.1 = ((bf16[4,416,128]{2,1,0:T(8,128)(2,1)}), bf16[4,416,128]{2,1,0:T(8,128)(2,1)S(1)}, u32[]{:S(2)}, u32[]{:S(2)}) async-start(bf16[4,416,128]{2,1,0:T(8,128)(2,1)} %get-tuple-element.57), calls=%async_computation.1 | async-start | bytes 851968 | tf_op jit(solution)/shard_map/all_to_all | solution.py:669
  60.8 2.3 %collective-permute-done.10.refs_2_ = bf16[256,384]{1,0:T(8,128)(2,1)S(1)} collective-permute-done((bf16[256,384]{1,0:T(8,128)(2,1)S(1)}, bf16[256,384]{1,0:T(8,128)(2,1)S(1)}, u32[]{:S(2)}, u32[]{:S(2)}) %collective-permute-start.10) | collective-permute-done | bytes 196640 | tf_op jit(solution)/shard_map/ppermute | solution.py:571
  63.1 5.8 %project_strided.1.refs_2_.refs_3_ = f32[2,256,1024]{2,1,0:T(8,128)} custom-call(s32[4]{0:T(128)S(1)} %pad_add_fusion.refs_0_, bf16[256,384]{1,0:T(8,128)(2,1)} %get-tuple-element.58.refs_1_, bf16[256,384]{1,0:T(8,128)(2,1)S(1)} %collective-permute-done.10.refs_2_, bf16[512,4096]{1,0:T(8,128)(2,1)} %refs_4_.5, ...), custom_call_target="tpu_custom_call" | custom-call | flops 1 | bytes 1 | tf_op jit(solution)/shard_map/project_strided/pallas_call | solution.py:111
  68.9 7.3 %all-to-all-done.1.refs_1_ = bf16[4,416,128]{2,1,0:T(8,128)(2,1)S(1)} async-done(((bf16[4,416,128]{2,1,0:T(8,128)(2,1)}), bf16[4,416,128]{2,1,0:T(8,128)(2,1)S(1)}, u32[]{:S(2)}, u32[]{:S(2)}) %all-to-all-start.1) | async-done | bytes 426016 | tf_op jit(solution)/shard_map/all_to_all | solution.py:669
  76.2 1.4 %combine.1 = (bf16[256,128]{1,0:T(8,128)(2,1)S(1)}, f32[8,1024]{1,0:T(8,128)S(1)}, bf16[4,96,128]{2,1,0:T(8,128)(2,1)S(1)}, bf16[4,96,128]{2,1,0:T(8,128)(2,1)}) custom-call(s32[4]{0:T(128)S(1)} %pad_add_fusion.refs_0_, bf16[4,416,128]{2,1,0:T(8,128)(2,1)S(1)} %all-to-all-done.1.refs_1_, f32[2,256,1024]{2,1,0:T(8,128)} %project_strided.1.refs_2_.refs_3_), custom_call_target="tpu_custom_call" | custom-call | flops 1 | bytes 1 | tf_op jit(solution)/shard_map/combine/pallas_call | solution.py:111
  77.9 9.4 %fixed_backward.1 = (bf16[2048,256]{1,0:T(8,128)(2,1)}, bf16[256,128]{1,0:T(8,128)(2,1)S(1)}, bf16[256,128]{1,0:T(8,128)(2,1)S(1)}, bf16[256,128]{1,0:T(8,128)(2...) custom-call(s32[4]{0:T(128)S(1)} %pad_add_fusion.refs_0_, bf16[1024,128]{1,0:T(8,128)(2,1)} %get-tuple-element.54.refs_1_, ...), custom_call_target="tpu_custom_call" | custom-call | flops 1 | bytes 1 | tf_op jit(solution)/shard_map/fixed_backward/pallas_call | solution.py:111
  87.3 7.2 %all-to-all-start.2 = ((bf16[16,128,256]{2,1,0:T(8,128)(2,1)}), bf16[16,128,256]{2,1,0:T(8,128)(2,1)S(1)}, u32[]{:S(2)}, u32[]{:S(2)}) async-start(bf16[16,128,256]{2,1,0:T(8,128)(2,1)} %bitcast.10), calls=%async_computation.2 | async-start | bytes 2097152 | tf_op jit(solution)/shard_map/all_to_all | solution.py:722
  94.6 3.8 %project_fixed.1 = (bf16[256,1024]{1,0:T(8,128)(2,1)S(1)}, bf16[256,1024]{1,0:T(8,128)(2,1)}) custom-call(s32[4]{0:T(128)S(1)} %pad_add_fusion.refs_0_, bf16[256,128]{1,0:T(8,128)(2,1)S(1)} %get-tuple-element.63.refs_1_, bf16[256,128]{1,0:T(8,128)(2,1)S(1)} %collective-permute-done.12.refs_2_, f32[2,256,1024]{2,1,0:T(8,128)} %project_strided.1.refs_2_.refs_3_, ...), custom_call_target="tpu_custom_call" | custom-call | flops 1 | bytes 1 | tf_op jit(solution)/shard_map/project_fixed/pallas_call | solution.py:111
  98.3 1.1 collective-permute-start.17
  99.4 2.8 %collective-permute-start.16 = (bf16[4,96,128]{2,1,0:T(8,128)(2,1)S(1)}, bf16[4,96,128]{2,1,0:T(8,128)(2,1)S(1)}, u32[]{:S(2)}, u32[]{:S(2)}) collective-permute-start(bf16[4,96,128]{2,1,0:T(8,128)(2,1)S(1)} %get-tuple-element.71), channel_id=1, source_target_pairs={{16,0},{32,16},{48,32},{64,48},{80,64},{96,80},{112,96},{128,112},... | collective-permute-start | bytes 294920 | tf_op jit(solution)/shard_map/ppermute | solution.py:689
  102.2 1.1 collective-permute-start.13
  103.2 3.1 %collective-permute-start.14 = (bf16[256,128]{1,0:T(8,128)(2,1)S(1)}, bf16[256,128]{1,0:T(8,128)(2,1)S(1)}, u32[]{:S(2)}, u32[]{:S(2)}) collective-permute-start(bf16[256,128]{1,0:T(8,128)(2,1)S(1)} %get-tuple-element.68), channel_id=1, source_target_pairs={{0,8},{4,12},{8,0},{12,4},{1,9},{5,13},{9,1},{13,5},{2,10},{6,14},... | collective-permute-start | bytes 196616 | tf_op jit(solution)/shard_map/ppermute | solution.py:575
  106.3 1.2 collective-permute-done.13.refs_6_
  107.5 8.8 %collective-permute-done.14.refs_7_ = bf16[256,128]{1,0:T(8,128)(2,1)S(1)} collective-permute-done((bf16[256,128]{1,0:T(8,128)(2,1)S(1)}, bf16[256,128]{1,0:T(8,128)(2,1)S(1)}, u32[]{:S(2)}, u32[]{:S(2)}) %collective-permute-start.14) | collective-permute-done | bytes 65568 | tf_op jit(solution)/shard_map/ppermute | solution.py:575
  116.4 1.4 %collective-permute-done.15.refs_8_ = bf16[256,128]{1,0:T(8,128)(2,1)S(1)} collective-permute-done((bf16[256,128]{1,0:T(8,128)(2,1)S(1)}, bf16[256,128]{1,0:T(8,128)(2,1)S(1)}, u32[]{:S(2)}, u32[]{:S(2)}) %collective-permute-start.15) | collective-permute-done | bytes 65568 | tf_op jit(solution)/shard_map/ppermute | solution.py:575
  117.8 3.8 %join_results.1 = (bf16[256,1024]{1,0:T(8,128)(2,1)}, bf16[256,512]{1,0:T(8,128)(2,1)}, bf16[256,512]{1,0:T(8,128)(2,1)}, bf16[256,512]{1,0:T(8,128)(2,1)}) custom-call(s32[4]{0:T(128)S(1)} %pad_add_fusion.refs_0_, s32[4,64]{1,0:T(4,128)} %bitcast.12, s32[1,128]{1,0:T(1,128)} %refs_2_.5, bf16[2048,256]{1,0:T(8,128)(2,1)S(1)} %bitcast.9, ...), custom_call_target="tpu_custom_call" | custom-call | flops 1 | bytes 1 | tf_op jit(solution)/shard_map/join_results/pallas_call | solution.py:111
  (22 shorter events, 1.6 us)
Async XLA Ops:
  0.6 19.9 %collective-permute-start.4 = (bf16[256,1024]{1,0:T(8,128)(2,1)}, bf16[256,1024]{1,0:T(8,128)(2,1)S(1)}, u32[]{:S(2)}, u32[]{:S(2)}) collective-permute-start(bf16[256,1024]{1,0:T(8,128)(2,1)} %refs_1_.2), channel_id=1, source_target_pairs={{0,2},{2,0},{1,3},{3,1},{4,6},{6,4},{5,7},{7,5},{8,10},{10,8},{9,1... | collective-permute-start | bytes 1572872 | tf_op jit(solution)/shard_map/ppermute | solution.py:571
  6.2 6.5 %collective-permute-start = (bf16[4,96,128]{2,1,0:T(8,128)(2,1)S(1)}, bf16[4,96,128]{2,1,0:T(8,128)(2,1)S(1)}, u32[]{:S(2)}, u32[]{:S(2)}) collective-permute-start(bf16[4,96,128]{2,1,0:T(8,128)(2,1)S(1)} %get-tuple-element.41.refs_2_), channel_id=1, source_target_pairs={{0,16},{16,32},{32,48},{48,64},{64,80},{80,96},{96,112},{112,128},... | collective-permute-start | bytes 294920 | tf_op jit(solution)/shard_map/ppermute | solution.py:607
  13.3 34.0 %all-to-all-start = ((bf16[16,128,256]{2,1,0:T(8,128)(2,1)}), bf16[16,128,256]{2,1,0:T(8,128)(2,1)S(1)}, u32[]{:S(2)}, u32[]{:S(2)}) async-start(bf16[16,128,256]{2,1,0:T(8,128)(2,1)} %get-tuple-element.51), calls=%async_computation | async-start | bytes 2097152 | tf_op jit(solution)/shard_map/all_to_all | solution.py:615
  20.5 10.9 %collective-permute-start.6 = (bf16[256,1024]{1,0:T(8,128)(2,1)}, bf16[256,1024]{1,0:T(8,128)(2,1)S(1)}, u32[]{:S(2)}, u32[]{:S(2)}) collective-permute-start(bf16[256,1024]{1,0:T(8,128)(2,1)} %refs_1_.2), channel_id=1, source_target_pairs={{0,1},{1,0},{2,3},{3,2},{4,5},{5,4},{6,7},{7,6},{8,9},{9,8},{10,11... | collective-permute-start | bytes 1572872 | tf_op jit(solution)/shard_map/ppermute | solution.py:571
  20.5 15.2 %collective-permute-start.5 = (bf16[256,1024]{1,0:T(8,128)(2,1)S(1)}, bf16[256,1024]{1,0:T(8,128)(2,1)S(1)}, u32[]{:S(2)}, u32[]{:S(2)}) collective-permute-start(bf16[256,1024]{1,0:T(8,128)(2,1)S(1)} %collective-permute-done.4.refs_1_), channel_id=1, source_target_pairs={{0,1},{1,0},{2,3},{3,2},{4,5},{5,4},{6,7},{7,6},{8,9},{9,8},{10,11... | collective-permute-start | bytes 1572872 | tf_op jit(solution)/shard_map/ppermute | solution.py:571
  21.0 18.4 %collective-permute-start.1 = (bf16[352,128]{1,0:T(8,128)(2,1)S(1)}, bf16[352,128]{1,0:T(8,128)(2,1)S(1)}, u32[]{:S(2)}, u32[]{:S(2)}) collective-permute-start(bf16[352,128]{1,0:T(8,128)(2,1)S(1)} %get-tuple-element.42), channel_id=1, source_target_pairs={{0,4},{4,8},{8,12},{12,0},{1,5},{5,9},{9,13},{13,1},{2,6},{6,10},{... | collective-permute-start | bytes 270344 | tf_op jit(solution)/shard_map/ppermute | solution.py:575
  24.3 17.8 %collective-permute-start.2 = (bf16[352,128]{1,0:T(8,128)(2,1)S(1)}, bf16[352,128]{1,0:T(8,128)(2,1)S(1)}, u32[]{:S(2)}, u32[]{:S(2)}) collective-permute-start(bf16[352,128]{1,0:T(8,128)(2,1)S(1)} %get-tuple-element.43), channel_id=1, source_target_pairs={{0,8},{4,12},{8,0},{12,4},{1,9},{5,13},{9,1},{13,5},{2,10},{6,14},... | collective-permute-start | bytes 270344 | tf_op jit(solution)/shard_map/ppermute | solution.py:575
  28.7 13.3 %collective-permute-start.3 = (bf16[352,128]{1,0:T(8,128)(2,1)S(1)}, bf16[352,128]{1,0:T(8,128)(2,1)S(1)}, u32[]{:S(2)}, u32[]{:S(2)}) collective-permute-start(bf16[352,128]{1,0:T(8,128)(2,1)S(1)} %get-tuple-element.44), channel_id=1, source_target_pairs={{0,12},{4,0},{8,4},{12,8},{1,13},{5,1},{9,5},{13,9},{2,14},{6,2},{... | collective-permute-start | bytes 270344 | tf_op jit(solution)/shard_map/ppermute | solution.py:575
  37.0 10.3 %collective-permute-start.7 = (bf16[256,128]{1,0:T(8,128)(2,1)S(1)}, bf16[256,128]{1,0:T(8,128)(2,1)S(1)}, u32[]{:S(2)}, u32[]{:S(2)}) collective-permute-start(bf16[256,128]{1,0:T(8,128)(2,1)S(1)} %get-tuple-element.49.refs_5_), channel_id=1, source_target_pairs={{0,4},{4,8},{8,12},{12,0},{1,5},{5,9},{9,13},{13,1},{2,6},{6,10},{... | collective-permute-start | bytes 196616 | tf_op jit(solution)/shard_map/ppermute | solution.py:575
  37.3 10.0 %collective-permute-start.8 = (bf16[256,128]{1,0:T(8,128)(2,1)S(1)}, bf16[256,128]{1,0:T(8,128)(2,1)S(1)}, u32[]{:S(2)}, u32[]{:S(2)}) collective-permute-start(bf16[256,128]{1,0:T(8,128)(2,1)S(1)} %get-tuple-element.49.refs_5_), channel_id=1, source_target_pairs={{0,8},{4,12},{8,0},{12,4},{1,9},{5,13},{9,1},{13,5},{2,10},{6,14},... | collective-permute-start | bytes 196616 | tf_op jit(solution)/shard_map/ppermute | solution.py:575
  39.4 9.3 %collective-permute-start.9 = (bf16[256,128]{1,0:T(8,128)(2,1)S(1)}, bf16[256,128]{1,0:T(8,128)(2,1)S(1)}, u32[]{:S(2)}, u32[]{:S(2)}) collective-permute-start(bf16[256,128]{1,0:T(8,128)(2,1)S(1)} %get-tuple-element.49.refs_5_), channel_id=1, source_target_pairs={{0,12},{4,0},{8,4},{12,8},{1,13},{5,1},{9,5},{13,9},{2,14},{6,2},{... | collective-permute-start | bytes 196616 | tf_op jit(solution)/shard_map/ppermute | solution.py:575
  55.5 7.6 %collective-permute-start.11 = (bf16[512,4096]{1,0:T(8,128)(2,1)}, bf16[512,4096]{1,0:T(8,128)(2,1)}, u32[]{:S(2)}, u32[]{:S(2)}) collective-permute-start(bf16[512,4096]{1,0:T(8,128)(2,1)} %refs_4_.5), channel_id=1, source_target_pairs={{0,1},{1,0},{2,3},{3,2},{4,5},{5,4},{6,7},{7,6},{8,9},{9,8},{10,11... | collective-permute-start | bytes 12582920 | tf_op jit(solution)/shard_map/ppermute | solution.py:571
  55.6 20.6 %all-to-all-start.1 = ((bf16[4,416,128]{2,1,0:T(8,128)(2,1)}), bf16[4,416,128]{2,1,0:T(8,128)(2,1)S(1)}, u32[]{:S(2)}, u32[]{:S(2)}) async-start(bf16[4,416,128]{2,1,0:T(8,128)(2,1)} %get-tuple-element.57), calls=%async_computation.1 | async-start | bytes 851968 | tf_op jit(solution)/shard_map/all_to_all | solution.py:669
  60.6 2.5 %collective-permute-start.10 = (bf16[256,384]{1,0:T(8,128)(2,1)S(1)}, bf16[256,384]{1,0:T(8,128)(2,1)S(1)}, u32[]{:S(2)}, u32[]{:S(2)}) collective-permute-start(bf16[256,384]{1,0:T(8,128)(2,1)S(1)} %get-tuple-element.59), channel_id=1, source_target_pairs={{0,1},{1,0},{2,3},{3,2},{4,5},{5,4},{6,7},{7,6},{8,9},{9,8},{10,11... | collective-permute-start | bytes 589832 | tf_op jit(solution)/shard_map/ppermute | solution.py:571
  77.5 9.8 %collective-permute-start.12 = (bf16[256,128]{1,0:T(8,128)(2,1)S(1)}, bf16[256,128]{1,0:T(8,128)(2,1)S(1)}, u32[]{:S(2)}, u32[]{:S(2)}) collective-permute-start(bf16[256,128]{1,0:T(8,128)(2,1)S(1)} %get-tuple-element.63.refs_1_), channel_id=1, source_target_pairs={{0,1},{1,0},{2,3},{3,2},{4,5},{5,4},{6,7},{7,6},{8,9},{9,8},{10,11... | collective-permute-start | bytes 196616 | tf_op jit(solution)/shard_map/ppermute | solution.py:571
  87.3 30.4 %all-to-all-start.2 = ((bf16[16,128,256]{2,1,0:T(8,128)(2,1)}), bf16[16,128,256]{2,1,0:T(8,128)(2,1)S(1)}, u32[]{:S(2)}, u32[]{:S(2)}) async-start(bf16[16,128,256]{2,1,0:T(8,128)(2,1)} %bitcast.10), calls=%async_computation.2 | async-start | bytes 2097152 | tf_op jit(solution)/shard_map/all_to_all | solution.py:722
  98.3 19.4 %collective-permute-start.17 = (bf16[256,1024]{1,0:T(8,128)(2,1)S(1)}, bf16[256,1024]{1,0:T(8,128)(2,1)S(1)}, u32[]{:S(2)}, u32[]{:S(2)}) collective-permute-start(bf16[256,1024]{1,0:T(8,128)(2,1)S(1)} %get-tuple-element.75), channel_id=1, source_target_pairs={{0,2},{2,0},{1,3},{3,1},{4,6},{6,4},{5,7},{7,5},{8,10},{10,8},{9,1... | collective-permute-start | bytes 1572872 | tf_op jit(solution)/shard_map/ppermute | solution.py:571
  99.4 18.3 %collective-permute-start.16 = (bf16[4,96,128]{2,1,0:T(8,128)(2,1)S(1)}, bf16[4,96,128]{2,1,0:T(8,128)(2,1)S(1)}, u32[]{:S(2)}, u32[]{:S(2)}) collective-permute-start(bf16[4,96,128]{2,1,0:T(8,128)(2,1)S(1)} %get-tuple-element.71), channel_id=1, source_target_pairs={{16,0},{32,16},{48,32},{64,48},{80,64},{96,80},{112,96},{128,112},... | collective-permute-start | bytes 294920 | tf_op jit(solution)/shard_map/ppermute | solution.py:689
  102.2 5.4 %collective-permute-start.13 = (bf16[256,128]{1,0:T(8,128)(2,1)S(1)}, bf16[256,128]{1,0:T(8,128)(2,1)S(1)}, u32[]{:S(2)}, u32[]{:S(2)}) collective-permute-start(bf16[256,128]{1,0:T(8,128)(2,1)S(1)} %get-tuple-element.67), channel_id=1, source_target_pairs={{0,12},{4,0},{8,4},{12,8},{1,13},{5,1},{9,5},{13,9},{2,14},{6,2},{... | collective-permute-start | bytes 196616 | tf_op jit(solution)/shard_map/ppermute | solution.py:575
  103.2 13.1 %collective-permute-start.14 = (bf16[256,128]{1,0:T(8,128)(2,1)S(1)}, bf16[256,128]{1,0:T(8,128)(2,1)S(1)}, u32[]{:S(2)}, u32[]{:S(2)}) collective-permute-start(bf16[256,128]{1,0:T(8,128)(2,1)S(1)} %get-tuple-element.68), channel_id=1, source_target_pairs={{0,8},{4,12},{8,0},{12,4},{1,9},{5,13},{9,1},{13,5},{2,10},{6,14},... | collective-permute-start | bytes 196616 | tf_op jit(solution)/shard_map/ppermute | solution.py:575
  106.3 11.4 %collective-permute-start.15 = (bf16[256,128]{1,0:T(8,128)(2,1)S(1)}, bf16[256,128]{1,0:T(8,128)(2,1)S(1)}, u32[]{:S(2)}, u32[]{:S(2)}) collective-permute-start(bf16[256,128]{1,0:T(8,128)(2,1)S(1)} %get-tuple-element.69), channel_id=1, source_target_pairs={{0,4},{4,8},{8,12},{12,0},{1,5},{5,9},{9,13},{13,1},{2,6},{6,10},{... | collective-permute-start | bytes 196616 | tf_op jit(solution)/shard_map/ppermute | solution.py:575

commit v6 on v5

--- a/solution.py
+++ b/solution.py
@@ -234,26 +234,25 @@
     return jnp.concatenate([a[:n], a[n:]], 1)
 
 
-def forward_kernel(
-    meta, q0, q1, q2, q3, g0, g1, g2, g3, kva, k, v, far, ob, q_all, g_all, kv_all,
-    s_ref, kv0, sems
-):
-    row, zh = meta[0], meta[1]
+def own_keys(k, v, kv0, sems):
     first = pl.ds(0, HEAD)
-    kept = [
+    copies = [
         pltpu.make_async_copy(k.at[:, first], kv0.at[:, first], sems.at[0]),
         pltpu.make_async_copy(
             v.at[:, first], kv0.at[:, pl.ds(HEAD, HEAD)], sems.at[1]
         ),
-        pltpu.make_async_copy(kva, kv_all, sems.at[2]),
     ]
-    for d, (q, g) in enumerate(((q0, g0), (q1, g1), (q2, g2), (q3, g3))):
-        at = pl.ds(d * TOK, TOK)
-        source = q.at[pl.ds(0, TOK)]
-        kept.append(pltpu.make_async_copy(source, q_all.at[at], sems.at[3 + d]))
-        kept.append(pltpu.make_async_copy(g, g_all.at[at], sems.at[7 + d]))
-    for copy in kept:
+    for copy in copies:
         copy.start()
+    return copies
+
+
+def forward_kernel(
+    meta, q0, q1, q2, q3, g0, g1, g2, g3, kva, k, v, far, ob0, ob1, ob2, ob3,
+    s_ref, kv0, sems
+):
+    row, zh = meta[0], meta[1]
+    brought = own_keys(k, v, kv0, sems)
     q = jnp.concatenate([q0[...], q1[:TOK], q2[:TOK], q3[:TOK]], 0)
     g = jnp.concatenate([g0[...], g1[...], g2[...], g3[...]], 0)
     masks = block_masks(row, zh)
@@ -292,7 +291,7 @@
     dots = dots * inv
     out = out * inv
 
-    for copy in kept:
+    for copy in brought:
         copy.wait()
     key, value = kv0[:, :HEAD], kv0[:, HEAD:]
     s = jnp.where(causal_t(), nt(key, q0[...]) * SCALE2, NEG)
@@ -320,25 +319,23 @@
     stats = jnp.concatenate(
         [stats[:, i * HEAD : (i + 1) * HEAD] for i in range(ALL // HEAD)], 0
     ).astype(BF)
-    for d in range(GROUP):
+    for d, ref in enumerate((ob0, ob1, ob2, ob3)):
         part = out[:, d * TOK : (d + 1) * TOK]
         if d == 0:
             part = wa * part + wb * own_out
-        to = lax.rem(zh - d + GROUP, GROUP)
-        ob[to, :TOK, :] = halves(part).astype(BF)
-        ob[to, TOK : TOK + STAT, :] = stats
-        ob[to, TOK + STAT :, :] = far[(d + 3) % 4]
-
-
-def combine_kernel(meta, oa, order, o, stat, sent, here):
-    zh = meta[1]
-    for u in range(4):
-        block = oa[lax.rem(zh + 1 + u, GROUP), TOK + STAT :, :]
-        sent[u] = block
-        here[u] = block
+        ref[:TOK, :] = halves(part).astype(BF)
+        ref[TOK : TOK + STAT, :] = stats
+        ref[TOK + STAT :, :] = far[(d + 3) % 4]
+
+
+def combine_kernel(meta, ob0, r1, r2, r3, order, o, stat, sent, here):
+    for u, ref in enumerate((r1, r2, r3, ob0)):
+        sent[u] = ref[TOK + STAT :, :]
+        here[u] = ref[TOK + STAT :, :]
+    sources = (ob0, r3, r2, r1)
     got = []
     for f in range(GROUP):
-        rows = oa[lax.rem(zh - f + GROUP, GROUP), TOK : TOK + STAT, :].astype(F32)
+        rows = sources[f][TOK : TOK + STAT, :].astype(F32)
         got.append(
             jnp.concatenate([rows[8 * i : 8 * i + 8] for i in range(STAT // 8)], 1)
         )
@@ -363,7 +360,7 @@
                 jnp.add,
                 [
                     shares[f]
-                    * whole(oa[lax.rem(zh - f + GROUP, GROUP), :TOK, :].astype(F32))
+                    * whole(sources[f][:TOK, :].astype(F32))
                     for f in range(GROUP)
                 ],
             )
@@ -373,49 +370,25 @@
 
 
 def backward_kernel(
-    meta, q_all, g_all, kv_all, k, v, stat, dkv, dq1, dq2, dq3, own, dq0,
-    qs, gs, kva, kv0, mine, made, sems
+    meta, q0, q1, q2, q3, g0, g1, g2, g3, kva, k, v, stat, dkv, dq1, dq2, dq3, own, dq0,
+    kv0, mine, made, sems, kv_sems
 ):
     row, zh = meta[0], meta[1]
-    first = pl.ds(0, HEAD)
+    brought = own_keys(k, v, kv0, kv_sems)
     steps = KEYS // TILE
-    brought = [
-        pltpu.make_async_copy(q_all, qs, sems.at[0]),
-        pltpu.make_async_copy(g_all, gs, sems.at[1]),
-        pltpu.make_async_copy(k.at[:, first], kv0.at[:, first], sems.at[2]),
-        pltpu.make_async_copy(
-            v.at[:, first], kv0.at[:, pl.ds(HEAD, HEAD)], sems.at[3]
-        ),
-    ]
-    tiles, sent = [], []
+    sent = []
     for j in range(steps):
         at = pl.ds(j * TILE, TILE)
-        tiles.append(pltpu.make_async_copy(kv_all.at[at], kva.at[at], sems.at[4 + j]))
-        sent.append(
-            pltpu.make_async_copy(made.at[at], dkv.at[at], sems.at[4 + steps + j])
-        )
-    sent.append(pltpu.make_async_copy(mine, own, sems.at[4 + 2 * steps]))
-    for copy in brought + tiles:
-        copy.start()
-    for copy in brought:
-        copy.wait()
+        sent.append(pltpu.make_async_copy(made.at[at], dkv.at[at], sems.at[j]))
+    sent.append(pltpu.make_async_copy(mine, own, sems.at[steps]))
+    q = jnp.concatenate([q0[...], q1[:TOK], q2[:TOK], q3[:TOK]], 0)
+    g = jnp.concatenate([g0[...], g1[...], g2[...], g3[...]], 0)
     log_sum, dot = stat[0:1, :], stat[1:2, :]
-    q, g = qs[...], gs[...]
-    q0, g0 = q[:TOK], g[:TOK]
-    key, value = kv0[:, :HEAD], kv0[:, HEAD:]
-    s = jnp.where(causal_t(), nt(key, q0) * SCALE2, NEG)
-    p = jnp.exp2(s - log_sum[:, :TOK])
-    mine[:, HEAD:] = nn(p.astype(BF), g0)
-    ds = (p * (nt(value, g0) - dot[:, :TOK])).astype(BF)
-    mine[:, :HEAD] = nn(ds, q0) * SCALE
-    dq_own = tn(key, ds)
-    sent[-1].start()
     masks = block_masks(row, zh)
     per = TILE // SUMM
     dq = jnp.zeros((HEAD, ALL), F32)
     for j in range(steps):
         at = slice(j * TILE, (j + 1) * TILE)
-        tiles[j].wait()
         key, value = kva[at, :HEAD], kva[at, HEAD:]
         s = nt(key, q)
         parts = []
@@ -430,6 +403,17 @@
         made[at, :HEAD] = (nn(ds, q) * SCALE).astype(BF)
         sent[j].start()
         dq = dq + tn(key, ds)
+        if j == steps // 2:
+            for copy in brought:
+                copy.wait()
+            key, value = kv0[:, :HEAD], kv0[:, HEAD:]
+            s = jnp.where(causal_t(), nt(key, q[:TOK]) * SCALE2, NEG)
+            p = jnp.exp2(s - log_sum[:, :TOK])
+            mine[:, HEAD:] = nn(p.astype(BF), g[:TOK])
+            ds = (p * (nt(value, g[:TOK]) - dot[:, :TOK])).astype(BF)
+            mine[:, :HEAD] = nn(ds, q[:TOK]) * SCALE
+            dq_own = tn(key, ds)
+            sent[-1].start()
     dq0[...] = (dq[:, :TOK] + dq_own) * SCALE
     for d, ref in ((1, dq1), (2, dq2), (3, dq3)):
         ref[...] = (halves(dq[:, d * TOK : (d + 1) * TOK]) * SCALE).astype(BF)
@@ -437,8 +421,29 @@
         copy.wait()
 
 
-def strided_kernel(meta, q, k, v, g, f1, f2, f3, last, o, dq, dkv, far, o_own):
+def strided_kernel(
+    meta, q, k, v, g, f1, f2, f3, last, o, far, dq, dkv, qs, ks, vs, dqs, dks, sems, out_s
+):
     row, zh = meta[0], meta[1]
+    brought, taken = [], []
+    for h in range(3):
+        for i, (ref, to) in enumerate(((q, qs), (k, ks), (v, vs))):
+            at = pl.ds((h + 1) * HEAD, HEAD)
+            brought.append(
+                pltpu.make_async_copy(ref.at[:, at], to.at[h], sems.at[3 * h + i])
+            )
+            brought[-1].start()
+        at = pl.ds(h * HEAD, HEAD)
+        also = pl.ds((h + 3) * HEAD, HEAD)
+        taken.append(
+            [
+                pltpu.make_async_copy(dqs.at[h], dq.at[:, at], out_s.at[3 * h]),
+                pltpu.make_async_copy(dks.at[h], dkv.at[:, at], out_s.at[3 * h + 1]),
+                pltpu.make_async_copy(
+                    dks.at[h + 3], dkv.at[:, also], out_s.at[3 * h + 2]
+                ),
+            ]
+        )
     slot = iota((TOK, 4 * REACH), 1) // REACH
     far_ok = (slot < zh) | (jnp.full((TOK, 4 * REACH), row, jnp.int32) > 0)
     near_ok = iota((TOK, TOK), 0) >= iota((TOK, TOK), 1)
@@ -451,7 +456,9 @@
     for h in range(3):
         at = slice((h + 1) * HEAD, (h + 2) * HEAD)
         to = slice(h * HEAD, (h + 1) * HEAD)
-        qh, kh, vh, gh = q[:, at], k[:, at], v[:, at], g[:, at]
+        for copy in brought[3 * h : 3 * h + 3]:
+            copy.wait()
+        qh, kh, vh, gh = qs[h], ks[h], vs[h], g[:, at]
         kf, vf = far_rows(h), far_rows(h + 3)
         s = jnp.where(near_ok, nt(qh, kh) * SCALE, NEG)
         sf = jnp.where(far_ok, nt(qh, kf) * SCALE, NEG)
@@ -466,89 +473,69 @@
         w, wf = p.astype(BF), pf.astype(BF)
         out = (nn(w, vh) + nn(wf, vf)).astype(BF)
         o[:, to] = out
-        o_own[:, to] = out
         delta = jnp.sum(gh.astype(F32) * out.astype(F32), axis=1, keepdims=True)
         ds = (p * (nt(gh, vh) - delta) * SCALE).astype(BF)
         dsf = (pf * (nt(gh, vf) - delta) * SCALE).astype(BF)
-        dq[:, to] = (nn(ds, kh) + nn(dsf, kf)).astype(BF)
-        dkv[:, to] = tn(ds, qh)
-        dkv[:, 3 * HEAD + h * HEAD : 3 * HEAD + (h + 1) * HEAD] = tn(w, gh)
+        dqs[h] = (nn(ds, kh) + nn(dsf, kf)).astype(BF)
+        dks[h] = tn(ds, qh)
+        dks[h + 3] = tn(w, gh)
+        for copy in taken[h]:
+            copy.start()
         dkf = tn(dsf, qh).astype(BF)
         dvf = tn(wf, gh).astype(BF)
         for u in range(4):
             rows = slice(u * REACH, (u + 1) * REACH)
             far[u, h * REACH : (h + 1) * REACH, :] = dkf[rows]
             far[u, (h + 3) * REACH : (h + 4) * REACH, :] = dvf[rows]
-
-
-def project_blocks(meta, w, w_c, first, here_w, beside_w, here_s, beside_s):
+    for group in taken:
+        for copy in group:
+            copy.wait()
+
+
+def project_strided_kernel(
+    meta, o, o_c, w, w_c, acc, fixed_w, fixed_wc, here_w, sems, ahead_sems
+):
     zl, c = meta[2], meta[3]
     places = ((1 - zl, c), (zl, c))
-    rows = pl.ds(first, here_w.shape[1])
-    return (
-        weight_blocks(w.at[rows], here_w, places, here_s),
-        weight_blocks(w_c.at[rows], beside_w, places, beside_s),
-    )
-
-
-def project_strided_kernel(meta, o, o_c, w, w_c, acc, *space):
-    here_w, beside_w = space[:2]
-    copies, beside_copies = project_blocks(meta, w, w_c, HEAD, *space)
-    for i in range(2):
+    copies = weight_blocks(w.at[pl.ds(HEAD, 3 * HEAD)], here_w, places, sems)
+    ahead = weight_blocks(w.at[pl.ds(0, HEAD)], fixed_w, places, ahead_sems)
+    wide = here_w.shape[2]
+    for i, (z, core) in enumerate(places):
+        at = pl.ds(pl.multiple_of((2 * z + core) * wide, wide), wide)
+        fixed_wc[i] = w_c[:HEAD, at]
+        total = nn(o_c[...], w_c[HEAD:, at])
         copies[i].wait()
-        total = nn(o[...], here_w[i])
-        beside_copies[i].wait()
-        acc[i] = total + nn(o_c[...], beside_w[i])
-
-
-def project_fixed_kernel(meta, o, o_c, acc, w, w_c, send, keep, got, sems, *space):
-    here_w, beside_w = space[:2]
-    before = [pltpu.make_async_copy(acc.at[i], got.at[i], sems.at[i]) for i in range(2)]
-    for copy in before:
-        copy.start()
-    copies, beside_copies = project_blocks(meta, w, w_c, 0, *space)
+        acc[i] = total + nn(o[...], here_w[i])
+    for copy in ahead:
+        copy.wait()
+
+
+def project_fixed_kernel(meta, o, o_c, acc, fixed_w, fixed_wc, order, send, keep):
     for i, ref in ((0, send), (1, keep)):
-        copies[i].wait()
-        beside_copies[i].wait()
-        total = nn(o[...], here_w[i]) + nn(o_c[...], beside_w[i])
-        before[i].wait()
-        ref[...] = (total + got[i]).astype(ref.dtype)
-
-
-def final_kernel(
-    meta,
-    soff_t,
-    sidx,
-    dkv,
-    own,
-    dq0,
-    dq1,
-    dq2,
-    dq3,
-    here,
-    after,
-    strided_dq,
-    strided,
-    keep,
-    over,
-    out,
-    qg,
-    kg,
-    vg,
-):
-    zh = meta[1]
-    shard = GROUP * meta[0] + meta[1]
+        total = acc[i] + nn(o[...], fixed_w[i]) + nn(o_c[...], fixed_wc[i])
+        ref[...] = total.astype(ref.dtype)
+
+
+def output_kernel(meta, keep, over, out):
     out[...] = (keep[...].astype(F32) + over[...].astype(F32)).astype(BF)
-    pick = summary_select(sidx[...])
-    fixed = own[...] + nn(jnp.concatenate([pick] * ROWS, 1), dkv[...])
-    kg[:, :HEAD] = fixed[:, :HEAD].astype(BF)
-    vg[:, :HEAD] = fixed[:, HEAD:].astype(BF)
+
+
+def query_kernel(meta, dq0, dq1, dq2, dq3, strided_dq, qg):
     total = dq0[...]
     for ref in (dq1, dq2, dq3):
         total = total + whole(ref[...].astype(F32))
     eye = ones_where(iota((HEAD, HEAD), 0) == iota((HEAD, HEAD), 1))
     qg[:, :HEAD] = tn(total.astype(BF), eye).astype(BF)
     qg[:, HEAD:] = strided_dq[...]
+
+
+def final_kernel(meta, soff_t, sidx, dkv, own, here, after, strided, kg, vg):
+    zh = meta[1]
+    shard = GROUP * meta[0] + meta[1]
+    pick = summary_select(sidx[...])
+    fixed = own[...] + nn(jnp.concatenate([pick] * ROWS, 1), dkv[...])
+    kg[:, :HEAD] = fixed[:, :HEAD].astype(BF)
+    vg[:, :HEAD] = fixed[:, HEAD:].astype(BF)
     sel = stride_select(soff_t[...], shard)
     slots = []
     for u in range(4):
@@ -632,57 +619,46 @@
         name="attention_grad_far",
     )
     gs = [g0] + [turn(g0, d) for d in (1, 2, 3)]
-    o_s, dq_s, dkv_s, far, o_own = call(
+    part = pltpu.VMEM((3, TOK, HEAD), BF)
+    o_s, far, dq_s, dkv_s = call(
         strided_kernel,
         [
             sds((TOK, 3 * HEAD)),
+            block,
             sds((TOK, 3 * HEAD)),
             sds((TOK, 6 * HEAD), F32),
-            block,
-            sds((TOK, 3 * HEAD)),
         ],
         [meta, queries, key_rows, value_rows, g, *qs[1:], last],
+        [part] * 4 + [pltpu.VMEM((6, TOK, HEAD), F32), dma(9), dma(9)],
         name="strided_heads",
-        fetch=range(1, 4),
-        store=[1, 2, 4],
+        raw=[1, 2, 3],
+        direct=[2, 3],
     )
     o_sc = swap(o_s, "c")
-    ob, q_all, g_all, kv_all = call(
+    own_space = pltpu.VMEM((TOK, 2 * HEAD), BF)
+    obs = call(
         forward_kernel,
-        [
-            sds((GROUP, TOK + STAT + FAR, HEAD)),
-            sds((ALL, HEAD)),
-            sds((ALL, HEAD)),
-            sds((KEYS, 2 * HEAD)),
-        ],
+        [sds((TOK + STAT + FAR, HEAD))] * 4,
         [meta, *qs, *gs, kva, key_rows, value_rows, far],
-        [
-            pltpu.VMEM((KEYS, ALL), F32),
-            pltpu.VMEM((TOK, 2 * HEAD), BF),
-            dma(11),
-        ],
+        [pltpu.VMEM((KEYS, ALL), F32), own_space, dma(2)],
         name="fixed_forward",
         raw=[10, 11],
-        direct=[1, 2, 3],
-    )
-    weight_c = swap(after(out_weight, q_all), "c")
-    oa = lax.all_to_all(ob, "zh", 0, 0, tiled=True)
-    (acc_out,) = call(
+    )
+    weight_c = swap(after(out_weight, obs[0]), "c")
+    oas = [obs[0]] + [turn(obs[d], -d) for d in (1, 2, 3)]
+    acc_out, fixed_w, fixed_wc = call(
         project_strided_kernel,
-        [sds((2, TOK, quarter), F32)],
-        [meta, o_own, o_sc, out_weight, weight_c],
-        [pltpu.VMEM((2, 3 * HEAD, quarter), BF)] * 2 + [dma(2)] * 2,
+        [sds((2, TOK, quarter), F32)] + [sds((2, HEAD, quarter))] * 2,
+        [meta, o_s, o_sc, out_weight, weight_c],
+        [pltpu.VMEM((2, 3 * HEAD, quarter), BF), dma(2), dma(2)],
         name="project_strided",
-        fetch=[1],
-        raw=[3, 4],
-        store=[0],
+        raw=[3],
     )
     o_f, stat, sent, here = call(
         combine_kernel,
         [sds((TOK, HEAD)), sds((8, ALL), F32), block, block],
-        [meta, oa, acc_out],
+        [meta, *oas, acc_out],
         name="combine",
-        raw=[2],
         store=[3],
     )
     o_fc = swap(o_f, "c")
@@ -692,45 +668,55 @@
         [sds((KEYS, 2 * HEAD))]
         + [sds((TOK, HEAD))] * 3
         + [sds((TOK, 2 * HEAD), F32), sds((HEAD, TOK), F32)],
-        [meta, q_all, g_all, kv_all, key_rows, value_rows, stat],
+        [meta, *qs, *gs, kva, key_rows, value_rows, stat],
         [
-            pltpu.VMEM((ALL, HEAD), BF),
-            pltpu.VMEM((ALL, HEAD), BF),
-            pltpu.VMEM((KEYS, 2 * HEAD), BF),
-            pltpu.VMEM((TOK, 2 * HEAD), BF),
+            own_space,
             pltpu.VMEM((TOK, 2 * HEAD), F32),
             pltpu.VMEM((KEYS, 2 * HEAD), BF),
-            dma(5 + 2 * (KEYS // TILE)),
+            dma(1 + KEYS // TILE),
+            dma(2),
         ],
         name="fixed_backward",
-        raw=range(1, 6),
+        raw=[10, 11],
         store=[5],
         direct=[0, 4],
     )
     send, keep = call(
         project_fixed_kernel,
         [sds((TOK, quarter))] * 2,
-        [meta, o_f, o_fc, acc_out, out_weight, weight_c],
-        [pltpu.VMEM((2, TOK, quarter), F32), dma(2)]
-        + [pltpu.VMEM((2, HEAD, quarter), BF)] * 2
-        + [dma(2)] * 2,
+        [meta, o_f, o_fc, acc_out, fixed_w, fixed_wc, dq0],
         name="project_fixed",
-        raw=[3, 4, 5],
+        raw=[6],
         store=[1],
     )
     over = swap(send, "zl")
     dkva = lax.all_to_all(
-        after(dkv, o_fc).reshape(ROWS, SUMM, 2 * HEAD), plane, 0, 0, tiled=True
+        after(dkv, keep).reshape(ROWS, SUMM, 2 * HEAD), plane, 0, 0, tiled=True
     ).reshape(KEYS, 2 * HEAD)
     dqs = [turn(dqs[d - 1], -d) for d in (1, 2, 3)]
-    return call(
+    (layer_out,) = call(
+        output_kernel,
+        [sds((TOK, quarter))],
+        [meta, keep, over],
+        name="join_output",
+        fetch=[1],
+        flops=7 * 10**9,
+    )
+    (query_grad,) = call(
+        query_kernel,
+        [sds((TOK, width))],
+        [meta, dq0, *dqs, dq_s],
+        name="join_query_grad",
+        fetch=[1, 5],
+    )
+    key_grad, value_grad = call(
         final_kernel,
-        [sds((TOK, quarter))] + [sds((TOK, width))] * 3,
-        [meta, soff_t, summary_index, dkva, own, dq0, *dqs, here, back, dq_s, dkv_s]
-        + [keep, over],
-        name="join_results",
-        fetch=[1, 2, 4, 5, 9, 11, 12, 13],
-    )
+        [sds((TOK, width))] * 2,
+        [meta, soff_t, summary_index, dkva, own, here, back, dkv_s],
+        name="join_key_grads",
+        fetch=[1, 2, 4, 5, 7],
+    )
+    return layer_out, query_grad, key_grad, value_grad
 
 
 def solution(mesh):

time: 123 us -> 114 us (0.927)
  waiting for transfers between devices: 26 us -> 14.9 us
  starting transfers between devices: 49 us -> 52.6 us
  Pallas kernels: 45.7 us -> 43.9 us
    all_to_all x2 -> x1, waiting for transfers between devices: 7.3 us -> 0.01 us  [shards(): lax.all_to_all(after(dkv, keep).reshape(ROWS, SUMM, 2 * HEAD), plane, 0,...]
    ppermute x9 -> x12, starting transfers between devices: 19.7 us -> 25.3 us  [turn(): return lax.ppermute(a, 'zh', [(i, (i + by) % GROUP) for i in range(GROUP)])]
    all_to_all x2 -> x1, starting transfers between devices: 12.2 us -> 7.23 us  [shards(): lax.all_to_all(after(dkv, keep).reshape(ROWS, SUMM, 2 * HEAD), plane, 0,...]
    ppermute x9 -> x12, waiting for transfers between devices: 12.8 us -> 9.79 us  [turn(): return lax.ppermute(a, 'zh', [(i, (i + by) % GROUP) for i in range(GROUP)])]
    ppermute x7, starting transfers between devices: 4.17 us -> 7.13 us  [swap(): return lax.ppermute(a, axis, [(0, 1), (1, 0)])]
    pallas_call x11 -> x13, Pallas kernels: 45.7 us -> 43.9 us  [call(): pl.pallas_call(body, out_shape=tuple((pltpu.HBM(s.shape, s.dtype) if i in...]
  transfers between devices with their start and end apart: 21 -> 23, of which waited for: 8 -> 9; matrix products, arithmetic and copies ran while one was open for 0% -> 0% of each run, Pallas kernels for 28% -> 28%
where the time goes in v6:
time: 114 us; the launch traced here: 113 us
  starting transfers between devices  52.6 us (46%)
  Pallas kernels  43.9 us (39%)
  waiting for transfers between devices  14.9 us (13%)
    pallas_call x13, Pallas kernels, call(): pl.pallas_call(body, out_shape=tuple((pltpu.HBM(s.shape, s.dtype) if i in...  43.9 us
    ppermute x12, starting transfers between devices, turn(): return lax.ppermute(a, 'zh', [(i, (i + by) % GROUP) for i in range(GROUP)])  25.3 us
    ppermute x12, waiting for transfers between devices, turn(): return lax.ppermute(a, 'zh', [(i, (i + by) % GROUP) for i in range(GROUP)])  9.79 us
    all_to_all x1, starting transfers between devices, shards(): lax.all_to_all(after(dkv, keep).reshape(ROWS, SUMM, 2 * HEAD), plane, 0,...  7.23 us
    all_to_all x1, starting transfers between devices, shards(): kva = lax.all_to_all(kvb, plane, 0, 0, tiled=True).reshape(KEYS, 2 * HEAD)  7.18 us
    ppermute x7, starting transfers between devices, swap(): return lax.ppermute(a, axis, [(0, 1), (1, 0)])  7.13 us
    ppermute x1, waiting for transfers between devices, shards(): before = lax.ppermute(picks, plane, [(i, i + 1) for i in range(ROWS - 1)])  3.44 us
    ppermute x1, starting transfers between devices, shards(): before = lax.ppermute(picks, plane, [(i, i + 1) for i in range(ROWS - 1)])  3.06 us
  transfers between devices with their start and end apart: 23, of which 9 were waited for; matrix products, arithmetic and copies ran while one was open for 0% of the time, Pallas kernels for 28%

profile of v6, /device:TPU:24, one launch (start us, length us, event | category | flops | bytes accessed | tf_op | source)
XLA Modules:
  0.0 112.6 jit_solution(3026774737966860166)
XLA Ops:
  0.6 2.0 %collective-permute-start.4 = (bf16[256,1024]{1,0:T(8,128)(2,1)}, bf16[256,1024]{1,0:T(8,128)(2,1)S(1)}, u32[]{:S(2)}, u32[]{:S(2)}) collective-permute-start(bf16[256,1024]{1,0:T(8,128)(2,1)} %refs_1_.2), channel_id=1, source_target_pairs={{0,2},{2,0},{1,3},{3,1},{4,6},{6,4},{5,7},{7,5},{8,10},{10,8},{9,1... | collective-permute-start | bytes 1572872 | tf_op jit(solution)/shard_map/ppermute | solution.py:558
  2.7 3.5 %pick_rows.1 = (bf16[16,128,256]{2,1,0:T(8,128)(2,1)}, bf16[256,128]{1,0:T(8,128)(2,1)S(1)}, bf16[4,96,128]{2,1,0:T(8,128)(2,1)S(1)}) custom-call(s32[4]{0:T(128)S(1)} %pad_add_fusion.refs_0_, s32[4,64]{1,0:T(4,128)} %bitcast.12, s32[1,128]{1,0:T(1,128)} %refs_2_.5, bf16[256,512]{1,0:T(8,128)(2,1)} %refs_10_.3, bf16[256,512]{1,0:T(8,128)(2,1)} %refs_11_.3, ...), custom_call_target="tpu_custom_call" | custom-call | flops 1 | bytes 1 | tf_op jit(solution)/shard_map/pick_rows/pallas_call | solution.py:111
  6.2 3.1 %collective-permute-start = (bf16[4,96,128]{2,1,0:T(8,128)(2,1)S(1)}, bf16[4,96,128]{2,1,0:T(8,128)(2,1)S(1)}, u32[]{:S(2)}, u32[]{:S(2)}) collective-permute-start(bf16[4,96,128]{2,1,0:T(8,128)(2,1)S(1)} %get-tuple-element.45.refs_2_), channel_id=1, source_target_pairs={{0,16},{16,32},{32,48},{48,64},{64,80},{80,96},{96,112},{112,128},... | collective-permute-start | bytes 294920 | tf_op jit(solution)/shard_map/ppermute | solution.py:594
  9.3 3.4 %collective-permute-done.refs_3_ = bf16[4,96,128]{2,1,0:T(8,128)(2,1)S(1)} collective-permute-done((bf16[4,96,128]{2,1,0:T(8,128)(2,1)S(1)}, bf16[4,96,128]{2,1,0:T(8,128)(2,1)S(1)}, u32[]{:S(2)}, u32[]{:S(2)}) %collective-permute-start) | collective-permute-done | bytes 98336 | tf_op jit(solution)/shard_map/ppermute | solution.py:594
  13.3 7.2 %all-to-all-start = ((bf16[16,128,256]{2,1,0:T(8,128)(2,1)}), bf16[16,128,256]{2,1,0:T(8,128)(2,1)S(1)}, u32[]{:S(2)}, u32[]{:S(2)}) async-start(bf16[16,128,256]{2,1,0:T(8,128)(2,1)} %get-tuple-element.55), calls=%async_computation | async-start | bytes 2097152 | tf_op jit(solution)/shard_map/all_to_all | solution.py:602
  21.0 3.3 %collective-permute-start.1 = (bf16[352,128]{1,0:T(8,128)(2,1)S(1)}, bf16[352,128]{1,0:T(8,128)(2,1)S(1)}, u32[]{:S(2)}, u32[]{:S(2)}) collective-permute-start(bf16[352,128]{1,0:T(8,128)(2,1)S(1)} %get-tuple-element.46), channel_id=1, source_target_pairs={{0,4},{4,8},{8,12},{12,0},{1,5},{5,9},{9,13},{13,1},{2,6},{6,10},{... | collective-permute-start | bytes 270344 | tf_op jit(solution)/shard_map/ppermute | solution.py:562
  24.3 4.5 %collective-permute-start.2 = (bf16[352,128]{1,0:T(8,128)(2,1)S(1)}, bf16[352,128]{1,0:T(8,128)(2,1)S(1)}, u32[]{:S(2)}, u32[]{:S(2)}) collective-permute-start(bf16[352,128]{1,0:T(8,128)(2,1)S(1)} %get-tuple-element.47), channel_id=1, source_target_pairs={{0,8},{4,12},{8,0},{12,4},{1,9},{5,13},{9,1},{13,5},{2,10},{6,14},... | collective-permute-start | bytes 270344 | tf_op jit(solution)/shard_map/ppermute | solution.py:562
  28.7 2.7 %collective-permute-start.3 = (bf16[352,128]{1,0:T(8,128)(2,1)S(1)}, bf16[352,128]{1,0:T(8,128)(2,1)S(1)}, u32[]{:S(2)}, u32[]{:S(2)}) collective-permute-start(bf16[352,128]{1,0:T(8,128)(2,1)S(1)} %get-tuple-element.48), channel_id=1, source_target_pairs={{0,12},{4,0},{8,4},{12,8},{1,13},{5,1},{9,5},{13,9},{2,14},{6,2},{... | collective-permute-start | bytes 270344 | tf_op jit(solution)/shard_map/ppermute | solution.py:562
  31.4 4.2 %attention_grad_near.1 = (f32[256,512]{1,0:T(8,128)S(1)}, bf16[2,512,1024]{2,1,0:T(8,128)(2,1)S(1)}) custom-call(s32[4]{0:T(128)S(1)} %pad_add_fusion.refs_0_, bf16[256,1024]{1,0:T(8,128)(2,1)} %refs_1_.2, bf16[256,1024]{1,0:T(8,128)(2,1)S(1)} %collective-permute-done.6.refs_2_, bf16[512,4096]{1,0:T(8,128)(2,1)} %refs_3_.7, ...), custom_call_target="tpu_custom_call" | custom-call | flops 1 | bytes 1 | tf_op jit(solution)/shard_map/attention_grad_near/pallas_call | solution.py:111
  35.7 1.3 %attention_grad_far.1 = (bf16[256,128]{1,0:T(8,128)(2,1)S(1)}, bf16[256,512]{1,0:T(8,128)(2,1)S(1)}) custom-call(s32[4]{0:T(128)S(1)} %pad_add_fusion.refs_0_, bf16[256,1024]{1,0:T(8,128)(2,1)S(1)} %collective-permute-done.4.refs_1_, bf16[256,1024]{1,0:T(8,128)(2,1)S(1)} %collective-permute-done.5.refs_2_, ...), custom_call_target="tpu_custom_call" | custom-call | flops 1 | bytes 1 | tf_op jit(solution)/shard_map/attention_grad_far/pallas_call | solution.py:111
  37.0 3.8 %collective-permute-start.8 = (bf16[256,128]{1,0:T(8,128)(2,1)S(1)}, bf16[256,128]{1,0:T(8,128)(2,1)S(1)}, u32[]{:S(2)}, u32[]{:S(2)}) collective-permute-start(bf16[256,128]{1,0:T(8,128)(2,1)S(1)} %get-tuple-element.53.refs_5_), channel_id=1, source_target_pairs={{0,8},{4,12},{8,0},{12,4},{1,9},{5,13},{9,1},{13,5},{2,10},{6,14},... | collective-permute-start | bytes 196616 | tf_op jit(solution)/shard_map/ppermute | solution.py:562
  40.9 5.1 %strided_heads.1 = (bf16[256,384]{1,0:T(8,128)(2,1)S(1)}, bf16[4,96,128]{2,1,0:T(8,128)(2,1)S(1)}, bf16[256,384]{1,0:T(8,128)(2,1)}, f32[256,768]{1,0:T(8,128)}) custom-call(s32[4]{0:T(128)S(1)} %pad_add_fusion.refs_0_, bf16[256,512]{1,0:T(8,128)(2,1)} %refs_1_.3, bf16[256,512]{1,0:T(8,128)(2,1)} %refs_10_.3, bf16[256,512]{1,0:T(8,128)(2,1)} %refs_11_.3, ...), custom_call_target="tpu_custom_call" | custom-call | flops 1 | bytes 1 | tf_op jit(solution)/shard_map/strided_heads/pallas_call | solution.py:111
  46.0 2.5 %collective-permute-done.7.refs_6_ = bf16[256,128]{1,0:T(8,128)(2,1)S(1)} collective-permute-done((bf16[256,128]{1,0:T(8,128)(2,1)S(1)}, bf16[256,128]{1,0:T(8,128)(2,1)S(1)}, u32[]{:S(2)}, u32[]{:S(2)}) %collective-permute-start.7) | collective-permute-done | bytes 65568 | tf_op jit(solution)/shard_map/ppermute | solution.py:562
  48.5 6.3 %fixed_forward.1 = (bf16[416,128]{1,0:T(8,128)(2,1)S(1)}, bf16[416,128]{1,0:T(8,128)(2,1)S(1)}, bf16[416,128]{1,0:T(8,128)(2,1)S(1)}, bf16[416,128]{1,0:T(8,128)(2,1)S(1)}) custom-call(s32[4]{0:T(128)S(1)} %pad_add_fusion.refs_0_, bf16[256,128]{1,0:T(8,128)(2,1)S(1)} %get-tuple-element.44.refs_1_, ...), custom_call_target="tpu_custom_call" | custom-call | flops 1 | bytes 1 | tf_op jit(solution)/shard_map/fixed_forward/pallas_call | solution.py:111
  55.4 1.6 %collective-permute-start.10 = (bf16[416,128]{1,0:T(8,128)(2,1)S(1)}, bf16[416,128]{1,0:T(8,128)(2,1)S(1)}, u32[]{:S(2)}, u32[]{:S(2)}) collective-permute-start(bf16[416,128]{1,0:T(8,128)(2,1)S(1)} %get-tuple-element.59), channel_id=1, source_target_pairs={{0,12},{4,0},{8,4},{12,8},{1,13},{5,1},{9,5},{13,9},{2,14},{6,2},{... | collective-permute-start | bytes 319496 | tf_op jit(solution)/shard_map/ppermute | solution.py:562
  57.1 3.0 %collective-permute-start.11 = (bf16[416,128]{1,0:T(8,128)(2,1)S(1)}, bf16[416,128]{1,0:T(8,128)(2,1)S(1)}, u32[]{:S(2)}, u32[]{:S(2)}) collective-permute-start(bf16[416,128]{1,0:T(8,128)(2,1)S(1)} %get-tuple-element.60), channel_id=1, source_target_pairs={{0,8},{4,12},{8,0},{12,4},{1,9},{5,13},{9,1},{13,5},{2,10},{6,14},... | collective-permute-start | bytes 319496 | tf_op jit(solution)/shard_map/ppermute | solution.py:562
  61.3 1.3 %collective-permute-done.14.refs_4_ = bf16[512,4096]{1,0:T(8,128)(2,1)S(1)} collective-permute-done((bf16[512,4096]{1,0:T(8,128)(2,1)}, bf16[512,4096]{1,0:T(8,128)(2,1)S(1)}, u32[]{:S(2)}, u32[]{:S(2)}) %collective-permute-start.14) | collective-permute-done | bytes 4194336 | tf_op jit(solution)/shard_map/ppermute | solution.py:558
  62.6 3.2 %project_strided.1 = (f32[2,256,1024]{2,1,0:T(8,128)S(1)}, bf16[2,128,1024]{2,1,0:T(8,128)(2,1)S(1)}, bf16[2,128,1024]{2,1,0:T(8,128)(2,1)S(1)}) custom-call(s32[4]{0:T(128)S(1)} %pad_add_fusion.refs_0_, bf16[256,384]{1,0:T(8,128)(2,1)S(1)} %get-tuple-element.62.refs_1_, bf16[256,384]{1,0:T(8,128)(2,1)S(1)} %collective-permute-done.13.refs_2_, ...), custom_call_target="tpu_custom_call" | custom-call | flops 1 | bytes 1 | tf_op jit(solution)/shard_map/project_strided/pallas_call | solution.py:111
  66.3 2.8 %collective-permute-done.11.refs_3_ = bf16[416,128]{1,0:T(8,128)(2,1)S(1)} collective-permute-done((bf16[416,128]{1,0:T(8,128)(2,1)S(1)}, bf16[416,128]{1,0:T(8,128)(2,1)S(1)}, u32[]{:S(2)}, u32[]{:S(2)}) %collective-permute-start.11) | collective-permute-done | bytes 106528 | tf_op jit(solution)/shard_map/ppermute | solution.py:562
  69.3 1.3 %combine.1 = (bf16[256,128]{1,0:T(8,128)(2,1)S(1)}, f32[8,1024]{1,0:T(8,128)S(1)}, bf16[4,96,128]{2,1,0:T(8,128)(2,1)S(1)}, bf16[4,96,128]{2,1,0:T(8,128)(2,1)}) custom-call(s32[4]{0:T(128)S(1)} %pad_add_fusion.refs_0_, bf16[416,128]{1,0:T(8,128)(2,1)S(1)} %get-tuple-element.58.refs_1_, bf16[416,128]{1,0:T(8,128)(2,1)S(1)} %collective-permute-done.10.refs_2_, ...), custom_call_target="tpu_custom_call" | custom-call | flops 1 | bytes 1 | tf_op jit(solution)/shard_map/combine/pallas_call | solution.py:111
  70.9 8.1 %fixed_backward.1 = (bf16[2048,256]{1,0:T(8,128)(2,1)}, bf16[256,128]{1,0:T(8,128)(2,1)S(1)}, bf16[256,128]{1,0:T(8,128)(2,1)S(1)}, bf16[256,128]{1,0:T(8,128)(2...) custom-call(s32[4]{0:T(128)S(1)} %pad_add_fusion.refs_0_, bf16[256,128]{1,0:T(8,128)(2,1)S(1)} %get-tuple-element.44.refs_1_, ...), custom_call_target="tpu_custom_call" | custom-call | flops 1 | bytes 1 | tf_op jit(solution)/shard_map/fixed_backward/pallas_call | solution.py:111
  79.0 2.0 %project_fixed.1 = (bf16[256,1024]{1,0:T(8,128)(2,1)S(1)}, bf16[256,1024]{1,0:T(8,128)(2,1)}) custom-call(s32[4]{0:T(128)S(1)} %pad_add_fusion.refs_0_, bf16[256,128]{1,0:T(8,128)(2,1)S(1)} %get-tuple-element.65.refs_1_, bf16[256,128]{1,0:T(8,128)(2,1)S(1)} %collective-permute-done.15.refs_2_, f32[2,256,1024]{2,1,0:T(8,128)S(1)} %get-tuple-element.64.refs_5_.refs_3_, ...), custom_call_target="tpu_custom_call" | custom-call | flops 1 | bytes 1 | tf_op jit(solution)/shard_map/project_fixed/pallas_call | solution.py:111
  81.1 3.7 %collective-permute-start.16 = (bf16[256,1024]{1,0:T(8,128)(2,1)S(1)}, bf16[256,1024]{1,0:T(8,128)(2,1)S(1)}, u32[]{:S(2)}, u32[]{:S(2)}) collective-permute-start(bf16[256,1024]{1,0:T(8,128)(2,1)S(1)} %get-tuple-element.71), channel_id=1, source_target_pairs={{0,2},{2,0},{1,3},{3,1},{4,6},{6,4},{5,7},{7,5},{8,10},{10,8},{9,1... | collective-permute-start | bytes 1572872 | tf_op jit(solution)/shard_map/ppermute | solution.py:558
  84.8 7.2 %all-to-all-start.1 = ((bf16[16,128,256]{2,1,0:T(8,128)(2,1)}), bf16[16,128,256]{2,1,0:T(8,128)(2,1)S(1)}, u32[]{:S(2)}, u32[]{:S(2)}) async-start(bf16[16,128,256]{2,1,0:T(8,128)(2,1)} %bitcast.11), calls=%async_computation.1 | async-start | bytes 2097152 | tf_op jit(solution)/shard_map/all_to_all | solution.py:693
  92.0 1.6 %collective-permute-start.17 = (bf16[256,128]{1,0:T(8,128)(2,1)S(1)}, bf16[256,128]{1,0:T(8,128)(2,1)S(1)}, u32[]{:S(2)}, u32[]{:S(2)}) collective-permute-start(bf16[256,128]{1,0:T(8,128)(2,1)S(1)} %get-tuple-element.72), channel_id=1, source_target_pairs={{0,12},{4,0},{8,4},{12,8},{1,13},{5,1},{9,5},{13,9},{2,14},{6,2},{... | collective-permute-start | bytes 196616 | tf_op jit(solution)/shard_map/ppermute | solution.py:562
  93.7 3.1 %collective-permute-start.18 = (bf16[256,128]{1,0:T(8,128)(2,1)S(1)}, bf16[256,128]{1,0:T(8,128)(2,1)S(1)}, u32[]{:S(2)}, u32[]{:S(2)}) collective-permute-start(bf16[256,128]{1,0:T(8,128)(2,1)S(1)} %get-tuple-element.73), channel_id=1, source_target_pairs={{0,8},{4,12},{8,0},{12,4},{1,9},{5,13},{9,1},{13,5},{2,10},{6,14},... | collective-permute-start | bytes 196616 | tf_op jit(solution)/shard_map/ppermute | solution.py:562
  97.5 2.8 %collective-permute-start.20 = (bf16[4,96,128]{2,1,0:T(8,128)(2,1)S(1)}, bf16[4,96,128]{2,1,0:T(8,128)(2,1)S(1)}, u32[]{:S(2)}, u32[]{:S(2)}) collective-permute-start(bf16[4,96,128]{2,1,0:T(8,128)(2,1)S(1)} %get-tuple-element.80), channel_id=1, source_target_pairs={{16,0},{32,16},{48,32},{64,48},{80,64},{96,80},{112,96},{128,112},... | collective-permute-start | bytes 294920 | tf_op jit(solution)/shard_map/ppermute | solution.py:665
  100.3 2.9 %collective-permute-done.18.refs_3_ = bf16[256,128]{1,0:T(8,128)(2,1)S(1)} collective-permute-done((bf16[256,128]{1,0:T(8,128)(2,1)S(1)}, bf16[256,128]{1,0:T(8,128)(2,1)S(1)}, u32[]{:S(2)}, u32[]{:S(2)}) %collective-permute-start.18) | collective-permute-done | bytes 65568 | tf_op jit(solution)/shard_map/ppermute | solution.py:562
  103.2 0.9 collective-permute-done.19.refs_4_
  104.1 2.5 %join_query_grad.1 = bf16[256,512]{1,0:T(8,128)(2,1)} custom-call(s32[4]{0:T(128)S(1)} %pad_add_fusion.refs_0_, f32[128,256]{1,0:T(8,128)} %get-tuple-element.69.refs_6_.refs_1_, bf16[256,128]{1,0:T(8,128)(2,1)S(1)} %collective-permute-done.17.refs_2_, bf16[256,128]{1,0:T(8,128)(2,1)S(1)} %collective-permute-done.18.refs_3_, ...), custom_call_target="tpu_custom_call" | custom-call | flops 1 | bytes 1 | tf_op jit(solution)/shard_map/join_query_grad/pallas_call | solution.py:111
  106.6 2.6 %join_output.1 = bf16[256,1024]{1,0:T(8,128)(2,1)} custom-call(s32[4]{0:T(128)S(1)} %pad_add_fusion.refs_0_, bf16[256,1024]{1,0:T(8,128)(2,1)} %get-tuple-element.70.refs_1_, bf16[256,1024]{1,0:T(8,128)(2,1)S(1)} %collective-permute-done.16.refs_2_), custom_call_target="tpu_custom_call" | custom-call | flops 7000000000 | bytes 1 | tf_op jit(solution)/shard_map/join_output/pallas_call | solution.py:111
  109.2 3.2 %join_key_grads.1 = (bf16[256,512]{1,0:T(8,128)(2,1)}, bf16[256,512]{1,0:T(8,128)(2,1)}) custom-call(s32[4]{0:T(128)S(1)} %pad_add_fusion.refs_0_, s32[4,64]{1,0:T(4,128)} %bitcast.13, s32[1,128]{1,0:T(1,128)} %refs_2_.5, bf16[2048,256]{1,0:T(8,128)(2,1)S(1)} %bitcast.10, f32[256,256]{1,0:T(8,128)} %get-tuple-element.78.refs_4_, ...), custom_call_target="tpu_custom_call" | custom-call | flops 1 | bytes 1 | tf_op jit(solution)/shard_map/join_key_grads/pallas_call | solution.py:111
  (28 shorter events, 4.9 us)
Async XLA Ops:
  0.6 19.9 %collective-permute-start.4 = (bf16[256,1024]{1,0:T(8,128)(2,1)}, bf16[256,1024]{1,0:T(8,128)(2,1)S(1)}, u32[]{:S(2)}, u32[]{:S(2)}) collective-permute-start(bf16[256,1024]{1,0:T(8,128)(2,1)} %refs_1_.2), channel_id=1, source_target_pairs={{0,2},{2,0},{1,3},{3,1},{4,6},{6,4},{5,7},{7,5},{8,10},{10,8},{9,1... | collective-permute-start | bytes 1572872 | tf_op jit(solution)/shard_map/ppermute | solution.py:558
  6.2 6.5 %collective-permute-start = (bf16[4,96,128]{2,1,0:T(8,128)(2,1)S(1)}, bf16[4,96,128]{2,1,0:T(8,128)(2,1)S(1)}, u32[]{:S(2)}, u32[]{:S(2)}) collective-permute-start(bf16[4,96,128]{2,1,0:T(8,128)(2,1)S(1)} %get-tuple-element.45.refs_2_), channel_id=1, source_target_pairs={{0,16},{16,32},{32,48},{48,64},{64,80},{80,96},{96,112},{112,128},... | collective-permute-start | bytes 294920 | tf_op jit(solution)/shard_map/ppermute | solution.py:594
  13.3 32.7 %all-to-all-start = ((bf16[16,128,256]{2,1,0:T(8,128)(2,1)}), bf16[16,128,256]{2,1,0:T(8,128)(2,1)S(1)}, u32[]{:S(2)}, u32[]{:S(2)}) async-start(bf16[16,128,256]{2,1,0:T(8,128)(2,1)} %get-tuple-element.55), calls=%async_computation | async-start | bytes 2097152 | tf_op jit(solution)/shard_map/all_to_all | solution.py:602
  20.5 10.9 %collective-permute-start.6 = (bf16[256,1024]{1,0:T(8,128)(2,1)}, bf16[256,1024]{1,0:T(8,128)(2,1)S(1)}, u32[]{:S(2)}, u32[]{:S(2)}) collective-permute-start(bf16[256,1024]{1,0:T(8,128)(2,1)} %refs_1_.2), channel_id=1, source_target_pairs={{0,1},{1,0},{2,3},{3,2},{4,5},{5,4},{6,7},{7,6},{8,9},{9,8},{10,11... | collective-permute-start | bytes 1572872 | tf_op jit(solution)/shard_map/ppermute | solution.py:558
  20.5 15.2 %collective-permute-start.5 = (bf16[256,1024]{1,0:T(8,128)(2,1)S(1)}, bf16[256,1024]{1,0:T(8,128)(2,1)S(1)}, u32[]{:S(2)}, u32[]{:S(2)}) collective-permute-start(bf16[256,1024]{1,0:T(8,128)(2,1)S(1)} %collective-permute-done.4.refs_1_), channel_id=1, source_target_pairs={{0,1},{1,0},{2,3},{3,2},{4,5},{5,4},{6,7},{7,6},{8,9},{9,8},{10,11... | collective-permute-start | bytes 1572872 | tf_op jit(solution)/shard_map/ppermute | solution.py:558
  21.0 19.9 %collective-permute-start.1 = (bf16[352,128]{1,0:T(8,128)(2,1)S(1)}, bf16[352,128]{1,0:T(8,128)(2,1)S(1)}, u32[]{:S(2)}, u32[]{:S(2)}) collective-permute-start(bf16[352,128]{1,0:T(8,128)(2,1)S(1)} %get-tuple-element.46), channel_id=1, source_target_pairs={{0,4},{4,8},{8,12},{12,0},{1,5},{5,9},{9,13},{13,1},{2,6},{6,10},{... | collective-permute-start | bytes 270344 | tf_op jit(solution)/shard_map/ppermute | solution.py:562
  24.3 16.6 %collective-permute-start.2 = (bf16[352,128]{1,0:T(8,128)(2,1)S(1)}, bf16[352,128]{1,0:T(8,128)(2,1)S(1)}, u32[]{:S(2)}, u32[]{:S(2)}) collective-permute-start(bf16[352,128]{1,0:T(8,128)(2,1)S(1)} %get-tuple-element.47), channel_id=1, source_target_pairs={{0,8},{4,12},{8,0},{12,4},{1,9},{5,13},{9,1},{13,5},{2,10},{6,14},... | collective-permute-start | bytes 270344 | tf_op jit(solution)/shard_map/ppermute | solution.py:562
  28.7 12.1 %collective-permute-start.3 = (bf16[352,128]{1,0:T(8,128)(2,1)S(1)}, bf16[352,128]{1,0:T(8,128)(2,1)S(1)}, u32[]{:S(2)}, u32[]{:S(2)}) collective-permute-start(bf16[352,128]{1,0:T(8,128)(2,1)S(1)} %get-tuple-element.48), channel_id=1, source_target_pairs={{0,12},{4,0},{8,4},{12,8},{1,13},{5,1},{9,5},{13,9},{2,14},{6,2},{... | collective-permute-start | bytes 270344 | tf_op jit(solution)/shard_map/ppermute | solution.py:562
  37.0 9.1 %collective-permute-start.9 = (bf16[256,128]{1,0:T(8,128)(2,1)S(1)}, bf16[256,128]{1,0:T(8,128)(2,1)S(1)}, u32[]{:S(2)}, u32[]{:S(2)}) collective-permute-start(bf16[256,128]{1,0:T(8,128)(2,1)S(1)} %get-tuple-element.53.refs_5_), channel_id=1, source_target_pairs={{0,12},{4,0},{8,4},{12,8},{1,13},{5,1},{9,5},{13,9},{2,14},{6,2},{... | collective-permute-start | bytes 196616 | tf_op jit(solution)/shard_map/ppermute | solution.py:562
  37.0 9.0 %collective-permute-start.8 = (bf16[256,128]{1,0:T(8,128)(2,1)S(1)}, bf16[256,128]{1,0:T(8,128)(2,1)S(1)}, u32[]{:S(2)}, u32[]{:S(2)}) collective-permute-start(bf16[256,128]{1,0:T(8,128)(2,1)S(1)} %get-tuple-element.53.refs_5_), channel_id=1, source_target_pairs={{0,8},{4,12},{8,0},{12,4},{1,9},{5,13},{9,1},{13,5},{2,10},{6,14},... | collective-permute-start | bytes 196616 | tf_op jit(solution)/shard_map/ppermute | solution.py:562
  40.9 7.6 %collective-permute-start.7 = (bf16[256,128]{1,0:T(8,128)(2,1)S(1)}, bf16[256,128]{1,0:T(8,128)(2,1)S(1)}, u32[]{:S(2)}, u32[]{:S(2)}) collective-permute-start(bf16[256,128]{1,0:T(8,128)(2,1)S(1)} %get-tuple-element.53.refs_5_), channel_id=1, source_target_pairs={{0,4},{4,8},{8,12},{12,0},{1,5},{5,9},{9,13},{13,1},{2,6},{6,10},{... | collective-permute-start | bytes 196616 | tf_op jit(solution)/shard_map/ppermute | solution.py:562
  54.8 7.7 %collective-permute-start.14 = (bf16[512,4096]{1,0:T(8,128)(2,1)}, bf16[512,4096]{1,0:T(8,128)(2,1)S(1)}, u32[]{:S(2)}, u32[]{:S(2)}) collective-permute-start(bf16[512,4096]{1,0:T(8,128)(2,1)} %refs_3_.7), channel_id=1, source_target_pairs={{0,1},{1,0},{2,3},{3,2},{4,5},{5,4},{6,7},{7,6},{8,9},{9,8},{10,11... | collective-permute-start | bytes 12582920 | tf_op jit(solution)/shard_map/ppermute | solution.py:558
  54.9 6.4 %collective-permute-start.13 = (bf16[256,384]{1,0:T(8,128)(2,1)S(1)}, bf16[256,384]{1,0:T(8,128)(2,1)S(1)}, u32[]{:S(2)}, u32[]{:S(2)}) collective-permute-start(bf16[256,384]{1,0:T(8,128)(2,1)S(1)} %get-tuple-element.62.refs_1_), channel_id=1, source_target_pairs={{0,1},{1,0},{2,3},{3,2},{4,5},{5,4},{6,7},{7,6},{8,9},{9,8},{10,11... | collective-permute-start | bytes 589832 | tf_op jit(solution)/shard_map/ppermute | solution.py:558
  55.4 10.9 %collective-permute-start.10 = (bf16[416,128]{1,0:T(8,128)(2,1)S(1)}, bf16[416,128]{1,0:T(8,128)(2,1)S(1)}, u32[]{:S(2)}, u32[]{:S(2)}) collective-permute-start(bf16[416,128]{1,0:T(8,128)(2,1)S(1)} %get-tuple-element.59), channel_id=1, source_target_pairs={{0,12},{4,0},{8,4},{12,8},{1,13},{5,1},{9,5},{13,9},{2,14},{6,2},{... | collective-permute-start | bytes 319496 | tf_op jit(solution)/shard_map/ppermute | solution.py:562
  57.1 12.0 %collective-permute-start.11 = (bf16[416,128]{1,0:T(8,128)(2,1)S(1)}, bf16[416,128]{1,0:T(8,128)(2,1)S(1)}, u32[]{:S(2)}, u32[]{:S(2)}) collective-permute-start(bf16[416,128]{1,0:T(8,128)(2,1)S(1)} %get-tuple-element.60), channel_id=1, source_target_pairs={{0,8},{4,12},{8,0},{12,4},{1,9},{5,13},{9,1},{13,5},{2,10},{6,14},... | collective-permute-start | bytes 319496 | tf_op jit(solution)/shard_map/ppermute | solution.py:562
  60.1 9.2 %collective-permute-start.12 = (bf16[416,128]{1,0:T(8,128)(2,1)S(1)}, bf16[416,128]{1,0:T(8,128)(2,1)S(1)}, u32[]{:S(2)}, u32[]{:S(2)}) collective-permute-start(bf16[416,128]{1,0:T(8,128)(2,1)S(1)} %get-tuple-element.61), channel_id=1, source_target_pairs={{0,4},{4,8},{8,12},{12,0},{1,5},{5,9},{9,13},{13,1},{2,6},{6,10},{... | collective-permute-start | bytes 319496 | tf_op jit(solution)/shard_map/ppermute | solution.py:562
  70.6 8.4 %collective-permute-start.15 = (bf16[256,128]{1,0:T(8,128)(2,1)S(1)}, bf16[256,128]{1,0:T(8,128)(2,1)S(1)}, u32[]{:S(2)}, u32[]{:S(2)}) collective-permute-start(bf16[256,128]{1,0:T(8,128)(2,1)S(1)} %get-tuple-element.65.refs_1_), channel_id=1, source_target_pairs={{0,1},{1,0},{2,3},{3,2},{4,5},{5,4},{6,7},{7,6},{8,9},{9,8},{10,11... | collective-permute-start | bytes 196616 | tf_op jit(solution)/shard_map/ppermute | solution.py:558
  81.1 25.5 %collective-permute-start.16 = (bf16[256,1024]{1,0:T(8,128)(2,1)S(1)}, bf16[256,1024]{1,0:T(8,128)(2,1)S(1)}, u32[]{:S(2)}, u32[]{:S(2)}) collective-permute-start(bf16[256,1024]{1,0:T(8,128)(2,1)S(1)} %get-tuple-element.71), channel_id=1, source_target_pairs={{0,2},{2,0},{1,3},{3,1},{4,6},{6,4},{5,7},{7,5},{8,10},{10,8},{9,1... | collective-permute-start | bytes 1572872 | tf_op jit(solution)/shard_map/ppermute | solution.py:558
  84.8 24.4 %all-to-all-start.1 = ((bf16[16,128,256]{2,1,0:T(8,128)(2,1)}), bf16[16,128,256]{2,1,0:T(8,128)(2,1)S(1)}, u32[]{:S(2)}, u32[]{:S(2)}) async-start(bf16[16,128,256]{2,1,0:T(8,128)(2,1)} %bitcast.11), calls=%async_computation.1 | async-start | bytes 2097152 | tf_op jit(solution)/shard_map/all_to_all | solution.py:693
  92.0 8.3 %collective-permute-start.17 = (bf16[256,128]{1,0:T(8,128)(2,1)S(1)}, bf16[256,128]{1,0:T(8,128)(2,1)S(1)}, u32[]{:S(2)}, u32[]{:S(2)}) collective-permute-start(bf16[256,128]{1,0:T(8,128)(2,1)S(1)} %get-tuple-element.72), channel_id=1, source_target_pairs={{0,12},{4,0},{8,4},{12,8},{1,13},{5,1},{9,5},{13,9},{2,14},{6,2},{... | collective-permute-start | bytes 196616 | tf_op jit(solution)/shard_map/ppermute | solution.py:562
  93.7 9.5 %collective-permute-start.18 = (bf16[256,128]{1,0:T(8,128)(2,1)S(1)}, bf16[256,128]{1,0:T(8,128)(2,1)S(1)}, u32[]{:S(2)}, u32[]{:S(2)}) collective-permute-start(bf16[256,128]{1,0:T(8,128)(2,1)S(1)} %get-tuple-element.73), channel_id=1, source_target_pairs={{0,8},{4,12},{8,0},{12,4},{1,9},{5,13},{9,1},{13,5},{2,10},{6,14},... | collective-permute-start | bytes 196616 | tf_op jit(solution)/shard_map/ppermute | solution.py:562
  96.8 7.4 %collective-permute-start.19 = (bf16[256,128]{1,0:T(8,128)(2,1)S(1)}, bf16[256,128]{1,0:T(8,128)(2,1)S(1)}, u32[]{:S(2)}, u32[]{:S(2)}) collective-permute-start(bf16[256,128]{1,0:T(8,128)(2,1)S(1)} %get-tuple-element.74), channel_id=1, source_target_pairs={{0,4},{4,8},{8,12},{12,0},{1,5},{5,9},{9,13},{13,1},{2,6},{6,10},{... | collective-permute-start | bytes 196616 | tf_op jit(solution)/shard_map/ppermute | solution.py:562
  97.5 11.6 %collective-permute-start.20 = (bf16[4,96,128]{2,1,0:T(8,128)(2,1)S(1)}, bf16[4,96,128]{2,1,0:T(8,128)(2,1)S(1)}, u32[]{:S(2)}, u32[]{:S(2)}) collective-permute-start(bf16[4,96,128]{2,1,0:T(8,128)(2,1)S(1)} %get-tuple-element.80), channel_id=1, source_target_pairs={{16,0},{32,16},{48,32},{64,48},{80,64},{96,80},{112,96},{128,112},... | collective-permute-start | bytes 294920 | tf_op jit(solution)/shard_map/ppermute | solution.py:665

commit v7 on v6

--- a/solution.py
+++ b/solution.py
@@ -181,21 +181,19 @@
             ref[TOK:, :] = before[d - 1]
 
 
-def grad_near_kernel(meta, up, up_c, w, order, acc, far_w, near_w, sems, far_sems):
+def grad_kernel(meta, up, up_c, up_z, up_zc, w, g0, g, own, blocks, sems, own_sem):
     zl, c = meta[2], meta[3]
-    copies = weight_blocks(w, near_w, ((zl, c), (zl, 1 - c)), sems)
-    far_copies = weight_blocks(w, far_w, ((1 - zl, c), (1 - zl, 1 - c)), far_sems)
-    copies[0].wait()
-    total = nt(up[...], near_w[0])
-    copies[1].wait()
-    acc[...] = total + nt(up_c[...], near_w[1])
-    for copy in far_copies:
-        copy.wait()
-
-
-def grad_far_kernel(meta, up_z, up_zc, far_w, acc, g0, g):
-    full = acc[...] + nt(up_z[...], far_w[0])
-    full = (full + nt(up_zc[...], far_w[1])).astype(BF)
+    places = ((zl, c), (zl, 1 - c), (1 - zl, c), (1 - zl, 1 - c))
+    mine = pltpu.make_async_copy(up, own, own_sem.at[0])
+    mine.start()
+    copies = weight_blocks(w, blocks, places, sems)
+    mine.wait()
+    total = None
+    for i, ref in enumerate((own, up_c, up_z, up_zc)):
+        copies[i].wait()
+        piece = nt(ref[...], blocks[i])
+        total = piece if total is None else total + piece
+    full = total.astype(BF)
     g0[...] = full[:, :HEAD]
     g[...] = full
 
@@ -422,17 +420,11 @@
 
 
 def strided_kernel(
-    meta, q, k, v, g, f1, f2, f3, last, o, far, dq, dkv, qs, ks, vs, dqs, dks, sems, out_s
+    meta, q, k, v, g, f1, f2, f3, last, o, far, dq, dkv, dqs, dks, out_s
 ):
     row, zh = meta[0], meta[1]
-    brought, taken = [], []
+    taken = []
     for h in range(3):
-        for i, (ref, to) in enumerate(((q, qs), (k, ks), (v, vs))):
-            at = pl.ds((h + 1) * HEAD, HEAD)
-            brought.append(
-                pltpu.make_async_copy(ref.at[:, at], to.at[h], sems.at[3 * h + i])
-            )
-            brought[-1].start()
         at = pl.ds(h * HEAD, HEAD)
         also = pl.ds((h + 3) * HEAD, HEAD)
         taken.append(
@@ -456,9 +448,7 @@
     for h in range(3):
         at = slice((h + 1) * HEAD, (h + 2) * HEAD)
         to = slice(h * HEAD, (h + 1) * HEAD)
-        for copy in brought[3 * h : 3 * h + 3]:
-            copy.wait()
-        qh, kh, vh, gh = qs[h], ks[h], vs[h], g[:, at]
+        qh, kh, vh, gh = q[:, at], k[:, at], v[:, at], g[:, at]
         kf, vf = far_rows(h), far_rows(h + 3)
         s = jnp.where(near_ok, nt(qh, kh) * SCALE, NEG)
         sf = jnp.where(far_ok, nt(qh, kf) * SCALE, NEG)
@@ -516,11 +506,8 @@
         ref[...] = total.astype(ref.dtype)
 
 
-def output_kernel(meta, keep, over, out):
+def output_kernel(meta, keep, over, dq0, dq1, dq2, dq3, strided_dq, out, qg):
     out[...] = (keep[...].astype(F32) + over[...].astype(F32)).astype(BF)
-
-
-def query_kernel(meta, dq0, dq1, dq2, dq3, strided_dq, qg):
     total = dq0[...]
     for ref in (dq1, dq2, dq3):
         total = total + whole(ref[...].astype(F32))
@@ -601,22 +588,19 @@
     kvb = after(kvb, last)
     kva = lax.all_to_all(kvb, plane, 0, 0, tiled=True).reshape(KEYS, 2 * HEAD)
     qs = [q0] + [turn(sent[d - 1], d) for d in (1, 2, 3)]
-    two_blocks = [pltpu.VMEM((2, width, quarter), BF), dma(2)]
-    acc, far_w = call(
-        grad_near_kernel,
-        [sds((TOK, width), F32), sds((2, width, quarter))],
-        [meta, upstream, up_c, out_weight, last],
-        two_blocks + [dma(2)],
-        name="attention_grad_near",
-        fetch=[1],
-        raw=[3],
-    )
     up_zc = swap(after(up_z, last), "c")
     g0, g = call(
-        grad_far_kernel,
+        grad_kernel,
         [sds((TOK, HEAD)), sds((TOK, width))],
-        [meta, up_z, up_zc, far_w, acc],
-        name="attention_grad_far",
+        [meta, upstream, up_c, up_z, up_zc, out_weight],
+        [
+            pltpu.VMEM((TOK, quarter), BF),
+            pltpu.VMEM((4, width, quarter), BF),
+            dma(4),
+            dma(1),
+        ],
+        name="attention_grad",
+        raw=[1, 5],
     )
     gs = [g0] + [turn(g0, d) for d in (1, 2, 3)]
     part = pltpu.VMEM((3, TOK, HEAD), BF)
@@ -629,9 +613,8 @@
             sds((TOK, 6 * HEAD), F32),
         ],
         [meta, queries, key_rows, value_rows, g, *qs[1:], last],
-        [part] * 4 + [pltpu.VMEM((6, TOK, HEAD), F32), dma(9), dma(9)],
+        [part, pltpu.VMEM((6, TOK, HEAD), F32), dma(9)],
         name="strided_heads",
-        raw=[1, 2, 3],
         direct=[2, 3],
     )
     o_sc = swap(o_s, "c")
@@ -659,7 +642,6 @@
         [sds((TOK, HEAD)), sds((8, ALL), F32), block, block],
         [meta, *oas, acc_out],
         name="combine",
-        store=[3],
     )
     o_fc = swap(o_f, "c")
     back = lax.ppermute(sent, plane, [(i + 1, i) for i in range(ROWS - 1)])
@@ -678,43 +660,34 @@
         ],
         name="fixed_backward",
         raw=[10, 11],
-        store=[5],
         direct=[0, 4],
     )
     send, keep = call(
         project_fixed_kernel,
         [sds((TOK, quarter))] * 2,
-        [meta, o_f, o_fc, acc_out, fixed_w, fixed_wc, dq0],
+        [meta, o_f, o_fc, acc_out, fixed_w, fixed_wc, own],
         name="project_fixed",
         raw=[6],
-        store=[1],
     )
     over = swap(send, "zl")
     dkva = lax.all_to_all(
         after(dkv, keep).reshape(ROWS, SUMM, 2 * HEAD), plane, 0, 0, tiled=True
     ).reshape(KEYS, 2 * HEAD)
     dqs = [turn(dqs[d - 1], -d) for d in (1, 2, 3)]
-    (layer_out,) = call(
+    layer_out, query_grad = call(
         output_kernel,
-        [sds((TOK, quarter))],
-        [meta, keep, over],
+        [sds((TOK, quarter)), sds((TOK, width))],
+        [meta, keep, over, dq0, *dqs, dq_s],
         name="join_output",
-        fetch=[1],
+        fetch=[7],
         flops=7 * 10**9,
-    )
-    (query_grad,) = call(
-        query_kernel,
-        [sds((TOK, width))],
-        [meta, dq0, *dqs, dq_s],
-        name="join_query_grad",
-        fetch=[1, 5],
     )
     key_grad, value_grad = call(
         final_kernel,
         [sds((TOK, width))] * 2,
         [meta, soff_t, summary_index, dkva, own, here, back, dkv_s],
         name="join_key_grads",
-        fetch=[1, 2, 4, 5, 7],
+        fetch=[1, 2, 4, 7],
     )
     return layer_out, query_grad, key_grad, value_grad
 

time: 114 us -> 111 us (0.974)
  Pallas kernels: 43.9 us -> 37.5 us
  waiting for transfers between devices: 14.9 us -> 19.2 us
    pallas_call x13 -> x11, Pallas kernels: 43.9 us -> 37.5 us  [call(): pl.pallas_call(body, out_shape=tuple((pltpu.HBM(s.shape, s.dtype) if i in...]
    ppermute x1, waiting for transfers between devices: 0.01 us -> 2.14 us  [shards(): back = lax.ppermute(sent, plane, [(i + 1, i) for i in range(ROWS - 1)])]
    ppermute x12, waiting for transfers between devices: 9.79 us -> 11.5 us  [turn(): return lax.ppermute(a, 'zh', [(i, (i + by) % GROUP) for i in range(GROUP)])]
  transfers between devices with their start and end apart: 23 -> 23, of which waited for: 9 -> 10; matrix products, arithmetic and copies ran while one was open for 0% -> 0% of each run, Pallas kernels for 28% -> 24%
where the time goes in v7:
time: 111 us; the launch traced here: 110 us
  starting transfers between devices  51.8 us (47%)
  Pallas kernels  37.5 us (34%)
  waiting for transfers between devices  19.2 us (17%)
    pallas_call x11, Pallas kernels, call(): pl.pallas_call(body, out_shape=tuple((pltpu.HBM(s.shape, s.dtype) if i in...  37.5 us
    ppermute x12, starting transfers between devices, turn(): return lax.ppermute(a, 'zh', [(i, (i + by) % GROUP) for i in range(GROUP)])  24.3 us
    ppermute x12, waiting for transfers between devices, turn(): return lax.ppermute(a, 'zh', [(i, (i + by) % GROUP) for i in range(GROUP)])  11.5 us
    all_to_all x1, starting transfers between devices, shards(): kva = lax.all_to_all(kvb, plane, 0, 0, tiled=True).reshape(KEYS, 2 * HEAD)  7.31 us
    all_to_all x1, starting transfers between devices, shards(): lax.all_to_all(after(dkv, keep).reshape(ROWS, SUMM, 2 * HEAD), plane, 0,...  7.24 us
    ppermute x7, starting transfers between devices, swap(): return lax.ppermute(a, axis, [(0, 1), (1, 0)])  7.12 us
    ppermute x1, waiting for transfers between devices, shards(): before = lax.ppermute(picks, plane, [(i, i + 1) for i in range(ROWS - 1)])  3.44 us
    ppermute x1, starting transfers between devices, shards(): before = lax.ppermute(picks, plane, [(i, i + 1) for i in range(ROWS - 1)])  3.06 us
  transfers between devices with their start and end apart: 23, of which 10 were waited for; matrix products, arithmetic and copies ran while one was open for 0% of the time, Pallas kernels for 24%

profile of v7, /device:TPU:24, one launch (start us, length us, event | category | flops | bytes accessed | tf_op | source)
XLA Modules:
  0.0 109.7 jit_solution(4805799380367181060)
XLA Ops:
  0.6 2.0 %collective-permute-start.5 = (bf16[256,1024]{1,0:T(8,128)(2,1)}, bf16[256,1024]{1,0:T(8,128)(2,1)S(1)}, u32[]{:S(2)}, u32[]{:S(2)}) collective-permute-start(bf16[256,1024]{1,0:T(8,128)(2,1)} %refs_1_.2), channel_id=1, source_target_pairs={{0,2},{2,0},{1,3},{3,1},{4,6},{6,4},{5,7},{7,5},{8,10},{10,8},{9,1... | collective-permute-start | bytes 1572872 | tf_op jit(solution)/shard_map/ppermute | solution.py:545
  2.7 3.5 %pick_rows.1 = (bf16[16,128,256]{2,1,0:T(8,128)(2,1)}, bf16[256,128]{1,0:T(8,128)(2,1)S(1)}, bf16[4,96,128]{2,1,0:T(8,128)(2,1)S(1)}) custom-call(s32[4]{0:T(128)S(1)} %pad_add_fusion.refs_0_, s32[4,64]{1,0:T(4,128)} %bitcast.12, s32[1,128]{1,0:T(1,128)} %refs_2_.5, bf16[256,512]{1,0:T(8,128)(2,1)} %refs_10_.3, bf16[256,512]{1,0:T(8,128)(2,1)} %refs_11_.3, ...), custom_call_target="tpu_custom_call" | custom-call | flops 1 | bytes 1 | tf_op jit(solution)/shard_map/pick_rows/pallas_call | solution.py:111
  6.2 3.1 %collective-permute-start = (bf16[4,96,128]{2,1,0:T(8,128)(2,1)S(1)}, bf16[4,96,128]{2,1,0:T(8,128)(2,1)S(1)}, u32[]{:S(2)}, u32[]{:S(2)}) collective-permute-start(bf16[4,96,128]{2,1,0:T(8,128)(2,1)S(1)} %get-tuple-element.45.refs_2_), channel_id=1, source_target_pairs={{0,16},{16,32},{32,48},{48,64},{64,80},{80,96},{96,112},{112,128},... | collective-permute-start | bytes 294920 | tf_op jit(solution)/shard_map/ppermute | solution.py:581
  9.3 3.4 %collective-permute-done.refs_3_ = bf16[4,96,128]{2,1,0:T(8,128)(2,1)S(1)} collective-permute-done((bf16[4,96,128]{2,1,0:T(8,128)(2,1)S(1)}, bf16[4,96,128]{2,1,0:T(8,128)(2,1)S(1)}, u32[]{:S(2)}, u32[]{:S(2)}) %collective-permute-start) | collective-permute-done | bytes 98336 | tf_op jit(solution)/shard_map/ppermute | solution.py:581
  13.3 7.3 %all-to-all-start = ((bf16[16,128,256]{2,1,0:T(8,128)(2,1)}), bf16[16,128,256]{2,1,0:T(8,128)(2,1)S(1)}, u32[]{:S(2)}, u32[]{:S(2)}) async-start(bf16[16,128,256]{2,1,0:T(8,128)(2,1)} %get-tuple-element.53), calls=%async_computation | async-start | bytes 2097152 | tf_op jit(solution)/shard_map/all_to_all | solution.py:589
  21.2 3.3 %collective-permute-start.1 = (bf16[352,128]{1,0:T(8,128)(2,1)S(1)}, bf16[352,128]{1,0:T(8,128)(2,1)S(1)}, u32[]{:S(2)}, u32[]{:S(2)}) collective-permute-start(bf16[352,128]{1,0:T(8,128)(2,1)S(1)} %get-tuple-element.46), channel_id=1, source_target_pairs={{0,4},{4,8},{8,12},{12,0},{1,5},{5,9},{9,13},{13,1},{2,6},{6,10},{... | collective-permute-start | bytes 270344 | tf_op jit(solution)/shard_map/ppermute | solution.py:549
  24.4 4.5 %collective-permute-start.2 = (bf16[352,128]{1,0:T(8,128)(2,1)S(1)}, bf16[352,128]{1,0:T(8,128)(2,1)S(1)}, u32[]{:S(2)}, u32[]{:S(2)}) collective-permute-start(bf16[352,128]{1,0:T(8,128)(2,1)S(1)} %get-tuple-element.47), channel_id=1, source_target_pairs={{0,8},{4,12},{8,0},{12,4},{1,9},{5,13},{9,1},{13,5},{2,10},{6,14},... | collective-permute-start | bytes 270344 | tf_op jit(solution)/shard_map/ppermute | solution.py:549
  28.9 2.7 %collective-permute-start.3 = (bf16[352,128]{1,0:T(8,128)(2,1)S(1)}, bf16[352,128]{1,0:T(8,128)(2,1)S(1)}, u32[]{:S(2)}, u32[]{:S(2)}) collective-permute-start(bf16[352,128]{1,0:T(8,128)(2,1)S(1)} %get-tuple-element.48), channel_id=1, source_target_pairs={{0,12},{4,0},{8,4},{12,8},{1,13},{5,1},{9,5},{13,9},{2,14},{6,2},{... | collective-permute-start | bytes 270344 | tf_op jit(solution)/shard_map/ppermute | solution.py:549
  31.6 4.1 %attention_grad.1 = (bf16[256,128]{1,0:T(8,128)(2,1)S(1)}, bf16[256,512]{1,0:T(8,128)(2,1)S(1)}) custom-call(s32[4]{0:T(128)S(1)} %pad_add_fusion.refs_0_, bf16[256,1024]{1,0:T(8,128)(2,1)} %refs_1_.2, bf16[256,1024]{1,0:T(8,128)(2,1)S(1)} %collective-permute-done.4.refs_2_, bf16[256,1024]{1,0:T(8,128)(2,1)S(1)} %collective-permute-done.5.refs_3_, ...), custom_call_target="tpu_custom_call" | custom-call | flops 1 | bytes 1 | tf_op jit(solution)/shard_map/attention_grad/pallas_call | solution.py:111
  35.8 3.8 %collective-permute-start.8 = (bf16[256,128]{1,0:T(8,128)(2,1)S(1)}, bf16[256,128]{1,0:T(8,128)(2,1)S(1)}, u32[]{:S(2)}, u32[]{:S(2)}) collective-permute-start(bf16[256,128]{1,0:T(8,128)(2,1)S(1)} %get-tuple-element.51.refs_5_), channel_id=1, source_target_pairs={{0,8},{4,12},{8,0},{12,4},{1,9},{5,13},{9,1},{13,5},{2,10},{6,14},... | collective-permute-start | bytes 196616 | tf_op jit(solution)/shard_map/ppermute | solution.py:549
  39.7 3.9 %strided_heads.1 = (bf16[256,384]{1,0:T(8,128)(2,1)S(1)}, bf16[4,96,128]{2,1,0:T(8,128)(2,1)S(1)}, bf16[256,384]{1,0:T(8,128)(2,1)}, f32[256,768]{1,0:T(8,128)}) custom-call(s32[4]{0:T(128)S(1)} %pad_add_fusion.refs_0_, bf16[256,512]{1,0:T(8,128)(2,1)S(1)} %copy-done.2, bf16[256,512]{1,0:T(8,128)(2,1)S(1)} %copy-done, bf16[256,512]{1,0:T(8,128)(2,1)S(1)} %copy-done.1, ...), custom_call_target="tpu_custom_call" | custom-call | flops 1 | bytes 1 | tf_op jit(solution)/shard_map/strided_heads/pallas_call | solution.py:111
  44.4 2.9 %collective-permute-done.7.refs_6_ = bf16[256,128]{1,0:T(8,128)(2,1)S(1)} collective-permute-done((bf16[256,128]{1,0:T(8,128)(2,1)S(1)}, bf16[256,128]{1,0:T(8,128)(2,1)S(1)}, u32[]{:S(2)}, u32[]{:S(2)}) %collective-permute-start.7) | collective-permute-done | bytes 65568 | tf_op jit(solution)/shard_map/ppermute | solution.py:549
  47.3 6.3 %fixed_forward.1 = (bf16[416,128]{1,0:T(8,128)(2,1)S(1)}, bf16[416,128]{1,0:T(8,128)(2,1)S(1)}, bf16[416,128]{1,0:T(8,128)(2,1)S(1)}, bf16[416,128]{1,0:T(8,128)(2,1)S(1)}) custom-call(s32[4]{0:T(128)S(1)} %pad_add_fusion.refs_0_, bf16[256,128]{1,0:T(8,128)(2,1)S(1)} %get-tuple-element.44.refs_1_, ...), custom_call_target="tpu_custom_call" | custom-call | flops 1 | bytes 1 | tf_op jit(solution)/shard_map/fixed_forward/pallas_call | solution.py:111
  54.2 1.3 %collective-permute-start.10 = (bf16[416,128]{1,0:T(8,128)(2,1)S(1)}, bf16[416,128]{1,0:T(8,128)(2,1)S(1)}, u32[]{:S(2)}, u32[]{:S(2)}) collective-permute-start(bf16[416,128]{1,0:T(8,128)(2,1)S(1)} %get-tuple-element.57), channel_id=1, source_target_pairs={{0,12},{4,0},{8,4},{12,8},{1,13},{5,1},{9,5},{13,9},{2,14},{6,2},{... | collective-permute-start | bytes 319496 | tf_op jit(solution)/shard_map/ppermute | solution.py:549
  55.4 3.4 %collective-permute-start.11 = (bf16[416,128]{1,0:T(8,128)(2,1)S(1)}, bf16[416,128]{1,0:T(8,128)(2,1)S(1)}, u32[]{:S(2)}, u32[]{:S(2)}) collective-permute-start(bf16[416,128]{1,0:T(8,128)(2,1)S(1)} %get-tuple-element.58), channel_id=1, source_target_pairs={{0,8},{4,12},{8,0},{12,4},{1,9},{5,13},{9,1},{13,5},{2,10},{6,14},... | collective-permute-start | bytes 319496 | tf_op jit(solution)/shard_map/ppermute | solution.py:549
  59.2 0.9 collective-permute-done.13.refs_2_
  60.1 1.3 %collective-permute-done.14.refs_4_ = bf16[512,4096]{1,0:T(8,128)(2,1)S(1)} collective-permute-done((bf16[512,4096]{1,0:T(8,128)(2,1)}, bf16[512,4096]{1,0:T(8,128)(2,1)S(1)}, u32[]{:S(2)}, u32[]{:S(2)}) %collective-permute-start.14) | collective-permute-done | bytes 4194336 | tf_op jit(solution)/shard_map/ppermute | solution.py:545
  61.3 3.2 %project_strided.1 = (f32[2,256,1024]{2,1,0:T(8,128)S(1)}, bf16[2,128,1024]{2,1,0:T(8,128)(2,1)S(1)}, bf16[2,128,1024]{2,1,0:T(8,128)(2,1)S(1)}) custom-call(s32[4]{0:T(128)S(1)} %pad_add_fusion.refs_0_, bf16[256,384]{1,0:T(8,128)(2,1)S(1)} %get-tuple-element.60.refs_1_, bf16[256,384]{1,0:T(8,128)(2,1)S(1)} %collective-permute-done.13.refs_2_, ...), custom_call_target="tpu_custom_call" | custom-call | flops 1 | bytes 1 | tf_op jit(solution)/shard_map/project_strided/pallas_call | solution.py:111
  64.6 2.8 %collective-permute-done.11.refs_3_ = bf16[416,128]{1,0:T(8,128)(2,1)S(1)} collective-permute-done((bf16[416,128]{1,0:T(8,128)(2,1)S(1)}, bf16[416,128]{1,0:T(8,128)(2,1)S(1)}, u32[]{:S(2)}, u32[]{:S(2)}) %collective-permute-start.11) | collective-permute-done | bytes 106528 | tf_op jit(solution)/shard_map/ppermute | solution.py:549
  68.0 0.8 combine.1
  69.2 8.1 %fixed_backward.1 = (bf16[2048,256]{1,0:T(8,128)(2,1)}, bf16[256,128]{1,0:T(8,128)(2,1)}, bf16[256,128]{1,0:T(8,128)(2,1)S(1)}, bf16[256,128]{1,0:T(8,128)(2,1)S...) custom-call(s32[4]{0:T(128)S(1)} %pad_add_fusion.refs_0_, bf16[256,128]{1,0:T(8,128)(2,1)S(1)} %get-tuple-element.44.refs_1_, ...), custom_call_target="tpu_custom_call" | custom-call | flops 1 | bytes 1 | tf_op jit(solution)/shard_map/fixed_backward/pallas_call | solution.py:111
  77.3 1.2 %project_fixed.1 = (bf16[256,1024]{1,0:T(8,128)(2,1)S(1)}, bf16[256,1024]{1,0:T(8,128)(2,1)S(1)}) custom-call(s32[4]{0:T(128)S(1)} %pad_add_fusion.refs_0_, bf16[256,128]{1,0:T(8,128)(2,1)S(1)} %get-tuple-element.63.refs_1_, bf16[256,128]{1,0:T(8,128)(2,1)S(1)} %collective-permute-done.15.refs_2_, f32[2,256,1024]{2,1,0:T(8,128)S(1)} %get-tuple-element.62.refs_5_.refs_3_, ...), custom_call_target="tpu_custom_call" | custom-call | flops 1 | bytes 1 | tf_op jit(solution)/shard_map/project_fixed/pallas_call | solution.py:111
  78.5 3.7 %collective-permute-start.16 = (bf16[256,1024]{1,0:T(8,128)(2,1)S(1)}, bf16[256,1024]{1,0:T(8,128)(2,1)S(1)}, u32[]{:S(2)}, u32[]{:S(2)}) collective-permute-start(bf16[256,1024]{1,0:T(8,128)(2,1)S(1)} %get-tuple-element.69), channel_id=1, source_target_pairs={{0,2},{2,0},{1,3},{3,1},{4,6},{6,4},{5,7},{7,5},{8,10},{10,8},{9,1... | collective-permute-start | bytes 1572872 | tf_op jit(solution)/shard_map/ppermute | solution.py:545
  82.2 7.2 %all-to-all-start.1 = ((bf16[16,128,256]{2,1,0:T(8,128)(2,1)}), bf16[16,128,256]{2,1,0:T(8,128)(2,1)S(1)}, u32[]{:S(2)}, u32[]{:S(2)}) async-start(bf16[16,128,256]{2,1,0:T(8,128)(2,1)} %bitcast.11), calls=%async_computation.1 | async-start | bytes 2097152 | tf_op jit(solution)/shard_map/all_to_all | solution.py:673
  89.5 1.3 %collective-permute-start.17 = (bf16[256,128]{1,0:T(8,128)(2,1)}, bf16[256,128]{1,0:T(8,128)(2,1)S(1)}, u32[]{:S(2)}, u32[]{:S(2)}) collective-permute-start(bf16[256,128]{1,0:T(8,128)(2,1)} %get-tuple-element.71), channel_id=1, source_target_pairs={{0,12},{4,0},{8,4},{12,8},{1,13},{5,1},{9,5},{13,9},{2,14},{6,2},{... | collective-permute-start | bytes 196616 | tf_op jit(solution)/shard_map/ppermute | solution.py:549
  90.7 3.5 %collective-permute-start.18 = (bf16[256,128]{1,0:T(8,128)(2,1)S(1)}, bf16[256,128]{1,0:T(8,128)(2,1)S(1)}, u32[]{:S(2)}, u32[]{:S(2)}) collective-permute-start(bf16[256,128]{1,0:T(8,128)(2,1)S(1)} %get-tuple-element.72), channel_id=1, source_target_pairs={{0,8},{4,12},{8,0},{12,4},{1,9},{5,13},{9,1},{13,5},{2,10},{6,14},... | collective-permute-start | bytes 196616 | tf_op jit(solution)/shard_map/ppermute | solution.py:549
  94.5 2.8 %collective-permute-start.20 = (bf16[4,96,128]{2,1,0:T(8,128)(2,1)S(1)}, bf16[4,96,128]{2,1,0:T(8,128)(2,1)S(1)}, u32[]{:S(2)}, u32[]{:S(2)}) collective-permute-start(bf16[4,96,128]{2,1,0:T(8,128)(2,1)S(1)} %copy-done.4), channel_id=1, source_target_pairs={{16,0},{32,16},{48,32},{64,48},{80,64},{96,80},{112,96},{128,112},... | collective-permute-start | bytes 294920 | tf_op jit(solution)/shard_map/ppermute | solution.py:647
  97.2 3.3 %collective-permute-done.18.refs_5_ = bf16[256,128]{1,0:T(8,128)(2,1)S(1)} collective-permute-done((bf16[256,128]{1,0:T(8,128)(2,1)S(1)}, bf16[256,128]{1,0:T(8,128)(2,1)S(1)}, u32[]{:S(2)}, u32[]{:S(2)}) %collective-permute-start.18) | collective-permute-done | bytes 65568 | tf_op jit(solution)/shard_map/ppermute | solution.py:549
  100.6 1.0 collective-permute-done.19.refs_6_
  101.5 2.7 %join_output.1 = (bf16[256,1024]{1,0:T(8,128)(2,1)}, bf16[256,512]{1,0:T(8,128)(2,1)}) custom-call(s32[4]{0:T(128)S(1)} %pad_add_fusion.refs_0_, bf16[256,1024]{1,0:T(8,128)(2,1)S(1)} %get-tuple-element.68.refs_1_, bf16[256,1024]{1,0:T(8,128)(2,1)S(1)} %collective-permute-done.16.refs_2_, f32[128,256]{1,0:T(8,128)S(1)} %get-tuple-element.70.refs_3_, ...), custom_call_target="tpu_custom_call" | custom-call | flops 7000000000 | bytes 1 | tf_op jit(solution)/shard_map/join_output/pallas_call | solution.py:111
  104.2 2.1 %collective-permute-done.20.refs_6_ = bf16[4,96,128]{2,1,0:T(8,128)(2,1)S(1)} collective-permute-done((bf16[4,96,128]{2,1,0:T(8,128)(2,1)S(1)}, bf16[4,96,128]{2,1,0:T(8,128)(2,1)S(1)}, u32[]{:S(2)}, u32[]{:S(2)}) %collective-permute-start.20) | collective-permute-done | bytes 98336 | tf_op jit(solution)/shard_map/ppermute | solution.py:647
  106.4 3.2 %join_key_grads.1 = (bf16[256,512]{1,0:T(8,128)(2,1)}, bf16[256,512]{1,0:T(8,128)(2,1)}) custom-call(s32[4]{0:T(128)S(1)} %pad_add_fusion.refs_0_, s32[4,64]{1,0:T(4,128)} %bitcast.13, s32[1,128]{1,0:T(1,128)} %refs_2_.5, bf16[2048,256]{1,0:T(8,128)(2,1)S(1)} %bitcast.10, f32[256,256]{1,0:T(8,128)} %get-tuple-element.67.refs_6_.refs_4_, ...), custom_call_target="tpu_custom_call" | custom-call | flops 1 | bytes 1 | tf_op jit(solution)/shard_map/join_key_grads/pallas_call | solution.py:111
  (36 shorter events, 4.3 us)
Async XLA Ops:
  0.6 20.0 %collective-permute-start.5 = (bf16[256,1024]{1,0:T(8,128)(2,1)}, bf16[256,1024]{1,0:T(8,128)(2,1)S(1)}, u32[]{:S(2)}, u32[]{:S(2)}) collective-permute-start(bf16[256,1024]{1,0:T(8,128)(2,1)} %refs_1_.2), channel_id=1, source_target_pairs={{0,2},{2,0},{1,3},{3,1},{4,6},{6,4},{5,7},{7,5},{8,10},{10,8},{9,1... | collective-permute-start | bytes 1572872 | tf_op jit(solution)/shard_map/ppermute | solution.py:545
  6.2 6.5 %collective-permute-start = (bf16[4,96,128]{2,1,0:T(8,128)(2,1)S(1)}, bf16[4,96,128]{2,1,0:T(8,128)(2,1)S(1)}, u32[]{:S(2)}, u32[]{:S(2)}) collective-permute-start(bf16[4,96,128]{2,1,0:T(8,128)(2,1)S(1)} %get-tuple-element.45.refs_2_), channel_id=1, source_target_pairs={{0,16},{16,32},{32,48},{48,64},{64,80},{80,96},{96,112},{112,128},... | collective-permute-start | bytes 294920 | tf_op jit(solution)/shard_map/ppermute | solution.py:581
  13.3 26.4 %copy-start = (bf16[256,512]{1,0:T(8,128)(2,1)S(1)}, bf16[256,512]{1,0:T(8,128)(2,1)}, u32[]{:S(2)}) copy-start(bf16[256,512]{1,0:T(8,128)(2,1)} %refs_10_.3) | copy-start | bytes 786436
  13.3 26.4 %copy-start.1 = (bf16[256,512]{1,0:T(8,128)(2,1)S(1)}, bf16[256,512]{1,0:T(8,128)(2,1)}, u32[]{:S(2)}) copy-start(bf16[256,512]{1,0:T(8,128)(2,1)} %refs_11_.3) | copy-start | bytes 786436
  13.3 26.4 %copy-start.2 = (bf16[256,512]{1,0:T(8,128)(2,1)S(1)}, bf16[256,512]{1,0:T(8,128)(2,1)}, u32[]{:S(2)}) copy-start(bf16[256,512]{1,0:T(8,128)(2,1)} %refs_1_.3) | copy-start | bytes 786436
  13.3 30.3 %all-to-all-start = ((bf16[16,128,256]{2,1,0:T(8,128)(2,1)}), bf16[16,128,256]{2,1,0:T(8,128)(2,1)S(1)}, u32[]{:S(2)}, u32[]{:S(2)}) async-start(bf16[16,128,256]{2,1,0:T(8,128)(2,1)} %get-tuple-element.53), calls=%async_computation | async-start | bytes 2097152 | tf_op jit(solution)/shard_map/all_to_all | solution.py:589
  20.6 10.9 %collective-permute-start.4 = (bf16[256,1024]{1,0:T(8,128)(2,1)}, bf16[256,1024]{1,0:T(8,128)(2,1)S(1)}, u32[]{:S(2)}, u32[]{:S(2)}) collective-permute-start(bf16[256,1024]{1,0:T(8,128)(2,1)} %refs_1_.2), channel_id=1, source_target_pairs={{0,1},{1,0},{2,3},{3,2},{4,5},{5,4},{6,7},{7,6},{8,9},{9,8},{10,11... | collective-permute-start | bytes 1572872 | tf_op jit(solution)/shard_map/ppermute | solution.py:545
  20.7 10.9 %collective-permute-start.6 = (bf16[256,1024]{1,0:T(8,128)(2,1)S(1)}, bf16[256,1024]{1,0:T(8,128)(2,1)S(1)}, u32[]{:S(2)}, u32[]{:S(2)}) collective-permute-start(bf16[256,1024]{1,0:T(8,128)(2,1)S(1)} %collective-permute-done.5.refs_3_), channel_id=1, source_target_pairs={{0,1},{1,0},{2,3},{3,2},{4,5},{5,4},{6,7},{7,6},{8,9},{9,8},{10,11... | collective-permute-start | bytes 1572872 | tf_op jit(solution)/shard_map/ppermute | solution.py:545
  21.2 18.5 %collective-permute-start.1 = (bf16[352,128]{1,0:T(8,128)(2,1)S(1)}, bf16[352,128]{1,0:T(8,128)(2,1)S(1)}, u32[]{:S(2)}, u32[]{:S(2)}) collective-permute-start(bf16[352,128]{1,0:T(8,128)(2,1)S(1)} %get-tuple-element.46), channel_id=1, source_target_pairs={{0,4},{4,8},{8,12},{12,0},{1,5},{5,9},{9,13},{13,1},{2,6},{6,10},{... | collective-permute-start | bytes 270344 | tf_op jit(solution)/shard_map/ppermute | solution.py:549
  24.4 15.2 %collective-permute-start.2 = (bf16[352,128]{1,0:T(8,128)(2,1)S(1)}, bf16[352,128]{1,0:T(8,128)(2,1)S(1)}, u32[]{:S(2)}, u32[]{:S(2)}) collective-permute-start(bf16[352,128]{1,0:T(8,128)(2,1)S(1)} %get-tuple-element.47), channel_id=1, source_target_pairs={{0,8},{4,12},{8,0},{12,4},{1,9},{5,13},{9,1},{13,5},{2,10},{6,14},... | collective-permute-start | bytes 270344 | tf_op jit(solution)/shard_map/ppermute | solution.py:549
  28.9 10.8 %collective-permute-start.3 = (bf16[352,128]{1,0:T(8,128)(2,1)S(1)}, bf16[352,128]{1,0:T(8,128)(2,1)S(1)}, u32[]{:S(2)}, u32[]{:S(2)}) collective-permute-start(bf16[352,128]{1,0:T(8,128)(2,1)S(1)} %get-tuple-element.48), channel_id=1, source_target_pairs={{0,12},{4,0},{8,4},{12,8},{1,13},{5,1},{9,5},{13,9},{2,14},{6,2},{... | collective-permute-start | bytes 270344 | tf_op jit(solution)/shard_map/ppermute | solution.py:549
  35.7 7.9 %collective-permute-start.9 = (bf16[256,128]{1,0:T(8,128)(2,1)S(1)}, bf16[256,128]{1,0:T(8,128)(2,1)S(1)}, u32[]{:S(2)}, u32[]{:S(2)}) collective-permute-start(bf16[256,128]{1,0:T(8,128)(2,1)S(1)} %get-tuple-element.51.refs_5_), channel_id=1, source_target_pairs={{0,12},{4,0},{8,4},{12,8},{1,13},{5,1},{9,5},{13,9},{2,14},{6,2},{... | collective-permute-start | bytes 196616 | tf_op jit(solution)/shard_map/ppermute | solution.py:549
  35.8 8.6 %collective-permute-start.8 = (bf16[256,128]{1,0:T(8,128)(2,1)S(1)}, bf16[256,128]{1,0:T(8,128)(2,1)S(1)}, u32[]{:S(2)}, u32[]{:S(2)}) collective-permute-start(bf16[256,128]{1,0:T(8,128)(2,1)S(1)} %get-tuple-element.51.refs_5_), channel_id=1, source_target_pairs={{0,8},{4,12},{8,0},{12,4},{1,9},{5,13},{9,1},{13,5},{2,10},{6,14},... | collective-permute-start | bytes 196616 | tf_op jit(solution)/shard_map/ppermute | solution.py:549
  39.6 7.6 %collective-permute-start.7 = (bf16[256,128]{1,0:T(8,128)(2,1)S(1)}, bf16[256,128]{1,0:T(8,128)(2,1)S(1)}, u32[]{:S(2)}, u32[]{:S(2)}) collective-permute-start(bf16[256,128]{1,0:T(8,128)(2,1)S(1)} %get-tuple-element.51.refs_5_), channel_id=1, source_target_pairs={{0,4},{4,8},{8,12},{12,0},{1,5},{5,9},{9,13},{13,1},{2,6},{6,10},{... | collective-permute-start | bytes 196616 | tf_op jit(solution)/shard_map/ppermute | solution.py:549
  53.6 7.7 %collective-permute-start.14 = (bf16[512,4096]{1,0:T(8,128)(2,1)}, bf16[512,4096]{1,0:T(8,128)(2,1)S(1)}, u32[]{:S(2)}, u32[]{:S(2)}) collective-permute-start(bf16[512,4096]{1,0:T(8,128)(2,1)} %refs_3_.5), channel_id=1, source_target_pairs={{0,1},{1,0},{2,3},{3,2},{4,5},{5,4},{6,7},{7,6},{8,9},{9,8},{10,11... | collective-permute-start | bytes 12582920 | tf_op jit(solution)/shard_map/ppermute | solution.py:545
  53.7 6.4 %collective-permute-start.13 = (bf16[256,384]{1,0:T(8,128)(2,1)S(1)}, bf16[256,384]{1,0:T(8,128)(2,1)S(1)}, u32[]{:S(2)}, u32[]{:S(2)}) collective-permute-start(bf16[256,384]{1,0:T(8,128)(2,1)S(1)} %get-tuple-element.60.refs_1_), channel_id=1, source_target_pairs={{0,1},{1,0},{2,3},{3,2},{4,5},{5,4},{6,7},{7,6},{8,9},{9,8},{10,11... | collective-permute-start | bytes 589832 | tf_op jit(solution)/shard_map/ppermute | solution.py:545
  54.2 10.4 %collective-permute-start.10 = (bf16[416,128]{1,0:T(8,128)(2,1)S(1)}, bf16[416,128]{1,0:T(8,128)(2,1)S(1)}, u32[]{:S(2)}, u32[]{:S(2)}) collective-permute-start(bf16[416,128]{1,0:T(8,128)(2,1)S(1)} %get-tuple-element.57), channel_id=1, source_target_pairs={{0,12},{4,0},{8,4},{12,8},{1,13},{5,1},{9,5},{13,9},{2,14},{6,2},{... | collective-permute-start | bytes 319496 | tf_op jit(solution)/shard_map/ppermute | solution.py:549
  55.4 11.9 %collective-permute-start.11 = (bf16[416,128]{1,0:T(8,128)(2,1)S(1)}, bf16[416,128]{1,0:T(8,128)(2,1)S(1)}, u32[]{:S(2)}, u32[]{:S(2)}) collective-permute-start(bf16[416,128]{1,0:T(8,128)(2,1)S(1)} %get-tuple-element.58), channel_id=1, source_target_pairs={{0,8},{4,12},{8,0},{12,4},{1,9},{5,13},{9,1},{13,5},{2,10},{6,14},... | collective-permute-start | bytes 319496 | tf_op jit(solution)/shard_map/ppermute | solution.py:549
  58.8 9.2 %collective-permute-start.12 = (bf16[416,128]{1,0:T(8,128)(2,1)S(1)}, bf16[416,128]{1,0:T(8,128)(2,1)S(1)}, u32[]{:S(2)}, u32[]{:S(2)}) collective-permute-start(bf16[416,128]{1,0:T(8,128)(2,1)S(1)} %get-tuple-element.59), channel_id=1, source_target_pairs={{0,4},{4,8},{8,12},{12,0},{1,5},{5,9},{9,13},{13,1},{2,6},{6,10},{... | collective-permute-start | bytes 319496 | tf_op jit(solution)/shard_map/ppermute | solution.py:549
  68.8 8.4 %copy-start.3 = (bf16[4,96,128]{2,1,0:T(8,128)(2,1)}, bf16[4,96,128]{2,1,0:T(8,128)(2,1)S(1)}, u32[]{:S(2)}) copy-start(bf16[4,96,128]{2,1,0:T(8,128)(2,1)S(1)} %get-tuple-element.80) | copy-start | bytes 294916
  68.9 8.4 %collective-permute-start.15 = (bf16[256,128]{1,0:T(8,128)(2,1)S(1)}, bf16[256,128]{1,0:T(8,128)(2,1)S(1)}, u32[]{:S(2)}, u32[]{:S(2)}) collective-permute-start(bf16[256,128]{1,0:T(8,128)(2,1)S(1)} %get-tuple-element.63.refs_1_), channel_id=1, source_target_pairs={{0,1},{1,0},{2,3},{3,2},{4,5},{5,4},{6,7},{7,6},{8,9},{9,8},{10,11... | collective-permute-start | bytes 196616 | tf_op jit(solution)/shard_map/ppermute | solution.py:545
  77.3 17.2 %copy-start.4 = (bf16[4,96,128]{2,1,0:T(8,128)(2,1)S(1)}, bf16[4,96,128]{2,1,0:T(8,128)(2,1)}, u32[]{:S(2)}) copy-start(bf16[4,96,128]{2,1,0:T(8,128)(2,1)} %copy-done.3) | copy-start | bytes 294916
  78.5 23.0 %collective-permute-start.16 = (bf16[256,1024]{1,0:T(8,128)(2,1)S(1)}, bf16[256,1024]{1,0:T(8,128)(2,1)S(1)}, u32[]{:S(2)}, u32[]{:S(2)}) collective-permute-start(bf16[256,1024]{1,0:T(8,128)(2,1)S(1)} %get-tuple-element.69), channel_id=1, source_target_pairs={{0,2},{2,0},{1,3},{3,1},{4,6},{6,4},{5,7},{7,5},{8,10},{10,8},{9,1... | collective-permute-start | bytes 1572872 | tf_op jit(solution)/shard_map/ppermute | solution.py:545
  82.2 24.1 %all-to-all-start.1 = ((bf16[16,128,256]{2,1,0:T(8,128)(2,1)}), bf16[16,128,256]{2,1,0:T(8,128)(2,1)S(1)}, u32[]{:S(2)}, u32[]{:S(2)}) async-start(bf16[16,128,256]{2,1,0:T(8,128)(2,1)} %bitcast.11), calls=%async_computation.1 | async-start | bytes 2097152 | tf_op jit(solution)/shard_map/all_to_all | solution.py:673
  89.5 7.8 %collective-permute-start.17 = (bf16[256,128]{1,0:T(8,128)(2,1)}, bf16[256,128]{1,0:T(8,128)(2,1)S(1)}, u32[]{:S(2)}, u32[]{:S(2)}) collective-permute-start(bf16[256,128]{1,0:T(8,128)(2,1)} %get-tuple-element.71), channel_id=1, source_target_pairs={{0,12},{4,0},{8,4},{12,8},{1,13},{5,1},{9,5},{13,9},{2,14},{6,2},{... | collective-permute-start | bytes 196616 | tf_op jit(solution)/shard_map/ppermute | solution.py:549
  90.7 9.8 %collective-permute-start.18 = (bf16[256,128]{1,0:T(8,128)(2,1)S(1)}, bf16[256,128]{1,0:T(8,128)(2,1)S(1)}, u32[]{:S(2)}, u32[]{:S(2)}) collective-permute-start(bf16[256,128]{1,0:T(8,128)(2,1)S(1)} %get-tuple-element.72), channel_id=1, source_target_pairs={{0,8},{4,12},{8,0},{12,4},{1,9},{5,13},{9,1},{13,5},{2,10},{6,14},... | collective-permute-start | bytes 196616 | tf_op jit(solution)/shard_map/ppermute | solution.py:549
  94.2 7.3 %collective-permute-start.19 = (bf16[256,128]{1,0:T(8,128)(2,1)S(1)}, bf16[256,128]{1,0:T(8,128)(2,1)S(1)}, u32[]{:S(2)}, u32[]{:S(2)}) collective-permute-start(bf16[256,128]{1,0:T(8,128)(2,1)S(1)} %get-tuple-element.73), channel_id=1, source_target_pairs={{0,4},{4,8},{8,12},{12,0},{1,5},{5,9},{9,13},{13,1},{2,6},{6,10},{... | collective-permute-start | bytes 196616 | tf_op jit(solution)/shard_map/ppermute | solution.py:549
  94.5 11.9 %collective-permute-start.20 = (bf16[4,96,128]{2,1,0:T(8,128)(2,1)S(1)}, bf16[4,96,128]{2,1,0:T(8,128)(2,1)S(1)}, u32[]{:S(2)}, u32[]{:S(2)}) collective-permute-start(bf16[4,96,128]{2,1,0:T(8,128)(2,1)S(1)} %copy-done.4), channel_id=1, source_target_pairs={{16,0},{32,16},{48,32},{64,48},{80,64},{96,80},{112,96},{128,112},... | collective-permute-start | bytes 294920 | tf_op jit(solution)/shard_map/ppermute | solution.py:647

commit v8 on v7

--- a/solution.py
+++ b/solution.py
@@ -369,7 +369,7 @@
 
 def backward_kernel(
     meta, q0, q1, q2, q3, g0, g1, g2, g3, kva, k, v, stat, dkv, dq1, dq2, dq3, own, dq0,
-    kv0, mine, made, sems, kv_sems
+    kv0, made, sems, kv_sems
 ):
     row, zh = meta[0], meta[1]
     brought = own_keys(k, v, kv0, kv_sems)
@@ -378,7 +378,6 @@
     for j in range(steps):
         at = pl.ds(j * TILE, TILE)
         sent.append(pltpu.make_async_copy(made.at[at], dkv.at[at], sems.at[j]))
-    sent.append(pltpu.make_async_copy(mine, own, sems.at[steps]))
     q = jnp.concatenate([q0[...], q1[:TOK], q2[:TOK], q3[:TOK]], 0)
     g = jnp.concatenate([g0[...], g1[...], g2[...], g3[...]], 0)
     log_sum, dot = stat[0:1, :], stat[1:2, :]
@@ -407,11 +406,10 @@
             key, value = kv0[:, :HEAD], kv0[:, HEAD:]
             s = jnp.where(causal_t(), nt(key, q[:TOK]) * SCALE2, NEG)
             p = jnp.exp2(s - log_sum[:, :TOK])
-            mine[:, HEAD:] = nn(p.astype(BF), g[:TOK])
+            own[:, HEAD:] = nn(p.astype(BF), g[:TOK])
             ds = (p * (nt(value, g[:TOK]) - dot[:, :TOK])).astype(BF)
-            mine[:, :HEAD] = nn(ds, q[:TOK]) * SCALE
+            own[:, :HEAD] = nn(ds, q[:TOK]) * SCALE
             dq_own = tn(key, ds)
-            sent[-1].start()
     dq0[...] = (dq[:, :TOK] + dq_own) * SCALE
     for d, ref in ((1, dq1), (2, dq2), (3, dq3)):
         ref[...] = (halves(dq[:, d * TOK : (d + 1) * TOK]) * SCALE).astype(BF)
@@ -420,22 +418,9 @@
 
 
 def strided_kernel(
-    meta, q, k, v, g, f1, f2, f3, last, o, far, dq, dkv, dqs, dks, out_s
+    meta, q, k, v, g, f1, f2, f3, last, o, far, dq, dkv
 ):
     row, zh = meta[0], meta[1]
-    taken = []
-    for h in range(3):
-        at = pl.ds(h * HEAD, HEAD)
-        also = pl.ds((h + 3) * HEAD, HEAD)
-        taken.append(
-            [
-                pltpu.make_async_copy(dqs.at[h], dq.at[:, at], out_s.at[3 * h]),
-                pltpu.make_async_copy(dks.at[h], dkv.at[:, at], out_s.at[3 * h + 1]),
-                pltpu.make_async_copy(
-                    dks.at[h + 3], dkv.at[:, also], out_s.at[3 * h + 2]
-                ),
-            ]
-        )
     slot = iota((TOK, 4 * REACH), 1) // REACH
     far_ok = (slot < zh) | (jnp.full((TOK, 4 * REACH), row, jnp.int32) > 0)
     near_ok = iota((TOK, TOK), 0) >= iota((TOK, TOK), 1)
@@ -466,20 +451,15 @@
         delta = jnp.sum(gh.astype(F32) * out.astype(F32), axis=1, keepdims=True)
         ds = (p * (nt(gh, vh) - delta) * SCALE).astype(BF)
         dsf = (pf * (nt(gh, vf) - delta) * SCALE).astype(BF)
-        dqs[h] = (nn(ds, kh) + nn(dsf, kf)).astype(BF)
-        dks[h] = tn(ds, qh)
-        dks[h + 3] = tn(w, gh)
-        for copy in taken[h]:
-            copy.start()
+        dq[:, to] = (nn(ds, kh) + nn(dsf, kf)).astype(BF)
+        dkv[:, to] = tn(ds, qh)
+        dkv[:, (h + 3) * HEAD : (h + 4) * HEAD] = tn(w, gh)
         dkf = tn(dsf, qh).astype(BF)
         dvf = tn(wf, gh).astype(BF)
         for u in range(4):
             rows = slice(u * REACH, (u + 1) * REACH)
             far[u, h * REACH : (h + 1) * REACH, :] = dkf[rows]
             far[u, (h + 3) * REACH : (h + 4) * REACH, :] = dvf[rows]
-    for group in taken:
-        for copy in group:
-            copy.wait()
 
 
 def project_strided_kernel(
@@ -584,8 +564,8 @@
         [sds((FAR, HEAD))] + [sds((TOK + FAR, HEAD))] * 3,
         [meta, q0, picks, before],
         name="bundle_queries",
-    )
-    kvb = after(kvb, last)
+        flops=3800000000,
+    )
     kva = lax.all_to_all(kvb, plane, 0, 0, tiled=True).reshape(KEYS, 2 * HEAD)
     qs = [q0] + [turn(sent[d - 1], d) for d in (1, 2, 3)]
     up_zc = swap(after(up_z, last), "c")
@@ -603,7 +583,6 @@
         raw=[1, 5],
     )
     gs = [g0] + [turn(g0, d) for d in (1, 2, 3)]
-    part = pltpu.VMEM((3, TOK, HEAD), BF)
     o_s, far, dq_s, dkv_s = call(
         strided_kernel,
         [
@@ -613,9 +592,7 @@
             sds((TOK, 6 * HEAD), F32),
         ],
         [meta, queries, key_rows, value_rows, g, *qs[1:], last],
-        [part, pltpu.VMEM((6, TOK, HEAD), F32), dma(9)],
         name="strided_heads",
-        direct=[2, 3],
     )
     o_sc = swap(o_s, "c")
     own_space = pltpu.VMEM((TOK, 2 * HEAD), BF)
@@ -653,21 +630,19 @@
         [meta, *qs, *gs, kva, key_rows, value_rows, stat],
         [
             own_space,
-            pltpu.VMEM((TOK, 2 * HEAD), F32),
             pltpu.VMEM((KEYS, 2 * HEAD), BF),
-            dma(1 + KEYS // TILE),
+            dma(KEYS // TILE),
             dma(2),
         ],
         name="fixed_backward",
         raw=[10, 11],
-        direct=[0, 4],
+        direct=[0],
     )
     send, keep = call(
         project_fixed_kernel,
         [sds((TOK, quarter))] * 2,
-        [meta, o_f, o_fc, acc_out, fixed_w, fixed_wc, own],
+        [meta, o_f, o_fc, acc_out, fixed_w, fixed_wc, dq0],
         name="project_fixed",
-        raw=[6],
     )
     over = swap(send, "zl")
     dkva = lax.all_to_all(
@@ -679,7 +654,6 @@
         [sds((TOK, quarter)), sds((TOK, width))],
         [meta, keep, over, dq0, *dqs, dq_s],
         name="join_output",
-        fetch=[7],
         flops=7 * 10**9,
     )
     key_grad, value_grad = call(
@@ -687,7 +661,7 @@
         [sds((TOK, width))] * 2,
         [meta, soff_t, summary_index, dkva, own, here, back, dkv_s],
         name="join_key_grads",
-        fetch=[1, 2, 4, 7],
+        fetch=[1, 2],
     )
     return layer_out, query_grad, key_grad, value_grad
 

time: 111 us -> 108 us (0.973)
  waiting for transfers between devices: 19.2 us -> 17 us
  Pallas kernels: 37.5 us -> 35.6 us
  local copies, waits for them, and re-layouts: 0.03 us -> 1.28 us
    ppermute x1, waiting for transfers between devices: 3.44 us -> 0.01 us  [shards(): before = lax.ppermute(picks, plane, [(i, i + 1) for i in range(ROWS - 1)])]
    pallas_call x11, Pallas kernels: 37.5 us -> 35.6 us  [call(): pl.pallas_call(body, out_shape=tuple((pltpu.HBM(s.shape, s.dtype) if i in...]
    unnamed x10 -> x14, local copies, waits for them, and re-layouts: 0.03 us -> 1.28 us
  transfers between devices with their start and end apart: 23 -> 23, of which waited for: 10 -> 9; matrix products, arithmetic and copies ran while one was open for 0% -> 0% of each run, Pallas kernels for 24% -> 23%
where the time goes in v8:
time: 108 us; the launch traced here: 107 us
  starting transfers between devices  51.8 us (48%)
  Pallas kernels  35.6 us (33%)
  waiting for transfers between devices  17 us (16%)
  local copies, waits for them, and re-layouts  1.28 us (1%)
    pallas_call x11, Pallas kernels, call(): pl.pallas_call(body, out_shape=tuple((pltpu.HBM(s.shape, s.dtype) if i in...  35.6 us
    ppermute x12, starting transfers between devices, turn(): return lax.ppermute(a, 'zh', [(i, (i + by) % GROUP) for i in range(GROUP)])  24.3 us
    ppermute x12, waiting for transfers between devices, turn(): return lax.ppermute(a, 'zh', [(i, (i + by) % GROUP) for i in range(GROUP)])  12.4 us
    all_to_all x1, starting transfers between devices, shards(): kva = lax.all_to_all(kvb, plane, 0, 0, tiled=True).reshape(KEYS, 2 * HEAD)  7.31 us
    all_to_all x1, starting transfers between devices, shards(): lax.all_to_all(after(dkv, keep).reshape(ROWS, SUMM, 2 * HEAD), plane, 0,...  7.22 us
    ppermute x7, starting transfers between devices, swap(): return lax.ppermute(a, axis, [(0, 1), (1, 0)])  7.13 us
    ppermute x1, starting transfers between devices, shards(): before = lax.ppermute(picks, plane, [(i, i + 1) for i in range(ROWS - 1)])  3.06 us
    ppermute x1, starting transfers between devices, shards(): back = lax.ppermute(sent, plane, [(i + 1, i) for i in range(ROWS - 1)])  2.75 us
  transfers between devices with their start and end apart: 23, of which 9 were waited for; matrix products, arithmetic and copies ran while one was open for 0% of the time, Pallas kernels for 23%

profile of v8, /device:TPU:24, one launch (start us, length us, event | category | flops | bytes accessed | tf_op | source)
XLA Modules:
  0.0 106.8 jit_solution(1715686756564556890)
XLA Ops:
  0.6 2.0 %collective-permute-start.5 = (bf16[256,1024]{1,0:T(8,128)(2,1)}, bf16[256,1024]{1,0:T(8,128)(2,1)S(1)}, u32[]{:S(2)}, u32[]{:S(2)}) collective-permute-start(bf16[256,1024]{1,0:T(8,128)(2,1)} %refs_1_.2), channel_id=1, source_target_pairs={{0,2},{2,0},{1,3},{3,1},{4,6},{6,4},{5,7},{7,5},{8,10},{10,8},{9,1... | collective-permute-start | bytes 1572872 | tf_op jit(solution)/shard_map/ppermute | solution.py:525
  2.7 3.5 %pick_rows.1 = (bf16[16,128,256]{2,1,0:T(8,128)(2,1)}, bf16[256,128]{1,0:T(8,128)(2,1)S(1)}, bf16[4,96,128]{2,1,0:T(8,128)(2,1)S(1)}) custom-call(s32[4]{0:T(128)S(1)} %pad_add_fusion.refs_0_, s32[4,64]{1,0:T(4,128)} %bitcast.12, s32[1,128]{1,0:T(1,128)} %refs_2_.5, bf16[256,512]{1,0:T(8,128)(2,1)} %refs_10_.3, bf16[256,512]{1,0:T(8,128)(2,1)} %refs_11_.3, ...), custom_call_target="tpu_custom_call" | custom-call | flops 1 | bytes 1 | tf_op jit(solution)/shard_map/pick_rows/pallas_call | solution.py:111
  6.2 3.1 %collective-permute-start = (bf16[4,96,128]{2,1,0:T(8,128)(2,1)S(1)}, bf16[4,96,128]{2,1,0:T(8,128)(2,1)S(1)}, u32[]{:S(2)}, u32[]{:S(2)}) collective-permute-start(bf16[4,96,128]{2,1,0:T(8,128)(2,1)S(1)} %get-tuple-element.44.refs_2_), channel_id=1, source_target_pairs={{0,16},{16,32},{32,48},{48,64},{64,80},{80,96},{96,112},{112,128},... | collective-permute-start | bytes 294920 | tf_op jit(solution)/shard_map/ppermute | solution.py:561
  9.3 7.3 %all-to-all-start = ((bf16[16,128,256]{2,1,0:T(8,128)(2,1)}), bf16[16,128,256]{2,1,0:T(8,128)(2,1)S(1)}, u32[]{:S(2)}, u32[]{:S(2)}) async-start(bf16[16,128,256]{2,1,0:T(8,128)(2,1)} %get-tuple-element.51), calls=%async_computation | async-start | bytes 2097152 | tf_op jit(solution)/shard_map/all_to_all | solution.py:569
  17.8 3.3 %collective-permute-start.1 = (bf16[352,128]{1,0:T(8,128)(2,1)S(1)}, bf16[352,128]{1,0:T(8,128)(2,1)S(1)}, u32[]{:S(2)}, u32[]{:S(2)}) collective-permute-start(bf16[352,128]{1,0:T(8,128)(2,1)S(1)} %get-tuple-element.45), channel_id=1, source_target_pairs={{0,4},{4,8},{8,12},{12,0},{1,5},{5,9},{9,13},{13,1},{2,6},{6,10},{... | collective-permute-start | bytes 270344 | tf_op jit(solution)/shard_map/ppermute | solution.py:529
  21.1 4.5 %collective-permute-start.2 = (bf16[352,128]{1,0:T(8,128)(2,1)S(1)}, bf16[352,128]{1,0:T(8,128)(2,1)S(1)}, u32[]{:S(2)}, u32[]{:S(2)}) collective-permute-start(bf16[352,128]{1,0:T(8,128)(2,1)S(1)} %get-tuple-element.46), channel_id=1, source_target_pairs={{0,8},{4,12},{8,0},{12,4},{1,9},{5,13},{9,1},{13,5},{2,10},{6,14},... | collective-permute-start | bytes 270344 | tf_op jit(solution)/shard_map/ppermute | solution.py:529
  25.6 2.7 %collective-permute-start.3 = (bf16[352,128]{1,0:T(8,128)(2,1)S(1)}, bf16[352,128]{1,0:T(8,128)(2,1)S(1)}, u32[]{:S(2)}, u32[]{:S(2)}) collective-permute-start(bf16[352,128]{1,0:T(8,128)(2,1)S(1)} %get-tuple-element.47), channel_id=1, source_target_pairs={{0,12},{4,0},{8,4},{12,8},{1,13},{5,1},{9,5},{13,9},{2,14},{6,2},{... | collective-permute-start | bytes 270344 | tf_op jit(solution)/shard_map/ppermute | solution.py:529
  28.3 4.1 %attention_grad.1 = (bf16[256,128]{1,0:T(8,128)(2,1)S(1)}, bf16[256,512]{1,0:T(8,128)(2,1)S(1)}) custom-call(s32[4]{0:T(128)S(1)} %pad_add_fusion.refs_0_, bf16[256,1024]{1,0:T(8,128)(2,1)} %refs_1_.2, bf16[256,1024]{1,0:T(8,128)(2,1)S(1)} %collective-permute-done.4.refs_2_, bf16[256,1024]{1,0:T(8,128)(2,1)S(1)} %collective-permute-done.5.refs_3_, ...), custom_call_target="tpu_custom_call" | custom-call | flops 1 | bytes 1 | tf_op jit(solution)/shard_map/attention_grad/pallas_call | solution.py:111
  32.5 3.8 %collective-permute-start.8 = (bf16[256,128]{1,0:T(8,128)(2,1)S(1)}, bf16[256,128]{1,0:T(8,128)(2,1)S(1)}, u32[]{:S(2)}, u32[]{:S(2)}) collective-permute-start(bf16[256,128]{1,0:T(8,128)(2,1)S(1)} %get-tuple-element.50.refs_5_), channel_id=1, source_target_pairs={{0,8},{4,12},{8,0},{12,4},{1,9},{5,13},{9,1},{13,5},{2,10},{6,14},... | collective-permute-start | bytes 196616 | tf_op jit(solution)/shard_map/ppermute | solution.py:529
  36.4 3.1 %strided_heads.1 = (bf16[256,384]{1,0:T(8,128)(2,1)S(1)}, bf16[4,96,128]{2,1,0:T(8,128)(2,1)S(1)}, bf16[256,384]{1,0:T(8,128)(2,1)S(1)}, f32[256,768]{1,0:T(8,128)S(1)}) custom-call(s32[4]{0:T(128)S(1)} %pad_add_fusion.refs_0_, bf16[256,512]{1,0:T(8,128)(2,1)S(1)} %copy-done.2, bf16[256,512]{1,0:T(8,128)(2,1)S(1)} %copy-done, ...), custom_call_target="tpu_custom_call" | custom-call | flops 1 | bytes 1 | tf_op jit(solution)/shard_map/strided_heads/pallas_call | solution.py:111
  39.5 1.7 %collective-permute-done.8.refs_7_ = bf16[256,128]{1,0:T(8,128)(2,1)S(1)} collective-permute-done((bf16[256,128]{1,0:T(8,128)(2,1)S(1)}, bf16[256,128]{1,0:T(8,128)(2,1)S(1)}, u32[]{:S(2)}, u32[]{:S(2)}) %collective-permute-start.8) | collective-permute-done | bytes 65568 | tf_op jit(solution)/shard_map/ppermute | solution.py:529
  41.1 2.8 %collective-permute-done.7.refs_6_ = bf16[256,128]{1,0:T(8,128)(2,1)S(1)} collective-permute-done((bf16[256,128]{1,0:T(8,128)(2,1)S(1)}, bf16[256,128]{1,0:T(8,128)(2,1)S(1)}, u32[]{:S(2)}, u32[]{:S(2)}) %collective-permute-start.7) | collective-permute-done | bytes 65568 | tf_op jit(solution)/shard_map/ppermute | solution.py:529
  44.0 6.3 %fixed_forward.1 = (bf16[416,128]{1,0:T(8,128)(2,1)S(1)}, bf16[416,128]{1,0:T(8,128)(2,1)S(1)}, bf16[416,128]{1,0:T(8,128)(2,1)S(1)}, bf16[416,128]{1,0:T(8,128)(2,1)S(1)}) custom-call(s32[4]{0:T(128)S(1)} %pad_add_fusion.refs_0_, bf16[256,128]{1,0:T(8,128)(2,1)S(1)} %get-tuple-element.43.refs_1_, ...), custom_call_target="tpu_custom_call" | custom-call | flops 1 | bytes 1 | tf_op jit(solution)/shard_map/fixed_forward/pallas_call | solution.py:111
  50.8 1.2 %collective-permute-start.10 = (bf16[416,128]{1,0:T(8,128)(2,1)S(1)}, bf16[416,128]{1,0:T(8,128)(2,1)S(1)}, u32[]{:S(2)}, u32[]{:S(2)}) collective-permute-start(bf16[416,128]{1,0:T(8,128)(2,1)S(1)} %get-tuple-element.55), channel_id=1, source_target_pairs={{0,12},{4,0},{8,4},{12,8},{1,13},{5,1},{9,5},{13,9},{2,14},{6,2},{... | collective-permute-start | bytes 319496 | tf_op jit(solution)/shard_map/ppermute | solution.py:529
  52.0 3.4 %collective-permute-start.11 = (bf16[416,128]{1,0:T(8,128)(2,1)S(1)}, bf16[416,128]{1,0:T(8,128)(2,1)S(1)}, u32[]{:S(2)}, u32[]{:S(2)}) collective-permute-start(bf16[416,128]{1,0:T(8,128)(2,1)S(1)} %get-tuple-element.56), channel_id=1, source_target_pairs={{0,8},{4,12},{8,0},{12,4},{1,9},{5,13},{9,1},{13,5},{2,10},{6,14},... | collective-permute-start | bytes 319496 | tf_op jit(solution)/shard_map/ppermute | solution.py:529
  55.8 0.9 collective-permute-done.13.refs_2_
  56.7 1.3 %collective-permute-done.14.refs_4_ = bf16[512,4096]{1,0:T(8,128)(2,1)S(1)} collective-permute-done((bf16[512,4096]{1,0:T(8,128)(2,1)}, bf16[512,4096]{1,0:T(8,128)(2,1)S(1)}, u32[]{:S(2)}, u32[]{:S(2)}) %collective-permute-start.14) | collective-permute-done | bytes 4194336 | tf_op jit(solution)/shard_map/ppermute | solution.py:525
  58.0 3.2 %project_strided.1 = (f32[2,256,1024]{2,1,0:T(8,128)S(1)}, bf16[2,128,1024]{2,1,0:T(8,128)(2,1)S(1)}, bf16[2,128,1024]{2,1,0:T(8,128)(2,1)S(1)}) custom-call(s32[4]{0:T(128)S(1)} %pad_add_fusion.refs_0_, bf16[256,384]{1,0:T(8,128)(2,1)S(1)} %get-tuple-element.58.refs_1_, bf16[256,384]{1,0:T(8,128)(2,1)S(1)} %collective-permute-done.13.refs_2_, ...), custom_call_target="tpu_custom_call" | custom-call | flops 1 | bytes 1 | tf_op jit(solution)/shard_map/project_strided/pallas_call | solution.py:111
  61.2 2.7 %collective-permute-done.11.refs_3_ = bf16[416,128]{1,0:T(8,128)(2,1)S(1)} collective-permute-done((bf16[416,128]{1,0:T(8,128)(2,1)S(1)}, bf16[416,128]{1,0:T(8,128)(2,1)S(1)}, u32[]{:S(2)}, u32[]{:S(2)}) %collective-permute-start.11) | collective-permute-done | bytes 106528 | tf_op jit(solution)/shard_map/ppermute | solution.py:529
  64.7 0.8 combine.1
  65.8 7.4 %fixed_backward.1 = (bf16[2048,256]{1,0:T(8,128)(2,1)}, bf16[256,128]{1,0:T(8,128)(2,1)S(1)}, bf16[256,128]{1,0:T(8,128)(2,1)S(1)}, bf16[256,128]{1,0:T(8,128)(2...) custom-call(s32[4]{0:T(128)S(1)} %pad_add_fusion.refs_0_, bf16[256,128]{1,0:T(8,128)(2,1)S(1)} %get-tuple-element.43.refs_1_, ...), custom_call_target="tpu_custom_call" | custom-call | flops 1 | bytes 1 | tf_op jit(solution)/shard_map/fixed_backward/pallas_call | solution.py:111
  74.5 1.8 %project_fixed.1 = (bf16[256,1024]{1,0:T(8,128)(2,1)}, bf16[256,1024]{1,0:T(8,128)(2,1)S(1)}) custom-call(s32[4]{0:T(128)S(1)} %pad_add_fusion.refs_0_, bf16[256,128]{1,0:T(8,128)(2,1)S(1)} %get-tuple-element.61.refs_1_, bf16[256,128]{1,0:T(8,128)(2,1)S(1)} %collective-permute-done.15.refs_2_, f32[2,256,1024]{2,1,0:T(8,128)S(1)} %get-tuple-element.60.refs_5_.refs_3_, ...), custom_call_target="tpu_custom_call" | custom-call | flops 1 | bytes 1 | tf_op jit(solution)/shard_map/project_fixed/pallas_call | solution.py:111
  76.3 3.6 %collective-permute-start.16 = (bf16[256,1024]{1,0:T(8,128)(2,1)}, bf16[256,1024]{1,0:T(8,128)(2,1)}, u32[]{:S(2)}, u32[]{:S(2)}) collective-permute-start(bf16[256,1024]{1,0:T(8,128)(2,1)} %get-tuple-element.67), channel_id=1, source_target_pairs={{0,2},{2,0},{1,3},{3,1},{4,6},{6,4},{5,7},{7,5},{8,10},{10,8},{9,1... | collective-permute-start | bytes 1572872 | tf_op jit(solution)/shard_map/ppermute | solution.py:525
  79.9 7.2 %all-to-all-start.1 = ((bf16[16,128,256]{2,1,0:T(8,128)(2,1)}), bf16[16,128,256]{2,1,0:T(8,128)(2,1)S(1)}, u32[]{:S(2)}, u32[]{:S(2)}) async-start(bf16[16,128,256]{2,1,0:T(8,128)(2,1)} %bitcast.11), calls=%async_computation.1 | async-start | bytes 2097152 | tf_op jit(solution)/shard_map/all_to_all | solution.py:648
  87.1 1.3 %collective-permute-start.17 = (bf16[256,128]{1,0:T(8,128)(2,1)S(1)}, bf16[256,128]{1,0:T(8,128)(2,1)S(1)}, u32[]{:S(2)}, u32[]{:S(2)}) collective-permute-start(bf16[256,128]{1,0:T(8,128)(2,1)S(1)} %copy-done.6), channel_id=1, source_target_pairs={{0,12},{4,0},{8,4},{12,8},{1,13},{5,1},{9,5},{13,9},{2,14},{6,2},{... | collective-permute-start | bytes 196616 | tf_op jit(solution)/shard_map/ppermute | solution.py:529
  88.4 3.5 %collective-permute-start.18 = (bf16[256,128]{1,0:T(8,128)(2,1)S(1)}, bf16[256,128]{1,0:T(8,128)(2,1)S(1)}, u32[]{:S(2)}, u32[]{:S(2)}) collective-permute-start(bf16[256,128]{1,0:T(8,128)(2,1)S(1)} %copy-done.4), channel_id=1, source_target_pairs={{0,8},{4,12},{8,0},{12,4},{1,9},{5,13},{9,1},{13,5},{2,10},{6,14},... | collective-permute-start | bytes 196616 | tf_op jit(solution)/shard_map/ppermute | solution.py:529
  92.2 2.8 %collective-permute-start.20 = (bf16[4,96,128]{2,1,0:T(8,128)(2,1)S(1)}, bf16[4,96,128]{2,1,0:T(8,128)(2,1)S(1)}, u32[]{:S(2)}, u32[]{:S(2)}) collective-permute-start(bf16[4,96,128]{2,1,0:T(8,128)(2,1)S(1)} %get-tuple-element.78), channel_id=1, source_target_pairs={{16,0},{32,16},{48,32},{64,48},{80,64},{96,80},{112,96},{128,112},... | collective-permute-start | bytes 294920 | tf_op jit(solution)/shard_map/ppermute | solution.py:624
  94.9 3.5 %collective-permute-done.18.refs_5_ = bf16[256,128]{1,0:T(8,128)(2,1)S(1)} collective-permute-done((bf16[256,128]{1,0:T(8,128)(2,1)S(1)}, bf16[256,128]{1,0:T(8,128)(2,1)S(1)}, u32[]{:S(2)}, u32[]{:S(2)}) %collective-permute-start.18) | collective-permute-done | bytes 65568 | tf_op jit(solution)/shard_map/ppermute | solution.py:529
  98.5 0.9 collective-permute-done.19.refs_6_
  99.4 2.3 %join_output.1 = (bf16[256,1024]{1,0:T(8,128)(2,1)}, bf16[256,512]{1,0:T(8,128)(2,1)}) custom-call(s32[4]{0:T(128)S(1)} %pad_add_fusion.refs_0_, bf16[256,1024]{1,0:T(8,128)(2,1)S(1)} %get-tuple-element.66.refs_1_, bf16[256,1024]{1,0:T(8,128)(2,1)} %collective-permute-done.16.refs_2_, f32[128,256]{1,0:T(8,128)S(1)} %get-tuple-element.65.refs_6_.refs_3_, ...), custom_call_target="tpu_custom_call" | custom-call | flops 7000000000 | bytes 1 | tf_op jit(solution)/shard_map/join_output/pallas_call | solution.py:111
  101.6 2.4 %collective-permute-done.20.refs_6_ = bf16[4,96,128]{2,1,0:T(8,128)(2,1)S(1)} collective-permute-done((bf16[4,96,128]{2,1,0:T(8,128)(2,1)S(1)}, bf16[4,96,128]{2,1,0:T(8,128)(2,1)S(1)}, u32[]{:S(2)}, u32[]{:S(2)}) %collective-permute-start.20) | collective-permute-done | bytes 98336 | tf_op jit(solution)/shard_map/ppermute | solution.py:624
  104.0 2.6 %join_key_grads.1 = (bf16[256,512]{1,0:T(8,128)(2,1)}, bf16[256,512]{1,0:T(8,128)(2,1)}) custom-call(s32[4]{0:T(128)S(1)} %pad_add_fusion.refs_0_, s32[4,64]{1,0:T(4,128)} %bitcast.13, s32[1,128]{1,0:T(1,128)} %refs_2_.5, bf16[2048,256]{1,0:T(8,128)(2,1)S(1)} %bitcast.10, f32[256,256]{1,0:T(8,128)S(1)} %get-tuple-element.76.refs_4_, ...), custom_call_target="tpu_custom_call" | custom-call | flops 1 | bytes 1 | tf_op jit(solution)/shard_map/join_key_grads/pallas_call | solution.py:111
  (40 shorter events, 4.8 us)
Async XLA Ops:
  0.6 16.6 %collective-permute-start.5 = (bf16[256,1024]{1,0:T(8,128)(2,1)}, bf16[256,1024]{1,0:T(8,128)(2,1)S(1)}, u32[]{:S(2)}, u32[]{:S(2)}) collective-permute-start(bf16[256,1024]{1,0:T(8,128)(2,1)} %refs_1_.2), channel_id=1, source_target_pairs={{0,2},{2,0},{1,3},{3,1},{4,6},{6,4},{5,7},{7,5},{8,10},{10,8},{9,1... | collective-permute-start | bytes 1572872 | tf_op jit(solution)/shard_map/ppermute | solution.py:525
  6.2 10.4 %collective-permute-start = (bf16[4,96,128]{2,1,0:T(8,128)(2,1)S(1)}, bf16[4,96,128]{2,1,0:T(8,128)(2,1)S(1)}, u32[]{:S(2)}, u32[]{:S(2)}) collective-permute-start(bf16[4,96,128]{2,1,0:T(8,128)(2,1)S(1)} %get-tuple-element.44.refs_2_), channel_id=1, source_target_pairs={{0,16},{16,32},{32,48},{48,64},{64,80},{80,96},{96,112},{112,128},... | collective-permute-start | bytes 294920 | tf_op jit(solution)/shard_map/ppermute | solution.py:561
  9.3 30.2 %all-to-all-start = ((bf16[16,128,256]{2,1,0:T(8,128)(2,1)}), bf16[16,128,256]{2,1,0:T(8,128)(2,1)S(1)}, u32[]{:S(2)}, u32[]{:S(2)}) async-start(bf16[16,128,256]{2,1,0:T(8,128)(2,1)} %get-tuple-element.51), calls=%async_computation | async-start | bytes 2097152 | tf_op jit(solution)/shard_map/all_to_all | solution.py:569
  16.6 11.7 %collective-permute-start.4 = (bf16[256,1024]{1,0:T(8,128)(2,1)}, bf16[256,1024]{1,0:T(8,128)(2,1)S(1)}, u32[]{:S(2)}, u32[]{:S(2)}) collective-permute-start(bf16[256,1024]{1,0:T(8,128)(2,1)} %refs_1_.2), channel_id=1, source_target_pairs={{0,1},{1,0},{2,3},{3,2},{4,5},{5,4},{6,7},{7,6},{8,9},{9,8},{10,11... | collective-permute-start | bytes 1572872 | tf_op jit(solution)/shard_map/ppermute | solution.py:525
  17.2 19.1 %copy-start = (bf16[256,512]{1,0:T(8,128)(2,1)S(1)}, bf16[256,512]{1,0:T(8,128)(2,1)}, u32[]{:S(2)}) copy-start(bf16[256,512]{1,0:T(8,128)(2,1)} %refs_10_.3) | copy-start | bytes 786436
  17.2 19.1 %copy-start.1 = (bf16[256,512]{1,0:T(8,128)(2,1)S(1)}, bf16[256,512]{1,0:T(8,128)(2,1)}, u32[]{:S(2)}) copy-start(bf16[256,512]{1,0:T(8,128)(2,1)} %refs_11_.3) | copy-start | bytes 786436
  17.2 19.1 %copy-start.2 = (bf16[256,512]{1,0:T(8,128)(2,1)S(1)}, bf16[256,512]{1,0:T(8,128)(2,1)}, u32[]{:S(2)}) copy-start(bf16[256,512]{1,0:T(8,128)(2,1)} %refs_1_.3) | copy-start | bytes 786436
  17.2 11.0 %collective-permute-start.6 = (bf16[256,1024]{1,0:T(8,128)(2,1)S(1)}, bf16[256,1024]{1,0:T(8,128)(2,1)S(1)}, u32[]{:S(2)}, u32[]{:S(2)}) collective-permute-start(bf16[256,1024]{1,0:T(8,128)(2,1)S(1)} %collective-permute-done.5.refs_3_), channel_id=1, source_target_pairs={{0,1},{1,0},{2,3},{3,2},{4,5},{5,4},{6,7},{7,6},{8,9},{9,8},{10,11... | collective-permute-start | bytes 1572872 | tf_op jit(solution)/shard_map/ppermute | solution.py:525
  17.8 18.5 %collective-permute-start.1 = (bf16[352,128]{1,0:T(8,128)(2,1)S(1)}, bf16[352,128]{1,0:T(8,128)(2,1)S(1)}, u32[]{:S(2)}, u32[]{:S(2)}) collective-permute-start(bf16[352,128]{1,0:T(8,128)(2,1)S(1)} %get-tuple-element.45), channel_id=1, source_target_pairs={{0,4},{4,8},{8,12},{12,0},{1,5},{5,9},{9,13},{13,1},{2,6},{6,10},{... | collective-permute-start | bytes 270344 | tf_op jit(solution)/shard_map/ppermute | solution.py:529
  21.1 15.2 %collective-permute-start.2 = (bf16[352,128]{1,0:T(8,128)(2,1)S(1)}, bf16[352,128]{1,0:T(8,128)(2,1)S(1)}, u32[]{:S(2)}, u32[]{:S(2)}) collective-permute-start(bf16[352,128]{1,0:T(8,128)(2,1)S(1)} %get-tuple-element.46), channel_id=1, source_target_pairs={{0,8},{4,12},{8,0},{12,4},{1,9},{5,13},{9,1},{13,5},{2,10},{6,14},... | collective-permute-start | bytes 270344 | tf_op jit(solution)/shard_map/ppermute | solution.py:529
  25.6 10.8 %collective-permute-start.3 = (bf16[352,128]{1,0:T(8,128)(2,1)S(1)}, bf16[352,128]{1,0:T(8,128)(2,1)S(1)}, u32[]{:S(2)}, u32[]{:S(2)}) collective-permute-start(bf16[352,128]{1,0:T(8,128)(2,1)S(1)} %get-tuple-element.47), channel_id=1, source_target_pairs={{0,12},{4,0},{8,4},{12,8},{1,13},{5,1},{9,5},{13,9},{2,14},{6,2},{... | collective-permute-start | bytes 270344 | tf_op jit(solution)/shard_map/ppermute | solution.py:529
  32.4 7.0 %collective-permute-start.9 = (bf16[256,128]{1,0:T(8,128)(2,1)S(1)}, bf16[256,128]{1,0:T(8,128)(2,1)S(1)}, u32[]{:S(2)}, u32[]{:S(2)}) collective-permute-start(bf16[256,128]{1,0:T(8,128)(2,1)S(1)} %get-tuple-element.50.refs_5_), channel_id=1, source_target_pairs={{0,12},{4,0},{8,4},{12,8},{1,13},{5,1},{9,5},{13,9},{2,14},{6,2},{... | collective-permute-start | bytes 196616 | tf_op jit(solution)/shard_map/ppermute | solution.py:529
  32.5 8.6 %collective-permute-start.8 = (bf16[256,128]{1,0:T(8,128)(2,1)S(1)}, bf16[256,128]{1,0:T(8,128)(2,1)S(1)}, u32[]{:S(2)}, u32[]{:S(2)}) collective-permute-start(bf16[256,128]{1,0:T(8,128)(2,1)S(1)} %get-tuple-element.50.refs_5_), channel_id=1, source_target_pairs={{0,8},{4,12},{8,0},{12,4},{1,9},{5,13},{9,1},{13,5},{2,10},{6,14},... | collective-permute-start | bytes 196616 | tf_op jit(solution)/shard_map/ppermute | solution.py:529
  36.3 7.6 %collective-permute-start.7 = (bf16[256,128]{1,0:T(8,128)(2,1)S(1)}, bf16[256,128]{1,0:T(8,128)(2,1)S(1)}, u32[]{:S(2)}, u32[]{:S(2)}) collective-permute-start(bf16[256,128]{1,0:T(8,128)(2,1)S(1)} %get-tuple-element.50.refs_5_), channel_id=1, source_target_pairs={{0,4},{4,8},{8,12},{12,0},{1,5},{5,9},{9,13},{13,1},{2,6},{6,10},{... | collective-permute-start | bytes 196616 | tf_op jit(solution)/shard_map/ppermute | solution.py:529
  50.2 7.7 %collective-permute-start.14 = (bf16[512,4096]{1,0:T(8,128)(2,1)}, bf16[512,4096]{1,0:T(8,128)(2,1)S(1)}, u32[]{:S(2)}, u32[]{:S(2)}) collective-permute-start(bf16[512,4096]{1,0:T(8,128)(2,1)} %refs_3_.5), channel_id=1, source_target_pairs={{0,1},{1,0},{2,3},{3,2},{4,5},{5,4},{6,7},{7,6},{8,9},{9,8},{10,11... | collective-permute-start | bytes 12582920 | tf_op jit(solution)/shard_map/ppermute | solution.py:525
  50.3 6.4 %collective-permute-start.13 = (bf16[256,384]{1,0:T(8,128)(2,1)S(1)}, bf16[256,384]{1,0:T(8,128)(2,1)S(1)}, u32[]{:S(2)}, u32[]{:S(2)}) collective-permute-start(bf16[256,384]{1,0:T(8,128)(2,1)S(1)} %get-tuple-element.58.refs_1_), channel_id=1, source_target_pairs={{0,1},{1,0},{2,3},{3,2},{4,5},{5,4},{6,7},{7,6},{8,9},{9,8},{10,11... | collective-permute-start | bytes 589832 | tf_op jit(solution)/shard_map/ppermute | solution.py:525
  50.8 10.4 %collective-permute-start.10 = (bf16[416,128]{1,0:T(8,128)(2,1)S(1)}, bf16[416,128]{1,0:T(8,128)(2,1)S(1)}, u32[]{:S(2)}, u32[]{:S(2)}) collective-permute-start(bf16[416,128]{1,0:T(8,128)(2,1)S(1)} %get-tuple-element.55), channel_id=1, source_target_pairs={{0,12},{4,0},{8,4},{12,8},{1,13},{5,1},{9,5},{13,9},{2,14},{6,2},{... | collective-permute-start | bytes 319496 | tf_op jit(solution)/shard_map/ppermute | solution.py:529
  52.0 11.9 %collective-permute-start.11 = (bf16[416,128]{1,0:T(8,128)(2,1)S(1)}, bf16[416,128]{1,0:T(8,128)(2,1)S(1)}, u32[]{:S(2)}, u32[]{:S(2)}) collective-permute-start(bf16[416,128]{1,0:T(8,128)(2,1)S(1)} %get-tuple-element.56), channel_id=1, source_target_pairs={{0,8},{4,12},{8,0},{12,4},{1,9},{5,13},{9,1},{13,5},{2,10},{6,14},... | collective-permute-start | bytes 319496 | tf_op jit(solution)/shard_map/ppermute | solution.py:529
  55.5 9.2 %collective-permute-start.12 = (bf16[416,128]{1,0:T(8,128)(2,1)S(1)}, bf16[416,128]{1,0:T(8,128)(2,1)S(1)}, u32[]{:S(2)}, u32[]{:S(2)}) collective-permute-start(bf16[416,128]{1,0:T(8,128)(2,1)S(1)} %get-tuple-element.57), channel_id=1, source_target_pairs={{0,4},{4,8},{8,12},{12,0},{1,5},{5,9},{9,13},{13,1},{2,6},{6,10},{... | collective-permute-start | bytes 319496 | tf_op jit(solution)/shard_map/ppermute | solution.py:529
  65.5 9.0 %collective-permute-start.15 = (bf16[256,128]{1,0:T(8,128)(2,1)S(1)}, bf16[256,128]{1,0:T(8,128)(2,1)S(1)}, u32[]{:S(2)}, u32[]{:S(2)}) collective-permute-start(bf16[256,128]{1,0:T(8,128)(2,1)S(1)} %get-tuple-element.61.refs_1_), channel_id=1, source_target_pairs={{0,1},{1,0},{2,3},{3,2},{4,5},{5,4},{6,7},{7,6},{8,9},{9,8},{10,11... | collective-permute-start | bytes 196616 | tf_op jit(solution)/shard_map/ppermute | solution.py:525
  73.2 0.6 copy-start.3
  73.9 0.6 copy-start.5
  74.5 12.6 %copy-start.6 = (bf16[256,128]{1,0:T(8,128)(2,1)S(1)}, bf16[256,128]{1,0:T(8,128)(2,1)}, u32[]{:S(2)}) copy-start(bf16[256,128]{1,0:T(8,128)(2,1)} %copy-done.5) | copy-start | bytes 196612
  74.5 13.9 %copy-start.4 = (bf16[256,128]{1,0:T(8,128)(2,1)S(1)}, bf16[256,128]{1,0:T(8,128)(2,1)}, u32[]{:S(2)}) copy-start(bf16[256,128]{1,0:T(8,128)(2,1)} %copy-done.3) | copy-start | bytes 196612
  76.3 23.1 %collective-permute-start.16 = (bf16[256,1024]{1,0:T(8,128)(2,1)}, bf16[256,1024]{1,0:T(8,128)(2,1)}, u32[]{:S(2)}, u32[]{:S(2)}) collective-permute-start(bf16[256,1024]{1,0:T(8,128)(2,1)} %get-tuple-element.67), channel_id=1, source_target_pairs={{0,2},{2,0},{1,3},{3,1},{4,6},{6,4},{5,7},{7,5},{8,10},{10,8},{9,1... | collective-permute-start | bytes 1572872 | tf_op jit(solution)/shard_map/ppermute | solution.py:525
  79.9 24.1 %all-to-all-start.1 = ((bf16[16,128,256]{2,1,0:T(8,128)(2,1)}), bf16[16,128,256]{2,1,0:T(8,128)(2,1)S(1)}, u32[]{:S(2)}, u32[]{:S(2)}) async-start(bf16[16,128,256]{2,1,0:T(8,128)(2,1)} %bitcast.11), calls=%async_computation.1 | async-start | bytes 2097152 | tf_op jit(solution)/shard_map/all_to_all | solution.py:648
  87.1 7.8 %collective-permute-start.17 = (bf16[256,128]{1,0:T(8,128)(2,1)S(1)}, bf16[256,128]{1,0:T(8,128)(2,1)S(1)}, u32[]{:S(2)}, u32[]{:S(2)}) collective-permute-start(bf16[256,128]{1,0:T(8,128)(2,1)S(1)} %copy-done.6), channel_id=1, source_target_pairs={{0,12},{4,0},{8,4},{12,8},{1,13},{5,1},{9,5},{13,9},{2,14},{6,2},{... | collective-permute-start | bytes 196616 | tf_op jit(solution)/shard_map/ppermute | solution.py:529
  88.4 10.1 %collective-permute-start.18 = (bf16[256,128]{1,0:T(8,128)(2,1)S(1)}, bf16[256,128]{1,0:T(8,128)(2,1)S(1)}, u32[]{:S(2)}, u32[]{:S(2)}) collective-permute-start(bf16[256,128]{1,0:T(8,128)(2,1)S(1)} %copy-done.4), channel_id=1, source_target_pairs={{0,8},{4,12},{8,0},{12,4},{1,9},{5,13},{9,1},{13,5},{2,10},{6,14},... | collective-permute-start | bytes 196616 | tf_op jit(solution)/shard_map/ppermute | solution.py:529
  91.9 7.4 %collective-permute-start.19 = (bf16[256,128]{1,0:T(8,128)(2,1)S(1)}, bf16[256,128]{1,0:T(8,128)(2,1)S(1)}, u32[]{:S(2)}, u32[]{:S(2)}) collective-permute-start(bf16[256,128]{1,0:T(8,128)(2,1)S(1)} %get-tuple-element.70), channel_id=1, source_target_pairs={{0,4},{4,8},{8,12},{12,0},{1,5},{5,9},{9,13},{13,1},{2,6},{6,10},{... | collective-permute-start | bytes 196616 | tf_op jit(solution)/shard_map/ppermute | solution.py:529
  92.2 11.9 %collective-permute-start.20 = (bf16[4,96,128]{2,1,0:T(8,128)(2,1)S(1)}, bf16[4,96,128]{2,1,0:T(8,128)(2,1)S(1)}, u32[]{:S(2)}, u32[]{:S(2)}) collective-permute-start(bf16[4,96,128]{2,1,0:T(8,128)(2,1)S(1)} %get-tuple-element.78), channel_id=1, source_target_pairs={{16,0},{32,16},{48,32},{64,48},{80,64},{96,80},{112,96},{128,112},... | collective-permute-start | bytes 294920 | tf_op jit(solution)/shard_map/ppermute | solution.py:624

commit v9 on v8

--- a/solution.py
+++ b/solution.py
@@ -369,7 +369,7 @@
 
 def backward_kernel(
     meta, q0, q1, q2, q3, g0, g1, g2, g3, kva, k, v, stat, dkv, dq1, dq2, dq3, own, dq0,
-    kv0, made, sems, kv_sems
+    kv0, mine, made, sems, kv_sems
 ):
     row, zh = meta[0], meta[1]
     brought = own_keys(k, v, kv0, kv_sems)
@@ -378,6 +378,7 @@
     for j in range(steps):
         at = pl.ds(j * TILE, TILE)
         sent.append(pltpu.make_async_copy(made.at[at], dkv.at[at], sems.at[j]))
+    sent.append(pltpu.make_async_copy(mine, own, sems.at[steps]))
     q = jnp.concatenate([q0[...], q1[:TOK], q2[:TOK], q3[:TOK]], 0)
     g = jnp.concatenate([g0[...], g1[...], g2[...], g3[...]], 0)
     log_sum, dot = stat[0:1, :], stat[1:2, :]
@@ -406,10 +407,11 @@
             key, value = kv0[:, :HEAD], kv0[:, HEAD:]
             s = jnp.where(causal_t(), nt(key, q[:TOK]) * SCALE2, NEG)
             p = jnp.exp2(s - log_sum[:, :TOK])
-            own[:, HEAD:] = nn(p.astype(BF), g[:TOK])
+            mine[:, HEAD:] = nn(p.astype(BF), g[:TOK])
             ds = (p * (nt(value, g[:TOK]) - dot[:, :TOK])).astype(BF)
-            own[:, :HEAD] = nn(ds, q[:TOK]) * SCALE
+            mine[:, :HEAD] = nn(ds, q[:TOK]) * SCALE
             dq_own = tn(key, ds)
+            sent[-1].start()
     dq0[...] = (dq[:, :TOK] + dq_own) * SCALE
     for d, ref in ((1, dq1), (2, dq2), (3, dq3)):
         ref[...] = (halves(dq[:, d * TOK : (d + 1) * TOK]) * SCALE).astype(BF)
@@ -630,13 +632,14 @@
         [meta, *qs, *gs, kva, key_rows, value_rows, stat],
         [
             own_space,
+            pltpu.VMEM((TOK, 2 * HEAD), F32),
             pltpu.VMEM((KEYS, 2 * HEAD), BF),
-            dma(KEYS // TILE),
+            dma(1 + KEYS // TILE),
             dma(2),
         ],
         name="fixed_backward",
         raw=[10, 11],
-        direct=[0],
+        direct=[0, 4],
     )
     send, keep = call(
         project_fixed_kernel,
@@ -661,7 +664,7 @@
         [sds((TOK, width))] * 2,
         [meta, soff_t, summary_index, dkva, own, here, back, dkv_s],
         name="join_key_grads",
-        fetch=[1, 2],
+        fetch=[1, 2, 4],
     )
     return layer_out, query_grad, key_grad, value_grad
 

time: 108 us -> 108 us (level)
  local copies, waits for them, and re-layouts: 1.28 us -> 0.02 us
    unnamed x14 -> x6, local copies, waits for them, and re-layouts: 1.28 us -> 0.02 us
where the time goes in v9:
time: 108 us; the launch traced here: 106 us
  starting transfers between devices  51.7 us (48%)
  Pallas kernels  36.6 us (34%)
  waiting for transfers between devices  17 us (16%)
    pallas_call x11, Pallas kernels, call(): pl.pallas_call(body, out_shape=tuple((pltpu.HBM(s.shape, s.dtype) if i in...  36.6 us
    ppermute x12, starting transfers between devices, turn(): return lax.ppermute(a, 'zh', [(i, (i + by) % GROUP) for i in range(GROUP)])  24.2 us
    ppermute x12, waiting for transfers between devices, turn(): return lax.ppermute(a, 'zh', [(i, (i + by) % GROUP) for i in range(GROUP)])  12.3 us
    all_to_all x1, starting transfers between devices, shards(): kva = lax.all_to_all(kvb, plane, 0, 0, tiled=True).reshape(KEYS, 2 * HEAD)  7.31 us
    all_to_all x1, starting transfers between devices, shards(): lax.all_to_all(after(dkv, keep).reshape(ROWS, SUMM, 2 * HEAD), plane, 0,...  7.2 us
    ppermute x7, starting transfers between devices, swap(): return lax.ppermute(a, axis, [(0, 1), (1, 0)])  7.13 us
    ppermute x1, starting transfers between devices, shards(): before = lax.ppermute(picks, plane, [(i, i + 1) for i in range(ROWS - 1)])  3.06 us
    ppermute x1, starting transfers between devices, shards(): back = lax.ppermute(sent, plane, [(i + 1, i) for i in range(ROWS - 1)])  2.75 us
  transfers between devices with their start and end apart: 23, of which 9 were waited for; matrix products, arithmetic and copies ran while one was open for 0% of the time, Pallas kernels for 23%

profile of v9, /device:TPU:24, one launch (start us, length us, event | category | flops | bytes accessed | tf_op | source)
XLA Modules:
  0.0 106.4 jit_solution(1432004515364576755)
XLA Ops:
  0.6 2.0 %collective-permute-start.5 = (bf16[256,1024]{1,0:T(8,128)(2,1)}, bf16[256,1024]{1,0:T(8,128)(2,1)S(1)}, u32[]{:S(2)}, u32[]{:S(2)}) collective-permute-start(bf16[256,1024]{1,0:T(8,128)(2,1)} %refs_1_.2), channel_id=1, source_target_pairs={{0,2},{2,0},{1,3},{3,1},{4,6},{6,4},{5,7},{7,5},{8,10},{10,8},{9,1... | collective-permute-start | bytes 1572872 | tf_op jit(solution)/shard_map/ppermute | solution.py:527
  2.7 3.5 %pick_rows.1 = (bf16[16,128,256]{2,1,0:T(8,128)(2,1)}, bf16[256,128]{1,0:T(8,128)(2,1)S(1)}, bf16[4,96,128]{2,1,0:T(8,128)(2,1)S(1)}) custom-call(s32[4]{0:T(128)S(1)} %pad_add_fusion.refs_0_, s32[4,64]{1,0:T(4,128)} %bitcast.12, s32[1,128]{1,0:T(1,128)} %refs_2_.5, bf16[256,512]{1,0:T(8,128)(2,1)} %refs_10_.3, bf16[256,512]{1,0:T(8,128)(2,1)} %refs_11_.3, ...), custom_call_target="tpu_custom_call" | custom-call | flops 1 | bytes 1 | tf_op jit(solution)/shard_map/pick_rows/pallas_call | solution.py:111
  6.2 3.1 %collective-permute-start = (bf16[4,96,128]{2,1,0:T(8,128)(2,1)S(1)}, bf16[4,96,128]{2,1,0:T(8,128)(2,1)S(1)}, u32[]{:S(2)}, u32[]{:S(2)}) collective-permute-start(bf16[4,96,128]{2,1,0:T(8,128)(2,1)S(1)} %get-tuple-element.44.refs_2_), channel_id=1, source_target_pairs={{0,16},{16,32},{32,48},{48,64},{64,80},{80,96},{96,112},{112,128},... | collective-permute-start | bytes 294920 | tf_op jit(solution)/shard_map/ppermute | solution.py:563
  9.3 7.3 %all-to-all-start = ((bf16[16,128,256]{2,1,0:T(8,128)(2,1)}), bf16[16,128,256]{2,1,0:T(8,128)(2,1)S(1)}, u32[]{:S(2)}, u32[]{:S(2)}) async-start(bf16[16,128,256]{2,1,0:T(8,128)(2,1)} %get-tuple-element.51), calls=%async_computation | async-start | bytes 2097152 | tf_op jit(solution)/shard_map/all_to_all | solution.py:571
  17.8 3.3 %collective-permute-start.1 = (bf16[352,128]{1,0:T(8,128)(2,1)S(1)}, bf16[352,128]{1,0:T(8,128)(2,1)S(1)}, u32[]{:S(2)}, u32[]{:S(2)}) collective-permute-start(bf16[352,128]{1,0:T(8,128)(2,1)S(1)} %get-tuple-element.45), channel_id=1, source_target_pairs={{0,4},{4,8},{8,12},{12,0},{1,5},{5,9},{9,13},{13,1},{2,6},{6,10},{... | collective-permute-start | bytes 270344 | tf_op jit(solution)/shard_map/ppermute | solution.py:531
  21.1 4.5 %collective-permute-start.2 = (bf16[352,128]{1,0:T(8,128)(2,1)S(1)}, bf16[352,128]{1,0:T(8,128)(2,1)S(1)}, u32[]{:S(2)}, u32[]{:S(2)}) collective-permute-start(bf16[352,128]{1,0:T(8,128)(2,1)S(1)} %get-tuple-element.46), channel_id=1, source_target_pairs={{0,8},{4,12},{8,0},{12,4},{1,9},{5,13},{9,1},{13,5},{2,10},{6,14},... | collective-permute-start | bytes 270344 | tf_op jit(solution)/shard_map/ppermute | solution.py:531
  25.6 2.7 %collective-permute-start.3 = (bf16[352,128]{1,0:T(8,128)(2,1)S(1)}, bf16[352,128]{1,0:T(8,128)(2,1)S(1)}, u32[]{:S(2)}, u32[]{:S(2)}) collective-permute-start(bf16[352,128]{1,0:T(8,128)(2,1)S(1)} %get-tuple-element.47), channel_id=1, source_target_pairs={{0,12},{4,0},{8,4},{12,8},{1,13},{5,1},{9,5},{13,9},{2,14},{6,2},{... | collective-permute-start | bytes 270344 | tf_op jit(solution)/shard_map/ppermute | solution.py:531
  28.2 4.1 %attention_grad.1 = (bf16[256,128]{1,0:T(8,128)(2,1)S(1)}, bf16[256,512]{1,0:T(8,128)(2,1)S(1)}) custom-call(s32[4]{0:T(128)S(1)} %pad_add_fusion.refs_0_, bf16[256,1024]{1,0:T(8,128)(2,1)} %refs_1_.2, bf16[256,1024]{1,0:T(8,128)(2,1)S(1)} %collective-permute-done.4.refs_2_, bf16[256,1024]{1,0:T(8,128)(2,1)S(1)} %collective-permute-done.5.refs_3_, ...), custom_call_target="tpu_custom_call" | custom-call | flops 1 | bytes 1 | tf_op jit(solution)/shard_map/attention_grad/pallas_call | solution.py:111
  32.5 3.8 %collective-permute-start.8 = (bf16[256,128]{1,0:T(8,128)(2,1)S(1)}, bf16[256,128]{1,0:T(8,128)(2,1)S(1)}, u32[]{:S(2)}, u32[]{:S(2)}) collective-permute-start(bf16[256,128]{1,0:T(8,128)(2,1)S(1)} %get-tuple-element.50.refs_5_), channel_id=1, source_target_pairs={{0,8},{4,12},{8,0},{12,4},{1,9},{5,13},{9,1},{13,5},{2,10},{6,14},... | collective-permute-start | bytes 196616 | tf_op jit(solution)/shard_map/ppermute | solution.py:531
  36.3 3.1 %strided_heads.1 = (bf16[256,384]{1,0:T(8,128)(2,1)S(1)}, bf16[4,96,128]{2,1,0:T(8,128)(2,1)S(1)}, bf16[256,384]{1,0:T(8,128)(2,1)S(1)}, f32[256,768]{1,0:T(8,128)S(1)}) custom-call(s32[4]{0:T(128)S(1)} %pad_add_fusion.refs_0_, bf16[256,512]{1,0:T(8,128)(2,1)S(1)} %copy-done.2, bf16[256,512]{1,0:T(8,128)(2,1)S(1)} %copy-done, ...), custom_call_target="tpu_custom_call" | custom-call | flops 1 | bytes 1 | tf_op jit(solution)/shard_map/strided_heads/pallas_call | solution.py:111
  39.4 1.7 %collective-permute-done.8.refs_7_ = bf16[256,128]{1,0:T(8,128)(2,1)S(1)} collective-permute-done((bf16[256,128]{1,0:T(8,128)(2,1)S(1)}, bf16[256,128]{1,0:T(8,128)(2,1)S(1)}, u32[]{:S(2)}, u32[]{:S(2)}) %collective-permute-start.8) | collective-permute-done | bytes 65568 | tf_op jit(solution)/shard_map/ppermute | solution.py:531
  41.2 2.8 %collective-permute-done.7.refs_6_ = bf16[256,128]{1,0:T(8,128)(2,1)S(1)} collective-permute-done((bf16[256,128]{1,0:T(8,128)(2,1)S(1)}, bf16[256,128]{1,0:T(8,128)(2,1)S(1)}, u32[]{:S(2)}, u32[]{:S(2)}) %collective-permute-start.7) | collective-permute-done | bytes 65568 | tf_op jit(solution)/shard_map/ppermute | solution.py:531
  43.9 6.3 %fixed_forward.1 = (bf16[416,128]{1,0:T(8,128)(2,1)S(1)}, bf16[416,128]{1,0:T(8,128)(2,1)S(1)}, bf16[416,128]{1,0:T(8,128)(2,1)S(1)}, bf16[416,128]{1,0:T(8,128)(2,1)S(1)}) custom-call(s32[4]{0:T(128)S(1)} %pad_add_fusion.refs_0_, bf16[256,128]{1,0:T(8,128)(2,1)S(1)} %get-tuple-element.43.refs_1_, ...), custom_call_target="tpu_custom_call" | custom-call | flops 1 | bytes 1 | tf_op jit(solution)/shard_map/fixed_forward/pallas_call | solution.py:111
  50.8 1.2 %collective-permute-start.10 = (bf16[416,128]{1,0:T(8,128)(2,1)S(1)}, bf16[416,128]{1,0:T(8,128)(2,1)S(1)}, u32[]{:S(2)}, u32[]{:S(2)}) collective-permute-start(bf16[416,128]{1,0:T(8,128)(2,1)S(1)} %get-tuple-element.55), channel_id=1, source_target_pairs={{0,12},{4,0},{8,4},{12,8},{1,13},{5,1},{9,5},{13,9},{2,14},{6,2},{... | collective-permute-start | bytes 319496 | tf_op jit(solution)/shard_map/ppermute | solution.py:531
  52.0 3.5 %collective-permute-start.11 = (bf16[416,128]{1,0:T(8,128)(2,1)S(1)}, bf16[416,128]{1,0:T(8,128)(2,1)S(1)}, u32[]{:S(2)}, u32[]{:S(2)}) collective-permute-start(bf16[416,128]{1,0:T(8,128)(2,1)S(1)} %get-tuple-element.56), channel_id=1, source_target_pairs={{0,8},{4,12},{8,0},{12,4},{1,9},{5,13},{9,1},{13,5},{2,10},{6,14},... | collective-permute-start | bytes 319496 | tf_op jit(solution)/shard_map/ppermute | solution.py:531
  55.8 0.9 collective-permute-done.13.refs_2_
  56.7 1.3 %collective-permute-done.14.refs_4_ = bf16[512,4096]{1,0:T(8,128)(2,1)S(1)} collective-permute-done((bf16[512,4096]{1,0:T(8,128)(2,1)}, bf16[512,4096]{1,0:T(8,128)(2,1)S(1)}, u32[]{:S(2)}, u32[]{:S(2)}) %collective-permute-start.14) | collective-permute-done | bytes 4194336 | tf_op jit(solution)/shard_map/ppermute | solution.py:527
  58.0 3.2 %project_strided.1 = (f32[2,256,1024]{2,1,0:T(8,128)S(1)}, bf16[2,128,1024]{2,1,0:T(8,128)(2,1)S(1)}, bf16[2,128,1024]{2,1,0:T(8,128)(2,1)S(1)}) custom-call(s32[4]{0:T(128)S(1)} %pad_add_fusion.refs_0_, bf16[256,384]{1,0:T(8,128)(2,1)S(1)} %get-tuple-element.58.refs_1_, bf16[256,384]{1,0:T(8,128)(2,1)S(1)} %collective-permute-done.13.refs_2_, ...), custom_call_target="tpu_custom_call" | custom-call | flops 1 | bytes 1 | tf_op jit(solution)/shard_map/project_strided/pallas_call | solution.py:111
  61.2 2.7 %collective-permute-done.11.refs_3_ = bf16[416,128]{1,0:T(8,128)(2,1)S(1)} collective-permute-done((bf16[416,128]{1,0:T(8,128)(2,1)S(1)}, bf16[416,128]{1,0:T(8,128)(2,1)S(1)}, u32[]{:S(2)}, u32[]{:S(2)}) %collective-permute-start.11) | collective-permute-done | bytes 106528 | tf_op jit(solution)/shard_map/ppermute | solution.py:531
  64.6 0.8 combine.1
  65.8 8.1 %fixed_backward.1 = (bf16[2048,256]{1,0:T(8,128)(2,1)}, bf16[256,128]{1,0:T(8,128)(2,1)}, bf16[256,128]{1,0:T(8,128)(2,1)S(1)}, bf16[256,128]{1,0:T(8,128)(2,1)S...) custom-call(s32[4]{0:T(128)S(1)} %pad_add_fusion.refs_0_, bf16[256,128]{1,0:T(8,128)(2,1)S(1)} %get-tuple-element.43.refs_1_, ...), custom_call_target="tpu_custom_call" | custom-call | flops 1 | bytes 1 | tf_op jit(solution)/shard_map/fixed_backward/pallas_call | solution.py:111
  73.9 1.8 %project_fixed.1 = (bf16[256,1024]{1,0:T(8,128)(2,1)}, bf16[256,1024]{1,0:T(8,128)(2,1)S(1)}) custom-call(s32[4]{0:T(128)S(1)} %pad_add_fusion.refs_0_, bf16[256,128]{1,0:T(8,128)(2,1)S(1)} %get-tuple-element.61.refs_1_, bf16[256,128]{1,0:T(8,128)(2,1)S(1)} %collective-permute-done.15.refs_2_, f32[2,256,1024]{2,1,0:T(8,128)S(1)} %get-tuple-element.60.refs_5_.refs_3_, ...), custom_call_target="tpu_custom_call" | custom-call | flops 1 | bytes 1 | tf_op jit(solution)/shard_map/project_fixed/pallas_call | solution.py:111
  75.6 3.6 %collective-permute-start.16 = (bf16[256,1024]{1,0:T(8,128)(2,1)}, bf16[256,1024]{1,0:T(8,128)(2,1)}, u32[]{:S(2)}, u32[]{:S(2)}) collective-permute-start(bf16[256,1024]{1,0:T(8,128)(2,1)} %get-tuple-element.67), channel_id=1, source_target_pairs={{0,2},{2,0},{1,3},{3,1},{4,6},{6,4},{5,7},{7,5},{8,10},{10,8},{9,1... | collective-permute-start | bytes 1572872 | tf_op jit(solution)/shard_map/ppermute | solution.py:527
  79.3 7.2 %all-to-all-start.1 = ((bf16[16,128,256]{2,1,0:T(8,128)(2,1)}), bf16[16,128,256]{2,1,0:T(8,128)(2,1)S(1)}, u32[]{:S(2)}, u32[]{:S(2)}) async-start(bf16[16,128,256]{2,1,0:T(8,128)(2,1)} %bitcast.11), calls=%async_computation.1 | async-start | bytes 2097152 | tf_op jit(solution)/shard_map/all_to_all | solution.py:651
  86.5 1.2 %collective-permute-start.17 = (bf16[256,128]{1,0:T(8,128)(2,1)}, bf16[256,128]{1,0:T(8,128)(2,1)S(1)}, u32[]{:S(2)}, u32[]{:S(2)}) collective-permute-start(bf16[256,128]{1,0:T(8,128)(2,1)} %get-tuple-element.68), channel_id=1, source_target_pairs={{0,12},{4,0},{8,4},{12,8},{1,13},{5,1},{9,5},{13,9},{2,14},{6,2},{... | collective-permute-start | bytes 196616 | tf_op jit(solution)/shard_map/ppermute | solution.py:531
  87.6 3.6 %collective-permute-start.18 = (bf16[256,128]{1,0:T(8,128)(2,1)S(1)}, bf16[256,128]{1,0:T(8,128)(2,1)S(1)}, u32[]{:S(2)}, u32[]{:S(2)}) collective-permute-start(bf16[256,128]{1,0:T(8,128)(2,1)S(1)} %get-tuple-element.69), channel_id=1, source_target_pairs={{0,8},{4,12},{8,0},{12,4},{1,9},{5,13},{9,1},{13,5},{2,10},{6,14},... | collective-permute-start | bytes 196616 | tf_op jit(solution)/shard_map/ppermute | solution.py:531
  91.4 2.8 %collective-permute-start.20 = (bf16[4,96,128]{2,1,0:T(8,128)(2,1)S(1)}, bf16[4,96,128]{2,1,0:T(8,128)(2,1)S(1)}, u32[]{:S(2)}, u32[]{:S(2)}) collective-permute-start(bf16[4,96,128]{2,1,0:T(8,128)(2,1)S(1)} %get-tuple-element.78), channel_id=1, source_target_pairs={{16,0},{32,16},{48,32},{64,48},{80,64},{96,80},{112,96},{128,112},... | collective-permute-start | bytes 294920 | tf_op jit(solution)/shard_map/ppermute | solution.py:626
  94.2 3.6 %collective-permute-done.18.refs_5_ = bf16[256,128]{1,0:T(8,128)(2,1)S(1)} collective-permute-done((bf16[256,128]{1,0:T(8,128)(2,1)S(1)}, bf16[256,128]{1,0:T(8,128)(2,1)S(1)}, u32[]{:S(2)}, u32[]{:S(2)}) %collective-permute-start.18) | collective-permute-done | bytes 65568 | tf_op jit(solution)/shard_map/ppermute | solution.py:531
  97.7 0.8 collective-permute-done.19.refs_6_
  98.6 2.3 %join_output.1 = (bf16[256,1024]{1,0:T(8,128)(2,1)}, bf16[256,512]{1,0:T(8,128)(2,1)}) custom-call(s32[4]{0:T(128)S(1)} %pad_add_fusion.refs_0_, bf16[256,1024]{1,0:T(8,128)(2,1)S(1)} %get-tuple-element.66.refs_1_, bf16[256,1024]{1,0:T(8,128)(2,1)} %collective-permute-done.16.refs_2_, f32[128,256]{1,0:T(8,128)S(1)} %get-tuple-element.65.refs_6_.refs_3_, ...), custom_call_target="tpu_custom_call" | custom-call | flops 7000000000 | bytes 1 | tf_op jit(solution)/shard_map/join_output/pallas_call | solution.py:111
  100.9 2.5 %collective-permute-done.20.refs_6_ = bf16[4,96,128]{2,1,0:T(8,128)(2,1)S(1)} collective-permute-done((bf16[4,96,128]{2,1,0:T(8,128)(2,1)S(1)}, bf16[4,96,128]{2,1,0:T(8,128)(2,1)S(1)}, u32[]{:S(2)}, u32[]{:S(2)}) %collective-permute-start.20) | collective-permute-done | bytes 98336 | tf_op jit(solution)/shard_map/ppermute | solution.py:626
  103.3 2.9 %join_key_grads.1 = (bf16[256,512]{1,0:T(8,128)(2,1)}, bf16[256,512]{1,0:T(8,128)(2,1)}) custom-call(s32[4]{0:T(128)S(1)} %pad_add_fusion.refs_0_, s32[4,64]{1,0:T(4,128)} %bitcast.13, s32[1,128]{1,0:T(1,128)} %refs_2_.5, bf16[2048,256]{1,0:T(8,128)(2,1)S(1)} %bitcast.10, f32[256,256]{1,0:T(8,128)} %get-tuple-element.76.refs_4_, ...), custom_call_target="tpu_custom_call" | custom-call | flops 1 | bytes 1 | tf_op jit(solution)/shard_map/join_key_grads/pallas_call | solution.py:111
  (32 shorter events, 3.5 us)
Async XLA Ops:
  0.6 16.6 %collective-permute-start.5 = (bf16[256,1024]{1,0:T(8,128)(2,1)}, bf16[256,1024]{1,0:T(8,128)(2,1)S(1)}, u32[]{:S(2)}, u32[]{:S(2)}) collective-permute-start(bf16[256,1024]{1,0:T(8,128)(2,1)} %refs_1_.2), channel_id=1, source_target_pairs={{0,2},{2,0},{1,3},{3,1},{4,6},{6,4},{5,7},{7,5},{8,10},{10,8},{9,1... | collective-permute-start | bytes 1572872 | tf_op jit(solution)/shard_map/ppermute | solution.py:527
  6.2 10.4 %collective-permute-start = (bf16[4,96,128]{2,1,0:T(8,128)(2,1)S(1)}, bf16[4,96,128]{2,1,0:T(8,128)(2,1)S(1)}, u32[]{:S(2)}, u32[]{:S(2)}) collective-permute-start(bf16[4,96,128]{2,1,0:T(8,128)(2,1)S(1)} %get-tuple-element.44.refs_2_), channel_id=1, source_target_pairs={{0,16},{16,32},{32,48},{48,64},{64,80},{80,96},{96,112},{112,128},... | collective-permute-start | bytes 294920 | tf_op jit(solution)/shard_map/ppermute | solution.py:563
  9.3 30.2 %all-to-all-start = ((bf16[16,128,256]{2,1,0:T(8,128)(2,1)}), bf16[16,128,256]{2,1,0:T(8,128)(2,1)S(1)}, u32[]{:S(2)}, u32[]{:S(2)}) async-start(bf16[16,128,256]{2,1,0:T(8,128)(2,1)} %get-tuple-element.51), calls=%async_computation | async-start | bytes 2097152 | tf_op jit(solution)/shard_map/all_to_all | solution.py:571
  16.6 11.7 %collective-permute-start.4 = (bf16[256,1024]{1,0:T(8,128)(2,1)}, bf16[256,1024]{1,0:T(8,128)(2,1)S(1)}, u32[]{:S(2)}, u32[]{:S(2)}) collective-permute-start(bf16[256,1024]{1,0:T(8,128)(2,1)} %refs_1_.2), channel_id=1, source_target_pairs={{0,1},{1,0},{2,3},{3,2},{4,5},{5,4},{6,7},{7,6},{8,9},{9,8},{10,11... | collective-permute-start | bytes 1572872 | tf_op jit(solution)/shard_map/ppermute | solution.py:527
  17.2 19.1 %copy-start = (bf16[256,512]{1,0:T(8,128)(2,1)S(1)}, bf16[256,512]{1,0:T(8,128)(2,1)}, u32[]{:S(2)}) copy-start(bf16[256,512]{1,0:T(8,128)(2,1)} %refs_10_.3) | copy-start | bytes 786436
  17.2 19.1 %copy-start.1 = (bf16[256,512]{1,0:T(8,128)(2,1)S(1)}, bf16[256,512]{1,0:T(8,128)(2,1)}, u32[]{:S(2)}) copy-start(bf16[256,512]{1,0:T(8,128)(2,1)} %refs_11_.3) | copy-start | bytes 786436
  17.2 19.1 %copy-start.2 = (bf16[256,512]{1,0:T(8,128)(2,1)S(1)}, bf16[256,512]{1,0:T(8,128)(2,1)}, u32[]{:S(2)}) copy-start(bf16[256,512]{1,0:T(8,128)(2,1)} %refs_1_.3) | copy-start | bytes 786436
  17.2 11.0 %collective-permute-start.6 = (bf16[256,1024]{1,0:T(8,128)(2,1)S(1)}, bf16[256,1024]{1,0:T(8,128)(2,1)S(1)}, u32[]{:S(2)}, u32[]{:S(2)}) collective-permute-start(bf16[256,1024]{1,0:T(8,128)(2,1)S(1)} %collective-permute-done.5.refs_3_), channel_id=1, source_target_pairs={{0,1},{1,0},{2,3},{3,2},{4,5},{5,4},{6,7},{7,6},{8,9},{9,8},{10,11... | collective-permute-start | bytes 1572872 | tf_op jit(solution)/shard_map/ppermute | solution.py:527
  17.8 18.5 %collective-permute-start.1 = (bf16[352,128]{1,0:T(8,128)(2,1)S(1)}, bf16[352,128]{1,0:T(8,128)(2,1)S(1)}, u32[]{:S(2)}, u32[]{:S(2)}) collective-permute-start(bf16[352,128]{1,0:T(8,128)(2,1)S(1)} %get-tuple-element.45), channel_id=1, source_target_pairs={{0,4},{4,8},{8,12},{12,0},{1,5},{5,9},{9,13},{13,1},{2,6},{6,10},{... | collective-permute-start | bytes 270344 | tf_op jit(solution)/shard_map/ppermute | solution.py:531
  21.1 15.2 %collective-permute-start.2 = (bf16[352,128]{1,0:T(8,128)(2,1)S(1)}, bf16[352,128]{1,0:T(8,128)(2,1)S(1)}, u32[]{:S(2)}, u32[]{:S(2)}) collective-permute-start(bf16[352,128]{1,0:T(8,128)(2,1)S(1)} %get-tuple-element.46), channel_id=1, source_target_pairs={{0,8},{4,12},{8,0},{12,4},{1,9},{5,13},{9,1},{13,5},{2,10},{6,14},... | collective-permute-start | bytes 270344 | tf_op jit(solution)/shard_map/ppermute | solution.py:531
  25.6 10.8 %collective-permute-start.3 = (bf16[352,128]{1,0:T(8,128)(2,1)S(1)}, bf16[352,128]{1,0:T(8,128)(2,1)S(1)}, u32[]{:S(2)}, u32[]{:S(2)}) collective-permute-start(bf16[352,128]{1,0:T(8,128)(2,1)S(1)} %get-tuple-element.47), channel_id=1, source_target_pairs={{0,12},{4,0},{8,4},{12,8},{1,13},{5,1},{9,5},{13,9},{2,14},{6,2},{... | collective-permute-start | bytes 270344 | tf_op jit(solution)/shard_map/ppermute | solution.py:531
  32.4 7.0 %collective-permute-start.9 = (bf16[256,128]{1,0:T(8,128)(2,1)S(1)}, bf16[256,128]{1,0:T(8,128)(2,1)S(1)}, u32[]{:S(2)}, u32[]{:S(2)}) collective-permute-start(bf16[256,128]{1,0:T(8,128)(2,1)S(1)} %get-tuple-element.50.refs_5_), channel_id=1, source_target_pairs={{0,12},{4,0},{8,4},{12,8},{1,13},{5,1},{9,5},{13,9},{2,14},{6,2},{... | collective-permute-start | bytes 196616 | tf_op jit(solution)/shard_map/ppermute | solution.py:531
  32.5 8.7 %collective-permute-start.8 = (bf16[256,128]{1,0:T(8,128)(2,1)S(1)}, bf16[256,128]{1,0:T(8,128)(2,1)S(1)}, u32[]{:S(2)}, u32[]{:S(2)}) collective-permute-start(bf16[256,128]{1,0:T(8,128)(2,1)S(1)} %get-tuple-element.50.refs_5_), channel_id=1, source_target_pairs={{0,8},{4,12},{8,0},{12,4},{1,9},{5,13},{9,1},{13,5},{2,10},{6,14},... | collective-permute-start | bytes 196616 | tf_op jit(solution)/shard_map/ppermute | solution.py:531
  36.3 7.6 %collective-permute-start.7 = (bf16[256,128]{1,0:T(8,128)(2,1)S(1)}, bf16[256,128]{1,0:T(8,128)(2,1)S(1)}, u32[]{:S(2)}, u32[]{:S(2)}) collective-permute-start(bf16[256,128]{1,0:T(8,128)(2,1)S(1)} %get-tuple-element.50.refs_5_), channel_id=1, source_target_pairs={{0,4},{4,8},{8,12},{12,0},{1,5},{5,9},{9,13},{13,1},{2,6},{6,10},{... | collective-permute-start | bytes 196616 | tf_op jit(solution)/shard_map/ppermute | solution.py:531
  50.2 7.7 %collective-permute-start.14 = (bf16[512,4096]{1,0:T(8,128)(2,1)}, bf16[512,4096]{1,0:T(8,128)(2,1)S(1)}, u32[]{:S(2)}, u32[]{:S(2)}) collective-permute-start(bf16[512,4096]{1,0:T(8,128)(2,1)} %refs_3_.5), channel_id=1, source_target_pairs={{0,1},{1,0},{2,3},{3,2},{4,5},{5,4},{6,7},{7,6},{8,9},{9,8},{10,11... | collective-permute-start | bytes 12582920 | tf_op jit(solution)/shard_map/ppermute | solution.py:527
  50.3 6.4 %collective-permute-start.13 = (bf16[256,384]{1,0:T(8,128)(2,1)S(1)}, bf16[256,384]{1,0:T(8,128)(2,1)S(1)}, u32[]{:S(2)}, u32[]{:S(2)}) collective-permute-start(bf16[256,384]{1,0:T(8,128)(2,1)S(1)} %get-tuple-element.58.refs_1_), channel_id=1, source_target_pairs={{0,1},{1,0},{2,3},{3,2},{4,5},{5,4},{6,7},{7,6},{8,9},{9,8},{10,11... | collective-permute-start | bytes 589832 | tf_op jit(solution)/shard_map/ppermute | solution.py:527
  50.8 10.4 %collective-permute-start.10 = (bf16[416,128]{1,0:T(8,128)(2,1)S(1)}, bf16[416,128]{1,0:T(8,128)(2,1)S(1)}, u32[]{:S(2)}, u32[]{:S(2)}) collective-permute-start(bf16[416,128]{1,0:T(8,128)(2,1)S(1)} %get-tuple-element.55), channel_id=1, source_target_pairs={{0,12},{4,0},{8,4},{12,8},{1,13},{5,1},{9,5},{13,9},{2,14},{6,2},{... | collective-permute-start | bytes 319496 | tf_op jit(solution)/shard_map/ppermute | solution.py:531
  52.0 11.9 %collective-permute-start.11 = (bf16[416,128]{1,0:T(8,128)(2,1)S(1)}, bf16[416,128]{1,0:T(8,128)(2,1)S(1)}, u32[]{:S(2)}, u32[]{:S(2)}) collective-permute-start(bf16[416,128]{1,0:T(8,128)(2,1)S(1)} %get-tuple-element.56), channel_id=1, source_target_pairs={{0,8},{4,12},{8,0},{12,4},{1,9},{5,13},{9,1},{13,5},{2,10},{6,14},... | collective-permute-start | bytes 319496 | tf_op jit(solution)/shard_map/ppermute | solution.py:531
  55.5 9.2 %collective-permute-start.12 = (bf16[416,128]{1,0:T(8,128)(2,1)S(1)}, bf16[416,128]{1,0:T(8,128)(2,1)S(1)}, u32[]{:S(2)}, u32[]{:S(2)}) collective-permute-start(bf16[416,128]{1,0:T(8,128)(2,1)S(1)} %get-tuple-element.57), channel_id=1, source_target_pairs={{0,4},{4,8},{8,12},{12,0},{1,5},{5,9},{9,13},{13,1},{2,6},{6,10},{... | collective-permute-start | bytes 319496 | tf_op jit(solution)/shard_map/ppermute | solution.py:531
  65.5 8.4 %collective-permute-start.15 = (bf16[256,128]{1,0:T(8,128)(2,1)S(1)}, bf16[256,128]{1,0:T(8,128)(2,1)S(1)}, u32[]{:S(2)}, u32[]{:S(2)}) collective-permute-start(bf16[256,128]{1,0:T(8,128)(2,1)S(1)} %get-tuple-element.61.refs_1_), channel_id=1, source_target_pairs={{0,1},{1,0},{2,3},{3,2},{4,5},{5,4},{6,7},{7,6},{8,9},{9,8},{10,11... | collective-permute-start | bytes 196616 | tf_op jit(solution)/shard_map/ppermute | solution.py:527
  75.6 23.0 %collective-permute-start.16 = (bf16[256,1024]{1,0:T(8,128)(2,1)}, bf16[256,1024]{1,0:T(8,128)(2,1)}, u32[]{:S(2)}, u32[]{:S(2)}) collective-permute-start(bf16[256,1024]{1,0:T(8,128)(2,1)} %get-tuple-element.67), channel_id=1, source_target_pairs={{0,2},{2,0},{1,3},{3,1},{4,6},{6,4},{5,7},{7,5},{8,10},{10,8},{9,1... | collective-permute-start | bytes 1572872 | tf_op jit(solution)/shard_map/ppermute | solution.py:527
  79.3 24.1 %all-to-all-start.1 = ((bf16[16,128,256]{2,1,0:T(8,128)(2,1)}), bf16[16,128,256]{2,1,0:T(8,128)(2,1)S(1)}, u32[]{:S(2)}, u32[]{:S(2)}) async-start(bf16[16,128,256]{2,1,0:T(8,128)(2,1)} %bitcast.11), calls=%async_computation.1 | async-start | bytes 2097152 | tf_op jit(solution)/shard_map/all_to_all | solution.py:651
  86.5 7.7 %collective-permute-start.17 = (bf16[256,128]{1,0:T(8,128)(2,1)}, bf16[256,128]{1,0:T(8,128)(2,1)S(1)}, u32[]{:S(2)}, u32[]{:S(2)}) collective-permute-start(bf16[256,128]{1,0:T(8,128)(2,1)} %get-tuple-element.68), channel_id=1, source_target_pairs={{0,12},{4,0},{8,4},{12,8},{1,13},{5,1},{9,5},{13,9},{2,14},{6,2},{... | collective-permute-start | bytes 196616 | tf_op jit(solution)/shard_map/ppermute | solution.py:531
  87.6 10.1 %collective-permute-start.18 = (bf16[256,128]{1,0:T(8,128)(2,1)S(1)}, bf16[256,128]{1,0:T(8,128)(2,1)S(1)}, u32[]{:S(2)}, u32[]{:S(2)}) collective-permute-start(bf16[256,128]{1,0:T(8,128)(2,1)S(1)} %get-tuple-element.69), channel_id=1, source_target_pairs={{0,8},{4,12},{8,0},{12,4},{1,9},{5,13},{9,1},{13,5},{2,10},{6,14},... | collective-permute-start | bytes 196616 | tf_op jit(solution)/shard_map/ppermute | solution.py:531
  91.2 7.4 %collective-permute-start.19 = (bf16[256,128]{1,0:T(8,128)(2,1)S(1)}, bf16[256,128]{1,0:T(8,128)(2,1)S(1)}, u32[]{:S(2)}, u32[]{:S(2)}) collective-permute-start(bf16[256,128]{1,0:T(8,128)(2,1)S(1)} %get-tuple-element.70), channel_id=1, source_target_pairs={{0,4},{4,8},{8,12},{12,0},{1,5},{5,9},{9,13},{13,1},{2,6},{6,10},{... | collective-permute-start | bytes 196616 | tf_op jit(solution)/shard_map/ppermute | solution.py:531
  91.4 11.9 %collective-permute-start.20 = (bf16[4,96,128]{2,1,0:T(8,128)(2,1)S(1)}, bf16[4,96,128]{2,1,0:T(8,128)(2,1)S(1)}, u32[]{:S(2)}, u32[]{:S(2)}) collective-permute-start(bf16[4,96,128]{2,1,0:T(8,128)(2,1)S(1)} %get-tuple-element.78), channel_id=1, source_target_pairs={{16,0},{32,16},{48,32},{64,48},{80,64},{96,80},{112,96},{128,112},... | collective-permute-start | bytes 294920 | tf_op jit(solution)/shard_map/ppermute | solution.py:626

commit v10 on v9

--- a/solution.py
+++ b/solution.py
@@ -664,7 +664,6 @@
         [sds((TOK, width))] * 2,
         [meta, soff_t, summary_index, dkva, own, here, back, dkv_s],
         name="join_key_grads",
-        fetch=[1, 2, 4],
     )
     return layer_out, query_grad, key_grad, value_grad
 

time: 108 us -> 106 us (0.981)
  Pallas kernels: 36.6 us -> 35 us
    pallas_call x11, Pallas kernels: 36.6 us -> 35 us  [call(): pl.pallas_call(body, out_shape=tuple((pltpu.HBM(s.shape, s.dtype) if i in...]
where the time goes in v10:
time: 106 us; the launch traced here: 105 us
  starting transfers between devices  51.7 us (49%)
  Pallas kernels  35 us (33%)
  waiting for transfers between devices  17.1 us (16%)
    pallas_call x11, Pallas kernels, call(): pl.pallas_call(body, out_shape=tuple((pltpu.HBM(s.shape, s.dtype) if i in...  35 us
    ppermute x12, starting transfers between devices, turn(): return lax.ppermute(a, 'zh', [(i, (i + by) % GROUP) for i in range(GROUP)])  24.3 us
    ppermute x12, waiting for transfers between devices, turn(): return lax.ppermute(a, 'zh', [(i, (i + by) % GROUP) for i in range(GROUP)])  12.5 us
    all_to_all x1, starting transfers between devices, shards(): kva = lax.all_to_all(kvb, plane, 0, 0, tiled=True).reshape(KEYS, 2 * HEAD)  7.31 us
    all_to_all x1, starting transfers between devices, shards(): lax.all_to_all(after(dkv, keep).reshape(ROWS, SUMM, 2 * HEAD), plane, 0,...  7.22 us
    ppermute x7, starting transfers between devices, swap(): return lax.ppermute(a, axis, [(0, 1), (1, 0)])  7.06 us
    ppermute x1, starting transfers between devices, shards(): before = lax.ppermute(picks, plane, [(i, i + 1) for i in range(ROWS - 1)])  3.06 us
    ppermute x1, starting transfers between devices, shards(): back = lax.ppermute(sent, plane, [(i + 1, i) for i in range(ROWS - 1)])  2.75 us
  transfers between devices with their start and end apart: 23, of which 9 were waited for; matrix products, arithmetic and copies ran while one was open for 0% of the time, Pallas kernels for 23%

profile of v10, /device:TPU:24, one launch (start us, length us, event | category | flops | bytes accessed | tf_op | source)
XLA Modules:
  0.0 104.7 jit_solution(3974155475599956639)
XLA Ops:
  0.6 2.0 %collective-permute-start.5 = (bf16[256,1024]{1,0:T(8,128)(2,1)}, bf16[256,1024]{1,0:T(8,128)(2,1)S(1)}, u32[]{:S(2)}, u32[]{:S(2)}) collective-permute-start(bf16[256,1024]{1,0:T(8,128)(2,1)} %refs_1_.2), channel_id=1, source_target_pairs={{0,2},{2,0},{1,3},{3,1},{4,6},{6,4},{5,7},{7,5},{8,10},{10,8},{9,1... | collective-permute-start | bytes 1572872 | tf_op jit(solution)/shard_map/ppermute | solution.py:527
  2.7 3.5 %pick_rows.1 = (bf16[16,128,256]{2,1,0:T(8,128)(2,1)}, bf16[256,128]{1,0:T(8,128)(2,1)S(1)}, bf16[4,96,128]{2,1,0:T(8,128)(2,1)S(1)}) custom-call(s32[4]{0:T(128)S(1)} %pad_add_fusion.refs_0_, s32[4,64]{1,0:T(4,128)} %bitcast.11, s32[1,128]{1,0:T(1,128)} %refs_2_.5, bf16[256,512]{1,0:T(8,128)(2,1)} %refs_10_.3, bf16[256,512]{1,0:T(8,128)(2,1)} %refs_11_.3, ...), custom_call_target="tpu_custom_call" | custom-call | flops 1 | bytes 1 | tf_op jit(solution)/shard_map/pick_rows/pallas_call | solution.py:111
  6.2 3.1 %collective-permute-start = (bf16[4,96,128]{2,1,0:T(8,128)(2,1)S(1)}, bf16[4,96,128]{2,1,0:T(8,128)(2,1)S(1)}, u32[]{:S(2)}, u32[]{:S(2)}) collective-permute-start(bf16[4,96,128]{2,1,0:T(8,128)(2,1)S(1)} %get-tuple-element.44.refs_2_), channel_id=1, source_target_pairs={{0,16},{16,32},{32,48},{48,64},{64,80},{80,96},{96,112},{112,128},... | collective-permute-start | bytes 294920 | tf_op jit(solution)/shard_map/ppermute | solution.py:563
  9.3 7.3 %all-to-all-start = ((bf16[16,128,256]{2,1,0:T(8,128)(2,1)}), bf16[16,128,256]{2,1,0:T(8,128)(2,1)S(1)}, u32[]{:S(2)}, u32[]{:S(2)}) async-start(bf16[16,128,256]{2,1,0:T(8,128)(2,1)} %get-tuple-element.51), calls=%async_computation | async-start | bytes 2097152 | tf_op jit(solution)/shard_map/all_to_all | solution.py:571
  17.8 3.3 %collective-permute-start.1 = (bf16[352,128]{1,0:T(8,128)(2,1)S(1)}, bf16[352,128]{1,0:T(8,128)(2,1)S(1)}, u32[]{:S(2)}, u32[]{:S(2)}) collective-permute-start(bf16[352,128]{1,0:T(8,128)(2,1)S(1)} %get-tuple-element.45), channel_id=1, source_target_pairs={{0,4},{4,8},{8,12},{12,0},{1,5},{5,9},{9,13},{13,1},{2,6},{6,10},{... | collective-permute-start | bytes 270344 | tf_op jit(solution)/shard_map/ppermute | solution.py:531
  21.1 4.5 %collective-permute-start.2 = (bf16[352,128]{1,0:T(8,128)(2,1)S(1)}, bf16[352,128]{1,0:T(8,128)(2,1)S(1)}, u32[]{:S(2)}, u32[]{:S(2)}) collective-permute-start(bf16[352,128]{1,0:T(8,128)(2,1)S(1)} %get-tuple-element.46), channel_id=1, source_target_pairs={{0,8},{4,12},{8,0},{12,4},{1,9},{5,13},{9,1},{13,5},{2,10},{6,14},... | collective-permute-start | bytes 270344 | tf_op jit(solution)/shard_map/ppermute | solution.py:531
  25.6 2.7 %collective-permute-start.3 = (bf16[352,128]{1,0:T(8,128)(2,1)S(1)}, bf16[352,128]{1,0:T(8,128)(2,1)S(1)}, u32[]{:S(2)}, u32[]{:S(2)}) collective-permute-start(bf16[352,128]{1,0:T(8,128)(2,1)S(1)} %get-tuple-element.47), channel_id=1, source_target_pairs={{0,12},{4,0},{8,4},{12,8},{1,13},{5,1},{9,5},{13,9},{2,14},{6,2},{... | collective-permute-start | bytes 270344 | tf_op jit(solution)/shard_map/ppermute | solution.py:531
  28.2 4.1 %attention_grad.1 = (bf16[256,128]{1,0:T(8,128)(2,1)S(1)}, bf16[256,512]{1,0:T(8,128)(2,1)S(1)}) custom-call(s32[4]{0:T(128)S(1)} %pad_add_fusion.refs_0_, bf16[256,1024]{1,0:T(8,128)(2,1)} %refs_1_.2, bf16[256,1024]{1,0:T(8,128)(2,1)S(1)} %collective-permute-done.4.refs_2_, bf16[256,1024]{1,0:T(8,128)(2,1)S(1)} %collective-permute-done.5.refs_3_, ...), custom_call_target="tpu_custom_call" | custom-call | flops 1 | bytes 1 | tf_op jit(solution)/shard_map/attention_grad/pallas_call | solution.py:111
  32.5 3.8 %collective-permute-start.8 = (bf16[256,128]{1,0:T(8,128)(2,1)S(1)}, bf16[256,128]{1,0:T(8,128)(2,1)S(1)}, u32[]{:S(2)}, u32[]{:S(2)}) collective-permute-start(bf16[256,128]{1,0:T(8,128)(2,1)S(1)} %get-tuple-element.50.refs_5_), channel_id=1, source_target_pairs={{0,8},{4,12},{8,0},{12,4},{1,9},{5,13},{9,1},{13,5},{2,10},{6,14},... | collective-permute-start | bytes 196616 | tf_op jit(solution)/shard_map/ppermute | solution.py:531
  36.4 3.1 %strided_heads.1 = (bf16[256,384]{1,0:T(8,128)(2,1)S(1)}, bf16[4,96,128]{2,1,0:T(8,128)(2,1)S(1)}, bf16[256,384]{1,0:T(8,128)(2,1)S(1)}, f32[256,768]{1,0:T(8,128)S(1)}) custom-call(s32[4]{0:T(128)S(1)} %pad_add_fusion.refs_0_, bf16[256,512]{1,0:T(8,128)(2,1)S(1)} %copy-done.2, bf16[256,512]{1,0:T(8,128)(2,1)S(1)} %copy-done, ...), custom_call_target="tpu_custom_call" | custom-call | flops 1 | bytes 1 | tf_op jit(solution)/shard_map/strided_heads/pallas_call | solution.py:111
  39.5 1.6 %collective-permute-done.8.refs_7_ = bf16[256,128]{1,0:T(8,128)(2,1)S(1)} collective-permute-done((bf16[256,128]{1,0:T(8,128)(2,1)S(1)}, bf16[256,128]{1,0:T(8,128)(2,1)S(1)}, u32[]{:S(2)}, u32[]{:S(2)}) %collective-permute-start.8) | collective-permute-done | bytes 65568 | tf_op jit(solution)/shard_map/ppermute | solution.py:531
  41.1 2.9 %collective-permute-done.7.refs_6_ = bf16[256,128]{1,0:T(8,128)(2,1)S(1)} collective-permute-done((bf16[256,128]{1,0:T(8,128)(2,1)S(1)}, bf16[256,128]{1,0:T(8,128)(2,1)S(1)}, u32[]{:S(2)}, u32[]{:S(2)}) %collective-permute-start.7) | collective-permute-done | bytes 65568 | tf_op jit(solution)/shard_map/ppermute | solution.py:531
  44.0 6.3 %fixed_forward.1 = (bf16[416,128]{1,0:T(8,128)(2,1)S(1)}, bf16[416,128]{1,0:T(8,128)(2,1)S(1)}, bf16[416,128]{1,0:T(8,128)(2,1)S(1)}, bf16[416,128]{1,0:T(8,128)(2,1)S(1)}) custom-call(s32[4]{0:T(128)S(1)} %pad_add_fusion.refs_0_, bf16[256,128]{1,0:T(8,128)(2,1)S(1)} %get-tuple-element.43.refs_1_, ...), custom_call_target="tpu_custom_call" | custom-call | flops 1 | bytes 1 | tf_op jit(solution)/shard_map/fixed_forward/pallas_call | solution.py:111
  50.8 1.3 %collective-permute-start.10 = (bf16[416,128]{1,0:T(8,128)(2,1)S(1)}, bf16[416,128]{1,0:T(8,128)(2,1)S(1)}, u32[]{:S(2)}, u32[]{:S(2)}) collective-permute-start(bf16[416,128]{1,0:T(8,128)(2,1)S(1)} %get-tuple-element.55), channel_id=1, source_target_pairs={{0,12},{4,0},{8,4},{12,8},{1,13},{5,1},{9,5},{13,9},{2,14},{6,2},{... | collective-permute-start | bytes 319496 | tf_op jit(solution)/shard_map/ppermute | solution.py:531
  52.1 3.4 %collective-permute-start.11 = (bf16[416,128]{1,0:T(8,128)(2,1)S(1)}, bf16[416,128]{1,0:T(8,128)(2,1)S(1)}, u32[]{:S(2)}, u32[]{:S(2)}) collective-permute-start(bf16[416,128]{1,0:T(8,128)(2,1)S(1)} %get-tuple-element.56), channel_id=1, source_target_pairs={{0,8},{4,12},{8,0},{12,4},{1,9},{5,13},{9,1},{13,5},{2,10},{6,14},... | collective-permute-start | bytes 319496 | tf_op jit(solution)/shard_map/ppermute | solution.py:531
  55.8 0.9 collective-permute-done.13.refs_2_
  56.7 1.3 %collective-permute-done.14.refs_4_ = bf16[512,4096]{1,0:T(8,128)(2,1)S(1)} collective-permute-done((bf16[512,4096]{1,0:T(8,128)(2,1)}, bf16[512,4096]{1,0:T(8,128)(2,1)S(1)}, u32[]{:S(2)}, u32[]{:S(2)}) %collective-permute-start.14) | collective-permute-done | bytes 4194336 | tf_op jit(solution)/shard_map/ppermute | solution.py:527
  58.0 3.2 %project_strided.1 = (f32[2,256,1024]{2,1,0:T(8,128)S(1)}, bf16[2,128,1024]{2,1,0:T(8,128)(2,1)S(1)}, bf16[2,128,1024]{2,1,0:T(8,128)(2,1)S(1)}) custom-call(s32[4]{0:T(128)S(1)} %pad_add_fusion.refs_0_, bf16[256,384]{1,0:T(8,128)(2,1)S(1)} %get-tuple-element.58.refs_1_, bf16[256,384]{1,0:T(8,128)(2,1)S(1)} %collective-permute-done.13.refs_2_, ...), custom_call_target="tpu_custom_call" | custom-call | flops 1 | bytes 1 | tf_op jit(solution)/shard_map/project_strided/pallas_call | solution.py:111
  61.2 2.8 %collective-permute-done.11.refs_3_ = bf16[416,128]{1,0:T(8,128)(2,1)S(1)} collective-permute-done((bf16[416,128]{1,0:T(8,128)(2,1)S(1)}, bf16[416,128]{1,0:T(8,128)(2,1)S(1)}, u32[]{:S(2)}, u32[]{:S(2)}) %collective-permute-start.11) | collective-permute-done | bytes 106528 | tf_op jit(solution)/shard_map/ppermute | solution.py:531
  64.7 0.8 combine.1
  65.9 7.4 %fixed_backward.1 = (bf16[2048,256]{1,0:T(8,128)(2,1)}, bf16[256,128]{1,0:T(8,128)(2,1)S(1)}, bf16[256,128]{1,0:T(8,128)(2,1)S(1)}, bf16[256,128]{1,0:T(8,128)(2...) custom-call(s32[4]{0:T(128)S(1)} %pad_add_fusion.refs_0_, bf16[256,128]{1,0:T(8,128)(2,1)S(1)} %get-tuple-element.43.refs_1_, ...), custom_call_target="tpu_custom_call" | custom-call | flops 1 | bytes 1 | tf_op jit(solution)/shard_map/fixed_backward/pallas_call | solution.py:111
  73.3 1.8 %project_fixed.1 = (bf16[256,1024]{1,0:T(8,128)(2,1)}, bf16[256,1024]{1,0:T(8,128)(2,1)S(1)}) custom-call(s32[4]{0:T(128)S(1)} %pad_add_fusion.refs_0_, bf16[256,128]{1,0:T(8,128)(2,1)S(1)} %get-tuple-element.61.refs_1_, bf16[256,128]{1,0:T(8,128)(2,1)S(1)} %collective-permute-done.15.refs_2_, f32[2,256,1024]{2,1,0:T(8,128)S(1)} %get-tuple-element.60.refs_5_.refs_3_, ...), custom_call_target="tpu_custom_call" | custom-call | flops 1 | bytes 1 | tf_op jit(solution)/shard_map/project_fixed/pallas_call | solution.py:111
  75.1 3.6 %collective-permute-start.16 = (bf16[256,1024]{1,0:T(8,128)(2,1)}, bf16[256,1024]{1,0:T(8,128)(2,1)}, u32[]{:S(2)}, u32[]{:S(2)}) collective-permute-start(bf16[256,1024]{1,0:T(8,128)(2,1)} %get-tuple-element.67), channel_id=1, source_target_pairs={{0,2},{2,0},{1,3},{3,1},{4,6},{6,4},{5,7},{7,5},{8,10},{10,8},{9,1... | collective-permute-start | bytes 1572872 | tf_op jit(solution)/shard_map/ppermute | solution.py:527
  78.7 7.2 %all-to-all-start.1 = ((bf16[16,128,256]{2,1,0:T(8,128)(2,1)}), bf16[16,128,256]{2,1,0:T(8,128)(2,1)S(1)}, u32[]{:S(2)}, u32[]{:S(2)}) async-start(bf16[16,128,256]{2,1,0:T(8,128)(2,1)} %bitcast.13), calls=%async_computation.1 | async-start | bytes 2097152 | tf_op jit(solution)/shard_map/all_to_all | solution.py:651
  85.9 1.2 %collective-permute-start.17 = (bf16[256,128]{1,0:T(8,128)(2,1)S(1)}, bf16[256,128]{1,0:T(8,128)(2,1)S(1)}, u32[]{:S(2)}, u32[]{:S(2)}) collective-permute-start(bf16[256,128]{1,0:T(8,128)(2,1)S(1)} %get-tuple-element.68), channel_id=1, source_target_pairs={{0,12},{4,0},{8,4},{12,8},{1,13},{5,1},{9,5},{13,9},{2,14},{6,2},{... | collective-permute-start | bytes 196616 | tf_op jit(solution)/shard_map/ppermute | solution.py:531
  87.1 3.5 %collective-permute-start.18 = (bf16[256,128]{1,0:T(8,128)(2,1)S(1)}, bf16[256,128]{1,0:T(8,128)(2,1)S(1)}, u32[]{:S(2)}, u32[]{:S(2)}) collective-permute-start(bf16[256,128]{1,0:T(8,128)(2,1)S(1)} %get-tuple-element.69), channel_id=1, source_target_pairs={{0,8},{4,12},{8,0},{12,4},{1,9},{5,13},{9,1},{13,5},{2,10},{6,14},... | collective-permute-start | bytes 196616 | tf_op jit(solution)/shard_map/ppermute | solution.py:531
  90.8 2.8 %collective-permute-start.20 = (bf16[4,96,128]{2,1,0:T(8,128)(2,1)S(1)}, bf16[4,96,128]{2,1,0:T(8,128)(2,1)S(1)}, u32[]{:S(2)}, u32[]{:S(2)}) collective-permute-start(bf16[4,96,128]{2,1,0:T(8,128)(2,1)S(1)} %get-tuple-element.78), channel_id=1, source_target_pairs={{16,0},{32,16},{48,32},{64,48},{80,64},{96,80},{112,96},{128,112},... | collective-permute-start | bytes 294920 | tf_op jit(solution)/shard_map/ppermute | solution.py:626
  93.6 3.6 %collective-permute-done.18.refs_5_ = bf16[256,128]{1,0:T(8,128)(2,1)S(1)} collective-permute-done((bf16[256,128]{1,0:T(8,128)(2,1)S(1)}, bf16[256,128]{1,0:T(8,128)(2,1)S(1)}, u32[]{:S(2)}, u32[]{:S(2)}) %collective-permute-start.18) | collective-permute-done | bytes 65568 | tf_op jit(solution)/shard_map/ppermute | solution.py:531
  97.2 0.9 collective-permute-done.19.refs_6_
  98.0 2.3 %join_output.1 = (bf16[256,1024]{1,0:T(8,128)(2,1)}, bf16[256,512]{1,0:T(8,128)(2,1)}) custom-call(s32[4]{0:T(128)S(1)} %pad_add_fusion.refs_0_, bf16[256,1024]{1,0:T(8,128)(2,1)S(1)} %get-tuple-element.66.refs_1_, bf16[256,1024]{1,0:T(8,128)(2,1)} %collective-permute-done.16.refs_2_, f32[128,256]{1,0:T(8,128)S(1)} %get-tuple-element.65.refs_6_.refs_3_, ...), custom_call_target="tpu_custom_call" | custom-call | flops 7000000000 | bytes 1 | tf_op jit(solution)/shard_map/join_output/pallas_call | solution.py:111
  100.4 2.4 %collective-permute-done.20.refs_6_ = bf16[4,96,128]{2,1,0:T(8,128)(2,1)S(1)} collective-permute-done((bf16[4,96,128]{2,1,0:T(8,128)(2,1)S(1)}, bf16[4,96,128]{2,1,0:T(8,128)(2,1)S(1)}, u32[]{:S(2)}, u32[]{:S(2)}) %collective-permute-start.20) | collective-permute-done | bytes 98336 | tf_op jit(solution)/shard_map/ppermute | solution.py:626
  102.8 1.9 %join_key_grads.1 = (bf16[256,512]{1,0:T(8,128)(2,1)}, bf16[256,512]{1,0:T(8,128)(2,1)}) custom-call(s32[4]{0:T(128)S(1)} %pad_add_fusion.refs_0_, s32[4,64]{1,0:T(4,128)S(1)} %bitcast.12, s32[1,128]{1,0:T(1,128)S(1)} %copy-done.5, bf16[2048,256]{1,0:T(8,128)(2,1)S(1)} %bitcast.10, f32[256,256]{1,0:T(8,128)S(1)} %copy-done.3, ...), custom_call_target="tpu_custom_call" | custom-call | flops 1 | bytes 1 | tf_op jit(solution)/shard_map/join_key_grads/pallas_call | solution.py:111
  (38 shorter events, 3.6 us)
Async XLA Ops:
  0.6 16.6 %collective-permute-start.5 = (bf16[256,1024]{1,0:T(8,128)(2,1)}, bf16[256,1024]{1,0:T(8,128)(2,1)S(1)}, u32[]{:S(2)}, u32[]{:S(2)}) collective-permute-start(bf16[256,1024]{1,0:T(8,128)(2,1)} %refs_1_.2), channel_id=1, source_target_pairs={{0,2},{2,0},{1,3},{3,1},{4,6},{6,4},{5,7},{7,5},{8,10},{10,8},{9,1... | collective-permute-start | bytes 1572872 | tf_op jit(solution)/shard_map/ppermute | solution.py:527
  6.2 10.4 %collective-permute-start = (bf16[4,96,128]{2,1,0:T(8,128)(2,1)S(1)}, bf16[4,96,128]{2,1,0:T(8,128)(2,1)S(1)}, u32[]{:S(2)}, u32[]{:S(2)}) collective-permute-start(bf16[4,96,128]{2,1,0:T(8,128)(2,1)S(1)} %get-tuple-element.44.refs_2_), channel_id=1, source_target_pairs={{0,16},{16,32},{32,48},{48,64},{64,80},{80,96},{96,112},{112,128},... | collective-permute-start | bytes 294920 | tf_op jit(solution)/shard_map/ppermute | solution.py:563
  9.3 30.2 %all-to-all-start = ((bf16[16,128,256]{2,1,0:T(8,128)(2,1)}), bf16[16,128,256]{2,1,0:T(8,128)(2,1)S(1)}, u32[]{:S(2)}, u32[]{:S(2)}) async-start(bf16[16,128,256]{2,1,0:T(8,128)(2,1)} %get-tuple-element.51), calls=%async_computation | async-start | bytes 2097152 | tf_op jit(solution)/shard_map/all_to_all | solution.py:571
  16.6 11.7 %collective-permute-start.4 = (bf16[256,1024]{1,0:T(8,128)(2,1)}, bf16[256,1024]{1,0:T(8,128)(2,1)S(1)}, u32[]{:S(2)}, u32[]{:S(2)}) collective-permute-start(bf16[256,1024]{1,0:T(8,128)(2,1)} %refs_1_.2), channel_id=1, source_target_pairs={{0,1},{1,0},{2,3},{3,2},{4,5},{5,4},{6,7},{7,6},{8,9},{9,8},{10,11... | collective-permute-start | bytes 1572872 | tf_op jit(solution)/shard_map/ppermute | solution.py:527
  17.2 19.1 %copy-start = (bf16[256,512]{1,0:T(8,128)(2,1)S(1)}, bf16[256,512]{1,0:T(8,128)(2,1)}, u32[]{:S(2)}) copy-start(bf16[256,512]{1,0:T(8,128)(2,1)} %refs_10_.3) | copy-start | bytes 786436
  17.2 19.1 %copy-start.1 = (bf16[256,512]{1,0:T(8,128)(2,1)S(1)}, bf16[256,512]{1,0:T(8,128)(2,1)}, u32[]{:S(2)}) copy-start(bf16[256,512]{1,0:T(8,128)(2,1)} %refs_11_.3) | copy-start | bytes 786436
  17.2 19.1 %copy-start.2 = (bf16[256,512]{1,0:T(8,128)(2,1)S(1)}, bf16[256,512]{1,0:T(8,128)(2,1)}, u32[]{:S(2)}) copy-start(bf16[256,512]{1,0:T(8,128)(2,1)} %refs_1_.3) | copy-start | bytes 786436
  17.2 11.0 %collective-permute-start.6 = (bf16[256,1024]{1,0:T(8,128)(2,1)S(1)}, bf16[256,1024]{1,0:T(8,128)(2,1)S(1)}, u32[]{:S(2)}, u32[]{:S(2)}) collective-permute-start(bf16[256,1024]{1,0:T(8,128)(2,1)S(1)} %collective-permute-done.5.refs_3_), channel_id=1, source_target_pairs={{0,1},{1,0},{2,3},{3,2},{4,5},{5,4},{6,7},{7,6},{8,9},{9,8},{10,11... | collective-permute-start | bytes 1572872 | tf_op jit(solution)/shard_map/ppermute | solution.py:527
  17.8 18.5 %collective-permute-start.1 = (bf16[352,128]{1,0:T(8,128)(2,1)S(1)}, bf16[352,128]{1,0:T(8,128)(2,1)S(1)}, u32[]{:S(2)}, u32[]{:S(2)}) collective-permute-start(bf16[352,128]{1,0:T(8,128)(2,1)S(1)} %get-tuple-element.45), channel_id=1, source_target_pairs={{0,4},{4,8},{8,12},{12,0},{1,5},{5,9},{9,13},{13,1},{2,6},{6,10},{... | collective-permute-start | bytes 270344 | tf_op jit(solution)/shard_map/ppermute | solution.py:531
  21.1 15.2 %collective-permute-start.2 = (bf16[352,128]{1,0:T(8,128)(2,1)S(1)}, bf16[352,128]{1,0:T(8,128)(2,1)S(1)}, u32[]{:S(2)}, u32[]{:S(2)}) collective-permute-start(bf16[352,128]{1,0:T(8,128)(2,1)S(1)} %get-tuple-element.46), channel_id=1, source_target_pairs={{0,8},{4,12},{8,0},{12,4},{1,9},{5,13},{9,1},{13,5},{2,10},{6,14},... | collective-permute-start | bytes 270344 | tf_op jit(solution)/shard_map/ppermute | solution.py:531
  25.6 10.8 %collective-permute-start.3 = (bf16[352,128]{1,0:T(8,128)(2,1)S(1)}, bf16[352,128]{1,0:T(8,128)(2,1)S(1)}, u32[]{:S(2)}, u32[]{:S(2)}) collective-permute-start(bf16[352,128]{1,0:T(8,128)(2,1)S(1)} %get-tuple-element.47), channel_id=1, source_target_pairs={{0,12},{4,0},{8,4},{12,8},{1,13},{5,1},{9,5},{13,9},{2,14},{6,2},{... | collective-permute-start | bytes 270344 | tf_op jit(solution)/shard_map/ppermute | solution.py:531
  32.4 7.0 %collective-permute-start.9 = (bf16[256,128]{1,0:T(8,128)(2,1)S(1)}, bf16[256,128]{1,0:T(8,128)(2,1)S(1)}, u32[]{:S(2)}, u32[]{:S(2)}) collective-permute-start(bf16[256,128]{1,0:T(8,128)(2,1)S(1)} %get-tuple-element.50.refs_5_), channel_id=1, source_target_pairs={{0,12},{4,0},{8,4},{12,8},{1,13},{5,1},{9,5},{13,9},{2,14},{6,2},{... | collective-permute-start | bytes 196616 | tf_op jit(solution)/shard_map/ppermute | solution.py:531
  32.5 8.6 %collective-permute-start.8 = (bf16[256,128]{1,0:T(8,128)(2,1)S(1)}, bf16[256,128]{1,0:T(8,128)(2,1)S(1)}, u32[]{:S(2)}, u32[]{:S(2)}) collective-permute-start(bf16[256,128]{1,0:T(8,128)(2,1)S(1)} %get-tuple-element.50.refs_5_), channel_id=1, source_target_pairs={{0,8},{4,12},{8,0},{12,4},{1,9},{5,13},{9,1},{13,5},{2,10},{6,14},... | collective-permute-start | bytes 196616 | tf_op jit(solution)/shard_map/ppermute | solution.py:531
  36.3 7.6 %collective-permute-start.7 = (bf16[256,128]{1,0:T(8,128)(2,1)S(1)}, bf16[256,128]{1,0:T(8,128)(2,1)S(1)}, u32[]{:S(2)}, u32[]{:S(2)}) collective-permute-start(bf16[256,128]{1,0:T(8,128)(2,1)S(1)} %get-tuple-element.50.refs_5_), channel_id=1, source_target_pairs={{0,4},{4,8},{8,12},{12,0},{1,5},{5,9},{9,13},{13,1},{2,6},{6,10},{... | collective-permute-start | bytes 196616 | tf_op jit(solution)/shard_map/ppermute | solution.py:531
  50.2 7.7 %collective-permute-start.14 = (bf16[512,4096]{1,0:T(8,128)(2,1)}, bf16[512,4096]{1,0:T(8,128)(2,1)S(1)}, u32[]{:S(2)}, u32[]{:S(2)}) collective-permute-start(bf16[512,4096]{1,0:T(8,128)(2,1)} %refs_3_.5), channel_id=1, source_target_pairs={{0,1},{1,0},{2,3},{3,2},{4,5},{5,4},{6,7},{7,6},{8,9},{9,8},{10,11... | collective-permute-start | bytes 12582920 | tf_op jit(solution)/shard_map/ppermute | solution.py:527
  50.3 6.4 %collective-permute-start.13 = (bf16[256,384]{1,0:T(8,128)(2,1)S(1)}, bf16[256,384]{1,0:T(8,128)(2,1)S(1)}, u32[]{:S(2)}, u32[]{:S(2)}) collective-permute-start(bf16[256,384]{1,0:T(8,128)(2,1)S(1)} %get-tuple-element.58.refs_1_), channel_id=1, source_target_pairs={{0,1},{1,0},{2,3},{3,2},{4,5},{5,4},{6,7},{7,6},{8,9},{9,8},{10,11... | collective-permute-start | bytes 589832 | tf_op jit(solution)/shard_map/ppermute | solution.py:527
  50.8 10.4 %collective-permute-start.10 = (bf16[416,128]{1,0:T(8,128)(2,1)S(1)}, bf16[416,128]{1,0:T(8,128)(2,1)S(1)}, u32[]{:S(2)}, u32[]{:S(2)}) collective-permute-start(bf16[416,128]{1,0:T(8,128)(2,1)S(1)} %get-tuple-element.55), channel_id=1, source_target_pairs={{0,12},{4,0},{8,4},{12,8},{1,13},{5,1},{9,5},{13,9},{2,14},{6,2},{... | collective-permute-start | bytes 319496 | tf_op jit(solution)/shard_map/ppermute | solution.py:531
  52.1 11.9 %collective-permute-start.11 = (bf16[416,128]{1,0:T(8,128)(2,1)S(1)}, bf16[416,128]{1,0:T(8,128)(2,1)S(1)}, u32[]{:S(2)}, u32[]{:S(2)}) collective-permute-start(bf16[416,128]{1,0:T(8,128)(2,1)S(1)} %get-tuple-element.56), channel_id=1, source_target_pairs={{0,8},{4,12},{8,0},{12,4},{1,9},{5,13},{9,1},{13,5},{2,10},{6,14},... | collective-permute-start | bytes 319496 | tf_op jit(solution)/shard_map/ppermute | solution.py:531
  55.5 9.3 %collective-permute-start.12 = (bf16[416,128]{1,0:T(8,128)(2,1)S(1)}, bf16[416,128]{1,0:T(8,128)(2,1)S(1)}, u32[]{:S(2)}, u32[]{:S(2)}) collective-permute-start(bf16[416,128]{1,0:T(8,128)(2,1)S(1)} %get-tuple-element.57), channel_id=1, source_target_pairs={{0,4},{4,8},{8,12},{12,0},{1,5},{5,9},{9,13},{13,1},{2,6},{6,10},{... | collective-permute-start | bytes 319496 | tf_op jit(solution)/shard_map/ppermute | solution.py:531
  65.6 7.8 %collective-permute-start.15 = (bf16[256,128]{1,0:T(8,128)(2,1)S(1)}, bf16[256,128]{1,0:T(8,128)(2,1)S(1)}, u32[]{:S(2)}, u32[]{:S(2)}) collective-permute-start(bf16[256,128]{1,0:T(8,128)(2,1)S(1)} %get-tuple-element.61.refs_1_), channel_id=1, source_target_pairs={{0,1},{1,0},{2,3},{3,2},{4,5},{5,4},{6,7},{7,6},{8,9},{9,8},{10,11... | collective-permute-start | bytes 196616 | tf_op jit(solution)/shard_map/ppermute | solution.py:527
  75.1 23.0 %collective-permute-start.16 = (bf16[256,1024]{1,0:T(8,128)(2,1)}, bf16[256,1024]{1,0:T(8,128)(2,1)}, u32[]{:S(2)}, u32[]{:S(2)}) collective-permute-start(bf16[256,1024]{1,0:T(8,128)(2,1)} %get-tuple-element.67), channel_id=1, source_target_pairs={{0,2},{2,0},{1,3},{3,1},{4,6},{6,4},{5,7},{7,5},{8,10},{10,8},{9,1... | collective-permute-start | bytes 1572872 | tf_op jit(solution)/shard_map/ppermute | solution.py:527
  78.7 24.1 %all-to-all-start.1 = ((bf16[16,128,256]{2,1,0:T(8,128)(2,1)}), bf16[16,128,256]{2,1,0:T(8,128)(2,1)S(1)}, u32[]{:S(2)}, u32[]{:S(2)}) async-start(bf16[16,128,256]{2,1,0:T(8,128)(2,1)} %bitcast.13), calls=%async_computation.1 | async-start | bytes 2097152 | tf_op jit(solution)/shard_map/all_to_all | solution.py:651
  85.9 7.7 %collective-permute-start.17 = (bf16[256,128]{1,0:T(8,128)(2,1)S(1)}, bf16[256,128]{1,0:T(8,128)(2,1)S(1)}, u32[]{:S(2)}, u32[]{:S(2)}) collective-permute-start(bf16[256,128]{1,0:T(8,128)(2,1)S(1)} %get-tuple-element.68), channel_id=1, source_target_pairs={{0,12},{4,0},{8,4},{12,8},{1,13},{5,1},{9,5},{13,9},{2,14},{6,2},{... | collective-permute-start | bytes 196616 | tf_op jit(solution)/shard_map/ppermute | solution.py:531
  87.1 10.1 %collective-permute-start.18 = (bf16[256,128]{1,0:T(8,128)(2,1)S(1)}, bf16[256,128]{1,0:T(8,128)(2,1)S(1)}, u32[]{:S(2)}, u32[]{:S(2)}) collective-permute-start(bf16[256,128]{1,0:T(8,128)(2,1)S(1)} %get-tuple-element.69), channel_id=1, source_target_pairs={{0,8},{4,12},{8,0},{12,4},{1,9},{5,13},{9,1},{13,5},{2,10},{6,14},... | collective-permute-start | bytes 196616 | tf_op jit(solution)/shard_map/ppermute | solution.py:531
  90.6 7.5 %collective-permute-start.19 = (bf16[256,128]{1,0:T(8,128)(2,1)S(1)}, bf16[256,128]{1,0:T(8,128)(2,1)S(1)}, u32[]{:S(2)}, u32[]{:S(2)}) collective-permute-start(bf16[256,128]{1,0:T(8,128)(2,1)S(1)} %get-tuple-element.70), channel_id=1, source_target_pairs={{0,4},{4,8},{8,12},{12,0},{1,5},{5,9},{9,13},{13,1},{2,6},{6,10},{... | collective-permute-start | bytes 196616 | tf_op jit(solution)/shard_map/ppermute | solution.py:531
  90.8 12.0 %collective-permute-start.20 = (bf16[4,96,128]{2,1,0:T(8,128)(2,1)S(1)}, bf16[4,96,128]{2,1,0:T(8,128)(2,1)S(1)}, u32[]{:S(2)}, u32[]{:S(2)}) collective-permute-start(bf16[4,96,128]{2,1,0:T(8,128)(2,1)S(1)} %get-tuple-element.78), channel_id=1, source_target_pairs={{16,0},{32,16},{48,32},{64,48},{80,64},{96,80},{112,96},{128,112},... | collective-permute-start | bytes 294920 | tf_op jit(solution)/shard_map/ppermute | solution.py:626
  98.0 4.8 %copy-start.3 = (f32[256,256]{1,0:T(8,128)S(1)}, f32[256,256]{1,0:T(8,128)}, u32[]{:S(2)}) copy-start(f32[256,256]{1,0:T(8,128)} %get-tuple-element.76.refs_4_) | copy-start | bytes 786436
  98.0 4.8 %copy-start.4 = (s32[64,4]{0,1:T(4,128)S(1)}, s32[64,4]{0,1:T(4,128)}, u32[]{:S(2)}) copy-start(s32[64,4]{0,1:T(4,128)} %param.13) | copy-start | bytes 3076
  98.0 4.8 %copy-start.5 = (s32[1,128]{1,0:T(1,128)S(1)}, s32[1,128]{1,0:T(1,128)}, u32[]{:S(2)}) copy-start(s32[1,128]{1,0:T(1,128)} %refs_2_.5) | copy-start | bytes 1540

commit v11 on v10

--- a/solution.py
+++ b/solution.py
@@ -527,6 +527,11 @@
     return lax.ppermute(a, axis, [(0, 1), (1, 0)])
 
 
+def turns(arrays, sign=1):
+    got = {d: turn(arrays[d - 1], sign * d) for d in (1, 3, 2)}
+    return [got[d] for d in (1, 2, 3)]
+
+
 def turn(a, by):
     return lax.ppermute(a, "zh", [(i, (i + by) % GROUP) for i in range(GROUP)])
 
@@ -569,7 +574,7 @@
         flops=3800000000,
     )
     kva = lax.all_to_all(kvb, plane, 0, 0, tiled=True).reshape(KEYS, 2 * HEAD)
-    qs = [q0] + [turn(sent[d - 1], d) for d in (1, 2, 3)]
+    qs = [q0] + turns(sent)
     up_zc = swap(after(up_z, last), "c")
     g0, g = call(
         grad_kernel,
@@ -584,7 +589,7 @@
         name="attention_grad",
         raw=[1, 5],
     )
-    gs = [g0] + [turn(g0, d) for d in (1, 2, 3)]
+    gs = [g0] + turns([g0] * 3)
     o_s, far, dq_s, dkv_s = call(
         strided_kernel,
         [
@@ -607,7 +612,7 @@
         raw=[10, 11],
     )
     weight_c = swap(after(out_weight, obs[0]), "c")
-    oas = [obs[0]] + [turn(obs[d], -d) for d in (1, 2, 3)]
+    oas = [obs[0]] + turns(obs[1:], -1)
     acc_out, fixed_w, fixed_wc = call(
         project_strided_kernel,
         [sds((2, TOK, quarter), F32)] + [sds((2, HEAD, quarter))] * 2,
@@ -651,7 +656,7 @@
     dkva = lax.all_to_all(
         after(dkv, keep).reshape(ROWS, SUMM, 2 * HEAD), plane, 0, 0, tiled=True
     ).reshape(KEYS, 2 * HEAD)
-    dqs = [turn(dqs[d - 1], -d) for d in (1, 2, 3)]
+    dqs = turns(dqs, -1)
     layer_out, query_grad = call(
         output_kernel,
         [sds((TOK, quarter)), sds((TOK, width))],

time: 106 us -> 106 us (level)
  no operation moved by 1% of the time
where the time goes in v11:
time: 106 us; the launch traced here: 105 us
  starting transfers between devices  51.7 us (49%)
  Pallas kernels  35 us (33%)
  waiting for transfers between devices  17.1 us (16%)
    pallas_call x11, Pallas kernels, call(): pl.pallas_call(body, out_shape=tuple((pltpu.HBM(s.shape, s.dtype) if i in...  35 us
    ppermute x12, starting transfers between devices, turn(): return lax.ppermute(a, 'zh', [(i, (i + by) % GROUP) for i in range(GROUP)])  24.3 us
    ppermute x12, waiting for transfers between devices, turn(): return lax.ppermute(a, 'zh', [(i, (i + by) % GROUP) for i in range(GROUP)])  12.5 us
    all_to_all x1, starting transfers between devices, shards(): kva = lax.all_to_all(kvb, plane, 0, 0, tiled=True).reshape(KEYS, 2 * HEAD)  7.31 us
    all_to_all x1, starting transfers between devices, shards(): lax.all_to_all(after(dkv, keep).reshape(ROWS, SUMM, 2 * HEAD), plane, 0,...  7.22 us
    ppermute x7, starting transfers between devices, swap(): return lax.ppermute(a, axis, [(0, 1), (1, 0)])  7.06 us
    ppermute x1, starting transfers between devices, shards(): before = lax.ppermute(picks, plane, [(i, i + 1) for i in range(ROWS - 1)])  3.06 us
    ppermute x1, starting transfers between devices, shards(): back = lax.ppermute(sent, plane, [(i + 1, i) for i in range(ROWS - 1)])  2.75 us
  transfers between devices with their start and end apart: 23, of which 9 were waited for; matrix products, arithmetic and copies ran while one was open for 0% of the time, Pallas kernels for 23%

profile of v11, /device:TPU:24, one launch (start us, length us, event | category | flops | bytes accessed | tf_op | source)
XLA Modules:
  0.0 104.7 jit_solution(3974155475599956639)
XLA Ops:
  0.6 2.0 %collective-permute-start.5 = (bf16[256,1024]{1,0:T(8,128)(2,1)}, bf16[256,1024]{1,0:T(8,128)(2,1)S(1)}, u32[]{:S(2)}, u32[]{:S(2)}) collective-permute-start(bf16[256,1024]{1,0:T(8,128)(2,1)} %refs_1_.2), channel_id=1, source_target_pairs={{0,2},{2,0},{1,3},{3,1},{4,6},{6,4},{5,7},{7,5},{8,10},{10,8},{9,1... | collective-permute-start | bytes 1572872 | tf_op jit(solution)/shard_map/ppermute | solution.py:527
  2.7 3.5 %pick_rows.1 = (bf16[16,128,256]{2,1,0:T(8,128)(2,1)}, bf16[256,128]{1,0:T(8,128)(2,1)S(1)}, bf16[4,96,128]{2,1,0:T(8,128)(2,1)S(1)}) custom-call(s32[4]{0:T(128)S(1)} %pad_add_fusion.refs_0_, s32[4,64]{1,0:T(4,128)} %bitcast.11, s32[1,128]{1,0:T(1,128)} %refs_2_.5, bf16[256,512]{1,0:T(8,128)(2,1)} %refs_10_.3, bf16[256,512]{1,0:T(8,128)(2,1)} %refs_11_.3, ...), custom_call_target="tpu_custom_call" | custom-call | flops 1 | bytes 1 | tf_op jit(solution)/shard_map/pick_rows/pallas_call | solution.py:111
  6.2 3.1 %collective-permute-start = (bf16[4,96,128]{2,1,0:T(8,128)(2,1)S(1)}, bf16[4,96,128]{2,1,0:T(8,128)(2,1)S(1)}, u32[]{:S(2)}, u32[]{:S(2)}) collective-permute-start(bf16[4,96,128]{2,1,0:T(8,128)(2,1)S(1)} %get-tuple-element.44.refs_2_), channel_id=1, source_target_pairs={{0,16},{16,32},{32,48},{48,64},{64,80},{80,96},{96,112},{112,128},... | collective-permute-start | bytes 294920 | tf_op jit(solution)/shard_map/ppermute | solution.py:568
  9.3 7.3 %all-to-all-start = ((bf16[16,128,256]{2,1,0:T(8,128)(2,1)}), bf16[16,128,256]{2,1,0:T(8,128)(2,1)S(1)}, u32[]{:S(2)}, u32[]{:S(2)}) async-start(bf16[16,128,256]{2,1,0:T(8,128)(2,1)} %get-tuple-element.51), calls=%async_computation | async-start | bytes 2097152 | tf_op jit(solution)/shard_map/all_to_all | solution.py:576
  17.8 3.3 %collective-permute-start.1 = (bf16[352,128]{1,0:T(8,128)(2,1)S(1)}, bf16[352,128]{1,0:T(8,128)(2,1)S(1)}, u32[]{:S(2)}, u32[]{:S(2)}) collective-permute-start(bf16[352,128]{1,0:T(8,128)(2,1)S(1)} %get-tuple-element.45), channel_id=1, source_target_pairs={{0,4},{4,8},{8,12},{12,0},{1,5},{5,9},{9,13},{13,1},{2,6},{6,10},{... | collective-permute-start | bytes 270344 | tf_op jit(solution)/shard_map/ppermute | solution.py:536
  21.1 4.5 %collective-permute-start.2 = (bf16[352,128]{1,0:T(8,128)(2,1)S(1)}, bf16[352,128]{1,0:T(8,128)(2,1)S(1)}, u32[]{:S(2)}, u32[]{:S(2)}) collective-permute-start(bf16[352,128]{1,0:T(8,128)(2,1)S(1)} %get-tuple-element.46), channel_id=1, source_target_pairs={{0,8},{4,12},{8,0},{12,4},{1,9},{5,13},{9,1},{13,5},{2,10},{6,14},... | collective-permute-start | bytes 270344 | tf_op jit(solution)/shard_map/ppermute | solution.py:536
  25.6 2.7 %collective-permute-start.3 = (bf16[352,128]{1,0:T(8,128)(2,1)S(1)}, bf16[352,128]{1,0:T(8,128)(2,1)S(1)}, u32[]{:S(2)}, u32[]{:S(2)}) collective-permute-start(bf16[352,128]{1,0:T(8,128)(2,1)S(1)} %get-tuple-element.47), channel_id=1, source_target_pairs={{0,12},{4,0},{8,4},{12,8},{1,13},{5,1},{9,5},{13,9},{2,14},{6,2},{... | collective-permute-start | bytes 270344 | tf_op jit(solution)/shard_map/ppermute | solution.py:536
  28.2 4.1 %attention_grad.1 = (bf16[256,128]{1,0:T(8,128)(2,1)S(1)}, bf16[256,512]{1,0:T(8,128)(2,1)S(1)}) custom-call(s32[4]{0:T(128)S(1)} %pad_add_fusion.refs_0_, bf16[256,1024]{1,0:T(8,128)(2,1)} %refs_1_.2, bf16[256,1024]{1,0:T(8,128)(2,1)S(1)} %collective-permute-done.4.refs_2_, bf16[256,1024]{1,0:T(8,128)(2,1)S(1)} %collective-permute-done.5.refs_3_, ...), custom_call_target="tpu_custom_call" | custom-call | flops 1 | bytes 1 | tf_op jit(solution)/shard_map/attention_grad/pallas_call | solution.py:111
  32.5 3.8 %collective-permute-start.8 = (bf16[256,128]{1,0:T(8,128)(2,1)S(1)}, bf16[256,128]{1,0:T(8,128)(2,1)S(1)}, u32[]{:S(2)}, u32[]{:S(2)}) collective-permute-start(bf16[256,128]{1,0:T(8,128)(2,1)S(1)} %get-tuple-element.50.refs_5_), channel_id=1, source_target_pairs={{0,8},{4,12},{8,0},{12,4},{1,9},{5,13},{9,1},{13,5},{2,10},{6,14},... | collective-permute-start | bytes 196616 | tf_op jit(solution)/shard_map/ppermute | solution.py:536
  36.4 3.1 %strided_heads.1 = (bf16[256,384]{1,0:T(8,128)(2,1)S(1)}, bf16[4,96,128]{2,1,0:T(8,128)(2,1)S(1)}, bf16[256,384]{1,0:T(8,128)(2,1)S(1)}, f32[256,768]{1,0:T(8,128)S(1)}) custom-call(s32[4]{0:T(128)S(1)} %pad_add_fusion.refs_0_, bf16[256,512]{1,0:T(8,128)(2,1)S(1)} %copy-done.2, bf16[256,512]{1,0:T(8,128)(2,1)S(1)} %copy-done, ...), custom_call_target="tpu_custom_call" | custom-call | flops 1 | bytes 1 | tf_op jit(solution)/shard_map/strided_heads/pallas_call | solution.py:111
  39.5 1.6 %collective-permute-done.8.refs_7_ = bf16[256,128]{1,0:T(8,128)(2,1)S(1)} collective-permute-done((bf16[256,128]{1,0:T(8,128)(2,1)S(1)}, bf16[256,128]{1,0:T(8,128)(2,1)S(1)}, u32[]{:S(2)}, u32[]{:S(2)}) %collective-permute-start.8) | collective-permute-done | bytes 65568 | tf_op jit(solution)/shard_map/ppermute | solution.py:536
  41.1 2.9 %collective-permute-done.7.refs_6_ = bf16[256,128]{1,0:T(8,128)(2,1)S(1)} collective-permute-done((bf16[256,128]{1,0:T(8,128)(2,1)S(1)}, bf16[256,128]{1,0:T(8,128)(2,1)S(1)}, u32[]{:S(2)}, u32[]{:S(2)}) %collective-permute-start.7) | collective-permute-done | bytes 65568 | tf_op jit(solution)/shard_map/ppermute | solution.py:536
  44.0 6.3 %fixed_forward.1 = (bf16[416,128]{1,0:T(8,128)(2,1)S(1)}, bf16[416,128]{1,0:T(8,128)(2,1)S(1)}, bf16[416,128]{1,0:T(8,128)(2,1)S(1)}, bf16[416,128]{1,0:T(8,128)(2,1)S(1)}) custom-call(s32[4]{0:T(128)S(1)} %pad_add_fusion.refs_0_, bf16[256,128]{1,0:T(8,128)(2,1)S(1)} %get-tuple-element.43.refs_1_, ...), custom_call_target="tpu_custom_call" | custom-call | flops 1 | bytes 1 | tf_op jit(solution)/shard_map/fixed_forward/pallas_call | solution.py:111
  50.8 1.3 %collective-permute-start.10 = (bf16[416,128]{1,0:T(8,128)(2,1)S(1)}, bf16[416,128]{1,0:T(8,128)(2,1)S(1)}, u32[]{:S(2)}, u32[]{:S(2)}) collective-permute-start(bf16[416,128]{1,0:T(8,128)(2,1)S(1)} %get-tuple-element.55), channel_id=1, source_target_pairs={{0,12},{4,0},{8,4},{12,8},{1,13},{5,1},{9,5},{13,9},{2,14},{6,2},{... | collective-permute-start | bytes 319496 | tf_op jit(solution)/shard_map/ppermute | solution.py:536
  52.1 3.4 %collective-permute-start.11 = (bf16[416,128]{1,0:T(8,128)(2,1)S(1)}, bf16[416,128]{1,0:T(8,128)(2,1)S(1)}, u32[]{:S(2)}, u32[]{:S(2)}) collective-permute-start(bf16[416,128]{1,0:T(8,128)(2,1)S(1)} %get-tuple-element.56), channel_id=1, source_target_pairs={{0,8},{4,12},{8,0},{12,4},{1,9},{5,13},{9,1},{13,5},{2,10},{6,14},... | collective-permute-start | bytes 319496 | tf_op jit(solution)/shard_map/ppermute | solution.py:536
  55.8 0.9 collective-permute-done.13.refs_2_
  56.7 1.3 %collective-permute-done.14.refs_4_ = bf16[512,4096]{1,0:T(8,128)(2,1)S(1)} collective-permute-done((bf16[512,4096]{1,0:T(8,128)(2,1)}, bf16[512,4096]{1,0:T(8,128)(2,1)S(1)}, u32[]{:S(2)}, u32[]{:S(2)}) %collective-permute-start.14) | collective-permute-done | bytes 4194336 | tf_op jit(solution)/shard_map/ppermute | solution.py:527
  58.0 3.2 %project_strided.1 = (f32[2,256,1024]{2,1,0:T(8,128)S(1)}, bf16[2,128,1024]{2,1,0:T(8,128)(2,1)S(1)}, bf16[2,128,1024]{2,1,0:T(8,128)(2,1)S(1)}) custom-call(s32[4]{0:T(128)S(1)} %pad_add_fusion.refs_0_, bf16[256,384]{1,0:T(8,128)(2,1)S(1)} %get-tuple-element.58.refs_1_, bf16[256,384]{1,0:T(8,128)(2,1)S(1)} %collective-permute-done.13.refs_2_, ...), custom_call_target="tpu_custom_call" | custom-call | flops 1 | bytes 1 | tf_op jit(solution)/shard_map/project_strided/pallas_call | solution.py:111
  61.2 2.8 %collective-permute-done.11.refs_3_ = bf16[416,128]{1,0:T(8,128)(2,1)S(1)} collective-permute-done((bf16[416,128]{1,0:T(8,128)(2,1)S(1)}, bf16[416,128]{1,0:T(8,128)(2,1)S(1)}, u32[]{:S(2)}, u32[]{:S(2)}) %collective-permute-start.11) | collective-permute-done | bytes 106528 | tf_op jit(solution)/shard_map/ppermute | solution.py:536
  64.7 0.8 combine.1
  65.9 7.4 %fixed_backward.1 = (bf16[2048,256]{1,0:T(8,128)(2,1)}, bf16[256,128]{1,0:T(8,128)(2,1)S(1)}, bf16[256,128]{1,0:T(8,128)(2,1)S(1)}, bf16[256,128]{1,0:T(8,128)(2...) custom-call(s32[4]{0:T(128)S(1)} %pad_add_fusion.refs_0_, bf16[256,128]{1,0:T(8,128)(2,1)S(1)} %get-tuple-element.43.refs_1_, ...), custom_call_target="tpu_custom_call" | custom-call | flops 1 | bytes 1 | tf_op jit(solution)/shard_map/fixed_backward/pallas_call | solution.py:111
  73.3 1.8 %project_fixed.1 = (bf16[256,1024]{1,0:T(8,128)(2,1)}, bf16[256,1024]{1,0:T(8,128)(2,1)S(1)}) custom-call(s32[4]{0:T(128)S(1)} %pad_add_fusion.refs_0_, bf16[256,128]{1,0:T(8,128)(2,1)S(1)} %get-tuple-element.61.refs_1_, bf16[256,128]{1,0:T(8,128)(2,1)S(1)} %collective-permute-done.15.refs_2_, f32[2,256,1024]{2,1,0:T(8,128)S(1)} %get-tuple-element.60.refs_5_.refs_3_, ...), custom_call_target="tpu_custom_call" | custom-call | flops 1 | bytes 1 | tf_op jit(solution)/shard_map/project_fixed/pallas_call | solution.py:111
  75.1 3.6 %collective-permute-start.16 = (bf16[256,1024]{1,0:T(8,128)(2,1)}, bf16[256,1024]{1,0:T(8,128)(2,1)}, u32[]{:S(2)}, u32[]{:S(2)}) collective-permute-start(bf16[256,1024]{1,0:T(8,128)(2,1)} %get-tuple-element.67), channel_id=1, source_target_pairs={{0,2},{2,0},{1,3},{3,1},{4,6},{6,4},{5,7},{7,5},{8,10},{10,8},{9,1... | collective-permute-start | bytes 1572872 | tf_op jit(solution)/shard_map/ppermute | solution.py:527
  78.7 7.2 %all-to-all-start.1 = ((bf16[16,128,256]{2,1,0:T(8,128)(2,1)}), bf16[16,128,256]{2,1,0:T(8,128)(2,1)S(1)}, u32[]{:S(2)}, u32[]{:S(2)}) async-start(bf16[16,128,256]{2,1,0:T(8,128)(2,1)} %bitcast.13), calls=%async_computation.1 | async-start | bytes 2097152 | tf_op jit(solution)/shard_map/all_to_all | solution.py:656
  85.9 1.2 %collective-permute-start.17 = (bf16[256,128]{1,0:T(8,128)(2,1)S(1)}, bf16[256,128]{1,0:T(8,128)(2,1)S(1)}, u32[]{:S(2)}, u32[]{:S(2)}) collective-permute-start(bf16[256,128]{1,0:T(8,128)(2,1)S(1)} %get-tuple-element.68), channel_id=1, source_target_pairs={{0,12},{4,0},{8,4},{12,8},{1,13},{5,1},{9,5},{13,9},{2,14},{6,2},{... | collective-permute-start | bytes 196616 | tf_op jit(solution)/shard_map/ppermute | solution.py:536
  87.1 3.5 %collective-permute-start.18 = (bf16[256,128]{1,0:T(8,128)(2,1)S(1)}, bf16[256,128]{1,0:T(8,128)(2,1)S(1)}, u32[]{:S(2)}, u32[]{:S(2)}) collective-permute-start(bf16[256,128]{1,0:T(8,128)(2,1)S(1)} %get-tuple-element.69), channel_id=1, source_target_pairs={{0,8},{4,12},{8,0},{12,4},{1,9},{5,13},{9,1},{13,5},{2,10},{6,14},... | collective-permute-start | bytes 196616 | tf_op jit(solution)/shard_map/ppermute | solution.py:536
  90.8 2.8 %collective-permute-start.20 = (bf16[4,96,128]{2,1,0:T(8,128)(2,1)S(1)}, bf16[4,96,128]{2,1,0:T(8,128)(2,1)S(1)}, u32[]{:S(2)}, u32[]{:S(2)}) collective-permute-start(bf16[4,96,128]{2,1,0:T(8,128)(2,1)S(1)} %get-tuple-element.78), channel_id=1, source_target_pairs={{16,0},{32,16},{48,32},{64,48},{80,64},{96,80},{112,96},{128,112},... | collective-permute-start | bytes 294920 | tf_op jit(solution)/shard_map/ppermute | solution.py:631
  93.6 3.6 %collective-permute-done.18.refs_5_ = bf16[256,128]{1,0:T(8,128)(2,1)S(1)} collective-permute-done((bf16[256,128]{1,0:T(8,128)(2,1)S(1)}, bf16[256,128]{1,0:T(8,128)(2,1)S(1)}, u32[]{:S(2)}, u32[]{:S(2)}) %collective-permute-start.18) | collective-permute-done | bytes 65568 | tf_op jit(solution)/shard_map/ppermute | solution.py:536
  97.2 0.9 collective-permute-done.19.refs_6_
  98.0 2.3 %join_output.1 = (bf16[256,1024]{1,0:T(8,128)(2,1)}, bf16[256,512]{1,0:T(8,128)(2,1)}) custom-call(s32[4]{0:T(128)S(1)} %pad_add_fusion.refs_0_, bf16[256,1024]{1,0:T(8,128)(2,1)S(1)} %get-tuple-element.66.refs_1_, bf16[256,1024]{1,0:T(8,128)(2,1)} %collective-permute-done.16.refs_2_, f32[128,256]{1,0:T(8,128)S(1)} %get-tuple-element.65.refs_6_.refs_3_, ...), custom_call_target="tpu_custom_call" | custom-call | flops 7000000000 | bytes 1 | tf_op jit(solution)/shard_map/join_output/pallas_call | solution.py:111
  100.4 2.4 %collective-permute-done.20.refs_6_ = bf16[4,96,128]{2,1,0:T(8,128)(2,1)S(1)} collective-permute-done((bf16[4,96,128]{2,1,0:T(8,128)(2,1)S(1)}, bf16[4,96,128]{2,1,0:T(8,128)(2,1)S(1)}, u32[]{:S(2)}, u32[]{:S(2)}) %collective-permute-start.20) | collective-permute-done | bytes 98336 | tf_op jit(solution)/shard_map/ppermute | solution.py:631
  102.8 1.9 %join_key_grads.1 = (bf16[256,512]{1,0:T(8,128)(2,1)}, bf16[256,512]{1,0:T(8,128)(2,1)}) custom-call(s32[4]{0:T(128)S(1)} %pad_add_fusion.refs_0_, s32[4,64]{1,0:T(4,128)S(1)} %bitcast.12, s32[1,128]{1,0:T(1,128)S(1)} %copy-done.5, bf16[2048,256]{1,0:T(8,128)(2,1)S(1)} %bitcast.10, f32[256,256]{1,0:T(8,128)S(1)} %copy-done.3, ...), custom_call_target="tpu_custom_call" | custom-call | flops 1 | bytes 1 | tf_op jit(solution)/shard_map/join_key_grads/pallas_call | solution.py:111
  (38 shorter events, 3.6 us)
Async XLA Ops:
  0.6 16.6 %collective-permute-start.5 = (bf16[256,1024]{1,0:T(8,128)(2,1)}, bf16[256,1024]{1,0:T(8,128)(2,1)S(1)}, u32[]{:S(2)}, u32[]{:S(2)}) collective-permute-start(bf16[256,1024]{1,0:T(8,128)(2,1)} %refs_1_.2), channel_id=1, source_target_pairs={{0,2},{2,0},{1,3},{3,1},{4,6},{6,4},{5,7},{7,5},{8,10},{10,8},{9,1... | collective-permute-start | bytes 1572872 | tf_op jit(solution)/shard_map/ppermute | solution.py:527
  6.2 10.4 %collective-permute-start = (bf16[4,96,128]{2,1,0:T(8,128)(2,1)S(1)}, bf16[4,96,128]{2,1,0:T(8,128)(2,1)S(1)}, u32[]{:S(2)}, u32[]{:S(2)}) collective-permute-start(bf16[4,96,128]{2,1,0:T(8,128)(2,1)S(1)} %get-tuple-element.44.refs_2_), channel_id=1, source_target_pairs={{0,16},{16,32},{32,48},{48,64},{64,80},{80,96},{96,112},{112,128},... | collective-permute-start | bytes 294920 | tf_op jit(solution)/shard_map/ppermute | solution.py:568
  9.3 30.2 %all-to-all-start = ((bf16[16,128,256]{2,1,0:T(8,128)(2,1)}), bf16[16,128,256]{2,1,0:T(8,128)(2,1)S(1)}, u32[]{:S(2)}, u32[]{:S(2)}) async-start(bf16[16,128,256]{2,1,0:T(8,128)(2,1)} %get-tuple-element.51), calls=%async_computation | async-start | bytes 2097152 | tf_op jit(solution)/shard_map/all_to_all | solution.py:576
  16.6 11.7 %collective-permute-start.4 = (bf16[256,1024]{1,0:T(8,128)(2,1)}, bf16[256,1024]{1,0:T(8,128)(2,1)S(1)}, u32[]{:S(2)}, u32[]{:S(2)}) collective-permute-start(bf16[256,1024]{1,0:T(8,128)(2,1)} %refs_1_.2), channel_id=1, source_target_pairs={{0,1},{1,0},{2,3},{3,2},{4,5},{5,4},{6,7},{7,6},{8,9},{9,8},{10,11... | collective-permute-start | bytes 1572872 | tf_op jit(solution)/shard_map/ppermute | solution.py:527
  17.2 19.1 %copy-start = (bf16[256,512]{1,0:T(8,128)(2,1)S(1)}, bf16[256,512]{1,0:T(8,128)(2,1)}, u32[]{:S(2)}) copy-start(bf16[256,512]{1,0:T(8,128)(2,1)} %refs_10_.3) | copy-start | bytes 786436
  17.2 19.1 %copy-start.1 = (bf16[256,512]{1,0:T(8,128)(2,1)S(1)}, bf16[256,512]{1,0:T(8,128)(2,1)}, u32[]{:S(2)}) copy-start(bf16[256,512]{1,0:T(8,128)(2,1)} %refs_11_.3) | copy-start | bytes 786436
  17.2 19.1 %copy-start.2 = (bf16[256,512]{1,0:T(8,128)(2,1)S(1)}, bf16[256,512]{1,0:T(8,128)(2,1)}, u32[]{:S(2)}) copy-start(bf16[256,512]{1,0:T(8,128)(2,1)} %refs_1_.3) | copy-start | bytes 786436
  17.2 11.0 %collective-permute-start.6 = (bf16[256,1024]{1,0:T(8,128)(2,1)S(1)}, bf16[256,1024]{1,0:T(8,128)(2,1)S(1)}, u32[]{:S(2)}, u32[]{:S(2)}) collective-permute-start(bf16[256,1024]{1,0:T(8,128)(2,1)S(1)} %collective-permute-done.5.refs_3_), channel_id=1, source_target_pairs={{0,1},{1,0},{2,3},{3,2},{4,5},{5,4},{6,7},{7,6},{8,9},{9,8},{10,11... | collective-permute-start | bytes 1572872 | tf_op jit(solution)/shard_map/ppermute | solution.py:527
  17.8 18.5 %collective-permute-start.1 = (bf16[352,128]{1,0:T(8,128)(2,1)S(1)}, bf16[352,128]{1,0:T(8,128)(2,1)S(1)}, u32[]{:S(2)}, u32[]{:S(2)}) collective-permute-start(bf16[352,128]{1,0:T(8,128)(2,1)S(1)} %get-tuple-element.45), channel_id=1, source_target_pairs={{0,4},{4,8},{8,12},{12,0},{1,5},{5,9},{9,13},{13,1},{2,6},{6,10},{... | collective-permute-start | bytes 270344 | tf_op jit(solution)/shard_map/ppermute | solution.py:536
  21.1 15.2 %collective-permute-start.2 = (bf16[352,128]{1,0:T(8,128)(2,1)S(1)}, bf16[352,128]{1,0:T(8,128)(2,1)S(1)}, u32[]{:S(2)}, u32[]{:S(2)}) collective-permute-start(bf16[352,128]{1,0:T(8,128)(2,1)S(1)} %get-tuple-element.46), channel_id=1, source_target_pairs={{0,8},{4,12},{8,0},{12,4},{1,9},{5,13},{9,1},{13,5},{2,10},{6,14},... | collective-permute-start | bytes 270344 | tf_op jit(solution)/shard_map/ppermute | solution.py:536
  25.6 10.8 %collective-permute-start.3 = (bf16[352,128]{1,0:T(8,128)(2,1)S(1)}, bf16[352,128]{1,0:T(8,128)(2,1)S(1)}, u32[]{:S(2)}, u32[]{:S(2)}) collective-permute-start(bf16[352,128]{1,0:T(8,128)(2,1)S(1)} %get-tuple-element.47), channel_id=1, source_target_pairs={{0,12},{4,0},{8,4},{12,8},{1,13},{5,1},{9,5},{13,9},{2,14},{6,2},{... | collective-permute-start | bytes 270344 | tf_op jit(solution)/shard_map/ppermute | solution.py:536
  32.4 7.0 %collective-permute-start.9 = (bf16[256,128]{1,0:T(8,128)(2,1)S(1)}, bf16[256,128]{1,0:T(8,128)(2,1)S(1)}, u32[]{:S(2)}, u32[]{:S(2)}) collective-permute-start(bf16[256,128]{1,0:T(8,128)(2,1)S(1)} %get-tuple-element.50.refs_5_), channel_id=1, source_target_pairs={{0,12},{4,0},{8,4},{12,8},{1,13},{5,1},{9,5},{13,9},{2,14},{6,2},{... | collective-permute-start | bytes 196616 | tf_op jit(solution)/shard_map/ppermute | solution.py:536
  32.5 8.6 %collective-permute-start.8 = (bf16[256,128]{1,0:T(8,128)(2,1)S(1)}, bf16[256,128]{1,0:T(8,128)(2,1)S(1)}, u32[]{:S(2)}, u32[]{:S(2)}) collective-permute-start(bf16[256,128]{1,0:T(8,128)(2,1)S(1)} %get-tuple-element.50.refs_5_), channel_id=1, source_target_pairs={{0,8},{4,12},{8,0},{12,4},{1,9},{5,13},{9,1},{13,5},{2,10},{6,14},... | collective-permute-start | bytes 196616 | tf_op jit(solution)/shard_map/ppermute | solution.py:536
  36.3 7.6 %collective-permute-start.7 = (bf16[256,128]{1,0:T(8,128)(2,1)S(1)}, bf16[256,128]{1,0:T(8,128)(2,1)S(1)}, u32[]{:S(2)}, u32[]{:S(2)}) collective-permute-start(bf16[256,128]{1,0:T(8,128)(2,1)S(1)} %get-tuple-element.50.refs_5_), channel_id=1, source_target_pairs={{0,4},{4,8},{8,12},{12,0},{1,5},{5,9},{9,13},{13,1},{2,6},{6,10},{... | collective-permute-start | bytes 196616 | tf_op jit(solution)/shard_map/ppermute | solution.py:536
  50.2 7.7 %collective-permute-start.14 = (bf16[512,4096]{1,0:T(8,128)(2,1)}, bf16[512,4096]{1,0:T(8,128)(2,1)S(1)}, u32[]{:S(2)}, u32[]{:S(2)}) collective-permute-start(bf16[512,4096]{1,0:T(8,128)(2,1)} %refs_3_.5), channel_id=1, source_target_pairs={{0,1},{1,0},{2,3},{3,2},{4,5},{5,4},{6,7},{7,6},{8,9},{9,8},{10,11... | collective-permute-start | bytes 12582920 | tf_op jit(solution)/shard_map/ppermute | solution.py:527
  50.3 6.4 %collective-permute-start.13 = (bf16[256,384]{1,0:T(8,128)(2,1)S(1)}, bf16[256,384]{1,0:T(8,128)(2,1)S(1)}, u32[]{:S(2)}, u32[]{:S(2)}) collective-permute-start(bf16[256,384]{1,0:T(8,128)(2,1)S(1)} %get-tuple-element.58.refs_1_), channel_id=1, source_target_pairs={{0,1},{1,0},{2,3},{3,2},{4,5},{5,4},{6,7},{7,6},{8,9},{9,8},{10,11... | collective-permute-start | bytes 589832 | tf_op jit(solution)/shard_map/ppermute | solution.py:527
  50.8 10.4 %collective-permute-start.10 = (bf16[416,128]{1,0:T(8,128)(2,1)S(1)}, bf16[416,128]{1,0:T(8,128)(2,1)S(1)}, u32[]{:S(2)}, u32[]{:S(2)}) collective-permute-start(bf16[416,128]{1,0:T(8,128)(2,1)S(1)} %get-tuple-element.55), channel_id=1, source_target_pairs={{0,12},{4,0},{8,4},{12,8},{1,13},{5,1},{9,5},{13,9},{2,14},{6,2},{... | collective-permute-start | bytes 319496 | tf_op jit(solution)/shard_map/ppermute | solution.py:536
  52.1 11.9 %collective-permute-start.11 = (bf16[416,128]{1,0:T(8,128)(2,1)S(1)}, bf16[416,128]{1,0:T(8,128)(2,1)S(1)}, u32[]{:S(2)}, u32[]{:S(2)}) collective-permute-start(bf16[416,128]{1,0:T(8,128)(2,1)S(1)} %get-tuple-element.56), channel_id=1, source_target_pairs={{0,8},{4,12},{8,0},{12,4},{1,9},{5,13},{9,1},{13,5},{2,10},{6,14},... | collective-permute-start | bytes 319496 | tf_op jit(solution)/shard_map/ppermute | solution.py:536
  55.5 9.3 %collective-permute-start.12 = (bf16[416,128]{1,0:T(8,128)(2,1)S(1)}, bf16[416,128]{1,0:T(8,128)(2,1)S(1)}, u32[]{:S(2)}, u32[]{:S(2)}) collective-permute-start(bf16[416,128]{1,0:T(8,128)(2,1)S(1)} %get-tuple-element.57), channel_id=1, source_target_pairs={{0,4},{4,8},{8,12},{12,0},{1,5},{5,9},{9,13},{13,1},{2,6},{6,10},{... | collective-permute-start | bytes 319496 | tf_op jit(solution)/shard_map/ppermute | solution.py:536
  65.6 7.8 %collective-permute-start.15 = (bf16[256,128]{1,0:T(8,128)(2,1)S(1)}, bf16[256,128]{1,0:T(8,128)(2,1)S(1)}, u32[]{:S(2)}, u32[]{:S(2)}) collective-permute-start(bf16[256,128]{1,0:T(8,128)(2,1)S(1)} %get-tuple-element.61.refs_1_), channel_id=1, source_target_pairs={{0,1},{1,0},{2,3},{3,2},{4,5},{5,4},{6,7},{7,6},{8,9},{9,8},{10,11... | collective-permute-start | bytes 196616 | tf_op jit(solution)/shard_map/ppermute | solution.py:527
  75.1 23.0 %collective-permute-start.16 = (bf16[256,1024]{1,0:T(8,128)(2,1)}, bf16[256,1024]{1,0:T(8,128)(2,1)}, u32[]{:S(2)}, u32[]{:S(2)}) collective-permute-start(bf16[256,1024]{1,0:T(8,128)(2,1)} %get-tuple-element.67), channel_id=1, source_target_pairs={{0,2},{2,0},{1,3},{3,1},{4,6},{6,4},{5,7},{7,5},{8,10},{10,8},{9,1... | collective-permute-start | bytes 1572872 | tf_op jit(solution)/shard_map/ppermute | solution.py:527
  78.7 24.1 %all-to-all-start.1 = ((bf16[16,128,256]{2,1,0:T(8,128)(2,1)}), bf16[16,128,256]{2,1,0:T(8,128)(2,1)S(1)}, u32[]{:S(2)}, u32[]{:S(2)}) async-start(bf16[16,128,256]{2,1,0:T(8,128)(2,1)} %bitcast.13), calls=%async_computation.1 | async-start | bytes 2097152 | tf_op jit(solution)/shard_map/all_to_all | solution.py:656
  85.9 7.7 %collective-permute-start.17 = (bf16[256,128]{1,0:T(8,128)(2,1)S(1)}, bf16[256,128]{1,0:T(8,128)(2,1)S(1)}, u32[]{:S(2)}, u32[]{:S(2)}) collective-permute-start(bf16[256,128]{1,0:T(8,128)(2,1)S(1)} %get-tuple-element.68), channel_id=1, source_target_pairs={{0,12},{4,0},{8,4},{12,8},{1,13},{5,1},{9,5},{13,9},{2,14},{6,2},{... | collective-permute-start | bytes 196616 | tf_op jit(solution)/shard_map/ppermute | solution.py:536
  87.1 10.1 %collective-permute-start.18 = (bf16[256,128]{1,0:T(8,128)(2,1)S(1)}, bf16[256,128]{1,0:T(8,128)(2,1)S(1)}, u32[]{:S(2)}, u32[]{:S(2)}) collective-permute-start(bf16[256,128]{1,0:T(8,128)(2,1)S(1)} %get-tuple-element.69), channel_id=1, source_target_pairs={{0,8},{4,12},{8,0},{12,4},{1,9},{5,13},{9,1},{13,5},{2,10},{6,14},... | collective-permute-start | bytes 196616 | tf_op jit(solution)/shard_map/ppermute | solution.py:536
  90.6 7.5 %collective-permute-start.19 = (bf16[256,128]{1,0:T(8,128)(2,1)S(1)}, bf16[256,128]{1,0:T(8,128)(2,1)S(1)}, u32[]{:S(2)}, u32[]{:S(2)}) collective-permute-start(bf16[256,128]{1,0:T(8,128)(2,1)S(1)} %get-tuple-element.70), channel_id=1, source_target_pairs={{0,4},{4,8},{8,12},{12,0},{1,5},{5,9},{9,13},{13,1},{2,6},{6,10},{... | collective-permute-start | bytes 196616 | tf_op jit(solution)/shard_map/ppermute | solution.py:536
  90.8 12.0 %collective-permute-start.20 = (bf16[4,96,128]{2,1,0:T(8,128)(2,1)S(1)}, bf16[4,96,128]{2,1,0:T(8,128)(2,1)S(1)}, u32[]{:S(2)}, u32[]{:S(2)}) collective-permute-start(bf16[4,96,128]{2,1,0:T(8,128)(2,1)S(1)} %get-tuple-element.78), channel_id=1, source_target_pairs={{16,0},{32,16},{48,32},{64,48},{80,64},{96,80},{112,96},{128,112},... | collective-permute-start | bytes 294920 | tf_op jit(solution)/shard_map/ppermute | solution.py:631
  98.0 4.8 %copy-start.3 = (f32[256,256]{1,0:T(8,128)S(1)}, f32[256,256]{1,0:T(8,128)}, u32[]{:S(2)}) copy-start(f32[256,256]{1,0:T(8,128)} %get-tuple-element.76.refs_4_) | copy-start | bytes 786436
  98.0 4.8 %copy-start.4 = (s32[64,4]{0,1:T(4,128)S(1)}, s32[64,4]{0,1:T(4,128)}, u32[]{:S(2)}) copy-start(s32[64,4]{0,1:T(4,128)} %param.13) | copy-start | bytes 3076
  98.0 4.8 %copy-start.5 = (s32[1,128]{1,0:T(1,128)S(1)}, s32[1,128]{1,0:T(1,128)}, u32[]{:S(2)}) copy-start(s32[1,128]{1,0:T(1,128)} %refs_2_.5) | copy-start | bytes 1540
